TPU v7x, 32 devices: a whole 2x2x4 slice. The times are simulated.
32 devices in a mesh: seq: 8 (over z, y), mp: 4 (over x, core).
Axes of the slice: x: 2, y: 2, z: 4, core: 2. Of those that a mesh axis runs over, the one named last changes fastest.
Arguments:
- inputs: bfloat16 [2048, 2560], P('seq'), may hold values from -6 to 6
- targets: bfloat16 [2048, 2560], P('seq'), may hold values from -6 to 6
- seq_ids: int32 [2048], P('seq'), may hold values from 0 to 1, as said below
- block_ids: int32 [2048], P('seq'), may hold values from 0 to 4, as said below
- attn_gain: bfloat16 [2560], P('seq'), may hold values from 0.5 to 1.5
- mlp_gain: bfloat16 [2560], P('seq'), may hold values from 0.5 to 1.5
- w_query: bfloat16 [2560, 2560], P('seq', 'mp'), may hold values from -0.125 to 0.125
- w_key: bfloat16 [2560, 640], P('seq', 'mp'), may hold values from -0.125 to 0.125
- w_value: bfloat16 [2560, 640], P('seq', 'mp'), may hold values from -0.125 to 0.125
- w_out: bfloat16 [2560, 2560], P('seq', 'mp'), may hold values from -2.5 to 2.5
- w_gate: bfloat16 [2560, 7168], P('seq', 'mp'), may hold values from -0.125 to 0.125
- w_up: bfloat16 [2560, 7168], P('seq', 'mp'), may hold values from -0.125 to 0.125
- w_down: bfloat16 [2560, 7168], P('seq', 'mp'), may hold values from -0.0625 to 0.0625
Outputs:
- layer_out: bfloat16 [2048, 2560], P('seq')
- input_grad: bfloat16 [2048, 2560], P('seq')
- grad_query: float32 [2560, 2560], P('seq', 'mp')
- grad_key: float32 [2560, 640], P('seq', 'mp')
- grad_value: float32 [2560, 640], P('seq', 'mp')
- grad_out: float32 [2560, 2560], P('seq', 'mp')
- grad_gate: float32 [2560, 7168], P('seq', 'mp')
- grad_up: float32 [2560, 7168], P('seq', 'mp')
- grad_down: float32 [2560, 7168], P('seq', 'mp')
- grad_attn_gain: float32 [2560], P('seq')
- grad_mlp_gain: float32 [2560], P('seq')
- rms_stream: float32 [], replicated
- rms_attn: float32 [], replicated
- rms_mlp: float32 [], replicated
Inputs may be any that keep to these rules, and one draw needn't show every extreme that they name: `seq_ids`: every index of seq holds 2 runs of 128 rows, one run of each sequence, in an order drawn for each index; the run of a sequence on index i holds its positions i * 128 to i * 128 + 127. `block_ids`: along a sequence's positions the block never falls, and no block holds more than 256 positions.
All inputs are finite; a program needn't handle non-finite values.
Results may differ from a plain program's by a relative error of at most 0.017.
Values may be sent and summed in bfloat16 or wider, within the bound.
No kernel may reach another device: no remote copies, remote signals or barrier semaphores. Data moves between devices by JAX's collectives and lax.ppermute only.
A program may use at most 192 MiB of HBM per device.

v0:
```python
import jax
import jax.numpy as jnp
from jax import lax
from jax.sharding import PartitionSpec as P

HEAD_DIM = 80
SPAN = 128


EPS = 1e-05
THETA = 1000000.0


def normed(value, gain):
    scale = lax.rsqrt(jnp.mean(value * value, axis=-1, keepdims=True) + EPS)
    return (value * scale * gain, scale)


def norm_back(grad, value, scale, gain):
    unit = value * scale
    gain_grad = jnp.sum(grad * unit, axis=0)
    scaled = grad * gain
    back = scale * (scaled - unit * jnp.mean(scaled * unit, axis=-1, keepdims=True))
    return (gain_grad, back)


def tables(place):
    half = HEAD_DIM // 2
    freq = THETA ** (-(jnp.arange(half, dtype=jnp.float32) * 2.0 / HEAD_DIM))
    angle = place[:, None] * freq[None, :]
    return (jnp.cos(angle), jnp.sin(angle))


def rotate(values, cosine, sine, sign):
    count = values.shape[0]
    heads = values.reshape(count, -1, HEAD_DIM)
    half = HEAD_DIM // 2
    first = heads[..., :half]
    second = heads[..., half:]
    cosine = cosine[:, None, :]
    sine = sine[:, None, :] * sign
    turned = jnp.concatenate(
        [first * cosine - second * sine, second * cosine + first * sine], axis=-1
    )
    return turned.reshape(count, -1)


def key_blocks(keys):
    key_all, value_all, seq_all, block_all = keys
    total = key_all.shape[0]
    width = 2048
    count = total // width
    return (
        key_all.reshape(count, width, -1, HEAD_DIM),
        value_all.reshape(count, width, -1, HEAD_DIM),
        seq_all.reshape(count, width),
        block_all.reshape(count, width),
    )


def scores_of(queries, kblock, sblock, bblock, seq_ids, block_ids):
    scores = jnp.einsum(
        "qhgd,nhd->qhgn", queries, kblock, preferred_element_type=jnp.float32
    ) * HEAD_DIM ** (-0.5)
    visible = (sblock[None, :] == seq_ids[:, None]) & (bblock[None, :] <= block_ids[:, None])
    return (scores, visible[:, None, None, :])


def on_device(
    inputs,
    targets,
    seq_ids,
    block_ids,
    attn_gain,
    mlp_gain,
    w_query,
    w_key,
    w_value,
    w_out,
    w_gate,
    w_up,
    w_down,
):
    rows = inputs.shape[0]
    full = (
        lax.all_gather(w_query, "seq", axis=0, tiled=True),
        lax.all_gather(w_key, "seq", axis=0, tiled=True),
        lax.all_gather(w_value, "seq", axis=0, tiled=True),
        lax.all_gather(w_out, "seq", axis=0, tiled=True),
        lax.all_gather(w_gate, "seq", axis=0, tiled=True),
        lax.all_gather(w_up, "seq", axis=0, tiled=True),
        lax.all_gather(w_down, "seq", axis=0, tiled=True),
        lax.all_gather(attn_gain, "seq", axis=0, tiled=True),
        lax.all_gather(mlp_gain, "seq", axis=0, tiled=True),
    )
    wq_full, wk_full, wv_full, wo_full, wg_full, wu_full, wd_full, gain_one, gain_two = full
    xin = inputs.astype(jnp.float32)
    first_f, scale_one = normed(xin, gain_one.astype(jnp.float32))
    first = first_f.astype(jnp.bfloat16)
    query = jnp.dot(first, wq_full, preferred_element_type=jnp.float32)
    key = jnp.dot(first, wk_full, preferred_element_type=jnp.float32)
    value = jnp.dot(first, wv_full, preferred_element_type=jnp.float32)
    kv_heads = key.shape[1] // HEAD_DIM
    group = query.shape[1] // key.shape[1]
    place = (lax.axis_index("seq") * SPAN + jnp.arange(rows, dtype=jnp.int32) % SPAN).astype(
        jnp.float32
    )
    cosine, sine = tables(place)
    query_r = rotate(query, cosine, sine, 1.0).astype(jnp.bfloat16)
    key_r = rotate(key, cosine, sine, 1.0).astype(jnp.bfloat16)
    value_r = value.astype(jnp.bfloat16)
    keys_all = (
        lax.all_gather(key_r, "seq", axis=0, tiled=True),
        lax.all_gather(value_r, "seq", axis=0, tiled=True),
        lax.all_gather(seq_ids, "seq", axis=0, tiled=True),
        lax.all_gather(block_ids, "seq", axis=0, tiled=True),
    )
    queries = query_r.reshape(rows, kv_heads, group, HEAD_DIM)
    blocks_in = key_blocks(keys_all)

    def totals_step(carry, blocks):
        top, total = carry
        kblock, vblock, sblock, bblock = blocks
        scores, visible = scores_of(queries, kblock, sblock, bblock, seq_ids, block_ids)
        masked = jnp.where(visible, scores, -1e30)
        new_top = jnp.maximum(top, masked.max(axis=-1))
        weights = jnp.where(visible, jnp.exp(masked - new_top[..., None]), 0.0)
        total = total * jnp.exp(top - new_top) + weights.sum(axis=-1)
        return ((new_top, total), None)

    start_top = jnp.full((rows, kv_heads, group), -1e30, jnp.float32)
    start_total = jnp.zeros((rows, kv_heads, group), jnp.float32)
    (top, total), unused = lax.scan(totals_step, (start_top, start_total), blocks_in)
    lse = top + jnp.log(total)

    def mix_step(acc, blocks):
        kblock, vblock, sblock, bblock = blocks
        scores, visible = scores_of(queries, kblock, sblock, bblock, seq_ids, block_ids)
        probs = jnp.where(visible, jnp.exp(scores - lse[..., None]), 0.0).astype(jnp.bfloat16)
        return (
            acc + jnp.einsum("qhgn,nhd->qhgd", probs, vblock, preferred_element_type=jnp.float32),
            None,
        )

    mixed_f32, unused = lax.scan(
        mix_step, jnp.zeros((rows, kv_heads, group, HEAD_DIM), jnp.float32), blocks_in
    )
    mixed = mixed_f32.reshape(rows, -1).astype(jnp.bfloat16)
    contract_last = (((1,), (1,)), ((), ()))
    contract_rows = (((0,), (0,)), ((), ()))
    branch_attn = lax.psum(
        lax.dot_general(mixed, wo_full, contract_last, preferred_element_type=jnp.float32).astype(
            jnp.bfloat16
        ),
        "mp",
    ).astype(jnp.float32)
    middle = xin + branch_attn
    second_f, scale_two = normed(middle, gain_two.astype(jnp.float32))
    second = second_f.astype(jnp.bfloat16)
    gate = jnp.dot(second, wg_full, preferred_element_type=jnp.float32)
    upper = jnp.dot(second, wu_full, preferred_element_type=jnp.float32)
    sigma = jax.nn.sigmoid(gate)
    silu_gate = gate * sigma
    hidden = (silu_gate * upper).astype(jnp.bfloat16)
    branch_mlp = lax.psum(
        lax.dot_general(hidden, wd_full, contract_last, preferred_element_type=jnp.float32).astype(
            jnp.bfloat16
        ),
        "mp",
    ).astype(jnp.float32)
    stream = middle + branch_mlp
    local_sums = (
        jnp.sum(stream * stream),
        jnp.sum(branch_attn * branch_attn),
        jnp.sum(branch_mlp * branch_mlp),
    )
    sums = lax.psum((local_sums[0], local_sums[1], local_sums[2]), "seq")
    entries = rows * lax.axis_size("seq") * inputs.shape[1]
    rms_stream = jnp.sqrt(sums[0] / entries + EPS)
    rms_attn = jnp.sqrt(sums[1] / entries + EPS)
    rms_mlp = jnp.sqrt(sums[2] / entries + EPS)
    full_back = (
        lax.all_gather(w_query, "seq", axis=0, tiled=True),
        lax.all_gather(w_key, "seq", axis=0, tiled=True),
        lax.all_gather(w_value, "seq", axis=0, tiled=True),
        lax.all_gather(w_out, "seq", axis=0, tiled=True),
        lax.all_gather(w_gate, "seq", axis=0, tiled=True),
        lax.all_gather(w_up, "seq", axis=0, tiled=True),
        lax.all_gather(w_down, "seq", axis=0, tiled=True),
        lax.all_gather(attn_gain, "seq", axis=0, tiled=True),
        lax.all_gather(mlp_gain, "seq", axis=0, tiled=True),
    )
    wq_b, wk_b, wv_b, wo_b, wg_b, wu_b, wd_b, gain_one_b, gain_two_b = full_back
    keys_back = (
        lax.all_gather(key_r, "seq", axis=0, tiled=True),
        lax.all_gather(value_r, "seq", axis=0, tiled=True),
        lax.all_gather(seq_ids, "seq", axis=0, tiled=True),
        lax.all_gather(block_ids, "seq", axis=0, tiled=True),
    )
    blocks_back = key_blocks(keys_back)
    d_out = (stream - targets.astype(jnp.float32)).astype(jnp.bfloat16)
    cot = d_out.astype(jnp.float32)
    grad_down = lax.dot_general(d_out, hidden, contract_rows, preferred_element_type=jnp.float32)
    d_hidden = jnp.dot(d_out, wd_b, preferred_element_type=jnp.float32)
    d_gate = (d_hidden * upper * sigma * (1.0 + gate * (1.0 - sigma))).astype(jnp.bfloat16)
    d_up = (d_hidden * silu_gate).astype(jnp.bfloat16)
    grad_gate = lax.dot_general(second, d_gate, contract_rows, preferred_element_type=jnp.float32)
    grad_up = lax.dot_general(second, d_up, contract_rows, preferred_element_type=jnp.float32)
    d_second = lax.dot_general(d_gate, wg_b, contract_last, preferred_element_type=jnp.float32)
    d_second = d_second + lax.dot_general(
        d_up, wu_b, contract_last, preferred_element_type=jnp.float32
    )
    d_second = lax.psum(d_second.astype(jnp.bfloat16), "mp").astype(jnp.float32)
    grad_gain_two, d_middle = norm_back(d_second, middle, scale_two, gain_two_b.astype(jnp.float32))
    d_middle = cot + d_middle
    d_attn = d_middle.astype(jnp.bfloat16)
    grad_out = lax.dot_general(d_attn, mixed, contract_rows, preferred_element_type=jnp.float32)
    d_mixed = jnp.dot(d_attn, wo_b, preferred_element_type=jnp.float32).astype(jnp.bfloat16)
    d_heads = d_mixed.reshape(rows, kv_heads, group, HEAD_DIM)
    delta = jnp.sum(d_heads.astype(jnp.float32) * mixed_f32, axis=-1)

    def grad_step(d_query, blocks):
        kblock, vblock, sblock, bblock = blocks
        scores, visible = scores_of(queries, kblock, sblock, bblock, seq_ids, block_ids)
        probs = jnp.where(visible, jnp.exp(scores - lse[..., None]), 0.0)
        d_probs = jnp.einsum("qhgd,nhd->qhgn", d_heads, vblock, preferred_element_type=jnp.float32)
        d_scores = (probs * (d_probs - delta[..., None])).astype(jnp.bfloat16)
        d_query = d_query + jnp.einsum(
            "qhgn,nhd->qhgd", d_scores, kblock, preferred_element_type=jnp.float32
        )
        d_key = jnp.einsum("qhgn,qhgd->nhd", d_scores, queries, preferred_element_type=jnp.float32)
        d_value = jnp.einsum(
            "qhgn,qhgd->nhd",
            probs.astype(jnp.bfloat16),
            d_heads,
            preferred_element_type=jnp.float32,
        )
        return (d_query, (d_key, d_value))

    d_query, (d_key_all, d_value_all) = lax.scan(
        grad_step, jnp.zeros((rows, kv_heads, group, HEAD_DIM), jnp.float32), blocks_back
    )
    total_keys = keys_back[0].shape[0]
    d_key_all = d_key_all.reshape(total_keys, -1) * HEAD_DIM ** (-0.5)
    d_value_all = d_value_all.reshape(total_keys, -1)
    d_key_own, d_value_own = (
        lax.psum_scatter(
            d_key_all.astype(jnp.bfloat16), "seq", scatter_dimension=0, tiled=True
        ).astype(jnp.float32),
        lax.psum_scatter(
            d_value_all.astype(jnp.bfloat16), "seq", scatter_dimension=0, tiled=True
        ).astype(jnp.float32),
    )
    d_query = rotate(d_query.reshape(rows, -1) * HEAD_DIM ** (-0.5), cosine, sine, -1.0).astype(
        jnp.bfloat16
    )
    d_key = rotate(d_key_own, cosine, sine, -1.0).astype(jnp.bfloat16)
    d_value = d_value_own.astype(jnp.bfloat16)
    grad_query = lax.dot_general(first, d_query, contract_rows, preferred_element_type=jnp.float32)
    grad_key = lax.dot_general(first, d_key, contract_rows, preferred_element_type=jnp.float32)
    grad_value = lax.dot_general(first, d_value, contract_rows, preferred_element_type=jnp.float32)
    d_first = lax.dot_general(d_query, wq_b, contract_last, preferred_element_type=jnp.float32)
    d_first = d_first + lax.dot_general(
        d_key, wk_b, contract_last, preferred_element_type=jnp.float32
    )
    d_first = d_first + lax.dot_general(
        d_value, wv_b, contract_last, preferred_element_type=jnp.float32
    )
    d_first = lax.psum(d_first.astype(jnp.bfloat16), "mp").astype(jnp.float32)
    grad_gain_one, d_input = norm_back(d_first, xin, scale_one, gain_one_b.astype(jnp.float32))
    input_grad = (d_middle + d_input).astype(jnp.bfloat16)
    owned = (
        lax.psum_scatter(
            grad_query.astype(jnp.bfloat16), "seq", scatter_dimension=0, tiled=True
        ).astype(jnp.float32),
        lax.psum_scatter(
            grad_key.astype(jnp.bfloat16), "seq", scatter_dimension=0, tiled=True
        ).astype(jnp.float32),
        lax.psum_scatter(
            grad_value.astype(jnp.bfloat16), "seq", scatter_dimension=0, tiled=True
        ).astype(jnp.float32),
        lax.psum_scatter(
            grad_out.astype(jnp.bfloat16), "seq", scatter_dimension=0, tiled=True
        ).astype(jnp.float32),
        lax.psum_scatter(
            grad_gate.astype(jnp.bfloat16), "seq", scatter_dimension=0, tiled=True
        ).astype(jnp.float32),
        lax.psum_scatter(
            grad_up.astype(jnp.bfloat16), "seq", scatter_dimension=0, tiled=True
        ).astype(jnp.float32),
        lax.psum_scatter(
            grad_down.astype(jnp.bfloat16), "seq", scatter_dimension=0, tiled=True
        ).astype(jnp.float32),
        lax.psum_scatter(
            grad_gain_one.astype(jnp.bfloat16), "seq", scatter_dimension=0, tiled=True
        ).astype(jnp.float32),
        lax.psum_scatter(
            grad_gain_two.astype(jnp.bfloat16), "seq", scatter_dimension=0, tiled=True
        ).astype(jnp.float32),
    )
    return (
        stream.astype(jnp.bfloat16),
        input_grad,
        owned[0],
        owned[1],
        owned[2],
        owned[3],
        owned[4],
        owned[5],
        owned[6],
        owned[7],
        owned[8],
        rms_stream,
        rms_attn,
        rms_mlp,
    )


def solution(mesh):
    return jax.shard_map(
        on_device,
        mesh=mesh,
        in_specs=(
            P("seq", None),
            P("seq", None),
            P("seq"),
            P("seq"),
            P("seq"),
            P("seq"),
            P("seq", "mp"),
            P("seq", "mp"),
            P("seq", "mp"),
            P("seq", "mp"),
            P("seq", "mp"),
            P("seq", "mp"),
            P("seq", "mp"),
        ),
        out_specs=(
            P("seq", None),
            P("seq", None),
            P("seq", "mp"),
            P("seq", "mp"),
            P("seq", "mp"),
            P("seq", "mp"),
            P("seq", "mp"),
            P("seq", "mp"),
            P("seq", "mp"),
            P("seq"),
            P("seq"),
            P(),
            P(),
            P(),
        ),
        check_vma=False,
    )
```

profile of v0, /device:TPU:0, one launch (start us, length us, event | category | flops | bytes accessed | tf_op | source)
XLA Modules:
  0.0 1785.8 jit_solution(4995901879449715852)
XLA Ops:
  14.2 39.7 %all-reduce.6 = (bf16[2560]{0:T(1024)(128)(2,1)S(1)}, bf16[2560]{0:T(1024)(128)(2,1)}) all-reduce(bf16[2560]{0:T(1024)(128)(2,1)S(1)} %dynamic-update-slice, bf16[2560]{0:T(1024)(128)(2,1)S(1)} %dynamic-update-slice.1), channel_id=1, replica_groups=mesh['seq'=8,'mp'=4] {'seq'}, use_global_device_ids=true, to_apply=%add | all-reduce | flops 5120 | bytes 20480
  53.9 17.0 all-gather.2
  70.9 18.3 %all-gather.1 = s32[8,1,256]{2,1,0:T(1,128)S(1)} all-gather(s32[1,1,256]{2,1,0:T(1,128)} %bitcast.151), channel_id=1, replica_groups=mesh['seq'=8,'mp'=4] {'seq'}, dimensions={0}, use_global_device_ids=true | all-gather | bytes 9216 | tf_op jit(solution)/shard_map/all_gather | solution.py:115
  89.2 35.6 %all-gather.3 = bf16[8,320,160]{1,2,0:T(8,128)(2,1)S(1)} all-gather(bf16[1,320,160]{1,2,0:T(8,128)(2,1)} %bitcast.145), channel_id=1, replica_groups=mesh['seq'=8,'mp'=4] {'seq'}, dimensions={0}, use_global_device_ids=true | all-gather | bytes 921600 | tf_op jit(solution)/shard_map/all_gather | solution.py:87
  126.7 34.7 %all-gather = bf16[8,320,160]{1,2,0:T(8,128)(2,1)S(1)} all-gather(bf16[1,320,160]{1,2,0:T(8,128)(2,1)S(1)} %bitcast.146), channel_id=1, replica_groups=mesh['seq'=8,'mp'=4] {'seq'}, dimensions={0}, use_global_device_ids=true | all-gather | bytes 921600 | tf_op jit(solution)/shard_map/all_gather | solution.py:88
  165.8 31.9 %all_gather.58 = bf16[2048,160]{0,1:T(8,128)(2,1)S(1)} all-gather(bf16[256,160]{0,1:T(8,128)(2,1)S(1)} %bitcast.141), channel_id=1, replica_groups=mesh['seq'=8,'mp'=4] {'seq'}, dimensions={0}, use_global_device_ids=true | all-gather | bytes 737280 | tf_op jit(solution)/shard_map/all_gather | solution.py:113
  197.7 31.9 %all_gather.54 = bf16[2048,160]{0,1:T(8,128)(2,1)S(1)} all-gather(bf16[256,160]{0,1:T(8,128)(2,1)S(1)} %convolution_convert_fusion.10), channel_id=1, replica_groups=mesh['seq'=8,'mp'=4] {'seq'}, dimensions={0}, use_global_device_ids=true | all-gather | bytes 737280 | tf_op jit(solution)/shard_map/all_gather | solution.py:114
  231.1 3.4 fusion.43
  234.7 2.9 fusion.4
  237.6 4.1 select_reduce_fusion
  243.3 4.0 fusion.51
  247.3 4.3 convolution_convert_fusion.6
  253.7 34.3 %all-reduce.12.cloned.1.call-done = bf16[256,2560]{1,0:T(8,128)(2,1)} async-done(((bf16[256,2560]{1,0:T(8,128)(2,1)}), bf16[256,2560]{1,0:T(8,128)(2,1)}) %all-reduce.12.cloned.1.call-update) | async-done | bytes 1310736 | tf_op jit(solution)/shard_map/psum | solution.py:151
  291.6 133.4 %all-gather.14.cloned.1.call-done = bf16[2560,1792]{1,0:T(8,128)(2,1)} async-done(((bf16[320,1792]{1,0:T(8,128)(2,1)}), bf16[2560,1792]{1,0:T(8,128)(2,1)}) %all-gather.14.cloned.1.call-update) | async-done | bytes 9175056 | tf_op jit(solution)/shard_map/all_gather | solution.py:90
  425.0 7.8 fusion.52
  432.7 127.3 %all-gather.16.cloned.1.call-done = bf16[2560,1792]{1,0:T(8,128)(2,1)} async-done(((bf16[320,1792]{1,0:T(8,128)(2,1)}), bf16[2560,1792]{1,0:T(8,128)(2,1)}) %all-gather.16.cloned.1.call-update) | async-done | bytes 9175056 | tf_op jit(solution)/shard_map/all_gather | solution.py:91
  560.1 8.6 multiply_convert_fusion.3
  568.7 126.5 %all-gather.18.cloned.1.call-done = bf16[2560,1792]{1,0:T(8,128)(2,1)} async-done(((bf16[320,1792]{1,0:T(8,128)(2,1)}), bf16[2560,1792]{1,0:T(8,128)(2,1)}) %all-gather.18.cloned.1.call-update) | async-done | bytes 9175056 | tf_op jit(solution)/shard_map/all_gather | solution.py:92
  695.2 7.5 convolution_convert_fusion.5
  703.0 37.0 %all-reduce.14.cloned.1.call-done = bf16[256,2560]{1,0:T(8,128)(2,1)} async-done(((bf16[256,2560]{1,0:T(8,128)(2,1)}), bf16[256,2560]{1,0:T(8,128)(2,1)}) %all-reduce.14.cloned.1.call-update) | async-done | bytes 1310736 | tf_op jit(solution)/shard_map/psum | solution.py:165
  740.0 3.3 fusion.22
  743.3 7.5 multiply_convert_fusion.1
  753.5 7.3 fusion.10
  761.0 38.8 %all-reduce.16.cloned.1.call-done = bf16[256,2560]{1,0:T(8,128)(2,1)} async-done(((bf16[256,2560]{1,0:T(8,128)(2,1)}), bf16[256,2560]{1,0:T(8,128)(2,1)}) %all-reduce.16.cloned.1.call-update) | async-done | bytes 1310736 | tf_op jit(solution)/shard_map/psum | solution.py:213
  799.9 5.1 fusion.23
  810.4 8.7 fusion.1
  819.1 3.6 fusion.30
  822.8 6.0 convolution_multiply_fusion
  828.8 8.5 fusion.29
  839.8 4.7 fusion.54
  844.5 41.1 %reduce-scatter.14.cloned.1.call-done = bf16[256,160]{0,1:T(8,128)(2,1)} async-done(((bf16[2048,160]{0,1:T(8,128)(2,1)}), bf16[256,160]{0,1:T(8,128)(2,1)}) %reduce-scatter.14.cloned.1.call-update) | async-done | bytes 81936 | tf_op jit(solution)/shard_map/reduce_scatter | solution.py:247
  886.6 4.1 convolution_add_fusion.1
  890.7 60.2 %reduce-scatter.16.cloned.1.call-done = bf16[256,160]{0,1:T(8,128)(2,1)} async-done(((bf16[2048,160]{0,1:T(8,128)(2,1)}), bf16[256,160]{0,1:T(8,128)(2,1)}) %reduce-scatter.16.cloned.1.call-update) | async-done | bytes 81936 | tf_op jit(solution)/shard_map/reduce_scatter | solution.py:250
  951.0 3.4 fusion.11
  959.5 5.5 convolution_convert_fusion.3
  965.9 3.0 convolution_convert_fusion.4
  970.1 7.5 convolution_convert_fusion
  978.8 7.5 convolution_convert_fusion.1
  987.5 7.5 convolution_convert_fusion.2
  995.8 20.1 %all-reduce.4 = (f32[]{:T(128)}, f32[]{:T(128)}, f32[]{:T(128)}) all-reduce(f32[]{:T(128)} %get-tuple-element.89, f32[]{:T(128)} %get-tuple-element.104, f32[]{:T(128)} %get-tuple-element.115), channel_id=1, replica_groups=mesh['seq'=8,'mp'=4] {'seq'}, use_global_device_ids=true, to_apply=%region_25.26 | all-reduce | flops 3 | bytes 24 | tf_op jit(solution)/shard_map/psum | solution.py:177
  1020.4 33.0 %all-reduce.5 = (bf16[2560]{0:T(1024)(128)(2,1)S(1)}, bf16[2560]{0:T(1024)(128)(2,1)S(1)}) all-reduce(bf16[2560]{0:T(1024)(128)(2,1)S(1)} %get-tuple-element.87, bf16[2560]{0:T(1024)(128)(2,1)S(1)} %copy-done.25), channel_id=11, replica_groups=mesh['seq'=8,'mp'=4] {'seq'}, use_global_device_ids=true, to_apply=%region_21.22.clone | all-reduce | flops 5120 | bytes 20480
  1054.1 5.2 fusion.17
  1062.0 65.7 %reduce-scatter.28.cloned.1.call-done = bf16[320,160]{1,0:T(8,128)(2,1)} async-done(((bf16[2560,160]{1,0:T(8,128)(2,1)}), bf16[320,160]{1,0:T(8,128)(2,1)}) %reduce-scatter.28.cloned.1.call-update) | async-done | bytes 102416
  1129.4 76.7 %reduce-scatter.20.cloned.1.call-done = bf16[320,640]{1,0:T(8,128)(2,1)} async-done(((bf16[2560,640]{1,0:T(8,128)(2,1)}), bf16[320,640]{1,0:T(8,128)(2,1)}) %reduce-scatter.20.cloned.1.call-update) | async-done | bytes 409616 | tf_op jit(solution)/shard_map/reduce_scatter | solution.py:282
  1208.1 77.1 %reduce-scatter.18.cloned.1.call-done = bf16[320,640]{1,0:T(8,128)(2,1)} async-done(((bf16[2560,640]{1,0:T(8,128)(2,1)}), bf16[320,640]{1,0:T(8,128)(2,1)}) %reduce-scatter.18.cloned.1.call-update) | async-done | bytes 409616 | tf_op jit(solution)/shard_map/reduce_scatter | solution.py:273
  1287.2 160.2 %reduce-scatter.26.cloned.1.call-done = bf16[320,1792]{1,0:T(8,128)(2,1)} async-done(((bf16[2560,1792]{1,0:T(8,128)(2,1)}), bf16[320,1792]{1,0:T(8,128)(2,1)}) %reduce-scatter.26.cloned.1.call-update) | async-done | bytes 1146896 | tf_op jit(solution)/shard_map/reduce_scatter | solution.py:291
  1450.2 160.1 %reduce-scatter.24.cloned.1.call-done = bf16[320,1792]{1,0:T(8,128)(2,1)} async-done(((bf16[2560,1792]{1,0:T(8,128)(2,1)}), bf16[320,1792]{1,0:T(8,128)(2,1)}) %reduce-scatter.24.cloned.1.call-update) | async-done | bytes 1146896 | tf_op jit(solution)/shard_map/reduce_scatter | solution.py:288
  1613.1 159.5 %reduce-scatter.22.cloned.1.call-done = bf16[320,1792]{1,0:T(8,128)(2,1)} async-done(((bf16[2560,1792]{1,0:T(8,128)(2,1)}), bf16[320,1792]{1,0:T(8,128)(2,1)}) %reduce-scatter.22.cloned.1.call-update) | async-done | bytes 1146896 | tf_op jit(solution)/shard_map/reduce_scatter | solution.py:285
  (177 shorter events, 62.6 us)
Async XLA Ops:
  7.2 223.9 %all-gather.10.cloned.1.call-start = ((), (), s32[]{:S(2)}) async-start(), calls=%async_computation.9 | async-start | bytes 3686400 | tf_op jit(solution)/shard_map/all_gather | solution.py:86
  7.9 239.4 %all-gather.12.cloned.1.call-start = ((), (), s32[]{:S(2)}) async-start(), calls=%async_computation.10 | async-start | bytes 3686400 | tf_op jit(solution)/shard_map/all_gather | solution.py:89
  8.7 279.3 %all-reduce.12.cloned.1.call-start = ((), (), s32[]{:S(2)}) async-start(), calls=%async_computation.11 | async-start | bytes 2621440 | tf_op jit(solution)/shard_map/psum | solution.py:151
  10.4 116.2 %copy-start.24 = (bf16[320,160]{0,1:T(8,128)(2,1)S(1)}, bf16[320,160]{0,1:T(8,128)(2,1)}, u32[]{:S(2)}) copy-start(bf16[320,160]{0,1:T(8,128)(2,1)} %param.21) | copy-start | bytes 307204
  126.6 36.6 %copy-start = (bf16[256,2560]{1,0:T(8,128)(2,1)S(1)}, bf16[256,2560]{1,0:T(8,128)(2,1)}, u32[]{:S(2)}) copy-start(bf16[256,2560]{1,0:T(8,128)(2,1)} %param.13) | copy-start | bytes 3932164
  162.4 3.4 copy-start.8
  165.1 64.5 %copy-start.31 = (s32[256]{0:T(256)S(1)}, s32[256]{0:T(256)}, u32[]{:S(2)}) copy-start(s32[256]{0:T(256)} %param.16) | copy-start | bytes 3076
  165.1 64.5 %copy-start.32 = (s32[256]{0:T(256)S(1)}, s32[256]{0:T(256)}, u32[]{:S(2)}) copy-start(s32[256]{0:T(256)} %param.15) | copy-start | bytes 3076
  197.7 37.0 %copy-start.6 = (bf16[2048,160]{0,1:T(8,128)(2,1)}, bf16[2048,160]{0,1:T(8,128)(2,1)S(1)}, u32[]{:S(2)}) copy-start(bf16[2048,160]{0,1:T(8,128)(2,1)S(1)} %all_gather.58) | copy-start | bytes 1966084
  229.6 12.1 copy-start.18
  231.1 3.5 copy-start.21
  237.6 5.7 copy-start.1
  241.7 5.7 copy-start.28
  247.3 4.4 copy-start.36
  251.7 173.3 %all-gather.14.cloned.1.call-start = ((), (), s32[]{:S(2)}) async-start(), calls=%async_computation.12 | async-start | bytes 10321920 | tf_op jit(solution)/shard_map/all_gather | solution.py:90
  252.3 307.8 %all-gather.16.cloned.1.call-start = ((), (), s32[]{:S(2)}) async-start(), calls=%async_computation.13 | async-start | bytes 10321920 | tf_op jit(solution)/shard_map/all_gather | solution.py:91
  252.9 442.3 %all-gather.18.cloned.1.call-start = ((), (), s32[]{:S(2)}) async-start(), calls=%async_computation.14 | async-start | bytes 10321920 | tf_op jit(solution)/shard_map/all_gather | solution.py:92
  253.4 486.6 %all-reduce.14.cloned.1.call-start = ((), (), s32[]{:S(2)}) async-start(), calls=%async_computation.15 | async-start | bytes 2621440 | tf_op jit(solution)/shard_map/psum | solution.py:165
  253.7 705.8 %copy-start.22 = (f32[2560]{0:T(1024)}, f32[2560]{0:T(1024)S(1)}, u32[]{:S(2)}) copy-start(f32[2560]{0:T(1024)S(1)} %convert_element_type.204) | copy-start | bytes 30724
  289.9 669.5 %copy-start.26 = (f32[256]{0:T(256)}, f32[256]{0:T(256)S(1)}, u32[]{:S(2)}) copy-start(f32[256]{0:T(256)S(1)} %add_rsqrt_fusion) | copy-start | bytes 3076
  702.8 97.1 %all-reduce.16.cloned.1.call-start = ((), (), s32[]{:S(2)}) async-start(), calls=%async_computation.16 | async-start | bytes 2621440 | tf_op jit(solution)/shard_map/psum | solution.py:213
  740.0 3.3 copy-start.37
  740.0 10.8 slice-start
  743.3 7.5 copy-start.4
  743.3 7.5 slice-start.1
  743.3 7.5 slice-start.2
  760.7 124.9 %reduce-scatter.14.cloned.1.call-start = ((), (), s32[]{:S(2)}) async-start(), calls=%async_computation.17 | async-start | bytes 737280 | tf_op jit(solution)/shard_map/reduce_scatter | solution.py:247
  799.9 5.1 copy-start.5
  799.9 5.1 copy-start.7
  799.9 5.1 copy-start.35
  819.1 3.6 copy-start.2
  822.7 6.1 copy-start.12
  822.7 6.1 copy-start.29
  822.8 128.2 %reduce-scatter.16.cloned.1.call-start = ((), (), s32[]{:S(2)}) async-start(), calls=%async_computation.18 | async-start | bytes 737280 | tf_op jit(solution)/shard_map/reduce_scatter | solution.py:250
  837.3 180.7 %all-reduce.18.cloned.1.call-start = ((), (), s32[]{:S(2)}) async-start(), calls=%async_computation.19 | async-start | bytes 2621440 | tf_op jit(solution)/shard_map/psum | solution.py:269
  839.8 46.7 %copy-start.19 = (f32[256,40]{0,1:T(8,128)S(1)}, f32[256,40]{0,1:T(8,128)}, u32[]{:S(2)}) copy-start(f32[256,40]{0,1:T(8,128)} %get-tuple-element.139) | copy-start | bytes 122884
  886.6 64.3 %copy-start.9 = (bf16[2560,160]{0,1:T(8,128)(2,1)S(1)}, bf16[2560,160]{0,1:T(8,128)(2,1)}, u32[]{:S(2)}) copy-start(bf16[2560,160]{0,1:T(8,128)(2,1)} %copy-done.8) | copy-start | bytes 2457604
  954.3 105.9 %reduce-scatter.30.cloned.1.call-start = ((), (), s32[]{:S(2)}) async-start(), calls=%async_computation.26 | async-start | bytes 1474560
  957.3 170.4 %reduce-scatter.28.cloned.1.call-start = ((), (), s32[]{:S(2)}) async-start(), calls=%async_computation.25 | async-start | bytes 1474560
  959.4 246.8 %reduce-scatter.20.cloned.1.call-start = ((), (), s32[]{:S(2)}) async-start(), calls=%async_computation.21 | async-start | bytes 3686400 | tf_op jit(solution)/shard_map/reduce_scatter | solution.py:282
  965.0 320.3 %reduce-scatter.18.cloned.1.call-start = ((), (), s32[]{:S(2)}) async-start(), calls=%async_computation.20 | async-start | bytes 3686400 | tf_op jit(solution)/shard_map/reduce_scatter | solution.py:273
  968.9 478.5 %reduce-scatter.26.cloned.1.call-start = ((), (), s32[]{:S(2)}) async-start(), calls=%async_computation.24 | async-start | bytes 10321920 | tf_op jit(solution)/shard_map/reduce_scatter | solution.py:291
  977.6 632.7 %reduce-scatter.24.cloned.1.call-start = ((), (), s32[]{:S(2)}) async-start(), calls=%async_computation.23 | async-start | bytes 10321920 | tf_op jit(solution)/shard_map/reduce_scatter | solution.py:288
  986.4 786.3 %reduce-scatter.22.cloned.1.call-start = ((), (), s32[]{:S(2)}) async-start(), calls=%async_computation.22 | async-start | bytes 10321920 | tf_op jit(solution)/shard_map/reduce_scatter | solution.py:285
  995.1 25.3 %copy-start.25 = (bf16[2560]{0:T(1024)(128)(2,1)S(1)}, bf16[2560]{0:T(1024)(128)(2,1)}, u32[]{:S(2)}) copy-start(bf16[2560]{0:T(1024)(128)(2,1)} %get-tuple-element.85) | copy-start | bytes 15364
  995.1 59.0 %copy-start.23 = (f32[2560]{0:T(1024)S(1)}, f32[2560]{0:T(1024)}, u32[]{:S(2)}) copy-start(f32[2560]{0:T(1024)} %copy-done.22) | copy-start | bytes 30724
  995.1 58.9 %copy-start.27 = (f32[256]{0:T(256)S(1)}, f32[256]{0:T(256)}, u32[]{:S(2)}) copy-start(f32[256]{0:T(256)} %copy-done.26) | copy-start | bytes 3076
  995.1 58.9 %copy-start.34 = (f32[256]{0:T(256)S(1)}, f32[256]{0:T(256)}, u32[]{:S(2)}) copy-start(f32[256]{0:T(256)} %copy-done.33) | copy-start | bytes 3076
  (11 other events, 19.3 us)
Sparse Core Ops, SparseCore 0:
  10.2 65.2 all-gather.9
  77.6 83.6 all-gather.11
  251.8 36.1 all-reduce.11
  290.0 134.8 all-gather.13
  427.0 133.0 all-gather.15
  562.1 133.0 all-gather.17
  702.9 37.1 all-reduce.13
  760.9 38.9 all-reduce.15
  822.9 62.7 reduce-scatter.13
  889.2 61.7 reduce-scatter.15
  954.5 37.9 all-reduce.17
  995.7 64.4 reduce-scatter.29
  1064.2 63.4 reduce-scatter.27
  1131.1 74.9 reduce-scatter.19
  1210.0 75.1 reduce-scatter.17
  1288.8 158.5 reduce-scatter.25
  1451.4 158.8 reduce-scatter.23
  1613.9 158.7 reduce-scatter.21
where the time goes:
time: 1790 us
  waiting for transfers between devices  1300 us (73%)
  blocking collectives  262 us (15%)
  matrix products  133 us (7%)
  other arithmetic  45.4 us (3%)
  between operations  21.9 us (1%)
  local copies, waits for them, and re-layouts  19.3 us (1%)
    reduce_scatter x1, waiting for transfers between devices, on_device(): lax.psum_scatter(grad_down.astype(jnp.bfloat16), 'seq', scatter_dimension...  160 us
    reduce_scatter x1, waiting for transfers between devices, on_device(): lax.psum_scatter(grad_up.astype(jnp.bfloat16), 'seq', scatter_dimension=0...  160 us
    reduce_scatter x1, waiting for transfers between devices, on_device(): lax.psum_scatter(grad_gate.astype(jnp.bfloat16), 'seq', scatter_dimension...  160 us
    all_gather x1, waiting for transfers between devices, on_device(): lax.all_gather(w_gate, 'seq', axis=0, tiled=True)  133 us
    all_gather x1, waiting for transfers between devices, on_device(): lax.all_gather(w_up, 'seq', axis=0, tiled=True)  127 us
    all_gather x1, waiting for transfers between devices, on_device(): lax.all_gather(w_down, 'seq', axis=0, tiled=True)  127 us
    reduce_scatter x1, waiting for transfers between devices, on_device(): lax.psum_scatter(grad_query.astype(jnp.bfloat16), 'seq', scatter_dimensio...  77.1 us
    reduce_scatter x1, waiting for transfers between devices, on_device(): lax.psum_scatter(grad_out.astype(jnp.bfloat16), 'seq', scatter_dimension=...  76.7 us
  transfers between devices with their start and end apart: 18, of which 15 were waited for; matrix products, arithmetic and copies ran while one was open for 7% of the time, Pallas kernels for 0%

commit v1 on v0

v1 whole, which is shorter than its diff:
```python
import jax
import jax.numpy as jnp
from jax import lax
from jax.sharding import PartitionSpec as P

HEAD_DIM = 80
SPAN = 128
EPS = 1e-05
THETA = 1000000.0
SEQS = 2
PARTS = 4
BF = jnp.bfloat16
F32 = jnp.float32

LAST = (((1,), (1,)), ((), ()))
ROWS = (((0,), (0,)), ((), ()))


def hop(value, axis, k):
    size = lax.axis_size(axis)
    return lax.ppermute(value, axis, [(i, i ^ k) for i in range(size)])


def dot(left, right, dims=(((1,), (0,)), ((), ()))):
    return lax.dot_general(left, right, dims, preferred_element_type=F32)


class Place:
    def __init__(self):
        self.inner = lax.axis_size("seq") // PARTS
        s = lax.axis_index("seq")
        m = lax.axis_index("mp")
        self.z = s // self.inner
        self.y = s % self.inner
        self.x = m // 2
        self.c = m % 2
        self.bits = []
        b = 1
        while b < self.inner:
            self.bits.append(b)
            b *= 2

    def hop_z(self, v, k):
        return hop(v, "seq", k * self.inner)

    def hop_y(self, v, b):
        return hop(v, "seq", b)

    def hop_x(self, v):
        return hop(v, "mp", 2)

    def hop_c(self, v):
        return hop(v, "mp", 1)

    def features_in(self, v):
        rows = v.shape[0]
        r = v.shape[1] // (PARTS * self.inner)
        v = v.reshape(rows, PARTS, self.inner, r).transpose(0, 2, 1, 3)
        return self.flip_y(v).reshape(rows, -1)

    def features_out(self, v):
        rows = v.shape[0]
        r = v.shape[1] // (PARTS * self.inner)
        v = self.flip_y(v.reshape(rows, self.inner, PARTS, r))
        return v.transpose(0, 2, 1, 3).reshape(rows, -1)

    def flip_y(self, v):
        for b in self.bits:
            w = v.reshape((v.shape[0], self.inner // (2 * b), 2, b) + v.shape[2:])
            w = w[:, :, ::-1].reshape(v.shape)
            v = jnp.where((self.y // b) % 2 == 1, w, v)
        return v

    def swap_z(self, pieces):
        got = []
        for k in range(PARTS):
            piece = lax.dynamic_index_in_dim(pieces, self.z ^ k, 0, keepdims=False)
            got.append(self.hop_z(piece, k) if k else piece)
        out = jnp.zeros(pieces.shape, pieces.dtype)
        for k in range(PARTS):
            out = lax.dynamic_update_index_in_dim(out, got[k], self.z ^ k, 0)
        return out

    def spread(self, buf):
        half = PARTS // 2

        def spread_y(v):
            for b in self.bits:
                v = jnp.concatenate([v, self.hop_y(v, b)], 0)
            return v

        first = spread_y(buf[None, :half])
        first = (first, self.hop_x(first))
        second = (buf[None, half:], self.hop_x(buf[None, half:]))
        second = tuple(spread_y(v) for v in second)
        return [
            jnp.concatenate([first[i], second[i]], 1).reshape(-1, buf.shape[-1]) for i in range(2)
        ]

    def collect(self, grads):
        half = PARTS // 2
        cols = grads[0].shape[-1]
        parts = [g.reshape(self.inner, PARTS, -1, cols) for g in grads]

        def collect_y(v):
            for b in reversed(self.bits):
                got = self.hop_y(v[b:], b)
                v = (v[:b].astype(F32) + got.astype(F32)).astype(BF)
            return v

        def collect_x(own, other):
            return (own.astype(F32) + self.hop_x(other).astype(F32)).astype(BF)

        first = collect_y(collect_x(parts[0][:, :half], parts[1][:, :half]))
        second = collect_x(collect_y(parts[0][:, half:]), collect_y(parts[1][:, half:]))
        return jnp.concatenate([first[0], second[0]], 0)

    def gather(self, own):
        one = self.hop_z(own, 1)
        two = self.hop_z(own, 2)
        three = self.hop_z(two, 1)
        mine = jnp.concatenate([own, one, two, three], 0)
        return mine, self.hop_c(mine)

    def scatter(self, mine, theirs):
        got = self.hop_c(theirs.astype(BF))
        both = mine + got.astype(F32)
        n = both.shape[0] // PARTS
        piece = [both[k * n : (k + 1) * n] for k in range(PARTS)]
        three = self.hop_z(piece[3].astype(BF), 1)
        two = self.hop_z((piece[2] + three.astype(F32)).astype(BF), 2)
        one = self.hop_z(piece[1].astype(BF), 1)
        return piece[0] + one.astype(F32) + two.astype(F32)


def tables(place):
    half = HEAD_DIM // 2
    freq = THETA ** (-(jnp.arange(half, dtype=F32) * 2.0 / HEAD_DIM))
    angle = place[:, None] * freq[None, :]
    return (jnp.cos(angle), jnp.sin(angle))


def rotate(values, cosine, sine, sign):
    count = values.shape[0]
    heads = values.reshape(count, -1, HEAD_DIM)
    half = HEAD_DIM // 2
    first = heads[..., :half]
    second = heads[..., half:]
    cosine = cosine[:, None, :]
    sine = sine[:, None, :] * sign
    turned = jnp.concatenate(
        [first * cosine - second * sine, second * cosine + first * sine], axis=-1
    )
    return turned.reshape(count, -1)


def scale_of(value):
    return lax.rsqrt(jnp.mean(value * value, axis=-1, keepdims=True) + EPS)


def norm_back(grad, value, scale, gain):
    unit = value * scale
    scaled = grad * gain
    back = scale * (scaled - unit * jnp.mean(scaled * unit, axis=-1, keepdims=True))
    return unit, back


def on_device(
    inputs,
    targets,
    seq_ids,
    block_ids,
    attn_gain,
    mlp_gain,
    w_query,
    w_key,
    w_value,
    w_out,
    w_gate,
    w_up,
    w_down,
):
    at = Place()
    inner = at.inner
    depth = w_query.shape[0]
    half_span = SPAN // 2
    kw = w_key.shape[1] // 2
    qw = w_query.shape[1] // PARTS
    fw = w_gate.shape[1] // PARTS

    def split(w):
        return w.reshape(depth, PARTS, -1).transpose(1, 0, 2)

    def split_kv(w):
        w = w.reshape(depth, 2, kw).transpose(1, 0, 2)
        return jnp.repeat(w, 2, axis=0)

    gains = jnp.broadcast_to(
        jnp.stack([attn_gain, mlp_gain], -1)[None], (PARTS, depth, 2)
    )
    pack_qkv = jnp.concatenate([split(w_query), split_kv(w_key), split_kv(w_value), gains], 2)
    pack_out = split(w_out)
    pack_up = jnp.concatenate([split(w_gate), split(w_up)], 2)
    pack_down = split(w_down)

    off = jnp.where(seq_ids[0] == at.x, 0, SPAN)
    row0 = off + at.c * half_span

    def own_rows(v):
        return at.features_in(lax.dynamic_slice_in_dim(v, row0, half_span, 0))

    x_own = own_rows(inputs)
    t_own = own_rows(targets).astype(F32)

    x_mine, x_theirs = at.gather(x_own)
    w_qkv = at.spread(at.swap_z(pack_qkv))
    ids = lax.dynamic_slice_in_dim(block_ids, off, SPAN, 0)
    ids = jnp.stack([ids] + [at.hop_z(ids, k) for k in range(1, PARTS)], 0)
    ids = ids.reshape(PARTS, 2, half_span).transpose(1, 0, 2)
    ids = jnp.where(at.c == 1, ids[::-1], ids).reshape(-1)
    key_ids = ids[None]
    for b in at.bits:
        key_ids = jnp.concatenate([key_ids, at.hop_y(key_ids, b)], 0)
    key_ids = key_ids.reshape(-1)

    w_o = at.spread(at.swap_z(pack_out))
    w_gu = at.spread(at.swap_z(pack_up))
    w_d = at.spread(at.swap_z(pack_down))

    gain = w_qkv[0][:, qw + 2 * kw :].astype(F32)
    gain_one = gain[:, 0][None]
    gain_two = gain[:, 1][None]

    x_all = jnp.concatenate([x_mine, x_theirs], 0).astype(F32)
    rows = x_all.shape[0]
    scale_one = scale_of(x_all)
    first = (x_all * scale_one * gain_one).astype(BF)
    count = jnp.arange(rows, dtype=jnp.int32)
    zz = at.z ^ ((count // half_span) % PARTS)
    cc = at.c ^ (count // (half_span * PARTS))
    place = ((zz * inner + at.y) * SPAN + cc * half_span + count % half_span).astype(F32)
    cosine, sine = tables(place)

    qkv = [dot(first, w[:, : qw + 2 * kw]) for w in w_qkv]
    query_r = [rotate(v[:, :qw], cosine, sine, 1.0).astype(BF) for v in qkv]
    key_r = [rotate(v[:, qw : qw + kw], cosine, sine, 1.0).astype(BF) for v in qkv]
    value_r = [v[:, qw + kw :].astype(BF) for v in qkv]
    kv = jnp.stack(key_r + value_r, 0)
    for b in at.bits:
        kv = jnp.concatenate([kv, at.hop_y(kv, b)], 1)
    keys = kv[:2]
    values = kv[2:]
    group = qw // HEAD_DIM
    queries = jnp.stack([v.reshape(rows, group, HEAD_DIM).transpose(1, 0, 2) for v in query_r], 0)
    factor = HEAD_DIM**-0.5
    visible = (key_ids[None, :] <= ids[:, None])[None, None]
    scores = jnp.einsum("xgqd,xkd->xgqk", queries, keys, preferred_element_type=F32) * factor
    masked = jnp.where(visible, scores, -1e30)
    top = masked.max(axis=-1, keepdims=True)
    weights = jnp.exp(masked - top)
    total = weights.sum(axis=-1, keepdims=True)
    lse = top + jnp.log(total)
    probs = jnp.where(visible, jnp.exp(scores - lse), 0.0)
    probs_b = probs.astype(BF)
    mixed_f = jnp.einsum("xgqk,xkd->xgqd", probs_b, values, preferred_element_type=F32)
    mixed = mixed_f.astype(BF).transpose(0, 2, 1, 3).reshape(2, rows, qw)

    def two_sides(v):
        n = rows // 2
        return v[:n], v[n:]

    partial = dot(mixed[0], w_o[0], LAST) + dot(mixed[1], w_o[1], LAST)
    branch_attn = at.scatter(*two_sides(partial))
    middle = x_own.astype(F32) + branch_attn
    scale_two = scale_of(middle)
    second_own = (middle * scale_two * gain_two).astype(BF)
    second = jnp.concatenate(at.gather(second_own), 0)
    gate_up = [dot(second, w) for w in w_gu]
    gate = [v[:, :fw] for v in gate_up]
    upper = [v[:, fw:] for v in gate_up]
    sigma = [jax.nn.sigmoid(g) for g in gate]
    silu = [g * s for g, s in zip(gate, sigma)]
    hidden = [(a * b).astype(BF) for a, b in zip(silu, upper)]
    partial = dot(hidden[0], w_d[0], LAST) + dot(hidden[1], w_d[1], LAST)
    branch_mlp = at.scatter(*two_sides(partial))
    stream = middle + branch_mlp

    sums = jnp.stack(
        [jnp.sum(stream * stream), jnp.sum(branch_attn * branch_attn), jnp.sum(branch_mlp * branch_mlp)]
    )
    sums = jnp.broadcast_to(sums[:, None], (3, 128))
    sums = sums + at.hop_c(sums)
    sums = sums + at.hop_x(sums)
    for b in at.bits:
        sums = sums + at.hop_y(sums, b)
    sums = sums + at.hop_z(sums, 1)
    sums = sums + at.hop_z(sums, 2)
    entries = inputs.shape[0] * lax.axis_size("seq") * inputs.shape[1]
    rms = jnp.sqrt(sums[:, 0] / entries + EPS)

    d_out_own = (stream - t_own).astype(BF)
    d_out = jnp.concatenate(at.gather(d_out_own), 0)
    grad_down = [dot(d_out, h, ROWS).astype(BF) for h in hidden]
    d_hidden = [dot(d_out, w) for w in w_d]
    d_gate_up = [
        jnp.concatenate(
            [
                (d * u * s * (1.0 + g * (1.0 - s))).astype(BF),
                (d * sg).astype(BF),
            ],
            1,
        )
        for d, u, s, g, sg in zip(d_hidden, upper, sigma, gate, silu)
    ]
    partial = dot(d_gate_up[0], w_gu[0], LAST) + dot(d_gate_up[1], w_gu[1], LAST)
    d_second = at.scatter(*two_sides(partial))
    grad_gu = [dot(second, d, ROWS).astype(BF) for d in d_gate_up]
    unit, back = norm_back(d_second, middle, scale_two, gain_two)
    grad_gain_two = jnp.sum(d_second * unit, axis=0)
    d_middle = d_out_own.astype(F32) + back
    d_attn = jnp.concatenate(at.gather(d_middle.astype(BF)), 0)
    grad_o = [dot(d_attn, mixed[i], ROWS).astype(BF) for i in range(2)]
    d_mix = [dot(d_attn, w).astype(BF) for w in w_o]
    d_heads = jnp.stack([v.reshape(rows, group, HEAD_DIM).transpose(1, 0, 2) for v in d_mix], 0)
    delta = jnp.sum(d_heads.astype(F32) * mixed_f, axis=-1, keepdims=True)
    d_probs = jnp.einsum("xgqd,xkd->xgqk", d_heads, values, preferred_element_type=F32)
    d_scores = (probs * (d_probs - delta)).astype(BF)
    d_query = jnp.einsum("xgqk,xkd->xgqd", d_scores, keys, preferred_element_type=F32) * factor
    d_keys = jnp.einsum("xgqk,xgqd->xkd", d_scores, queries, preferred_element_type=F32) * factor
    d_values = jnp.einsum("xgqk,xgqd->xkd", probs_b, d_heads, preferred_element_type=F32)
    d_kv = jnp.concatenate([d_keys, d_values], 0).reshape(4, inner, rows, HEAD_DIM)
    for b in reversed(at.bits):
        got = at.hop_y(d_kv[:, b:].astype(BF), b)
        d_kv = d_kv[:, :b] + got.astype(F32)
    d_kv = d_kv[:, 0]
    d_qkv = []
    for i in range(2):
        d_q = d_query[i].transpose(1, 0, 2).reshape(rows, qw)
        d_qkv.append(
            jnp.concatenate(
                [
                    rotate(d_q, cosine, sine, -1.0),
                    rotate(d_kv[i], cosine, sine, -1.0),
                    d_kv[2 + i],
                ],
                1,
            ).astype(BF)
        )
    partial = sum(dot(d, w[:, : qw + 2 * kw], LAST) for d, w in zip(d_qkv, w_qkv))
    d_first = at.scatter(*two_sides(partial))
    grad_gain_one = jnp.sum(partial * (x_all * scale_one), axis=0)
    grad_qkv = [dot(first, d, ROWS).astype(BF) for d in d_qkv]
    gain_grads = jnp.stack([grad_gain_one, grad_gain_two], -1).astype(BF)
    grad_qkv = [jnp.concatenate([g, gain_grads], 1) for g in grad_qkv]

    x_f = x_own.astype(F32)
    unit, back = norm_back(d_first, x_f, scale_of(x_f), gain_one)
    input_grad_own = (d_middle + back).astype(BF)

    def whole_rows(own):
        v = at.features_out(own)
        other = at.hop_c(v)
        v = jnp.where(at.c == 0, jnp.concatenate([v, other], 0), jnp.concatenate([other, v], 0))
        other = at.hop_x(v)
        return jnp.where(off == 0, jnp.concatenate([v, other], 0), jnp.concatenate([other, v], 0))

    layer_out = whole_rows(stream.astype(BF))
    input_grad = whole_rows(input_grad_own)

    def joined(pieces):
        return pieces.astype(F32).transpose(1, 0, 2).reshape(depth, -1)

    got_down = at.swap_z(at.collect(grad_down))
    got_gu = at.swap_z(at.collect(grad_gu))
    got_out = at.swap_z(at.collect(grad_o))
    got_qkv = at.swap_z(at.collect(grad_qkv))
    kv_got = got_qkv[:, :, qw:].astype(F32)
    kv_sum = kv_got.reshape(2, 2, depth, -1).sum(1)
    gains_sum = kv_sum[:, :, 2 * kw :].sum(0)
    gains_sum = gains_sum + at.hop_c(gains_sum)
    return (
        layer_out,
        input_grad,
        joined(got_qkv[:, :, :qw]),
        joined(kv_sum[:, :, :kw]),
        joined(kv_sum[:, :, kw : 2 * kw]),
        joined(got_out),
        joined(got_gu[:, :, :fw]),
        joined(got_gu[:, :, fw:]),
        joined(got_down),
        gains_sum[:, 0],
        gains_sum[:, 1],
        rms[0],
        rms[1],
        rms[2],
    )


def solution(mesh):
    return jax.shard_map(
        on_device,
        mesh=mesh,
        in_specs=(
            P("seq", None),
            P("seq", None),
            P("seq"),
            P("seq"),
            P("seq"),
            P("seq"),
            P("seq", "mp"),
            P("seq", "mp"),
            P("seq", "mp"),
            P("seq", "mp"),
            P("seq", "mp"),
            P("seq", "mp"),
            P("seq", "mp"),
        ),
        out_specs=(
            P("seq", None),
            P("seq", None),
            P("seq", "mp"),
            P("seq", "mp"),
            P("seq", "mp"),
            P("seq", "mp"),
            P("seq", "mp"),
            P("seq", "mp"),
            P("seq", "mp"),
            P("seq"),
            P("seq"),
            P(),
            P(),
            P(),
        ),
        check_vma=False,
    )
```

time: 1790 us -> 926 us (0.52)
  waiting for transfers between devices: 1300 us -> 395 us
  blocking collectives: 262 us -> 0 us
  local copies, waits for them, and re-layouts: 19.3 us -> 214 us
  starting transfers between devices: 2 us -> 141 us
  matrix products: 133 us -> 67.5 us
  other arithmetic: 45.4 us -> 92.4 us
    reduce_scatter x7 -> x0, waiting for transfers between devices: 735 us -> none  [the longest x1 160 us: on_device(): lax.psum_scatter(grad_down.astype(jnp.bfloat16), 'seq', scatter_dimension...]
    ppermute x0 -> x112, waiting for transfers between devices: none -> 395 us  [hop(): return lax.ppermute(value, axis, [(i, i ^ k) for i in range(size)])]
    all_gather x5 -> x0, waiting for transfers between devices: 387 us -> none  [the longest x1 133 us: on_device(): lax.all_gather(w_gate, 'seq', axis=0, tiled=True)]
    all_gather x6 -> x0, blocking collectives: 169 us -> none  [the longest x1 35.6 us: on_device(): lax.all_gather(w_key, 'seq', axis=0, tiled=True)]
    ppermute x0 -> x112, starting transfers between devices: none -> 141 us  [hop(): return lax.ppermute(value, axis, [(i, i ^ k) for i in range(size)])]
    psum x4 -> x0, waiting for transfers between devices: 110 us -> none  [the longest x1 38.8 us: on_device(): d_second = lax.psum(d_second.astype(jnp.bfloat16), 'mp').astype(jnp.float32)]
    unnamed x2 -> x0, blocking collectives: 72.7 us -> none
    reshape x0 -> x29, local copies, waits for them, and re-layouts: none -> 71.1 us  [the longest x6 19.2 us: joined(): return pieces.astype(F32).transpose(1, 0, 2).reshape(depth, -1)]
  transfers between devices with their start and end apart: 18 -> 112, of which waited for: 15 -> 42; matrix products, arithmetic and copies ran while one was open for 7% -> 36% of each run, Pallas kernels for 0% -> 0%
where the time goes in v1:
time: 926 us; the launch traced here: 914 us
  waiting for transfers between devices  395 us (43%)
  local copies, waits for them, and re-layouts  214 us (23%)
  starting transfers between devices  141 us (15%)
  other arithmetic  92.4 us (10%)
  matrix products  67.5 us (7%)
    ppermute x112, waiting for transfers between devices, hop(): return lax.ppermute(value, axis, [(i, i ^ k) for i in range(size)])  395 us
    ppermute x112, starting transfers between devices, hop(): return lax.ppermute(value, axis, [(i, i ^ k) for i in range(size)])  141 us
    dot_general x24, matrix products, dot(): return lax.dot_general(left, right, dims, preferred_element_type=F32)  55.3 us
    unnamed x264, local copies, waits for them, and re-layouts  34.7 us
    dynamic_update_slice x28, local copies, waits for them, and re-layouts, swap_z(): out = lax.dynamic_update_index_in_dim(out, got[k], self.z ^ k, 0)  21.3 us
    reshape x6, local copies, waits for them, and re-layouts, joined(): return pieces.astype(F32).transpose(1, 0, 2).reshape(depth, -1)  19.2 us
  transfers between devices with their start and end apart: 112, of which 42 were waited for; matrix products, arithmetic and copies ran while one was open for 36% of the time, Pallas kernels for 0%

profile of v1, /device:TPU:0, one launch (start us, length us, event | category | flops | bytes accessed | tf_op | source)
XLA Modules:
  0.0 914.3 jit_solution(6366520444059118126)
XLA Ops:
  12.5 3.9 collective-permute-start.2
  16.5 4.5 reshape.588
  21.0 4.5 reshape.589
  27.8 4.5 reshape.591
  32.3 6.6 constant_dynamic-slice_fusion.1
  38.9 11.9 %fusion.14 = (bf16[1,320,896]{2,0,1:T(2,128)(2,1)}, bf16[1,320,896]{2,0,1:T(2,128)(2,1)S(1)}, bf16[1,320,896]{2,0,1:T(2,128)(2,1)}, bf16[1,320,896]{2,0,1:T(2,128)(2,1)}) fusion(s32[]{:T(128)S(6)} %select_n.230, bf16[4,320,448]{2,0,1:T(4,128)(2,1)S(1)} %bitcast.354, bf16[4,320,448]{2,0,1:T(4,128)(2,1)S(1)} %bitcast.355, s32[]{:T(128)S(6)} %select_n.227, ...), kind=kLoop, calls=%fused_computation.110 | loop fusion | flops 4587520 | bytes 4587536 | tf_op jit(solution)/shard_map/concatenate | solution.py:203
  83.6 6.5 collective-permute-done.18
  93.8 4.6 collective-permute-done.19
  98.4 3.6 collective-permute-start.10
  117.6 6.7 collective-permute-done.20
  148.0 4.6 reshape.579
  183.4 4.6 reshape.581
  195.2 7.6 collective-permute-done.16
  214.1 28.0 %collective-permute-done.39 = bf16[320,448]{1,0:T(8,128)(2,1)} collective-permute-done((bf16[320,448]{1,0:T(8,128)(2,1)}, bf16[320,448]{1,0:T(8,128)(2,1)}, u32[]{:S(2)}, u32[]{:S(2)}) %collective-permute-start.39) | collective-permute-done | bytes 286752 | tf_op jit(solution)/shard_map/ppermute | solution.py:21
  254.4 5.6 collective-permute-done.27
  261.3 28.0 %collective-permute-done.41 = bf16[1,2,320,448]{3,2,1,0:T(8,128)(2,1)S(1)} collective-permute-done((bf16[1,2,320,448]{3,2,1,0:T(8,128)(2,1)S(1)}, bf16[1,2,320,448]{3,2,1,0:T(8,128)(2,1)S(1)}, u32[]{:S(2)}, u32[]{:S(2)}) %collective-permute-start.41) | collective-permute-done | bytes 573472 | tf_op jit(solution)/shard_map/ppermute | solution.py:21
  296.0 10.9 %collective-permute-done.42 = bf16[1,2,320,448]{3,2,1,0:T(8,128)(2,1)S(1)} collective-permute-done((bf16[1,2,320,448]{3,2,1,0:T(8,128)(2,1)S(1)}, bf16[1,2,320,448]{3,2,1,0:T(8,128)(2,1)S(1)}, u32[]{:S(2)}, u32[]{:S(2)}) %collective-permute-start.42) | collective-permute-done | bytes 573472 | tf_op jit(solution)/shard_map/ppermute | solution.py:21
  308.3 36.0 %collective-permute-done.48 = bf16[1,2,320,448]{3,2,1,0:T(8,128)(2,1)S(1)} collective-permute-done((bf16[1,2,320,448]{3,2,1,0:T(8,128)(2,1)S(1)}, bf16[1,2,320,448]{3,2,1,0:T(8,128)(2,1)S(1)}, u32[]{:S(2)}, u32[]{:S(2)}) %collective-permute-start.48) | collective-permute-done | bytes 573472 | tf_op jit(solution)/shard_map/ppermute | solution.py:21
  348.7 11.5 %collective-permute-done.30 = bf16[64,2560]{1,0:T(8,128)(2,1)S(1)} collective-permute-done((bf16[64,2560]{1,0:T(8,128)(2,1)S(1)}, bf16[64,2560]{1,0:T(8,128)(2,1)S(1)}, u32[]{:S(2)}, u32[]{:S(2)}) %collective-permute-start.30) | collective-permute-done | bytes 327712 | tf_op jit(solution)/shard_map/ppermute | solution.py:21
  360.8 34.6 %collective-permute-done.46 = bf16[2,2,320,448]{3,2,1,0:T(8,128)(2,1)S(1)} collective-permute-done((bf16[2,2,320,448]{3,2,1,0:T(8,128)(2,1)S(1)}, bf16[2,2,320,448]{3,2,1,0:T(8,128)(2,1)S(1)}, u32[]{:S(2)}, u32[]{:S(2)}) %collective-permute-start.46) | collective-permute-done | bytes 1146912 | tf_op jit(solution)/shard_map/ppermute | solution.py:21
  414.7 8.5 collective-permute-done.51
  424.0 9.9 %collective-permute-done.50 = bf16[64,2560]{1,0:T(8,128)(2,1)S(1)} collective-permute-done((bf16[64,2560]{1,0:T(8,128)(2,1)S(1)}, bf16[64,2560]{1,0:T(8,128)(2,1)S(1)}, u32[]{:S(2)}, u32[]{:S(2)}) %collective-permute-start.50) | collective-permute-done | bytes 327712 | tf_op jit(solution)/shard_map/ppermute | solution.py:21
  434.0 5.5 collective-permute-done.52
  481.2 4.4 collective-permute-done.57
  489.0 5.8 collective-permute-done.54
  510.1 5.2 fusion.48
  515.4 5.1 convolution_add_fusion.3
  532.9 4.4 convolution_convert_fusion
  553.6 23.9 %collective-permute-done.98 = bf16[2,2,320,448]{3,2,1,0:T(8,128)(2,1)S(1)} collective-permute-done((bf16[2,2,320,448]{3,2,1,0:T(8,128)(2,1)S(1)}, bf16[2,2,320,448]{3,2,1,0:T(8,128)(2,1)S(1)}, u32[]{:S(2)}, u32[]{:S(2)}) %collective-permute-start.98) | collective-permute-done | bytes 1146912 | tf_op jit(solution)/shard_map/ppermute | solution.py:21
  582.2 25.7 %collective-permute-done.99 = bf16[1,2,320,448]{3,2,1,0:T(8,128)(2,1)S(1)} collective-permute-done((bf16[1,2,320,448]{3,2,1,0:T(8,128)(2,1)S(1)}, bf16[1,2,320,448]{3,2,1,0:T(8,128)(2,1)S(1)}, u32[]{:S(2)}, u32[]{:S(2)}) %collective-permute-start.99) | collective-permute-done | bytes 573472 | tf_op jit(solution)/shard_map/ppermute | solution.py:21
  611.4 12.3 %collective-permute-done.62 = bf16[64,2560]{1,0:T(8,128)(2,1)S(1)} collective-permute-done((bf16[64,2560]{1,0:T(8,128)(2,1)S(1)}, bf16[64,2560]{1,0:T(8,128)(2,1)S(1)}, u32[]{:S(2)}, u32[]{:S(2)}) %collective-permute-start.62) | collective-permute-done | bytes 327712 | tf_op jit(solution)/shard_map/ppermute | solution.py:21
  628.6 18.9 %collective-permute-done.104 = bf16[320,448]{1,0:T(8,128)(2,1)S(1)} collective-permute-done((bf16[320,448]{1,0:T(8,128)(2,1)S(1)}, bf16[320,448]{1,0:T(8,128)(2,1)S(1)}, u32[]{:S(2)}, u32[]{:S(2)}) %collective-permute-start.104) | collective-permute-done | bytes 286752 | tf_op jit(solution)/shard_map/ppermute | solution.py:21
  647.5 14.6 %collective-permute-start.63 = (bf16[64,2560]{1,0:T(8,128)(2,1)}, bf16[64,2560]{1,0:T(8,128)(2,1)S(1)}, u32[]{:S(2)}, u32[]{:S(2)}) collective-permute-start(bf16[64,2560]{1,0:T(8,128)(2,1)} %get-tuple-element.111), channel_id=1, source_target_pairs={{0,8},{4,12},{8,0},{12,4},{16,24},{20,28},{24,16},{28,20},{1,9},{5... | collective-permute-start | bytes 983048 | tf_op jit(solution)/shard_map/ppermute | solution.py:21
  665.7 4.5 reshape.644
  675.5 8.0 collective-permute-done.65
  687.1 13.0 %collective-permute-done.91 = bf16[1,2,320,896]{3,2,1,0:T(8,128)(2,1)S(1)} collective-permute-done((bf16[1,2,320,896]{3,2,1,0:T(8,128)(2,1)S(1)}, bf16[1,2,320,896]{3,2,1,0:T(8,128)(2,1)S(1)}, u32[]{:S(2)}, u32[]{:S(2)}) %collective-permute-start.91) | collective-permute-done | bytes 1146912 | tf_op jit(solution)/shard_map/ppermute | solution.py:21
  739.7 4.8 collective-permute-done.96
  754.1 4.2 fusion.4
  760.3 5.5 reshape.611
  784.5 6.4 collective-permute-done.83
  792.8 7.5 collective-permute-start.87
  815.8 4.0 copy.351
  825.7 5.6 collective-permute-done.88
  835.7 8.6 collective-permute-done.78
  853.1 10.1 %collective-permute-done.70 = bf16[64,2560]{1,0:T(8,128)(2,1)S(1)} collective-permute-done((bf16[64,2560]{1,0:T(8,128)(2,1)S(1)}, bf16[64,2560]{1,0:T(8,128)(2,1)S(1)}, u32[]{:S(2)}, u32[]{:S(2)}) %collective-permute-start.70) | collective-permute-done | bytes 327712 | tf_op jit(solution)/shard_map/ppermute | solution.py:21
  870.8 5.1 collective-permute-done.79
  883.4 4.7 collective-permute-done.71
  900.4 12.2 %collective-permute-done.73 = bf16[128,2560]{1,0:T(8,128)(2,1)S(1)} collective-permute-done((bf16[128,2560]{1,0:T(8,128)(2,1)S(1)}, bf16[128,2560]{1,0:T(8,128)(2,1)S(1)}, u32[]{:S(2)}, u32[]{:S(2)}) %collective-permute-start.73) | collective-permute-done | bytes 655392 | tf_op jit(solution)/shard_map/ppermute | solution.py:21
  (754 shorter events, 432.8 us)
Async XLA Ops:
  6.3 126.7 %collective-permute-start.4 = (bf16[64,2560]{1,0:T(8,128)(2,1)S(1)}, bf16[64,2560]{1,0:T(8,128)(2,1)}, u32[]{:S(2)}, u32[]{:S(2)}) collective-permute-start(bf16[64,2560]{1,0:T(8,128)(2,1)S(1)} %reshape.573), channel_id=1, source_target_pairs={{0,8},{4,12},{8,0},{12,4},{16,24},{20,28},{24,16},{28,20},{1,9},{5... | collective-permute-start | bytes 983048 | tf_op jit(solution)/shard_map/ppermute | solution.py:21
  9.4 124.9 %collective-permute-start.5 = (bf16[64,2560]{1,0:T(8,128)(2,1)S(1)}, bf16[64,2560]{1,0:T(8,128)(2,1)}, u32[]{:S(2)}, u32[]{:S(2)}) collective-permute-start(bf16[64,2560]{1,0:T(8,128)(2,1)S(1)} %reshape.573), channel_id=1, source_target_pairs={{0,16},{4,20},{8,24},{12,28},{16,0},{20,4},{24,8},{28,12},{1,17},{... | collective-permute-start | bytes 983048 | tf_op jit(solution)/shard_map/ppermute | solution.py:21
  12.0 48.5 %collective-permute-start = (s32[128]{0:T(128)S(1)}, s32[128]{0:T(128)}, u32[]{:S(2)}, u32[]{:S(2)}) collective-permute-start(s32[128]{0:T(128)S(1)} %dynamic_slice.98), channel_id=1, source_target_pairs={{0,8},{4,12},{8,0},{12,4},{16,24},{20,28},{24,16},{28,20},{1,9},{5... | collective-permute-start | bytes 1544 | tf_op jit(solution)/shard_map/ppermute | solution.py:21
  12.5 48.8 %collective-permute-start.1 = (s32[128]{0:T(128)S(1)}, s32[128]{0:T(128)}, u32[]{:S(2)}, u32[]{:S(2)}) collective-permute-start(s32[128]{0:T(128)S(1)} %dynamic_slice.98), channel_id=1, source_target_pairs={{0,16},{4,20},{8,24},{12,28},{16,0},{20,4},{24,8},{28,12},{1,17},{... | collective-permute-start | bytes 1544 | tf_op jit(solution)/shard_map/ppermute | solution.py:21
  12.5 50.0 %collective-permute-start.2 = (s32[128]{0:T(128)S(1)}, s32[128]{0:T(128)S(1)}, u32[]{:S(2)}, u32[]{:S(2)}) collective-permute-start(s32[128]{0:T(128)S(1)} %dynamic_slice.98), channel_id=1, source_target_pairs={{0,24},{4,28},{8,16},{12,20},{16,8},{20,12},{24,0},{28,4},{1,25},{... | collective-permute-start | bytes 1544 | tf_op jit(solution)/shard_map/ppermute | solution.py:21
  60.5 42.4 %collective-permute-start.8 = (bf16[320,322]{1,0:T(8,128)(2,1)}, bf16[320,322]{1,0:T(8,128)(2,1)}, u32[]{:S(2)}, u32[]{:S(2)}) collective-permute-start(bf16[320,322]{1,0:T(8,128)(2,1)} %bitcast.392), channel_id=1, source_target_pairs={{0,8},{4,12},{8,0},{12,4},{16,24},{20,28},{24,16},{28,20},{1,9},{5... | collective-permute-start | bytes 618248 | tf_op jit(solution)/shard_map/ppermute | solution.py:21
  61.3 42.8 %collective-permute-start.9 = (bf16[320,322]{1,0:T(8,128)(2,1)}, bf16[320,322]{1,0:T(8,128)(2,1)}, u32[]{:S(2)}, u32[]{:S(2)}) collective-permute-start(bf16[320,322]{1,0:T(8,128)(2,1)} %bitcast.391), channel_id=1, source_target_pairs={{0,16},{4,20},{8,24},{12,28},{16,0},{20,4},{24,8},{28,12},{1,17},{... | collective-permute-start | bytes 618248 | tf_op jit(solution)/shard_map/ppermute | solution.py:21
  106.8 32.5 %collective-permute-start.23 = (bf16[1,2,320,160]{2,3,1,0:T(8,128)(2,1)}, bf16[1,2,320,160]{2,3,1,0:T(8,128)(2,1)}, u32[]{:S(2)}, u32[]{:S(2)}) collective-permute-start(bf16[1,2,320,160]{2,3,1,0:T(8,128)(2,1)} %get-tuple-element.194), channel_id=1, source_target_pairs={{0,2},{1,3},{2,0},{3,1},{4,6},{5,7},{6,4},{7,5},{8,10},{9,11},{10,... | collective-permute-start | bytes 614408 | tf_op jit(solution)/shard_map/ppermute | solution.py:21
  124.7 37.7 %collective-permute-start.14 = (bf16[1,2,320,322]{2,3,1,0:T(8,128)(2,1)}, bf16[1,2,320,322]{2,3,1,0:T(8,128)(2,1)}, u32[]{:S(2)}, u32[]{:S(2)}) collective-permute-start(bf16[1,2,320,322]{2,3,1,0:T(8,128)(2,1)} %get-tuple-element.166), channel_id=1, source_target_pairs={{0,2},{1,3},{2,0},{3,1},{4,6},{5,7},{6,4},{7,5},{8,10},{9,11},{10,... | collective-permute-start | bytes 1236488 | tf_op jit(solution)/shard_map/ppermute | solution.py:21
  164.9 78.9 %collective-permute-start.33 = (bf16[320,896]{1,0:T(8,128)(2,1)}, bf16[320,896]{1,0:T(8,128)(2,1)}, u32[]{:S(2)}, u32[]{:S(2)}) collective-permute-start(bf16[320,896]{1,0:T(8,128)(2,1)} %bitcast.331), channel_id=1, source_target_pairs={{0,8},{4,12},{8,0},{12,4},{16,24},{20,28},{24,16},{28,20},{1,9},{5... | collective-permute-start | bytes 1720328 | tf_op jit(solution)/shard_map/ppermute | solution.py:21
  167.1 77.9 %collective-permute-start.34 = (bf16[320,896]{1,0:T(8,128)(2,1)}, bf16[320,896]{1,0:T(8,128)(2,1)}, u32[]{:S(2)}, u32[]{:S(2)}) collective-permute-start(bf16[320,896]{1,0:T(8,128)(2,1)} %bitcast.330), channel_id=1, source_target_pairs={{0,16},{4,20},{8,24},{12,28},{16,0},{20,4},{24,8},{28,12},{1,17},{... | collective-permute-start | bytes 1720328 | tf_op jit(solution)/shard_map/ppermute | solution.py:21
  173.9 72.3 %collective-permute-start.35 = (bf16[320,896]{1,0:T(8,128)(2,1)}, bf16[320,896]{1,0:T(8,128)(2,1)}, u32[]{:S(2)}, u32[]{:S(2)}) collective-permute-start(bf16[320,896]{1,0:T(8,128)(2,1)} %bitcast.387), channel_id=1, source_target_pairs={{0,24},{4,28},{8,16},{12,20},{16,8},{20,12},{24,0},{28,4},{1,25},{... | collective-permute-start | bytes 1720328 | tf_op jit(solution)/shard_map/ppermute | solution.py:21
  177.9 64.3 %collective-permute-start.39 = (bf16[320,448]{1,0:T(8,128)(2,1)}, bf16[320,448]{1,0:T(8,128)(2,1)}, u32[]{:S(2)}, u32[]{:S(2)}) collective-permute-start(bf16[320,448]{1,0:T(8,128)(2,1)} %bitcast.389), channel_id=1, source_target_pairs={{0,16},{4,20},{8,24},{12,28},{16,0},{20,4},{24,8},{28,12},{1,17},{... | collective-permute-start | bytes 860168 | tf_op jit(solution)/shard_map/ppermute | solution.py:21
  202.7 46.7 %collective-permute-start.40 = (bf16[320,448]{1,0:T(8,128)(2,1)S(1)}, bf16[320,448]{1,0:T(8,128)(2,1)S(1)}, u32[]{:S(2)}, u32[]{:S(2)}) collective-permute-start(bf16[320,448]{1,0:T(8,128)(2,1)S(1)} %bitcast.388), channel_id=1, source_target_pairs={{0,24},{4,28},{8,16},{12,20},{16,8},{20,12},{24,0},{28,4},{1,25},{... | collective-permute-start | bytes 860168 | tf_op jit(solution)/shard_map/ppermute | solution.py:21
  247.5 43.2 %collective-permute-start.36 = (bf16[1,2,320,896]{3,2,1,0:T(8,128)(2,1)S(1)}, bf16[1,2,320,896]{3,2,1,0:T(8,128)(2,1)S(1)}, u32[]{:S(2)}, u32[]{:S(2)}) collective-permute-start(bf16[1,2,320,896]{3,2,1,0:T(8,128)(2,1)S(1)} %get-tuple-element.143), channel_id=1, source_target_pairs={{0,4},{4,0},{8,12},{12,8},{16,20},{20,16},{24,28},{28,24},{1,5},{5... | collective-permute-start | bytes 3440648 | tf_op jit(solution)/shard_map/ppermute | solution.py:21
  251.5 37.7 %collective-permute-start.41 = (bf16[1,2,320,448]{3,2,1,0:T(8,128)(2,1)S(1)}, bf16[1,2,320,448]{3,2,1,0:T(8,128)(2,1)S(1)}, u32[]{:S(2)}, u32[]{:S(2)}) collective-permute-start(bf16[1,2,320,448]{3,2,1,0:T(8,128)(2,1)S(1)} %get-tuple-element.157), channel_id=1, source_target_pairs={{0,4},{4,0},{8,12},{12,8},{16,20},{20,16},{24,28},{28,24},{1,5},{5... | collective-permute-start | bytes 1720328 | tf_op jit(solution)/shard_map/ppermute | solution.py:21
  252.4 39.4 %collective-permute-start.26 = (bf16[64,2560]{1,0:T(8,128)(2,1)S(1)}, bf16[64,2560]{1,0:T(8,128)(2,1)S(1)}, u32[]{:S(2)}, u32[]{:S(2)}) collective-permute-start(bf16[64,2560]{1,0:T(8,128)(2,1)S(1)} %get-tuple-element.163), channel_id=1, source_target_pairs={{0,8},{4,12},{8,0},{12,4},{16,24},{20,28},{24,16},{28,20},{1,9},{5... | collective-permute-start | bytes 983048 | tf_op jit(solution)/shard_map/ppermute | solution.py:21
  260.0 33.0 %collective-permute-start.28 = (bf16[64,2560]{1,0:T(8,128)(2,1)S(1)}, bf16[64,2560]{1,0:T(8,128)(2,1)S(1)}, u32[]{:S(2)}, u32[]{:S(2)}) collective-permute-start(bf16[64,2560]{1,0:T(8,128)(2,1)S(1)} %fusion.38), channel_id=1, source_target_pairs={{0,16},{4,20},{8,24},{12,28},{16,0},{20,4},{24,8},{28,12},{1,17},{... | collective-permute-start | bytes 983048 | tf_op jit(solution)/shard_map/ppermute | solution.py:21
  260.7 34.2 %collective-permute-start.47 = (bf16[1,2,320,448]{3,2,1,0:T(8,128)(2,1)S(1)}, bf16[1,2,320,448]{3,2,1,0:T(8,128)(2,1)S(1)}, u32[]{:S(2)}, u32[]{:S(2)}) collective-permute-start(bf16[1,2,320,448]{3,2,1,0:T(8,128)(2,1)S(1)} %get-tuple-element.158), channel_id=1, source_target_pairs={{0,2},{1,3},{2,0},{3,1},{4,6},{5,7},{6,4},{7,5},{8,10},{9,11},{10,... | collective-permute-start | bytes 1720328 | tf_op jit(solution)/shard_map/ppermute | solution.py:21
  290.7 55.2 %collective-permute-start.37 = (bf16[1,2,320,896]{3,2,1,0:T(8,128)(2,1)S(1)}, bf16[1,2,320,896]{3,2,1,0:T(8,128)(2,1)S(1)}, u32[]{:S(2)}, u32[]{:S(2)}) collective-permute-start(bf16[1,2,320,896]{3,2,1,0:T(8,128)(2,1)S(1)} %get-tuple-element.144), channel_id=1, source_target_pairs={{0,4},{4,0},{8,12},{12,8},{16,20},{20,16},{24,28},{28,24},{1,5},{5... | collective-permute-start | bytes 3440648 | tf_op jit(solution)/shard_map/ppermute | solution.py:21
  291.8 52.5 %collective-permute-start.44 = (bf16[1,2,320,896]{3,2,1,0:T(8,128)(2,1)S(1)}, bf16[1,2,320,896]{3,2,1,0:T(8,128)(2,1)S(1)}, u32[]{:S(2)}, u32[]{:S(2)}) collective-permute-start(bf16[1,2,320,896]{3,2,1,0:T(8,128)(2,1)S(1)} %get-tuple-element.144), channel_id=1, source_target_pairs={{0,2},{1,3},{2,0},{3,1},{4,6},{5,7},{6,4},{7,5},{8,10},{9,11},{10,... | collective-permute-start | bytes 3440648 | tf_op jit(solution)/shard_map/ppermute | solution.py:21
  293.0 103.0 %collective-permute-start.43 = (bf16[2,2,320,896]{3,2,1,0:T(8,128)(2,1)S(1)}, bf16[2,2,320,896]{3,2,1,0:T(8,128)(2,1)S(1)}, u32[]{:S(2)}, u32[]{:S(2)}) collective-permute-start(bf16[2,2,320,896]{3,2,1,0:T(8,128)(2,1)S(1)} %pad_maximum_fusion.4), channel_id=1, source_target_pairs={{0,2},{1,3},{2,0},{3,1},{4,6},{5,7},{6,4},{7,5},{8,10},{9,11},{10,... | collective-permute-start | bytes 6881288 | tf_op jit(solution)/shard_map/ppermute | solution.py:21
  294.8 100.6 %collective-permute-start.46 = (bf16[2,2,320,448]{3,2,1,0:T(8,128)(2,1)S(1)}, bf16[2,2,320,448]{3,2,1,0:T(8,128)(2,1)S(1)}, u32[]{:S(2)}, u32[]{:S(2)}) collective-permute-start(bf16[2,2,320,448]{3,2,1,0:T(8,128)(2,1)S(1)} %pad_maximum_fusion.7), channel_id=1, source_target_pairs={{0,2},{1,3},{2,0},{3,1},{4,6},{5,7},{6,4},{7,5},{8,10},{9,11},{10,... | collective-permute-start | bytes 3440648 | tf_op jit(solution)/shard_map/ppermute | solution.py:21
  306.9 37.3 %collective-permute-start.48 = (bf16[1,2,320,448]{3,2,1,0:T(8,128)(2,1)S(1)}, bf16[1,2,320,448]{3,2,1,0:T(8,128)(2,1)S(1)}, u32[]{:S(2)}, u32[]{:S(2)}) collective-permute-start(bf16[1,2,320,448]{3,2,1,0:T(8,128)(2,1)S(1)} %collective-permute-done.47), channel_id=1, source_target_pairs={{0,4},{4,0},{8,12},{12,8},{16,20},{20,16},{24,28},{28,24},{1,5},{5... | collective-permute-start | bytes 1720328 | tf_op jit(solution)/shard_map/ppermute | solution.py:21
  344.3 51.7 %collective-permute-start.45 = (bf16[1,2,320,896]{3,2,1,0:T(8,128)(2,1)S(1)}, bf16[1,2,320,896]{3,2,1,0:T(8,128)(2,1)S(1)}, u32[]{:S(2)}, u32[]{:S(2)}) collective-permute-start(bf16[1,2,320,896]{3,2,1,0:T(8,128)(2,1)S(1)} %collective-permute-done.44), channel_id=1, source_target_pairs={{0,4},{4,0},{8,12},{12,8},{16,20},{20,16},{24,28},{28,24},{1,5},{5... | collective-permute-start | bytes 3440648 | tf_op jit(solution)/shard_map/ppermute | solution.py:21
  345.9 49.8 %collective-permute-start.29 = (bf16[64,2560]{1,0:T(8,128)(2,1)S(1)}, bf16[64,2560]{1,0:T(8,128)(2,1)S(1)}, u32[]{:S(2)}, u32[]{:S(2)}) collective-permute-start(bf16[64,2560]{1,0:T(8,128)(2,1)S(1)} %get-tuple-element.122), channel_id=1, source_target_pairs={{0,8},{4,12},{8,0},{12,4},{16,24},{20,28},{24,16},{28,20},{1,9},{5... | collective-permute-start | bytes 983048 | tf_op jit(solution)/shard_map/ppermute | solution.py:21
  360.2 35.6 %collective-permute-start.31 = (bf16[64,2560]{1,0:T(8,128)(2,1)S(1)}, bf16[64,2560]{1,0:T(8,128)(2,1)S(1)}, u32[]{:S(2)}, u32[]{:S(2)}) collective-permute-start(bf16[64,2560]{1,0:T(8,128)(2,1)S(1)} %collective-permute-done.30), channel_id=1, source_target_pairs={{0,8},{4,12},{8,0},{12,4},{16,24},{20,28},{24,16},{28,20},{1,9},{5... | collective-permute-start | bytes 983048 | tf_op jit(solution)/shard_map/ppermute | solution.py:21
  521.7 29.2 %collective-permute-start.59 = (bf16[256,2560]{1,0:T(8,128)(2,1)}, bf16[256,2560]{1,0:T(8,128)(2,1)}, u32[]{:S(2)}, u32[]{:S(2)}) collective-permute-start(bf16[256,2560]{1,0:T(8,128)(2,1)} %slice.818), channel_id=1, source_target_pairs={{0,1},{1,0},{2,3},{3,2},{4,5},{5,4},{6,7},{7,6},{8,9},{9,8},{10,11... | collective-permute-start | bytes 3932168 | tf_op jit(solution)/shard_map/ppermute | solution.py:21
  539.1 38.4 %collective-permute-start.98 = (bf16[2,2,320,448]{3,2,1,0:T(8,128)(2,1)S(1)}, bf16[2,2,320,448]{3,2,1,0:T(8,128)(2,1)S(1)}, u32[]{:S(2)}, u32[]{:S(2)}) collective-permute-start(bf16[2,2,320,448]{3,2,1,0:T(8,128)(2,1)S(1)} %slice.648), channel_id=1, source_target_pairs={{0,2},{1,3},{2,0},{3,1},{4,6},{5,7},{6,4},{7,5},{8,10},{9,11},{10,... | collective-permute-start | bytes 3440648 | tf_op jit(solution)/shard_map/ppermute | solution.py:21
  540.0 38.8 %collective-permute-start.93 = (bf16[1,2,320,896]{3,2,1,0:T(8,128)(2,1)S(1)}, bf16[1,2,320,896]{3,2,1,0:T(8,128)(2,1)S(1)}, u32[]{:S(2)}, u32[]{:S(2)}) collective-permute-start(bf16[1,2,320,896]{3,2,1,0:T(8,128)(2,1)S(1)} %slice.644), channel_id=1, source_target_pairs={{0,4},{4,0},{8,12},{12,8},{16,20},{20,16},{24,28},{28,24},{1,5},{5... | collective-permute-start | bytes 3440648 | tf_op jit(solution)/shard_map/ppermute | solution.py:21
  546.6 138.1 %collective-permute-start.92 = (bf16[1,2,320,896]{3,2,1,0:T(8,128)(2,1)}, bf16[1,2,320,896]{3,2,1,0:T(8,128)(2,1)}, u32[]{:S(2)}, u32[]{:S(2)}) collective-permute-start(bf16[1,2,320,896]{3,2,1,0:T(8,128)(2,1)} %slice.642), channel_id=1, source_target_pairs={{0,4},{4,0},{8,12},{12,8},{16,20},{20,16},{24,28},{28,24},{1,5},{5... | collective-permute-start | bytes 3440648 | tf_op jit(solution)/shard_map/ppermute | solution.py:21
  549.4 120.8 %collective-permute-start.90 = (bf16[2,2,320,896]{3,2,1,0:T(8,128)(2,1)}, bf16[2,2,320,896]{3,2,1,0:T(8,128)(2,1)}, u32[]{:S(2)}, u32[]{:S(2)}) collective-permute-start(bf16[2,2,320,896]{3,2,1,0:T(8,128)(2,1)} %slice.638), channel_id=1, source_target_pairs={{0,2},{1,3},{2,0},{3,1},{4,6},{5,7},{6,4},{7,5},{8,10},{9,11},{10,... | collective-permute-start | bytes 6881288 | tf_op jit(solution)/shard_map/ppermute | solution.py:21
  552.7 28.6 %collective-permute-start.61 = (bf16[64,2560]{1,0:T(8,128)(2,1)S(1)}, bf16[64,2560]{1,0:T(8,128)(2,1)S(1)}, u32[]{:S(2)}, u32[]{:S(2)}) collective-permute-start(bf16[64,2560]{1,0:T(8,128)(2,1)S(1)} %get-tuple-element.154), channel_id=1, source_target_pairs={{0,8},{4,12},{8,0},{12,4},{16,24},{20,28},{24,16},{28,20},{1,9},{5... | collective-permute-start | bytes 983048 | tf_op jit(solution)/shard_map/ppermute | solution.py:21
  577.9 29.9 %collective-permute-start.99 = (bf16[1,2,320,448]{3,2,1,0:T(8,128)(2,1)S(1)}, bf16[1,2,320,448]{3,2,1,0:T(8,128)(2,1)S(1)}, u32[]{:S(2)}, u32[]{:S(2)}) collective-permute-start(bf16[1,2,320,448]{3,2,1,0:T(8,128)(2,1)S(1)} %slice.650), channel_id=1, source_target_pairs={{0,4},{4,0},{8,12},{12,8},{16,20},{20,16},{24,28},{28,24},{1,5},{5... | collective-permute-start | bytes 1720328 | tf_op jit(solution)/shard_map/ppermute | solution.py:21
  580.1 104.6 %collective-permute-start.94 = (bf16[1,2,320,896]{3,2,1,0:T(8,128)(2,1)}, bf16[1,2,320,896]{3,2,1,0:T(8,128)(2,1)}, u32[]{:S(2)}, u32[]{:S(2)}) collective-permute-start(bf16[1,2,320,896]{3,2,1,0:T(8,128)(2,1)} %add_convert_fusion.3), channel_id=1, source_target_pairs={{0,2},{1,3},{2,0},{3,1},{4,6},{5,7},{6,4},{7,5},{8,10},{9,11},{10,... | collective-permute-start | bytes 3440648 | tf_op jit(solution)/shard_map/ppermute | solution.py:21
  581.3 28.9 %collective-permute-start.60 = (bf16[64,2560]{1,0:T(8,128)(2,1)S(1)}, bf16[64,2560]{1,0:T(8,128)(2,1)S(1)}, u32[]{:S(2)}, u32[]{:S(2)}) collective-permute-start(bf16[64,2560]{1,0:T(8,128)(2,1)S(1)} %get-tuple-element.153), channel_id=1, source_target_pairs={{0,8},{4,12},{8,0},{12,4},{16,24},{20,28},{24,16},{28,20},{1,9},{5... | collective-permute-start | bytes 983048 | tf_op jit(solution)/shard_map/ppermute | solution.py:21
  647.5 28.0 %collective-permute-start.63 = (bf16[64,2560]{1,0:T(8,128)(2,1)}, bf16[64,2560]{1,0:T(8,128)(2,1)S(1)}, u32[]{:S(2)}, u32[]{:S(2)}) collective-permute-start(bf16[64,2560]{1,0:T(8,128)(2,1)} %get-tuple-element.111), channel_id=1, source_target_pairs={{0,8},{4,12},{8,0},{12,4},{16,24},{20,28},{24,16},{28,20},{1,9},{5... | collective-permute-start | bytes 983048 | tf_op jit(solution)/shard_map/ppermute | solution.py:21
  702.5 34.7 %collective-permute-start.95 = (bf16[320,896]{1,0:T(8,128)(2,1)}, bf16[320,896]{1,0:T(8,128)(2,1)}, u32[]{:S(2)}, u32[]{:S(2)}) collective-permute-start(bf16[320,896]{1,0:T(8,128)(2,1)} %get-tuple-element.141), channel_id=1, source_target_pairs={{0,8},{4,12},{8,0},{12,4},{16,24},{20,28},{24,16},{28,20},{1,9},{5... | collective-permute-start | bytes 1720328 | tf_op jit(solution)/shard_map/ppermute | solution.py:21
  702.8 41.7 %collective-permute-start.96 = (bf16[320,896]{1,0:T(8,128)(2,1)}, bf16[320,896]{1,0:T(8,128)(2,1)}, u32[]{:S(2)}, u32[]{:S(2)}) collective-permute-start(bf16[320,896]{1,0:T(8,128)(2,1)} %get-tuple-element.142), channel_id=1, source_target_pairs={{0,16},{4,20},{8,24},{12,28},{16,0},{20,4},{24,8},{28,12},{1,17},{... | collective-permute-start | bytes 1720328 | tf_op jit(solution)/shard_map/ppermute | solution.py:21
  704.8 40.9 %collective-permute-start.97 = (bf16[320,896]{1,0:T(8,128)(2,1)}, bf16[320,896]{1,0:T(8,128)(2,1)}, u32[]{:S(2)}, u32[]{:S(2)}) collective-permute-start(bf16[320,896]{1,0:T(8,128)(2,1)} %get-tuple-element.139), channel_id=1, source_target_pairs={{0,24},{4,28},{8,16},{12,20},{16,8},{20,12},{24,0},{28,4},{1,25},{... | collective-permute-start | bytes 1720328 | tf_op jit(solution)/shard_map/ppermute | solution.py:21
  737.2 45.3 %collective-permute-start.84 = (bf16[1,2,320,160]{2,3,1,0:T(8,128)(2,1)}, bf16[1,2,320,160]{2,3,1,0:T(8,128)(2,1)}, u32[]{:S(2)}, u32[]{:S(2)}) collective-permute-start(bf16[1,2,320,160]{2,3,1,0:T(8,128)(2,1)} %copy.364), channel_id=1, source_target_pairs={{0,4},{4,0},{8,12},{12,8},{16,20},{20,16},{24,28},{28,24},{1,5},{5... | collective-permute-start | bytes 614408 | tf_op jit(solution)/shard_map/ppermute | solution.py:21
  744.5 36.9 %collective-permute-start.82 = (bf16[2,2,320,160]{2,3,1,0:T(8,128)(2,1)}, bf16[2,2,320,160]{2,3,1,0:T(8,128)(2,1)}, u32[]{:S(2)}, u32[]{:S(2)}) collective-permute-start(bf16[2,2,320,160]{2,3,1,0:T(8,128)(2,1)} %copy.362), channel_id=1, source_target_pairs={{0,2},{1,3},{2,0},{3,1},{4,6},{5,7},{6,4},{7,5},{8,10},{9,11},{10,... | collective-permute-start | bytes 1228808 | tf_op jit(solution)/shard_map/ppermute | solution.py:21
  748.9 34.5 %collective-permute-start.86 = (bf16[1,2,320,160]{2,3,1,0:T(8,128)(2,1)S(1)}, bf16[1,2,320,160]{2,3,1,0:T(8,128)(2,1)}, u32[]{:S(2)}, u32[]{:S(2)}) collective-permute-start(bf16[1,2,320,160]{2,3,1,0:T(8,128)(2,1)S(1)} %add_convert_fusion.17), channel_id=1, source_target_pairs={{0,2},{1,3},{2,0},{3,1},{4,6},{5,7},{6,4},{7,5},{8,10},{9,11},{10,... | collective-permute-start | bytes 614408 | tf_op jit(solution)/shard_map/ppermute | solution.py:21
  772.2 50.3 %collective-permute-start.77 = (bf16[1,2,320,322]{3,2,1,0:T(8,128)(2,1)}, bf16[1,2,320,322]{3,2,1,0:T(8,128)(2,1)}, u32[]{:S(2)}, u32[]{:S(2)}) collective-permute-start(bf16[1,2,320,322]{3,2,1,0:T(8,128)(2,1)} %copy.360), channel_id=1, source_target_pairs={{0,4},{4,0},{8,12},{12,8},{16,20},{20,16},{24,28},{28,24},{1,5},{5... | collective-permute-start | bytes 1236488 | tf_op jit(solution)/shard_map/ppermute | solution.py:21
  776.4 56.5 %collective-permute-start.74 = (bf16[2,2,320,322]{3,2,1,0:T(8,128)(2,1)}, bf16[2,2,320,322]{3,2,1,0:T(8,128)(2,1)}, u32[]{:S(2)}, u32[]{:S(2)}) collective-permute-start(bf16[2,2,320,322]{3,2,1,0:T(8,128)(2,1)} %copy.323), channel_id=1, source_target_pairs={{0,2},{1,3},{2,0},{3,1},{4,6},{5,7},{6,4},{7,5},{8,10},{9,11},{10,... | collective-permute-start | bytes 2472968 | tf_op jit(solution)/shard_map/ppermute | solution.py:21
  781.4 63.2 %collective-permute-start.68 = (bf16[256,2560]{1,0:T(8,128)(2,1)}, bf16[256,2560]{1,0:T(8,128)(2,1)}, u32[]{:S(2)}, u32[]{:S(2)}) collective-permute-start(bf16[256,2560]{1,0:T(8,128)(2,1)} %slice.817), channel_id=1, source_target_pairs={{0,1},{1,0},{2,3},{3,2},{4,5},{5,4},{6,7},{7,6},{8,9},{9,8},{10,11... | collective-permute-start | bytes 3932168 | tf_op jit(solution)/shard_map/ppermute | solution.py:21
  822.5 41.6 %collective-permute-start.89 = (bf16[320,160]{0,1:T(8,128)(2,1)}, bf16[320,160]{0,1:T(8,128)(2,1)S(1)}, u32[]{:S(2)}, u32[]{:S(2)}) collective-permute-start(bf16[320,160]{0,1:T(8,128)(2,1)} %get-tuple-element.185), channel_id=1, source_target_pairs={{0,24},{4,28},{8,16},{12,20},{16,8},{20,12},{24,0},{28,4},{1,25},{... | collective-permute-start | bytes 307208 | tf_op jit(solution)/shard_map/ppermute | solution.py:21
  851.0 27.8 %collective-permute-start.81 = (bf16[320,322]{1,0:T(8,128)(2,1)}, bf16[320,322]{1,0:T(8,128)(2,1)}, u32[]{:S(2)}, u32[]{:S(2)}) collective-permute-start(bf16[320,322]{1,0:T(8,128)(2,1)} %get-tuple-element.175), channel_id=1, source_target_pairs={{0,24},{4,28},{8,16},{12,20},{16,8},{20,12},{24,0},{28,4},{1,25},{... | collective-permute-start | bytes 618248 | tf_op jit(solution)/shard_map/ppermute | solution.py:21
  (185 other events, 2330.1 us)

commit v2 on v1

v2 whole, which is shorter than its diff:
```python
import functools

import jax
import jax.numpy as jnp
from jax import lax
from jax.experimental import pallas as pl
from jax.experimental.pallas import tpu as pltpu
from jax.sharding import PartitionSpec as P

HEAD_DIM = 80
SPAN = 128
EPS = 1e-05
THETA = 1000000.0
PARTS = 4
BF = jnp.bfloat16
F32 = jnp.float32
FACTOR = HEAD_DIM**-0.5
LOG2E = 1.4426950408889634
LIMIT = 56 * 1024 * 1024

PLAIN = (((1,), (0,)), ((), ()))
LAST = (((1,), (1,)), ((), ()))
ROWS = (((0,), (0,)), ((), ()))

VM = pl.BlockSpec(memory_space=pltpu.VMEM)
SM = pl.BlockSpec(memory_space=pltpu.SMEM)
ANY = pl.BlockSpec(memory_space=pl.ANY)


def shape(dims, kind=BF):
    return jax.ShapeDtypeStruct(tuple(dims), kind)


def call(body, outs, in_specs, out_specs, scratch=(), flops=0, moved=0):
    return pl.pallas_call(
        body,
        out_shape=outs,
        in_specs=in_specs,
        out_specs=out_specs,
        scratch_shapes=list(scratch),
        compiler_params=pltpu.CompilerParams(vmem_limit_bytes=LIMIT),
        cost_estimate=pl.CostEstimate(flops=int(flops), bytes_accessed=int(moved), transcendentals=0),
    )


def hop(value, axis, k):
    size = lax.axis_size(axis)
    return lax.ppermute(value, axis, [(i, i ^ k) for i in range(size)])


def dot(left, right, dims=PLAIN):
    return lax.dot_general(left, right, dims, preferred_element_type=F32)


def put(refs, values):
    for ref, value in zip(refs, values):
        ref[...] = value.astype(ref.dtype)


def joined(values, width):
    values = [v.astype(F32) for v in values]
    have = sum(v.shape[1] for v in values)
    if have < width:
        values.append(jnp.zeros((values[0].shape[0], width - have), F32))
    return jnp.concatenate(values, axis=1).astype(BF)


def pack_body(takes, width, z_ref, *refs):
    count = len(takes)
    ins, outs = refs[:count], refs[count:]
    for k in range(PARTS):
        part = z_ref[0] ^ k
        for j in range(PARTS):

            @pl.when(part == j)
            def _():
                values = [ref[:, pl.ds(step * (j // share), step)] for ref, (step, share) in zip(ins, takes)]
                outs[k][...] = joined(values, width)


def pack(z, arrays, takes, width):
    depth = arrays[0].shape[0]
    return call(
        functools.partial(pack_body, takes, width),
        [shape((depth, width))] * PARTS,
        [SM] + [VM] * len(arrays),
        [VM] * PARTS,
        moved=depth * width * 2 * 8,
    )(z, *arrays)


def place_body(back, z_ref, *refs):
    pieces, halves = (refs[2:6], refs[:2]) if back else (refs[:4], refs[4:6])
    depth = pieces[0].shape[0]
    for k in range(PARTS):
        part = z_ref[0] ^ k
        for j in range(PARTS):

            @pl.when(part == j)
            def _():
                spot = pl.ds((j % 2) * depth, depth)
                if back:
                    pieces[k][...] = halves[j // 2][spot, :]
                else:
                    halves[j // 2][spot, :] = pieces[k][...]


def to_halves(z, pieces):
    depth, cols = pieces[0].shape
    return call(
        functools.partial(place_body, False),
        [shape((2 * depth, cols))] * 2,
        [SM] + [VM] * 4,
        [VM] * 2,
        moved=depth * cols * 16,
    )(z, *pieces)


def to_pieces(z, halves):
    depth, cols = halves[0].shape
    depth //= 2
    return call(
        functools.partial(place_body, True),
        [shape((depth, cols))] * 4,
        [SM] + [VM] * 2,
        [VM] * 4,
        moved=depth * cols * 16,
    )(z, *halves)


def unpack_body(takes, z_ref, *refs):
    ins, outs = refs[:PARTS], refs[PARTS:]
    for ref, (start, step, share) in zip(outs, takes):
        if share == 2:
            ref[...] = jnp.zeros_like(ref)
    for k in range(PARTS):
        part = z_ref[0] ^ k
        for j in range(PARTS):

            @pl.when(part == j)
            def _():
                for ref, (start, step, share) in zip(outs, takes):
                    value = ins[k][:, pl.ds(start, step)].astype(F32)
                    spot = pl.ds(step * (j // share), step)
                    if share == 1:
                        ref[:, spot] = value
                    else:
                        ref[:, spot] += value


def unpack(z, pieces, takes):
    depth = pieces[0].shape[0]
    return call(
        functools.partial(unpack_body, takes),
        [shape((depth, step * PARTS // share), F32) for start, step, share in takes],
        [SM] + [VM] * 4,
        [VM] * len(takes),
        moved=depth * pieces[0].shape[1] * 24,
    )(z, *pieces)


def fetch(pieces, store, sem, base=0):
    copies = []
    step = pieces[0].shape[0]
    for p, piece in enumerate(pieces):
        spot = store.at[pl.ds(p * step, step)]
        copies.append(pltpu.make_async_copy(piece, spot, sem.at[base + p]))
        copies[-1].start()

    def wait():
        for c in copies:
            c.wait()

    return wait


def rotated(value, cosine, sine):
    half = HEAD_DIM // 2
    a, b = value[:, :half], value[:, half:]
    return jnp.concatenate([a * cosine - b * sine, b * cosine + a * sine], axis=1)


def project_body(qw, x_mine, x_theirs, cosine, sine, *refs):
    w = refs[:8]
    first, q_ref, kv_ref, gains = refs[8:12]
    store, sem = refs[12:]
    waits = [fetch(w[4 * i : 4 * i + 4], store.at[i], sem, 4 * i) for i in range(2)]
    rows = x_mine.shape[0]
    waits[0]()
    step = w[0].shape[0]
    spot = 480 - 384
    for p in range(4):
        tail = store[0, pl.ds(p * step, step), 384:512].astype(F32).T
        gains[:, pl.ds(p * step, step)] = tail[spot : spot + 8]
    gain = gains[0:1, :]
    for i, ref in enumerate((x_mine, x_theirs)):
        x = ref[...].astype(F32)
        scale = lax.rsqrt(jnp.mean(x * x, axis=-1, keepdims=True) + EPS)
        first[pl.ds(i * rows, rows), :] = (x * scale * gain).astype(BF)
    cos, sin = cosine[...], sine[...]
    queries, keys, values = [], [], []
    for i in range(2):
        if i:
            waits[1]()
        out = dot(first[...], store[i])
        for start in range(0, qw, HEAD_DIM):
            queries.append(rotated(out[:, start : start + HEAD_DIM], cos, sin))
        keys.append(rotated(out[:, qw : qw + HEAD_DIM], cos, sin))
        values.append(out[:, qw + HEAD_DIM : qw + 2 * HEAD_DIM])
    q_ref[...] = jnp.concatenate(queries, axis=1).astype(BF)
    kv_ref[...] = jnp.concatenate(keys + values, axis=1).astype(BF)


def project(x_mine, x_theirs, cosine, sine, w, qw):
    rows, width = x_mine.shape
    return call(
        functools.partial(project_body, qw),
        [shape((2 * rows, width)), shape((2 * rows, 2 * qw)), shape((2 * rows, 4 * HEAD_DIM)), shape((8, width), F32)],
        [VM] * 4 + [ANY] * 8,
        [VM] * 4,
        [pltpu.VMEM((2, width, 512), BF), pltpu.SemaphoreType.DMA((8,))],
        flops=4 * 2 * rows * width * 512,
        moved=2 * width * 512 * 2 + 4 * rows * width * 2,
    )(x_mine, x_theirs, cosine, sine, *w)


def out_sides(partial, mine, theirs):
    n = mine.shape[0]
    mine[...] = partial[:n]
    theirs[...] = partial[n:].astype(theirs.dtype)


def each(count, step, start):
    if count <= 2:
        for s in range(count):
            start = step(s, start)
        return start
    return lax.fori_loop(0, count, step, start)


def reader(kvs, rows):
    def read(s, lane):
        spot = pl.ds(lane * HEAD_DIM, HEAD_DIM)
        if len(kvs) > 1:
            return kvs[s][:, spot]
        return kvs[0][pl.ds(pl.multiple_of(s * rows, rows), rows), spot]

    return read


def attend_body(sides, q_ref, key_ids, row_ids, *refs):
    arrays = sides if sides <= 2 else 1
    kvs, refs = refs[:arrays], refs[arrays:]
    w = refs[:8]
    mixed = refs[8:10]
    lse, mine, theirs = refs[10:13]
    store, sem = refs[13:]
    waits = [fetch(w[4 * i : 4 * i + 4], store.at[i], sem, 4 * i) for i in range(2)]
    rows = q_ref.shape[0]
    qw = q_ref.shape[1] // 2
    ids = row_ids[...]
    read = reader(kvs, rows)

    def look(s):
        return key_ids[pl.ds(s * rows, rows), :] <= ids

    looks = [look(s) for s in range(sides)] if sides <= 2 else None
    lse[...] = jnp.zeros_like(lse)
    head = 0
    c = FACTOR * LOG2E
    for i in range(2):
        outs = []
        for start in range(i * qw, (i + 1) * qw, HEAD_DIM):
            q = q_ref[:, start : start + HEAD_DIM]

            def score(s):
                seen = looks[s] if looks else look(s)
                return jnp.where(seen, dot(read(s, i), q, LAST), -1e30)

            scores = [score(s) for s in range(sides)] if sides <= 2 else None

            def highest(s, top):
                value = scores[s] if scores else score(s)
                return jnp.maximum(top, jnp.max(value, axis=0, keepdims=True))

            top = each(sides, highest, jnp.full((1, rows), -1e30, F32))

            def gathered(s, carry):
                total, out = carry
                value = scores[s] if scores else score(s)
                p = jnp.exp2(value * c - top * c)
                total = total + jnp.sum(p, axis=0, keepdims=True)
                return total, out + dot(read(s, 2 + i), p.astype(BF), ROWS)

            nothing = (jnp.zeros((1, rows), F32), jnp.zeros((HEAD_DIM, rows), F32))
            total, out = each(sides, gathered, nothing)
            outs.append(out / total)
            lse[head : head + 1, :] = top * c + jnp.log2(total)
            head += 1
        fill = jnp.zeros((512 - 320 - qw, rows), F32)
        tall = jnp.concatenate([jnp.zeros((320, rows), F32)] + outs + [fill], axis=0)
        mixed[i][...] = tall.T.astype(BF)
    for i in range(2):
        waits[i]()
    partial = dot(mixed[0][...], store[0], LAST) + dot(mixed[1][...], store[1], LAST)
    out_sides(partial, mine, theirs)


def attend(q, kvs, key_ids, row_ids, w):
    rows = q.shape[0]
    width = 4 * w[0].shape[0]
    sides = key_ids.shape[0] // rows
    return call(
        functools.partial(attend_body, sides),
        [shape((rows, 512))] * 2
        + [shape((8, rows), F32), shape((rows // 2, width), F32), shape((rows // 2, width))],
        [VM] * (3 + len(kvs)) + [ANY] * 8,
        [VM] * 5,
        [pltpu.VMEM((2, width, 512), BF), pltpu.SemaphoreType.DMA((8,))],
        flops=4 * rows * width * 512 + 16 * rows * rows * sides * HEAD_DIM,
        moved=2 * width * 512 * 2 + rows * width * 3,
    )(q, key_ids, row_ids, *kvs, *w)


def padded(value, width):
    return jnp.concatenate([value, jnp.zeros((value.shape[0], width - value.shape[1]), value.dtype)], axis=1)


def feed_body(fw, n_mine, n_theirs, *refs):
    gu, down = refs[:8], refs[8:16]
    hidden, slope, silu = refs[16:18], refs[18:20], refs[20:22]
    mine, theirs = refs[22:24]
    gu_store, down_store, sem = refs[24:]
    waits = [fetch(gu[4 * i : 4 * i + 4], gu_store.at[i], sem, 4 * i) for i in range(2)]
    waits += [fetch(down[4 * i : 4 * i + 4], down_store.at[i], sem, 8 + 4 * i) for i in range(2)]
    rows = n_mine.shape[0]
    for i in range(2):
        waits[i]()
        for side, ref in enumerate((n_mine, n_theirs)):
            out = dot(ref[...], gu_store[i])
            gate, upper = out[:, :fw], out[:, fw:]
            sigma = jax.nn.sigmoid(gate)
            act = gate * sigma
            spot = pl.ds(side * rows, rows)
            hidden[i][spot, :] = padded(act * upper, 512).astype(BF)
            slope[i][spot, :] = padded(upper * (sigma + act * (1.0 - sigma)), 512).astype(BF)
            silu[i][spot, :] = padded(act, 512).astype(BF)
    waits[2]()
    waits[3]()
    for side, ref in ((1, theirs), (0, mine)):
        spot = pl.ds(side * rows, rows)
        ref[...] = (
            dot(hidden[0][spot, :], down_store[0], LAST) + dot(hidden[1][spot, :], down_store[1], LAST)
        ).astype(ref.dtype)


def feed(n_mine, n_theirs, gu, down, fw):
    rows, width = n_mine.shape
    return call(
        functools.partial(feed_body, fw),
        [shape((2 * rows, 512))] * 6 + [shape((rows, width), F32), shape((rows, width))],
        [VM] * 2 + [ANY] * 16,
        [VM] * 8,
        [pltpu.VMEM((2, width, 2 * fw), BF), pltpu.VMEM((2, width, 512), BF), pltpu.SemaphoreType.DMA((16,))],
        flops=4 * rows * width * 2 * (2 * fw + 512),
        moved=2 * width * (2 * fw + 512) * 2,
    )(n_mine, n_theirs, *gu, *down)


def feed_back_body(fw, d_mine, d_theirs, *refs):
    slope, silu = refs[:2], refs[2:4]
    gu, down = refs[4:12], refs[12:20]
    d_gu = refs[20:22]
    mine, theirs = refs[22:24]
    gu_store, down_store, sem = refs[24:]
    waits = [fetch(down[4 * i : 4 * i + 4], down_store.at[i], sem, 8 + 4 * i) for i in range(2)]
    waits += [fetch(gu[4 * i : 4 * i + 4], gu_store.at[i], sem, 4 * i) for i in range(2)]
    rows = d_mine.shape[0]
    for i in range(2):
        waits[i]()
        for side, ref in enumerate((d_mine, d_theirs)):
            spot = pl.ds(side * rows, rows)
            out = dot(ref[...], down_store[i])
            a = (out * slope[i][spot, :].astype(F32))[:, :fw]
            b = (out * silu[i][spot, :].astype(F32))[:, :fw]
            d_gu[i][spot, :] = jnp.concatenate([a, b], axis=1).astype(BF)
    waits[2]()
    waits[3]()
    for side, ref in ((1, theirs), (0, mine)):
        spot = pl.ds(side * rows, rows)
        ref[...] = (
            dot(d_gu[0][spot, :], gu_store[0], LAST) + dot(d_gu[1][spot, :], gu_store[1], LAST)
        ).astype(ref.dtype)


def feed_back(d_mine, d_theirs, slope, silu, gu, down, fw):
    rows, width = d_mine.shape
    return call(
        functools.partial(feed_back_body, fw),
        [shape((2 * rows, 2 * fw))] * 2 + [shape((rows, width), F32), shape((rows, width))],
        [VM] * 6 + [ANY] * 16,
        [VM] * 4,
        [pltpu.VMEM((2, width, 2 * fw), BF), pltpu.VMEM((2, width, 512), BF), pltpu.SemaphoreType.DMA((16,))],
        flops=4 * rows * width * 2 * (2 * fw + 512),
        moved=2 * width * (2 * fw + 512) * 2,
    )(d_mine, d_theirs, *slope, *silu, *gu, *down)


def weight_grad_body(left_mine, left_theirs, *refs):
    right = refs[:2]
    outs = refs[2:10]
    store, sem = refs[10:]
    rows = left_mine.shape[0]
    step = outs[0].shape[0]
    copies = []
    for p in range(4):
        spot = pl.ds(p * step, step)
        for i in range(2):
            n = 4 * i + p
            value = dot(left_mine[:, spot], right[i][:rows, :], ROWS)
            value += dot(left_theirs[:, spot], right[i][rows:, :], ROWS)
            store[n] = value.astype(BF)
            copies.append(pltpu.make_async_copy(store.at[n], outs[n], sem.at[n]))
            copies[-1].start()
    for c in copies:
        c.wait()


def weight_grad(left_mine, left_theirs, right):
    rows, width = left_mine.shape
    cols = right[0].shape[1]
    step = width // 4
    return call(
        weight_grad_body,
        [shape((step, cols))] * 8,
        [VM] * 4,
        [ANY] * 8,
        [pltpu.VMEM((8, step, cols), BF), pltpu.SemaphoreType.DMA((8,))],
        flops=4 * 2 * rows * width * cols,
        moved=2 * width * cols * 2,
    )(left_mine, left_theirs, *right)


def attend_back_body(sides, d_mine, d_theirs, q_ref, key_ids, row_ids, lse, cosine, sine, *refs):
    arrays = sides if sides <= 2 else 1
    kvs, refs = refs[:arrays], refs[arrays:]
    w = refs[:8]
    dq_ref, own_ref, send_ref = refs[8:11]
    store, mix, d_kv, sem = refs[11:]
    waits = [fetch(w[4 * i : 4 * i + 4], store.at[i], sem, 4 * i) for i in range(2)]
    rows = q_ref.shape[0]
    half = rows // 2
    qw = q_ref.shape[1] // 2
    for i in range(2):
        waits[i]()
        for side, ref in enumerate((d_mine, d_theirs)):
            mix[i, pl.ds(side * half, half), :] = dot(ref[...], store[i])[:, 320 : 320 + qw].astype(BF)
    ids = row_ids[...]
    read = reader(kvs, rows)

    def look(s):
        return key_ids[pl.ds(s * rows, rows), :] <= ids

    looks = [look(s) for s in range(sides)] if sides <= 2 else None
    d_q = []
    c = FACTOR * LOG2E
    head = 0
    for i in range(2):
        for start in range(0, qw, HEAD_DIM):
            q = q_ref[:, i * qw + start : i * qw + start + HEAD_DIM]
            dm = mix[i, :, start : start + HEAD_DIM]
            level = lse[head : head + 1, :]
            head += 1

            def pair(s):
                seen = looks[s] if looks else look(s)
                p = jnp.where(seen, jnp.exp2(dot(read(s, i), q, LAST) * c - level), 0.0)
                return p, dot(read(s, 2 + i), dm, LAST)

            held = [pair(s) for s in range(sides)] if sides <= 2 else None

            def weigh(s, delta):
                p, dp = held[s] if held else pair(s)
                return delta + jnp.sum(p * dp, axis=0, keepdims=True)

            delta = each(sides, weigh, jnp.zeros((1, rows), F32))

            def grads(s, out):
                p, dp = held[s] if held else pair(s)
                ds = (p * (dp - delta)).astype(BF)
                d_value = dot(p.astype(BF), dm)
                d_key = dot(ds, q)
                if start == 0:
                    d_kv[2 + i, s] = d_value
                    d_kv[i, s] = d_key
                else:
                    d_kv[2 + i, s] += d_value
                    d_kv[i, s] += d_key
                return out + dot(read(s, i), ds, ROWS)

            d_q.append(each(sides, grads, jnp.zeros((HEAD_DIM, rows), F32)))
    tall = jnp.concatenate(d_q + [jnp.zeros((512 - 4 * HEAD_DIM, rows), F32)], axis=0).T * FACTOR
    cos, sin = cosine[...], sine[...]
    dq_ref[...] = jnp.concatenate(
        [rotated(tall[:, h * HEAD_DIM : (h + 1) * HEAD_DIM], cos, -sin) for h in range(4)], axis=1
    ).astype(BF)
    for s in range(sides):
        value = jnp.concatenate([d_kv[0, s] * FACTOR, d_kv[1, s] * FACTOR, d_kv[2, s], d_kv[3, s]], axis=1)
        if s == 0:
            own_ref[...] = value
        else:
            send_ref[pl.ds((s - 1) * rows, rows), :] = value.astype(BF)


def attend_back(d_mine, d_theirs, q, kvs, key_ids, row_ids, lse, cosine, sine, w):
    rows = q.shape[0]
    width = d_mine.shape[1]
    sides = key_ids.shape[0] // rows
    cols = kvs[0].shape[1]
    return call(
        functools.partial(attend_back_body, sides),
        [shape(q.shape), shape((rows, cols), F32), shape(((sides - 1) * rows, cols))],
        [VM] * (8 + len(kvs)) + [ANY] * 8,
        [VM] * 3,
        [
            pltpu.VMEM((2, width, 512), BF),
            pltpu.VMEM((2, rows, q.shape[1] // 2), BF),
            pltpu.VMEM((4, sides, rows, HEAD_DIM), F32),
            pltpu.SemaphoreType.DMA((8,)),
        ],
        flops=4 * rows * width * 512 + 40 * rows * rows * sides * HEAD_DIM,
        moved=2 * width * 512 * 2,
    )(d_mine, d_theirs, q, key_ids, row_ids, lse, cosine, sine, *kvs, *w)


def project_back_body(x_mine, x_theirs, dq_ref, own_ref, got_ref, cosine, sine, *refs):
    w = refs[:8]
    d_qkv = refs[8:10]
    mine, theirs, gain_ref = refs[10:13]
    store, sem = refs[13:]
    waits = [fetch(w[4 * i : 4 * i + 4], store.at[i], sem, 4 * i) for i in range(2)]
    qw = dq_ref.shape[1] // 2
    cos, sin = cosine[...], sine[...]
    d_kv = own_ref[...] + got_ref[...].astype(F32)
    d_q = dq_ref[...].astype(F32)
    rows = d_q.shape[0]
    for i in range(2):
        d_k = rotated(d_kv[:, i * HEAD_DIM : (i + 1) * HEAD_DIM], cos, -sin)
        d_v = d_kv[:, (2 + i) * HEAD_DIM : (3 + i) * HEAD_DIM]
        d_qkv[i][...] = padded(
            jnp.concatenate([d_q[:, i * qw : (i + 1) * qw], d_k, d_v], axis=1), 512
        ).astype(BF)
    for i in range(2):
        waits[i]()
    half = rows // 2
    total = 0.0
    for side, ref, x_ref in ((1, theirs, x_theirs), (0, mine, x_mine)):
        spot = pl.ds(side * half, half)
        part = dot(d_qkv[0][spot, :], store[0], LAST) + dot(d_qkv[1][spot, :], store[1], LAST)
        ref[...] = part.astype(ref.dtype)
        x = x_ref[...].astype(F32)
        scale = lax.rsqrt(jnp.mean(x * x, axis=-1, keepdims=True) + EPS)
        total = total + jnp.sum(part * (x * scale), axis=0, keepdims=True)
    gain_ref[...] = total


def project_back(x_mine, x_theirs, dq, own, got, cosine, sine, w):
    rows, width = x_mine.shape
    return call(
        project_back_body,
        [shape((2 * rows, 512))] * 2 + [shape((rows, width), F32), shape((rows, width)), shape((1, width), F32)],
        [VM] * 7 + [ANY] * 8,
        [VM] * 5,
        [pltpu.VMEM((2, width, 512), BF), pltpu.SemaphoreType.DMA((8,))],
        flops=8 * rows * width * 512,
        moved=2 * width * 512 * 2 + rows * width * 8,
    )(x_mine, x_theirs, dq, own, got, cosine, sine, *w)


def attn_grad_body(first, d_mine, d_theirs, gain_one, gain_two, *refs):
    d_qkv, mixed = refs[:2], refs[2:4]
    outs = refs[4:12]
    store, sem = refs[12:]
    half = d_mine.shape[0]
    step = outs[0].shape[0]
    copies = []
    for p in range(4):
        spot = pl.ds(p * step, step)
        tall = jnp.concatenate(
            [
                jnp.zeros((96, step), F32),
                gain_one[:, spot],
                gain_two[:, spot],
                jnp.zeros((30, step), F32),
            ],
            axis=0,
        ).T
        tall = jnp.concatenate([jnp.zeros((step, 384), F32), tall], axis=1)
        for i in range(2):
            n = 4 * i + p
            value = dot(first[:, spot], d_qkv[i][...], ROWS)
            value += dot(d_mine[:, spot], mixed[i][:half, :], ROWS)
            value += dot(d_theirs[:, spot], mixed[i][half:, :], ROWS)
            store[n] = (value + tall).astype(BF)
            copies.append(pltpu.make_async_copy(store.at[n], outs[n], sem.at[n]))
            copies[-1].start()
    for c in copies:
        c.wait()


def attn_grad(first, d_mine, d_theirs, gain_one, gain_two, d_qkv, mixed):
    rows, width = first.shape
    step = width // 4
    return call(
        attn_grad_body,
        [shape((step, 512))] * 8,
        [VM] * 9,
        [ANY] * 8,
        [pltpu.VMEM((8, step, 512), BF), pltpu.SemaphoreType.DMA((8,))],
        flops=8 * rows * width * 512,
        moved=2 * width * 512 * 2,
    )(first, d_mine, d_theirs, gain_one, gain_two, *d_qkv, *mixed)


class Place:
    def __init__(self):
        self.inner = lax.axis_size("seq") // PARTS
        s = lax.axis_index("seq")
        m = lax.axis_index("mp")
        self.z = s // self.inner
        self.y = s % self.inner
        self.x = m // 2
        self.c = m % 2
        self.zs = self.z.reshape(1).astype(jnp.int32)
        self.bits = []
        b = 1
        while b < self.inner:
            self.bits.append(b)
            b *= 2

    def hop_z(self, v, k):
        return hop(v, "seq", k * self.inner)

    def hop_y(self, v, b):
        return hop(v, "seq", b)

    def hop_x(self, v):
        return hop(v, "mp", 2)

    def hop_c(self, v):
        return hop(v, "mp", 1)

    def flip_y(self, v):
        for b in self.bits:
            w = v.reshape((v.shape[0], self.inner // (2 * b), 2, b) + v.shape[2:])
            w = w[:, :, ::-1].reshape(v.shape)
            v = jnp.where((self.y // b) % 2 == 1, w, v)
        return v

    def features_in(self, v):
        rows = v.shape[0]
        v = v.reshape(rows * 2, 2, self.inner, -1).transpose(0, 2, 1, 3)
        return self.flip_y(v).reshape(rows, -1)

    def features_out(self, v):
        rows = v.shape[0]
        v = self.flip_y(v.reshape(rows * 2, self.inner, 2, -1))
        return v.transpose(0, 2, 1, 3).reshape(rows, -1)

    def swap_z(self, pieces):
        return [pieces[0]] + [self.hop_z(pieces[k], k) for k in range(1, PARTS)]

    def spread_y(self, v):
        for b in self.bits[:-1]:
            v = jnp.concatenate([v, self.hop_y(v, b)], 0)
        return [v, self.hop_y(v, self.bits[-1])]

    def spread(self, halves):
        a = self.spread_y(halves[0])
        b_other = self.hop_x(halves[1])
        b = self.spread_y(halves[1])
        a_other = [self.hop_x(v) for v in a]
        b_other = self.spread_y(b_other)
        return a + b + a_other + b_other

    def collect(self, grads):
        def add(own, got):
            return (own.astype(F32) + got.astype(F32)).astype(BF)

        def collect_y(v):
            value = add(v[0], self.hop_y(v[1], self.bits[-1]))
            for b in reversed(self.bits[:-1]):
                n = value.shape[0] // 2
                value = add(value[:n], self.hop_y(value[n:], b))
            return value

        own, other = grads[:4], grads[4:]
        a = collect_y([add(own[i], self.hop_x(other[i])) for i in range(2)])
        b = add(collect_y(own[2:]), self.hop_x(collect_y(other[2:])))
        return [a, b]

    def gather(self, own):
        one = self.hop_z(own, 1)
        two = self.hop_z(own, 2)
        three = self.hop_z(two, 1)
        mine = jnp.concatenate([own, one, two, three], 0)
        return mine, self.hop_c(mine)

    def scatter(self, mine, theirs):
        got = self.hop_c(theirs)
        n = mine.shape[0] // PARTS

        def piece(k):
            spot = slice(k * n, (k + 1) * n)
            return mine[spot] + got[spot].astype(F32)

        three = self.hop_z(piece(3).astype(BF), 1)
        two = self.hop_z((piece(2) + three.astype(F32)).astype(BF), 2)
        one = self.hop_z(piece(1).astype(BF), 1)
        return piece(0) + one.astype(F32) + two.astype(F32)


def tables(place):
    half = HEAD_DIM // 2
    freq = THETA ** (-(jnp.arange(half, dtype=F32) * 2.0 / HEAD_DIM))
    angle = place[:, None] * freq[None, :]
    return (jnp.cos(angle), jnp.sin(angle))


def scale_of(value):
    return lax.rsqrt(jnp.mean(value * value, axis=-1, keepdims=True) + EPS)


def norm_back(grad, value, scale, gain):
    unit = value * scale
    scaled = grad * gain
    back = scale * (scaled - unit * jnp.mean(scaled * unit, axis=-1, keepdims=True))
    return unit, back


def on_device(
    inputs,
    targets,
    seq_ids,
    block_ids,
    attn_gain,
    mlp_gain,
    w_query,
    w_key,
    w_value,
    w_out,
    w_gate,
    w_up,
    w_down,
):
    at = Place()
    inner = at.inner
    half_span = SPAN // 2
    kw = w_key.shape[1] // 2
    qw = w_query.shape[1] // PARTS
    fw = w_gate.shape[1] // PARTS

    off = jnp.where(seq_ids[0] == at.x, 0, SPAN)
    row0 = off + at.c * half_span

    def own_rows(v):
        return at.features_in(lax.dynamic_slice_in_dim(v, row0, half_span, 0))

    gains = jnp.stack([attn_gain, mlp_gain], -1)
    takes = [(qw, 1), (kw, 2), (kw, 2), (qw, 1), (2, 4)]
    pieces_qo = pack(at.zs, [w_query, w_key, w_value, w_out, gains], takes, 512)
    x_own = own_rows(inputs)
    w_qo = at.spread(to_halves(at.zs, at.swap_z(pieces_qo)))
    x_mine, x_theirs = at.gather(x_own)

    ids = lax.dynamic_slice_in_dim(block_ids, off, SPAN, 0)
    ids = jnp.stack([ids] + [at.hop_z(ids, k) for k in range(1, PARTS)], 0)
    ids = ids.reshape(PARTS, 2, half_span).transpose(1, 0, 2)
    ids = jnp.where(at.c == 1, ids[::-1], ids).reshape(-1)
    key_ids = ids[None]
    for b in at.bits:
        key_ids = jnp.concatenate([key_ids, at.hop_y(key_ids, b)], 0)
    key_ids = key_ids.reshape(-1, 1)
    row_ids = ids.reshape(1, -1)

    pieces_gu = pack(at.zs, [w_gate, w_up], [(fw, 1), (fw, 1)], 2 * fw)
    w_gu = at.spread(to_halves(at.zs, at.swap_z(pieces_gu)))
    pieces_d = pack(at.zs, [w_down], [(fw, 1)], 512)
    w_d = at.spread(to_halves(at.zs, at.swap_z(pieces_d)))

    rows = 2 * PARTS * half_span
    count = jnp.arange(rows, dtype=jnp.int32)
    zz = at.z ^ ((count // half_span) % PARTS)
    cc = at.c ^ (count // (half_span * PARTS))
    place = ((zz * inner + at.y) * SPAN + cc * half_span + count % half_span).astype(F32)
    cosine, sine = tables(place)

    first, query, kv, gain = project(x_mine, x_theirs, cosine, sine, w_qo, qw)
    gain_one, gain_two = gain[0:1], gain[1:2]
    kvs = [kv]
    for b in at.bits:
        kvs = kvs + [at.hop_y(v, b) for v in kvs]
    if inner > 2:
        kvs = [jnp.concatenate(kvs, 0)]
    mixed_a, mixed_b, lse, mine, theirs = attend(query, kvs, key_ids, row_ids, w_qo)
    branch_attn = at.scatter(mine, theirs)
    middle = x_own.astype(F32) + branch_attn
    scale_two = scale_of(middle)
    n_mine, n_theirs = at.gather((middle * scale_two * gain_two).astype(BF))
    out = feed(n_mine, n_theirs, w_gu, w_d, fw)
    hidden, slope, silu, (mine, theirs) = out[:2], out[2:4], out[4:6], out[6:]
    branch_mlp = at.scatter(mine, theirs)
    stream = middle + branch_mlp

    t_own = own_rows(targets).astype(F32)
    d_own = (stream - t_own).astype(BF)
    d_mine, d_theirs = at.gather(d_own)
    out = feed_back(d_mine, d_theirs, slope, silu, w_gu, w_d, fw)
    d_gu, (mine, theirs) = out[:2], out[2:]
    grad_d = weight_grad(d_mine, d_theirs, hidden)
    d_second = at.scatter(mine, theirs)
    grad_gu = weight_grad(n_mine, n_theirs, d_gu)
    unit, back = norm_back(d_second, middle, scale_two, gain_two)
    grad_gain_two = jnp.sum(d_second * unit, axis=0, keepdims=True)
    d_middle = d_own.astype(F32) + back
    a_mine, a_theirs = at.gather(d_middle.astype(BF))
    out = attend_back(a_mine, a_theirs, query, kvs, key_ids, row_ids, lse, cosine, sine, w_qo)
    d_query, d_kv, sent = out
    if inner > 2:
        sent = jnp.concatenate([d_kv, sent.astype(F32)], 0)
        for b in reversed(at.bits[1:]):
            n = sent.shape[0] // 2
            sent = sent[:n] + at.hop_y(sent[n:].astype(BF), b).astype(F32)
        d_kv, sent = sent[:rows], sent[rows:].astype(BF)
    got = at.hop_y(sent, at.bits[0])
    out = project_back(x_mine, x_theirs, d_query, d_kv, got, cosine, sine, w_qo)
    d_qkv, mine, theirs, grad_gain_one = out[:2], out[2], out[3], out[4]
    d_first = at.scatter(mine, theirs)
    grad_qo = attn_grad(
        first, a_mine, a_theirs, grad_gain_one, grad_gain_two, d_qkv, (mixed_a, mixed_b)
    )

    x_f = x_own.astype(F32)
    unit, back = norm_back(d_first, x_f, scale_of(x_f), gain_one)
    input_grad_own = (d_middle + back).astype(BF)

    sums = jnp.stack(
        [jnp.sum(stream * stream), jnp.sum(branch_attn * branch_attn), jnp.sum(branch_mlp * branch_mlp)]
    )
    sums = jnp.broadcast_to(sums[:, None], (3, 128))
    sums = sums + at.hop_c(sums)
    sums = sums + at.hop_x(sums)
    for b in at.bits:
        sums = sums + at.hop_y(sums, b)
    sums = sums + at.hop_z(sums, 1)
    sums = sums + at.hop_z(sums, 2)
    entries = inputs.shape[0] * lax.axis_size("seq") * inputs.shape[1]
    rms = jnp.sqrt(sums[:, 0] / entries + EPS)

    def whole_rows(own):
        v = at.features_out(own)
        other = at.hop_c(v)
        v = jnp.where(at.c == 0, jnp.concatenate([v, other], 0), jnp.concatenate([other, v], 0))
        other = at.hop_x(v)
        return jnp.where(off == 0, jnp.concatenate([v, other], 0), jnp.concatenate([other, v], 0))

    layer_out = whole_rows(stream.astype(BF))
    input_grad = whole_rows(input_grad_own)

    def arrive(grads):
        return at.swap_z(to_pieces(at.zs, at.collect(grads)))

    (g_down,) = unpack(at.zs, arrive(grad_d), [(0, fw, 1)])
    g_gate, g_up = unpack(at.zs, arrive(grad_gu), [(0, fw, 1), (fw, fw, 1)])
    takes = [(0, qw, 1), (qw, kw, 2), (qw + kw, kw, 2), (qw + 2 * kw, qw, 1), (480, 2, 4)]
    got_qo = arrive(grad_qo)
    g_query, g_key, g_value, g_out = unpack(at.zs, got_qo, takes[:4])
    gains_sum = sum(p[:, 480:482].astype(F32) for p in got_qo)
    gains_sum = gains_sum + at.hop_c(gains_sum)
    return (
        layer_out,
        input_grad,
        g_query,
        g_key,
        g_value,
        g_out,
        g_gate,
        g_up,
        g_down,
        gains_sum[:, 0],
        gains_sum[:, 1],
        rms[0],
        rms[1],
        rms[2],
    )
def solution(mesh):
    return jax.shard_map(
        on_device,
        mesh=mesh,
        in_specs=(
            P("seq", None),
            P("seq", None),
            P("seq"),
            P("seq"),
            P("seq"),
            P("seq"),
            P("seq", "mp"),
            P("seq", "mp"),
            P("seq", "mp"),
            P("seq", "mp"),
            P("seq", "mp"),
            P("seq", "mp"),
            P("seq", "mp"),
        ),
        out_specs=(
            P("seq", None),
            P("seq", None),
            P("seq", "mp"),
            P("seq", "mp"),
            P("seq", "mp"),
            P("seq", "mp"),
            P("seq", "mp"),
            P("seq", "mp"),
            P("seq", "mp"),
            P("seq"),
            P("seq"),
            P(),
            P(),
            P(),
        ),
        check_vma=False,
    )
```

time: 926 us -> 834 us (0.901)
  local copies, waits for them, and re-layouts: 214 us -> 34 us
  Pallas kernels: 0 us -> 138 us
  matrix products: 67.5 us -> 0 us
  waiting for transfers between devices: 395 us -> 458 us
  other arithmetic: 92.4 us -> 50 us
    pallas_call x0 -> x21, Pallas kernels: none -> 138 us  [the longest x1 15.5 us: attend_back(): call(functools.partial(attend_back_body, sides), [shape(q.shape), shape((...]
    dot_general x30 -> x0, matrix products: 67.5 us -> none  [the longest x24 55.3 us: dot(): return lax.dot_general(left, right, dims, preferred_element_type=F32)]
    reshape x26 -> x8, local copies, waits for them, and re-layouts: 68.5 us -> 3.8 us  [the longest x4 1.99 us: features_in(): v = v.reshape(rows * 2, 2, self.inner, -1).transpose(0, 2, 1, 3)]
    ppermute x112 -> x102, waiting for transfers between devices: 395 us -> 458 us  [hop(): return lax.ppermute(value, axis, [(i, i ^ k) for i in range(size)])]
    concatenate x19 -> x0, other arithmetic: 27.2 us -> none  [the longest x1 11.9 us: on_device(): pack_up = jnp.concatenate([split(w_gate), split(w_up)], 2)]
    dynamic_update_slice x28 -> x0, local copies, waits for them, and re-layouts: 21.3 us -> none  [swap_z(): out = lax.dynamic_update_index_in_dim(out, got[k], self.z ^ k, 0)]
    convert_element_type x19 -> x23, other arithmetic: 13.1 us -> 33.2 us  [the longest x12 24.1 us: add(): return (own.astype(F32) + got.astype(F32)).astype(BF)]
    slice x37 -> x1, local copies, waits for them, and re-layouts: 19.2 us -> 1.01 us  [on_device(): gain_one, gain_two = (gain[0:1], gain[1:2])]
  transfers between devices with their start and end apart: 112 -> 102, of which waited for: 42 -> 56; matrix products, arithmetic and copies ran while one was open for 36% -> 7% of each run, Pallas kernels for 0% -> 11%
where the time goes in v2:
time: 834 us; the launch traced here: 818 us
  waiting for transfers between devices  458 us (55%)
  Pallas kernels  138 us (17%)
  starting transfers between devices  135 us (16%)
  other arithmetic  50 us (6%)
  local copies, waits for them, and re-layouts  34 us (4%)
    ppermute x102, waiting for transfers between devices, hop(): return lax.ppermute(value, axis, [(i, i ^ k) for i in range(size)])  458 us
    ppermute x102, starting transfers between devices, hop(): return lax.ppermute(value, axis, [(i, i ^ k) for i in range(size)])  135 us
    convert_element_type x12, other arithmetic, add(): return (own.astype(F32) + got.astype(F32)).astype(BF)  24.1 us
    unnamed x153, local copies, waits for them, and re-layouts  17.9 us
  transfers between devices with their start and end apart: 102, of which 56 were waited for; matrix products, arithmetic and copies ran while one was open for 7% of the time, Pallas kernels for 11%

profile of v2, /device:TPU:0, one launch (start us, length us, event | category | flops | bytes accessed | tf_op | source)
XLA Modules:
  0.0 818.4 jit_solution(9100121853698320770)
XLA Ops:
  21.4 15.9 %collective-permute-done.4.refs_1_ = bf16[320,512]{1,0:T(8,128)(2,1)S(1)} collective-permute-done((bf16[320,512]{1,0:T(8,128)(2,1)}, bf16[320,512]{1,0:T(8,128)(2,1)S(1)}, u32[]{:S(2)}, u32[]{:S(2)}) %collective-permute-start.4) | collective-permute-done | bytes 327712 | tf_op jit(solution)/shard_map/ppermute | solution.py:48
  37.3 9.6 %collective-permute-done.5.refs_2_ = bf16[320,512]{1,0:T(8,128)(2,1)S(1)} collective-permute-done((bf16[320,512]{1,0:T(8,128)(2,1)}, bf16[320,512]{1,0:T(8,128)(2,1)S(1)}, u32[]{:S(2)}, u32[]{:S(2)}) %collective-permute-start.5) | collective-permute-done | bytes 327712 | tf_op jit(solution)/shard_map/ppermute | solution.py:48
  53.3 7.4 collective-permute-start.2
  60.8 7.3 collective-permute-done.2
  82.1 10.4 %collective-permute-done.8.refs_3_.refs_5_ = bf16[640,512]{1,0:T(8,128)(2,1)} collective-permute-done((bf16[640,512]{1,0:T(8,128)(2,1)}, bf16[640,512]{1,0:T(8,128)(2,1)}, u32[]{:S(2)}, u32[]{:S(2)}) %collective-permute-start.8) | collective-permute-done | bytes 655392 | tf_op jit(solution)/shard_map/ppermute | solution.py:48
  95.2 11.2 %collective-permute-done.10.refs_5_.refs_7_ = bf16[640,512]{1,0:T(8,128)(2,1)} collective-permute-done((bf16[640,512]{1,0:T(8,128)(2,1)}, bf16[640,512]{1,0:T(8,128)(2,1)}, u32[]{:S(2)}, u32[]{:S(2)}) %collective-permute-start.10) | collective-permute-done | bytes 655392 | tf_op jit(solution)/shard_map/ppermute | solution.py:48
  107.4 9.7 %shard_map.238 = (bf16[512,2560]{1,0:T(8,128)(2,1)}, bf16[512,320]{1,0:T(8,128)(2,1)}, bf16[512,320]{1,0:T(8,128)(2,1)}, f32[8,2560]{1,0:T(8,128)}) custom-call(bf16[256,2560]{1,0:T(8,128)(2,1)} %copy-done.3, bf16[256,2560]{1,0:T(8,128)(2,1)} %copy-done.4, f32[512,40]{1,0:T(8,128)} %get-tuple-element.274.cosine, f32[512,40]{1,0:T(8,128)} %get-tuple-element.273.sine, ...), custom_call_target="tpu_custom_call" | custom-call | flops 2684354560 | bytes 10485760 | tf_op jit(solution)/shard_map/pallas_call | solution.py:216
  119.3 6.4 collective-permute-done.16
  127.5 10.3 %shard_map.239 = (bf16[512,512]{1,0:T(8,128)(2,1)}, bf16[512,512]{1,0:T(8,128)(2,1)}, f32[8,512]{1,0:T(8,128)}, f32[256,2560]{1,0:T(8,128)}, bf16[256,2560]{1,0:T(8,128)(2,1)}) custom-call(bf16[512,320]{1,0:T(8,128)(2,1)} %get-tuple-element.109.q_ref, s32[1024,1]{1,0:T(8,128)} %bitcast.33, s32[1,512]{1,0:T(1,128)} %copy-done.49, ...), custom_call_target="tpu_custom_call" | custom-call | flops 3355443200 | bytes 9175040 | tf_op jit(solution)/shard_map/pallas_call | solution.py:313
  151.7 8.6 %collective-permute-done.20 = bf16[64,2560]{1,0:T(8,128)(2,1)S(1)} collective-permute-done((bf16[64,2560]{1,0:T(8,128)(2,1)S(1)}, bf16[64,2560]{1,0:T(8,128)(2,1)S(1)}, u32[]{:S(2)}, u32[]{:S(2)}) %collective-permute-start.20) | collective-permute-done | bytes 327712 | tf_op jit(solution)/shard_map/ppermute | solution.py:48
  170.6 4.7 collective-permute-done.37.refs_3_
  184.3 10.6 %collective-permute-done.21 = bf16[64,2560]{1,0:T(8,128)(2,1)S(1)} collective-permute-done((bf16[64,2560]{1,0:T(8,128)(2,1)}, bf16[64,2560]{1,0:T(8,128)(2,1)S(1)}, u32[]{:S(2)}, u32[]{:S(2)}) %collective-permute-start.21) | collective-permute-done | bytes 327712 | tf_op jit(solution)/shard_map/ppermute | solution.py:48
  197.9 9.5 %collective-permute-done.26.refs_1_ = bf16[320,896]{1,0:T(8,128)(2,1)S(1)} collective-permute-done((bf16[320,896]{1,0:T(8,128)(2,1)}, bf16[320,896]{1,0:T(8,128)(2,1)S(1)}, u32[]{:S(2)}, u32[]{:S(2)}) %collective-permute-start.26) | collective-permute-done | bytes 573472 | tf_op jit(solution)/shard_map/ppermute | solution.py:48
  208.1 30.7 %collective-permute-done.27.refs_2_ = bf16[320,896]{1,0:T(8,128)(2,1)S(1)} collective-permute-done((bf16[320,896]{1,0:T(8,128)(2,1)}, bf16[320,896]{1,0:T(8,128)(2,1)S(1)}, u32[]{:S(2)}, u32[]{:S(2)}) %collective-permute-start.27) | collective-permute-done | bytes 573472 | tf_op jit(solution)/shard_map/ppermute | solution.py:48
  244.0 12.7 %collective-permute-start.22 = (bf16[64,2560]{1,0:T(8,128)(2,1)S(1)}, bf16[64,2560]{1,0:T(8,128)(2,1)S(1)}, u32[]{:S(2)}, u32[]{:S(2)}) collective-permute-start(bf16[64,2560]{1,0:T(8,128)(2,1)S(1)} %multiply_convert_fusion), channel_id=1, source_target_pairs={{0,8},{4,12},{8,0},{12,4},{16,24},{20,28},{24,16},{28,20},{1,9},{5... | collective-permute-start | bytes 983048 | tf_op jit(solution)/shard_map/ppermute | solution.py:48
  258.2 7.1 collective-permute-done.22
  271.3 6.3 collective-permute-done.40.refs_12_.refs_16_
  277.6 11.4 %collective-permute-done.41.refs_13_.refs_17_ = bf16[640,512]{1,0:T(8,128)(2,1)S(1)} collective-permute-done((bf16[640,512]{1,0:T(8,128)(2,1)}, bf16[640,512]{1,0:T(8,128)(2,1)S(1)}, u32[]{:S(2)}, u32[]{:S(2)}) %collective-permute-start.41) | collective-permute-done | bytes 655392 | tf_op jit(solution)/shard_map/ppermute | solution.py:48
  293.1 24.1 %collective-permute-done.30.refs_3_.refs_7_ = bf16[640,896]{1,0:T(8,128)(2,1)S(1)} collective-permute-done((bf16[640,896]{1,0:T(8,128)(2,1)S(1)}, bf16[640,896]{1,0:T(8,128)(2,1)S(1)}, u32[]{:S(2)}, u32[]{:S(2)}) %collective-permute-start.30) | collective-permute-done | bytes 1146912 | tf_op jit(solution)/shard_map/ppermute | solution.py:48
  318.8 19.7 %collective-permute-done.32.refs_5_.refs_9_ = bf16[640,896]{1,0:T(8,128)(2,1)S(1)} collective-permute-done((bf16[640,896]{1,0:T(8,128)(2,1)S(1)}, bf16[640,896]{1,0:T(8,128)(2,1)S(1)}, u32[]{:S(2)}, u32[]{:S(2)}) %collective-permute-start.32) | collective-permute-done | bytes 1146912 | tf_op jit(solution)/shard_map/ppermute | solution.py:48
  341.5 14.8 %shard_map.244 = (bf16[512,512]{1,0:T(8,128)(2,1)}, bf16[512,512]{1,0:T(8,128)(2,1)}, bf16[512,512]{1,0:T(8,128)(2,1)}, bf16[512,512]{1,0:T(8,128)(2,1)}, bf16[5...) custom-call(bf16[256,2560]{1,0:T(8,128)(2,1)} %copy-done.5, ...), custom_call_target="tpu_custom_call" | custom-call | flops 7381975040 | bytes 14417920 | tf_op jit(solution)/shard_map/pallas_call | solution.py:359
  362.2 19.3 %collective-permute-start.46 = (bf16[64,2560]{1,0:T(8,128)(2,1)S(1)}, bf16[64,2560]{1,0:T(8,128)(2,1)S(1)}, u32[]{:S(2)}, u32[]{:S(2)}) collective-permute-start(bf16[64,2560]{1,0:T(8,128)(2,1)S(1)} %get-tuple-element.268), channel_id=1, source_target_pairs={{0,8},{4,12},{8,0},{12,4},{16,24},{20,28},{24,16},{28,20},{1,9},{5... | collective-permute-start | bytes 983048 | tf_op jit(solution)/shard_map/ppermute | solution.py:48
  381.6 8.5 %collective-permute-done.46 = bf16[64,2560]{1,0:T(8,128)(2,1)S(1)} collective-permute-done((bf16[64,2560]{1,0:T(8,128)(2,1)S(1)}, bf16[64,2560]{1,0:T(8,128)(2,1)S(1)}, u32[]{:S(2)}, u32[]{:S(2)}) %collective-permute-start.46) | collective-permute-done | bytes 327712 | tf_op jit(solution)/shard_map/ppermute | solution.py:48
  399.9 9.1 %collective-permute-done.47 = bf16[64,2560]{1,0:T(8,128)(2,1)} collective-permute-done((bf16[64,2560]{1,0:T(8,128)(2,1)}, bf16[64,2560]{1,0:T(8,128)(2,1)}, u32[]{:S(2)}, u32[]{:S(2)}) %collective-permute-start.47) | collective-permute-done | bytes 327712 | tf_op jit(solution)/shard_map/ppermute | solution.py:48
  413.6 12.7 %collective-permute-done.51 = bf16[64,2560]{1,0:T(8,128)(2,1)S(1)} collective-permute-done((bf16[64,2560]{1,0:T(8,128)(2,1)S(1)}, bf16[64,2560]{1,0:T(8,128)(2,1)S(1)}, u32[]{:S(2)}, u32[]{:S(2)}) %collective-permute-start.51) | collective-permute-done | bytes 327712 | tf_op jit(solution)/shard_map/ppermute | solution.py:48
  426.5 9.4 %collective-permute-done.52 = bf16[64,2560]{1,0:T(8,128)(2,1)S(1)} collective-permute-done((bf16[64,2560]{1,0:T(8,128)(2,1)S(1)}, bf16[64,2560]{1,0:T(8,128)(2,1)S(1)}, u32[]{:S(2)}, u32[]{:S(2)}) %collective-permute-start.52) | collective-permute-done | bytes 327712 | tf_op jit(solution)/shard_map/ppermute | solution.py:48
  440.2 14.8 %shard_map.245 = (bf16[512,896]{1,0:T(8,128)(2,1)}, bf16[512,896]{1,0:T(8,128)(2,1)}, f32[256,2560]{1,0:T(8,128)}, bf16[256,2560]{1,0:T(8,128)(2,1)}) custom-call(bf16[256,2560]{1,0:T(8,128)(2,1)} %copy-done.7, bf16[256,2560]{1,0:T(8,128)(2,1)} %copy-done.53, bf16[512,512]{1,0:T(8,128)(2,1)} %get-tuple-element.128.refs_0_, ...), custom_call_target="tpu_custom_call" | custom-call | flops 7381975040 | bytes 14417920 | tf_op jit(solution)/shard_map/pallas_call | solution.py:398
  462.1 8.5 %collective-permute-done.56 = bf16[64,2560]{1,0:T(8,128)(2,1)S(1)} collective-permute-done((bf16[64,2560]{1,0:T(8,128)(2,1)S(1)}, bf16[64,2560]{1,0:T(8,128)(2,1)S(1)}, u32[]{:S(2)}, u32[]{:S(2)}) %collective-permute-start.56) | collective-permute-done | bytes 327712 | tf_op jit(solution)/shard_map/ppermute | solution.py:48
  475.6 5.7 collective-permute-done.55
  481.3 5.5 collective-permute-done.57
  498.1 4.4 collective-permute-done.59
  503.6 5.9 shard_map.254
  511.6 4.8 collective-permute-done.60
  517.8 9.4 %shard_map.251 = (bf16[640,896]{1,0:T(8,128)(2,1)}, bf16[640,896]{1,0:T(8,128)(2,1)}, bf16[640,896]{1,0:T(8,128)(2,1)}, bf16[640,896]{1,0:T(8,128)(2,1)}, bf16[6...) custom-call(bf16[256,2560]{1,0:T(8,128)(2,1)} %copy-done.5, ...), custom_call_target="tpu_custom_call" | custom-call | flops 4697620480 | bytes 9175040 | tf_op jit(solution)/shard_map/pallas_call | solution.py:433
  536.1 15.5 %shard_map.246 = (bf16[512,320]{1,0:T(8,128)(2,1)}, f32[512,320]{1,0:T(8,128)}, bf16[512,320]{1,0:T(8,128)(2,1)}) custom-call(bf16[256,2560]{1,0:T(8,128)(2,1)} %copy-done.6, bf16[256,2560]{1,0:T(8,128)(2,1)} %collective-permute-done.61.d_theirs, bf16[512,320]{1,0:T(8,128)(2,1)} %get-tuple-element.109.q_ref, s32[1024,1]{1,0:T(8,128)} %bitcast.34, ...), custom_call_target="tpu_custom_call" | custom-call | flops 4362076160 | bytes 5242880 | tf_op jit(solution)/shard_map/pallas_call | solution.py:520
  560.3 9.3 %collective-permute-done.90 = bf16[640,512]{1,0:T(8,128)(2,1)S(1)} collective-permute-done((bf16[640,512]{1,0:T(8,128)(2,1)}, bf16[640,512]{1,0:T(8,128)(2,1)S(1)}, u32[]{:S(2)}, u32[]{:S(2)}) %collective-permute-start.90) | collective-permute-done | bytes 655392 | tf_op jit(solution)/shard_map/ppermute | solution.py:48
  571.2 21.0 %collective-permute-done.62.got_ref = bf16[512,320]{1,0:T(8,128)(2,1)S(1)} collective-permute-done((bf16[512,320]{1,0:T(8,128)(2,1)}, bf16[512,320]{1,0:T(8,128)(2,1)S(1)}, u32[]{:S(2)}, u32[]{:S(2)}) %collective-permute-start.62) | collective-permute-done | bytes 327712 | tf_op jit(solution)/shard_map/ppermute | solution.py:48
  592.9 9.7 %shard_map.247 = (bf16[512,512]{1,0:T(8,128)(2,1)}, bf16[512,512]{1,0:T(8,128)(2,1)}, f32[256,2560]{1,0:T(8,128)}, bf16[256,2560]{1,0:T(8,128)(2,1)}, f32[1,2560]{1,0:T(1,128)}) custom-call(bf16[256,2560]{1,0:T(8,128)(2,1)} %copy-done.3, bf16[256,2560]{1,0:T(8,128)(2,1)} %copy-done.4, bf16[512,320]{1,0:T(8,128)(2,1)} %get-tuple-element.135.dq_ref, ...), custom_call_target="tpu_custom_call" | custom-call | flops 2684354560 | bytes 10485760 | tf_op jit(solution)/shard_map/pallas_call | solution.py:569
  623.4 21.8 %collective-permute-done.78 = bf16[640,896]{1,0:T(8,128)(2,1)} collective-permute-done((bf16[640,896]{1,0:T(8,128)(2,1)}, bf16[640,896]{1,0:T(8,128)(2,1)}, u32[]{:S(2)}, u32[]{:S(2)}) %collective-permute-start.78) | collective-permute-done | bytes 1146912 | tf_op jit(solution)/shard_map/ppermute | solution.py:48
  651.8 9.8 %shard_map.248 = (bf16[640,512]{1,0:T(8,128)(2,1)}, bf16[640,512]{1,0:T(8,128)(2,1)}, bf16[640,512]{1,0:T(8,128)(2,1)}, bf16[640,512]{1,0:T(8,128)(2,1)}, bf16[6...) custom-call(bf16[512,2560]{1,0:T(8,128)(2,1)} %get-tuple-element.140.first, ...), custom_call_target="tpu_custom_call" | custom-call | flops 5368709120 | bytes 5242880 | tf_op jit(solution)/shard_map/pallas_call | solution.py:614
  666.4 13.2 %collective-permute-done.73 = bf16[640,512]{1,0:T(8,128)(2,1)S(1)} collective-permute-done((bf16[640,512]{1,0:T(8,128)(2,1)}, bf16[640,512]{1,0:T(8,128)(2,1)S(1)}, u32[]{:S(2)}, u32[]{:S(2)}) %collective-permute-start.73) | collective-permute-done | bytes 655392 | tf_op jit(solution)/shard_map/ppermute | solution.py:48
  685.9 4.0 collective-permute-done.66
  698.2 5.2 collective-permute-done.74
  719.7 11.7 %collective-permute-done.94.refs_2_ = bf16[320,512]{1,0:T(8,128)(2,1)S(1)} collective-permute-done((bf16[320,512]{1,0:T(8,128)(2,1)S(1)}, bf16[320,512]{1,0:T(8,128)(2,1)S(1)}, u32[]{:S(2)}, u32[]{:S(2)}) %collective-permute-start.94) | collective-permute-done | bytes 327712 | tf_op jit(solution)/shard_map/ppermute | solution.py:48
  731.4 6.7 collective-permute-done.75.refs_1_
  738.1 33.7 %collective-permute-done.76.refs_2_ = bf16[320,512]{1,0:T(8,128)(2,1)S(1)} collective-permute-done((bf16[320,512]{1,0:T(8,128)(2,1)}, bf16[320,512]{1,0:T(8,128)(2,1)S(1)}, u32[]{:S(2)}, u32[]{:S(2)}) %collective-permute-start.76) | collective-permute-done | bytes 327712 | tf_op jit(solution)/shard_map/ppermute | solution.py:48
  781.0 22.4 %collective-permute-done.85.refs_2_ = bf16[320,896]{1,0:T(8,128)(2,1)S(1)} collective-permute-done((bf16[320,896]{1,0:T(8,128)(2,1)S(1)}, bf16[320,896]{1,0:T(8,128)(2,1)S(1)}, u32[]{:S(2)}, u32[]{:S(2)}) %collective-permute-start.85) | collective-permute-done | bytes 573472 | tf_op jit(solution)/shard_map/ppermute | solution.py:48
  804.4 4.4 shard_map.253
  (430 shorter events, 261.0 us)
Async XLA Ops:
  5.6 55.2 %collective-permute-start = (bf16[64,2560]{1,0:T(8,128)(2,1)S(1)}, bf16[64,2560]{1,0:T(8,128)(2,1)S(1)}, u32[]{:S(2)}, u32[]{:S(2)}) collective-permute-start(bf16[64,2560]{1,0:T(8,128)(2,1)S(1)} %reshape.178), channel_id=1, source_target_pairs={{0,8},{4,12},{8,0},{12,4},{16,24},{20,28},{24,16},{28,20},{1,9},{5... | collective-permute-start | bytes 983048 | tf_op jit(solution)/shard_map/ppermute | solution.py:48
  8.7 44.6 %collective-permute-start.1 = (bf16[64,2560]{1,0:T(8,128)(2,1)S(1)}, bf16[64,2560]{1,0:T(8,128)(2,1)S(1)}, u32[]{:S(2)}, u32[]{:S(2)}) collective-permute-start(bf16[64,2560]{1,0:T(8,128)(2,1)S(1)} %reshape.178), channel_id=1, source_target_pairs={{0,16},{4,20},{8,24},{12,28},{16,0},{20,4},{24,8},{28,12},{1,17},{... | collective-permute-start | bytes 983048 | tf_op jit(solution)/shard_map/ppermute | solution.py:48
  17.4 29.5 %collective-permute-start.5 = (bf16[320,512]{1,0:T(8,128)(2,1)}, bf16[320,512]{1,0:T(8,128)(2,1)S(1)}, u32[]{:S(2)}, u32[]{:S(2)}) collective-permute-start(bf16[320,512]{1,0:T(8,128)(2,1)} %get-tuple-element.105), channel_id=1, source_target_pairs={{0,16},{4,20},{8,24},{12,28},{16,0},{20,4},{24,8},{28,12},{1,17},{... | collective-permute-start | bytes 983048 | tf_op jit(solution)/shard_map/ppermute | solution.py:48
  17.4 29.5 %collective-permute-start.6 = (bf16[320,512]{1,0:T(8,128)(2,1)}, bf16[320,512]{1,0:T(8,128)(2,1)S(1)}, u32[]{:S(2)}, u32[]{:S(2)}) collective-permute-start(bf16[320,512]{1,0:T(8,128)(2,1)} %get-tuple-element.106), channel_id=1, source_target_pairs={{0,24},{4,28},{8,16},{12,20},{16,8},{20,12},{24,0},{28,4},{1,25},{... | collective-permute-start | bytes 983048 | tf_op jit(solution)/shard_map/ppermute | solution.py:48
  50.3 27.4 %collective-permute-start.7 = (bf16[640,512]{1,0:T(8,128)(2,1)}, bf16[640,512]{1,0:T(8,128)(2,1)}, u32[]{:S(2)}, u32[]{:S(2)}) collective-permute-start(bf16[640,512]{1,0:T(8,128)(2,1)} %get-tuple-element.107.refs_0_.refs_2_), channel_id=1, source_target_pairs={{0,4},{4,0},{8,12},{12,8},{16,20},{20,16},{24,28},{28,24},{1,5},{5... | collective-permute-start | bytes 1966088 | tf_op jit(solution)/shard_map/ppermute | solution.py:48
  51.8 27.4 %collective-permute-start.11 = (bf16[640,512]{1,0:T(8,128)(2,1)}, bf16[640,512]{1,0:T(8,128)(2,1)}, u32[]{:S(2)}, u32[]{:S(2)}) collective-permute-start(bf16[640,512]{1,0:T(8,128)(2,1)} %get-tuple-element.108.refs_2_.refs_4_), channel_id=1, source_target_pairs={{0,2},{1,3},{2,0},{3,1},{4,6},{5,7},{6,4},{7,5},{8,10},{9,11},{10,... | collective-permute-start | bytes 1966088 | tf_op jit(solution)/shard_map/ppermute | solution.py:48
  68.1 38.2 %collective-permute-start.3 = (bf16[256,2560]{1,0:T(8,128)(2,1)S(1)}, bf16[256,2560]{1,0:T(8,128)(2,1)S(1)}, u32[]{:S(2)}, u32[]{:S(2)}) collective-permute-start(bf16[256,2560]{1,0:T(8,128)(2,1)S(1)} %constant_dynamic-update-slice_fusion.x_mine), channel_id=1, source_target_pairs={{0,1},{1,0},{2,3},{3,2},{4,5},{5,4},{6,7},{7,6},{8,9},{9,8},{10,11... | collective-permute-start | bytes 3932168 | tf_op jit(solution)/shard_map/ppermute | solution.py:48
  77.7 28.6 %collective-permute-start.10 = (bf16[640,512]{1,0:T(8,128)(2,1)}, bf16[640,512]{1,0:T(8,128)(2,1)}, u32[]{:S(2)}, u32[]{:S(2)}) collective-permute-start(bf16[640,512]{1,0:T(8,128)(2,1)} %collective-permute-done.7.refs_1_.refs_3_), channel_id=1, source_target_pairs={{0,2},{1,3},{2,0},{3,1},{4,6},{5,7},{6,4},{7,5},{8,10},{9,11},{10,... | collective-permute-start | bytes 1966088 | tf_op jit(solution)/shard_map/ppermute | solution.py:48
  79.2 27.2 %collective-permute-start.12 = (bf16[640,512]{1,0:T(8,128)(2,1)}, bf16[640,512]{1,0:T(8,128)(2,1)}, u32[]{:S(2)}, u32[]{:S(2)}) collective-permute-start(bf16[640,512]{1,0:T(8,128)(2,1)} %collective-permute-done.11.refs_6_.refs_8_), channel_id=1, source_target_pairs={{0,4},{4,0},{8,12},{12,8},{16,20},{20,16},{24,28},{28,24},{1,5},{5... | collective-permute-start | bytes 1966088 | tf_op jit(solution)/shard_map/ppermute | solution.py:48
  149.2 26.0 %collective-permute-start.37 = (bf16[320,512]{1,0:T(8,128)(2,1)}, bf16[320,512]{1,0:T(8,128)(2,1)S(1)}, u32[]{:S(2)}, u32[]{:S(2)}) collective-permute-start(bf16[320,512]{1,0:T(8,128)(2,1)} %get-tuple-element.123), channel_id=1, source_target_pairs={{0,24},{4,28},{8,16},{12,20},{16,8},{20,12},{24,0},{28,4},{1,25},{... | collective-permute-start | bytes 983048 | tf_op jit(solution)/shard_map/ppermute | solution.py:48
  151.7 31.9 %collective-permute-start.19 = (bf16[64,2560]{1,0:T(8,128)(2,1)S(1)}, bf16[64,2560]{1,0:T(8,128)(2,1)S(1)}, u32[]{:S(2)}, u32[]{:S(2)}) collective-permute-start(bf16[64,2560]{1,0:T(8,128)(2,1)S(1)} %get-tuple-element.269), channel_id=1, source_target_pairs={{0,8},{4,12},{8,0},{12,4},{16,24},{20,28},{24,16},{28,20},{1,9},{5... | collective-permute-start | bytes 983048 | tf_op jit(solution)/shard_map/ppermute | solution.py:48
  161.2 33.7 %collective-permute-start.21 = (bf16[64,2560]{1,0:T(8,128)(2,1)}, bf16[64,2560]{1,0:T(8,128)(2,1)S(1)}, u32[]{:S(2)}, u32[]{:S(2)}) collective-permute-start(bf16[64,2560]{1,0:T(8,128)(2,1)} %add_convert_fusion.27), channel_id=1, source_target_pairs={{0,16},{4,20},{8,24},{12,28},{16,0},{20,4},{24,8},{28,12},{1,17},{... | collective-permute-start | bytes 983048 | tf_op jit(solution)/shard_map/ppermute | solution.py:48
  168.1 39.3 %collective-permute-start.26 = (bf16[320,896]{1,0:T(8,128)(2,1)}, bf16[320,896]{1,0:T(8,128)(2,1)S(1)}, u32[]{:S(2)}, u32[]{:S(2)}) collective-permute-start(bf16[320,896]{1,0:T(8,128)(2,1)} %get-tuple-element.115), channel_id=1, source_target_pairs={{0,8},{4,12},{8,0},{12,4},{16,24},{20,28},{24,16},{28,20},{1,9},{5... | collective-permute-start | bytes 1720328 | tf_op jit(solution)/shard_map/ppermute | solution.py:48
  168.9 69.8 %collective-permute-start.27 = (bf16[320,896]{1,0:T(8,128)(2,1)}, bf16[320,896]{1,0:T(8,128)(2,1)S(1)}, u32[]{:S(2)}, u32[]{:S(2)}) collective-permute-start(bf16[320,896]{1,0:T(8,128)(2,1)} %get-tuple-element.116), channel_id=1, source_target_pairs={{0,16},{4,20},{8,24},{12,28},{16,0},{20,4},{24,8},{28,12},{1,17},{... | collective-permute-start | bytes 1720328 | tf_op jit(solution)/shard_map/ppermute | solution.py:48
  176.0 62.8 %collective-permute-start.28 = (bf16[320,896]{1,0:T(8,128)(2,1)}, bf16[320,896]{1,0:T(8,128)(2,1)S(1)}, u32[]{:S(2)}, u32[]{:S(2)}) collective-permute-start(bf16[320,896]{1,0:T(8,128)(2,1)} %get-tuple-element.117), channel_id=1, source_target_pairs={{0,24},{4,28},{8,16},{12,20},{16,8},{20,12},{24,0},{28,4},{1,25},{... | collective-permute-start | bytes 1720328 | tf_op jit(solution)/shard_map/ppermute | solution.py:48
  183.6 60.4 %collective-permute-start.42 = (bf16[640,512]{1,0:T(8,128)(2,1)}, bf16[640,512]{1,0:T(8,128)(2,1)}, u32[]{:S(2)}, u32[]{:S(2)}) collective-permute-start(bf16[640,512]{1,0:T(8,128)(2,1)} %get-tuple-element.125.refs_10_.refs_14_), channel_id=1, source_target_pairs={{0,2},{1,3},{2,0},{3,1},{4,6},{5,7},{6,4},{7,5},{8,10},{9,11},{10,... | collective-permute-start | bytes 1966088 | tf_op jit(solution)/shard_map/ppermute | solution.py:48
  195.6 61.1 %collective-permute-start.39 = (bf16[640,512]{1,0:T(8,128)(2,1)}, bf16[640,512]{1,0:T(8,128)(2,1)}, u32[]{:S(2)}, u32[]{:S(2)}) collective-permute-start(bf16[640,512]{1,0:T(8,128)(2,1)} %get-tuple-element.125.refs_10_.refs_14_), channel_id=1, source_target_pairs={{0,4},{4,0},{8,12},{12,8},{16,20},{20,16},{24,28},{28,24},{1,5},{5... | collective-permute-start | bytes 1966088 | tf_op jit(solution)/shard_map/ppermute | solution.py:48
  207.4 36.1 %collective-permute-start.38 = (bf16[640,512]{1,0:T(8,128)(2,1)}, bf16[640,512]{1,0:T(8,128)(2,1)}, u32[]{:S(2)}, u32[]{:S(2)}) collective-permute-start(bf16[640,512]{1,0:T(8,128)(2,1)} %get-tuple-element.124.refs_8_.refs_12_), channel_id=1, source_target_pairs={{0,4},{4,0},{8,12},{12,8},{16,20},{20,16},{24,28},{28,24},{1,5},{5... | collective-permute-start | bytes 1966088 | tf_op jit(solution)/shard_map/ppermute | solution.py:48
  243.0 48.1 %collective-permute-start.29 = (bf16[640,896]{1,0:T(8,128)(2,1)}, bf16[640,896]{1,0:T(8,128)(2,1)S(1)}, u32[]{:S(2)}, u32[]{:S(2)}) collective-permute-start(bf16[640,896]{1,0:T(8,128)(2,1)} %get-tuple-element.118.refs_0_.refs_4_), channel_id=1, source_target_pairs={{0,4},{4,0},{8,12},{12,8},{16,20},{20,16},{24,28},{28,24},{1,5},{5... | collective-permute-start | bytes 3440648 | tf_op jit(solution)/shard_map/ppermute | solution.py:48
  243.5 49.1 %collective-permute-start.33 = (bf16[640,896]{1,0:T(8,128)(2,1)}, bf16[640,896]{1,0:T(8,128)(2,1)S(1)}, u32[]{:S(2)}, u32[]{:S(2)}) collective-permute-start(bf16[640,896]{1,0:T(8,128)(2,1)} %get-tuple-element.119.refs_2_.refs_6_), channel_id=1, source_target_pairs={{0,2},{1,3},{2,0},{3,1},{4,6},{5,7},{6,4},{7,5},{8,10},{9,11},{10,... | collective-permute-start | bytes 3440648 | tf_op jit(solution)/shard_map/ppermute | solution.py:48
  277.6 62.9 %collective-permute-start.25 = (bf16[256,2560]{1,0:T(8,128)(2,1)S(1)}, bf16[256,2560]{1,0:T(8,128)(2,1)S(1)}, u32[]{:S(2)}, u32[]{:S(2)}) collective-permute-start(bf16[256,2560]{1,0:T(8,128)(2,1)S(1)} %pad_maximum_fusion.n_mine.left_mine), channel_id=1, source_target_pairs={{0,1},{1,0},{2,3},{3,2},{4,5},{5,4},{6,7},{7,6},{8,9},{9,8},{10,11... | collective-permute-start | bytes 3932168 | tf_op jit(solution)/shard_map/ppermute | solution.py:48
  289.0 28.2 %collective-permute-start.30 = (bf16[640,896]{1,0:T(8,128)(2,1)S(1)}, bf16[640,896]{1,0:T(8,128)(2,1)S(1)}, u32[]{:S(2)}, u32[]{:S(2)}) collective-permute-start(bf16[640,896]{1,0:T(8,128)(2,1)S(1)} %copy-done.55), channel_id=1, source_target_pairs={{0,4},{4,0},{8,12},{12,8},{16,20},{20,16},{24,28},{28,24},{1,5},{5... | collective-permute-start | bytes 3440648 | tf_op jit(solution)/shard_map/ppermute | solution.py:48
  290.5 28.3 %collective-permute-start.31 = (bf16[640,896]{1,0:T(8,128)(2,1)S(1)}, bf16[640,896]{1,0:T(8,128)(2,1)S(1)}, u32[]{:S(2)}, u32[]{:S(2)}) collective-permute-start(bf16[640,896]{1,0:T(8,128)(2,1)S(1)} %copy-done.54), channel_id=1, source_target_pairs={{0,2},{1,3},{2,0},{3,1},{4,6},{5,7},{6,4},{7,5},{8,10},{9,11},{10,... | collective-permute-start | bytes 3440648 | tf_op jit(solution)/shard_map/ppermute | solution.py:48
  291.1 47.4 %collective-permute-start.32 = (bf16[640,896]{1,0:T(8,128)(2,1)S(1)}, bf16[640,896]{1,0:T(8,128)(2,1)S(1)}, u32[]{:S(2)}, u32[]{:S(2)}) collective-permute-start(bf16[640,896]{1,0:T(8,128)(2,1)S(1)} %collective-permute-done.29.refs_1_.refs_5_), channel_id=1, source_target_pairs={{0,2},{1,3},{2,0},{3,1},{4,6},{5,7},{6,4},{7,5},{8,10},{9,11},{10,... | collective-permute-start | bytes 3440648 | tf_op jit(solution)/shard_map/ppermute | solution.py:48
  292.6 45.9 %collective-permute-start.34 = (bf16[640,896]{1,0:T(8,128)(2,1)S(1)}, bf16[640,896]{1,0:T(8,128)(2,1)S(1)}, u32[]{:S(2)}, u32[]{:S(2)}) collective-permute-start(bf16[640,896]{1,0:T(8,128)(2,1)S(1)} %collective-permute-done.33.refs_6_.refs_10_), channel_id=1, source_target_pairs={{0,4},{4,0},{8,12},{12,8},{16,20},{20,16},{24,28},{28,24},{1,5},{5... | collective-permute-start | bytes 3440648 | tf_op jit(solution)/shard_map/ppermute | solution.py:48
  362.2 27.8 %collective-permute-start.46 = (bf16[64,2560]{1,0:T(8,128)(2,1)S(1)}, bf16[64,2560]{1,0:T(8,128)(2,1)S(1)}, u32[]{:S(2)}, u32[]{:S(2)}) collective-permute-start(bf16[64,2560]{1,0:T(8,128)(2,1)S(1)} %get-tuple-element.268), channel_id=1, source_target_pairs={{0,8},{4,12},{8,0},{12,4},{16,24},{20,28},{24,16},{28,20},{1,9},{5... | collective-permute-start | bytes 983048 | tf_op jit(solution)/shard_map/ppermute | solution.py:48
  527.2 28.4 %collective-permute-start.82 = (bf16[640,896]{1,0:T(8,128)(2,1)}, bf16[640,896]{1,0:T(8,128)(2,1)S(1)}, u32[]{:S(2)}, u32[]{:S(2)}) collective-permute-start(bf16[640,896]{1,0:T(8,128)(2,1)} %get-tuple-element.171), channel_id=1, source_target_pairs={{0,4},{4,0},{8,12},{12,8},{16,20},{20,16},{24,28},{28,24},{1,5},{5... | collective-permute-start | bytes 3440648 | tf_op jit(solution)/shard_map/ppermute | solution.py:48
  528.8 28.4 %collective-permute-start.79 = (bf16[640,896]{1,0:T(8,128)(2,1)}, bf16[640,896]{1,0:T(8,128)(2,1)S(1)}, u32[]{:S(2)}, u32[]{:S(2)}) collective-permute-start(bf16[640,896]{1,0:T(8,128)(2,1)} %get-tuple-element.167), channel_id=1, source_target_pairs={{0,2},{1,3},{2,0},{3,1},{4,6},{5,7},{6,4},{7,5},{8,10},{9,11},{10,... | collective-permute-start | bytes 3440648 | tf_op jit(solution)/shard_map/ppermute | solution.py:48
  532.0 37.7 %collective-permute-start.90 = (bf16[640,512]{1,0:T(8,128)(2,1)}, bf16[640,512]{1,0:T(8,128)(2,1)S(1)}, u32[]{:S(2)}, u32[]{:S(2)}) collective-permute-start(bf16[640,512]{1,0:T(8,128)(2,1)} %get-tuple-element.185), channel_id=1, source_target_pairs={{0,4},{4,0},{8,12},{12,8},{16,20},{20,16},{24,28},{28,24},{1,5},{5... | collective-permute-start | bytes 1966088 | tf_op jit(solution)/shard_map/ppermute | solution.py:48
  534.6 68.0 %collective-permute-start.87 = (bf16[640,512]{1,0:T(8,128)(2,1)}, bf16[640,512]{1,0:T(8,128)(2,1)S(1)}, u32[]{:S(2)}, u32[]{:S(2)}) collective-permute-start(bf16[640,512]{1,0:T(8,128)(2,1)} %get-tuple-element.181), channel_id=1, source_target_pairs={{0,2},{1,3},{2,0},{3,1},{4,6},{5,7},{6,4},{7,5},{8,10},{9,11},{10,... | collective-permute-start | bytes 1966088 | tf_op jit(solution)/shard_map/ppermute | solution.py:48
  551.6 52.4 %collective-permute-start.92 = (bf16[640,512]{1,0:T(8,128)(2,1)}, bf16[640,512]{1,0:T(8,128)(2,1)}, u32[]{:S(2)}, u32[]{:S(2)}) collective-permute-start(bf16[640,512]{1,0:T(8,128)(2,1)} %add_convert_fusion.7), channel_id=1, source_target_pairs={{0,2},{1,3},{2,0},{3,1},{4,6},{5,7},{6,4},{7,5},{8,10},{9,11},{10,... | collective-permute-start | bytes 1966088 | tf_op jit(solution)/shard_map/ppermute | solution.py:48
  555.6 49.9 %collective-permute-start.89 = (bf16[640,512]{1,0:T(8,128)(2,1)}, bf16[640,512]{1,0:T(8,128)(2,1)}, u32[]{:S(2)}, u32[]{:S(2)}) collective-permute-start(bf16[640,512]{1,0:T(8,128)(2,1)} %add_convert_fusion.10), channel_id=1, source_target_pairs={{0,4},{4,0},{8,12},{12,8},{16,20},{20,16},{24,28},{28,24},{1,5},{5... | collective-permute-start | bytes 1966088 | tf_op jit(solution)/shard_map/ppermute | solution.py:48
  557.1 35.0 %collective-permute-start.62 = (bf16[512,320]{1,0:T(8,128)(2,1)}, bf16[512,320]{1,0:T(8,128)(2,1)S(1)}, u32[]{:S(2)}, u32[]{:S(2)}) collective-permute-start(bf16[512,320]{1,0:T(8,128)(2,1)} %get-tuple-element.137), channel_id=1, source_target_pairs={{0,4},{4,0},{8,12},{12,8},{16,20},{20,16},{24,28},{28,24},{1,5},{5... | collective-permute-start | bytes 983048 | tf_op jit(solution)/shard_map/ppermute | solution.py:48
  569.7 47.0 %collective-permute-start.81 = (bf16[640,896]{1,0:T(8,128)(2,1)}, bf16[640,896]{1,0:T(8,128)(2,1)S(1)}, u32[]{:S(2)}, u32[]{:S(2)}) collective-permute-start(bf16[640,896]{1,0:T(8,128)(2,1)} %get-tuple-element.169), channel_id=1, source_target_pairs={{0,4},{4,0},{8,12},{12,8},{16,20},{20,16},{24,28},{28,24},{1,5},{5... | collective-permute-start | bytes 3440648 | tf_op jit(solution)/shard_map/ppermute | solution.py:48
  592.1 28.5 %collective-permute-start.83 = (bf16[640,896]{1,0:T(8,128)(2,1)}, bf16[640,896]{1,0:T(8,128)(2,1)}, u32[]{:S(2)}, u32[]{:S(2)}) collective-permute-start(bf16[640,896]{1,0:T(8,128)(2,1)} %add_convert_fusion.1), channel_id=1, source_target_pairs={{0,2},{1,3},{2,0},{3,1},{4,6},{5,7},{6,4},{7,5},{8,10},{9,11},{10,... | collective-permute-start | bytes 3440648 | tf_op jit(solution)/shard_map/ppermute | solution.py:48
  602.7 42.6 %collective-permute-start.78 = (bf16[640,896]{1,0:T(8,128)(2,1)}, bf16[640,896]{1,0:T(8,128)(2,1)}, u32[]{:S(2)}, u32[]{:S(2)}) collective-permute-start(bf16[640,896]{1,0:T(8,128)(2,1)} %get-tuple-element.165), channel_id=1, source_target_pairs={{0,2},{1,3},{2,0},{3,1},{4,6},{5,7},{6,4},{7,5},{8,10},{9,11},{10,... | collective-permute-start | bytes 3440648 | tf_op jit(solution)/shard_map/ppermute | solution.py:48
  604.0 41.2 %collective-permute-start.80 = (bf16[640,896]{1,0:T(8,128)(2,1)}, bf16[640,896]{1,0:T(8,128)(2,1)}, u32[]{:S(2)}, u32[]{:S(2)}) collective-permute-start(bf16[640,896]{1,0:T(8,128)(2,1)} %add_convert_fusion.4), channel_id=1, source_target_pairs={{0,4},{4,0},{8,12},{12,8},{16,20},{20,16},{24,28},{28,24},{1,5},{5... | collective-permute-start | bytes 3440648 | tf_op jit(solution)/shard_map/ppermute | solution.py:48
  605.5 46.1 %collective-permute-start.63 = (bf16[256,2560]{1,0:T(8,128)(2,1)}, bf16[256,2560]{1,0:T(8,128)(2,1)S(1)}, u32[]{:S(2)}, u32[]{:S(2)}) collective-permute-start(bf16[256,2560]{1,0:T(8,128)(2,1)} %get-tuple-element.139), channel_id=1, source_target_pairs={{0,1},{1,0},{2,3},{3,2},{4,5},{5,4},{6,7},{7,6},{8,9},{9,8},{10,11... | collective-permute-start | bytes 3932168 | tf_op jit(solution)/shard_map/ppermute | solution.py:48
  616.7 98.5 %collective-permute-start.49 = (bf16[128,2560]{1,0:T(8,128)(2,1)S(1)}, bf16[128,2560]{1,0:T(8,128)(2,1)}, u32[]{:S(2)}, u32[]{:S(2)}) collective-permute-start(bf16[128,2560]{1,0:T(8,128)(2,1)S(1)} %maximum_select_fusion.2), channel_id=1, source_target_pairs={{0,2},{1,3},{2,0},{3,1},{4,6},{5,7},{6,4},{7,5},{8,10},{9,11},{10,... | collective-permute-start | bytes 1966088 | tf_op jit(solution)/shard_map/ppermute | solution.py:48
  663.3 31.6 %collective-permute-start.72 = (bf16[640,512]{1,0:T(8,128)(2,1)}, bf16[640,512]{1,0:T(8,128)(2,1)}, u32[]{:S(2)}, u32[]{:S(2)}) collective-permute-start(bf16[640,512]{1,0:T(8,128)(2,1)} %get-tuple-element.151), channel_id=1, source_target_pairs={{0,4},{4,0},{8,12},{12,8},{16,20},{20,16},{24,28},{28,24},{1,5},{5... | collective-permute-start | bytes 1966088 | tf_op jit(solution)/shard_map/ppermute | solution.py:48
  707.8 67.2 %collective-permute-start.95 = (bf16[320,512]{1,0:T(8,128)(2,1)S(1)}, bf16[320,512]{1,0:T(8,128)(2,1)S(1)}, u32[]{:S(2)}, u32[]{:S(2)}) collective-permute-start(bf16[320,512]{1,0:T(8,128)(2,1)S(1)} %copy-done.68), channel_id=1, source_target_pairs={{0,24},{4,28},{8,16},{12,20},{16,8},{20,12},{24,0},{28,4},{1,25},{... | collective-permute-start | bytes 983048 | tf_op jit(solution)/shard_map/ppermute | solution.py:48
  715.2 56.6 %collective-permute-start.76 = (bf16[320,512]{1,0:T(8,128)(2,1)}, bf16[320,512]{1,0:T(8,128)(2,1)S(1)}, u32[]{:S(2)}, u32[]{:S(2)}) collective-permute-start(bf16[320,512]{1,0:T(8,128)(2,1)} %get-tuple-element.156), channel_id=1, source_target_pairs={{0,16},{4,20},{8,24},{12,28},{16,0},{20,4},{24,8},{28,12},{1,17},{... | collective-permute-start | bytes 983048 | tf_op jit(solution)/shard_map/ppermute | solution.py:48
  717.4 56.1 %collective-permute-start.77 = (bf16[320,512]{1,0:T(8,128)(2,1)}, bf16[320,512]{1,0:T(8,128)(2,1)S(1)}, u32[]{:S(2)}, u32[]{:S(2)}) collective-permute-start(bf16[320,512]{1,0:T(8,128)(2,1)} %get-tuple-element.157), channel_id=1, source_target_pairs={{0,24},{4,28},{8,16},{12,20},{16,8},{20,12},{24,0},{28,4},{1,25},{... | collective-permute-start | bytes 983048 | tf_op jit(solution)/shard_map/ppermute | solution.py:48
  731.4 49.6 %collective-permute-start.84 = (bf16[320,896]{1,0:T(8,128)(2,1)}, bf16[320,896]{1,0:T(8,128)(2,1)S(1)}, u32[]{:S(2)}, u32[]{:S(2)}) collective-permute-start(bf16[320,896]{1,0:T(8,128)(2,1)} %get-tuple-element.173), channel_id=1, source_target_pairs={{0,8},{4,12},{8,0},{12,4},{16,24},{20,28},{24,16},{28,20},{1,9},{5... | collective-permute-start | bytes 1720328 | tf_op jit(solution)/shard_map/ppermute | solution.py:48
  738.1 65.3 %collective-permute-start.85 = (bf16[320,896]{1,0:T(8,128)(2,1)S(1)}, bf16[320,896]{1,0:T(8,128)(2,1)S(1)}, u32[]{:S(2)}, u32[]{:S(2)}) collective-permute-start(bf16[320,896]{1,0:T(8,128)(2,1)S(1)} %copy-done.66), channel_id=1, source_target_pairs={{0,16},{4,20},{8,24},{12,28},{16,0},{20,4},{24,8},{28,12},{1,17},{... | collective-permute-start | bytes 1720328 | tf_op jit(solution)/shard_map/ppermute | solution.py:48
  771.8 31.6 %collective-permute-start.86 = (bf16[320,896]{1,0:T(8,128)(2,1)S(1)}, bf16[320,896]{1,0:T(8,128)(2,1)S(1)}, u32[]{:S(2)}, u32[]{:S(2)}) collective-permute-start(bf16[320,896]{1,0:T(8,128)(2,1)S(1)} %copy-done.65), channel_id=1, source_target_pairs={{0,24},{4,28},{8,16},{12,20},{16,8},{20,12},{24,0},{28,4},{1,25},{... | collective-permute-start | bytes 1720328 | tf_op jit(solution)/shard_map/ppermute | solution.py:48
  773.5 43.4 %collective-permute-start.68 = (bf16[128,2560]{1,0:T(8,128)(2,1)S(1)}, bf16[128,2560]{1,0:T(8,128)(2,1)S(1)}, u32[]{:S(2)}, u32[]{:S(2)}) collective-permute-start(bf16[128,2560]{1,0:T(8,128)(2,1)S(1)} %maximum_select_fusion.3), channel_id=1, source_target_pairs={{0,2},{1,3},{2,0},{3,1},{4,6},{5,7},{6,4},{7,5},{8,10},{9,11},{10,... | collective-permute-start | bytes 1966088 | tf_op jit(solution)/shard_map/ppermute | solution.py:48
  775.1 40.9 %collective-permute-start.96 = (f32[320,2]{1,0:T(8,128)S(1)}, f32[320,2]{1,0:T(8,128)S(1)}, u32[]{:S(2)}, u32[]{:S(2)}) collective-permute-start(f32[320,2]{1,0:T(8,128)S(1)} %convert_add_fusion.4), channel_id=1, source_target_pairs={{0,1},{1,0},{2,3},{3,2},{4,5},{5,4},{6,7},{7,6},{8,9},{9,8},{10,11... | collective-permute-start | bytes 7688 | tf_op jit(solution)/shard_map/ppermute | solution.py:48
  (126 other events, 1983.5 us)

commit v3 on v2

v3 whole, which is shorter than its diff:
```python
import functools

import jax
import jax.numpy as jnp
from jax import lax
from jax.experimental import pallas as pl
from jax.experimental.pallas import tpu as pltpu
from jax.sharding import PartitionSpec as P

HEAD_DIM = 80
SPAN = 128
EPS = 1e-05
THETA = 1000000.0
PARTS = 4
BF = jnp.bfloat16
F32 = jnp.float32
FACTOR = HEAD_DIM**-0.5
LOG2E = 1.4426950408889634
LIMIT = 56 * 1024 * 1024

PLAIN = (((1,), (0,)), ((), ()))
LAST = (((1,), (1,)), ((), ()))
ROWS = (((0,), (0,)), ((), ()))

VM = pl.BlockSpec(memory_space=pltpu.VMEM)
SM = pl.BlockSpec(memory_space=pltpu.SMEM)
ANY = pl.BlockSpec(memory_space=pl.ANY)


def shape(dims, kind=BF):
    return jax.ShapeDtypeStruct(tuple(dims), kind)


def call(body, outs, in_specs, out_specs, scratch=()):
    return pl.pallas_call(
        body,
        out_shape=outs,
        in_specs=in_specs,
        out_specs=out_specs,
        scratch_shapes=list(scratch),
        compiler_params=pltpu.CompilerParams(vmem_limit_bytes=LIMIT),
    )


def hop(value, axis, k):
    size = lax.axis_size(axis)
    return lax.ppermute(value, axis, [(i, i ^ k) for i in range(size)])


def dot(left, right, dims=PLAIN):
    return lax.dot_general(left, right, dims, preferred_element_type=F32)


def joined(values, width):
    values = [v.astype(F32) for v in values]
    have = sum(v.shape[1] for v in values)
    if have < width:
        values.append(jnp.zeros((values[0].shape[0], width - have), F32))
    return jnp.concatenate(values, axis=1).astype(BF)


def pack_body(takes, width, z_ref, *refs):
    count = len(takes)
    ins, outs = refs[:count], refs[count:]
    for k in range(PARTS):
        part = z_ref[0] ^ k
        for j in range(PARTS):

            @pl.when(part == j)
            def _():
                values = [ref[:, pl.ds(step * (j // share), step)] for ref, (step, share) in zip(ins, takes)]
                outs[k][...] = joined(values, width)


def pack(z, arrays, takes, width):
    depth = arrays[0].shape[0]
    return call(
        functools.partial(pack_body, takes, width),
        [shape((depth, width))] * PARTS,
        [SM] + [VM] * len(arrays),
        [VM] * PARTS,
    )(z, *arrays)


def unpack_body(takes, z_ref, *refs):
    ins, outs = refs[:PARTS], refs[PARTS:]
    for ref, (start, step, share) in zip(outs, takes):
        if share == 2:
            ref[...] = jnp.zeros_like(ref)
    for k in range(PARTS):
        part = z_ref[0] ^ k
        for j in range(PARTS):

            @pl.when(part == j)
            def _():
                for ref, (start, step, share) in zip(outs, takes):
                    value = ins[k][:, pl.ds(start, step)].astype(F32)
                    spot = pl.ds(step * (j // share), step)
                    if share == 1:
                        ref[:, spot] = value
                    else:
                        ref[:, spot] += value


def unpack(z, pieces, takes):
    depth = pieces[0].shape[0]
    return call(
        functools.partial(unpack_body, takes),
        [shape((depth, step * PARTS // share), F32) for start, step, share in takes],
        [SM] + [VM] * 4,
        [VM] * len(takes),
    )(z, *pieces)


def fetch(pieces, store, sem, base=0):
    copies = []
    step = pieces[0].shape[0]
    for p, piece in enumerate(pieces):
        spot = store.at[pl.ds(p * step, step)]
        copies.append(pltpu.make_async_copy(piece, spot, sem.at[base + p]))
        copies[-1].start()

    def wait():
        for c in copies:
            c.wait()

    return wait


def swapped(value, width, k):
    count = value.shape[1] // width
    return jnp.concatenate([value[:, (i ^ k) * width : (i ^ k) * width + width] for i in range(count)], axis=1)


def relative(value, index, count):
    width = value.shape[1] // count
    b = 1
    while b < count:
        turned = swapped(value, width, b)
        value = jnp.where((index // b) % 2 == 1, turned, value)
        b *= 2
    return value


def own_rows_body(count, where_ref, ids, x_ref, t_ref, x_out, t_out):
    spot = pl.ds(pl.multiple_of(where_ref[0], 64), 64)
    width = x_ref.shape[1]
    x = relative(x_ref[spot, :].astype(F32), where_ref[1], count)
    x_out[:, :width] = x.astype(BF)
    x_out[:, width:] = jnp.broadcast_to(ids[spot, :].astype(F32), (64, 128)).astype(BF)
    t_out[...] = relative(t_ref[spot, :].astype(F32), where_ref[1], count).astype(BF)


def own_rows(where, ids, x, t, count):
    width = x.shape[1]
    return call(
        functools.partial(own_rows_body, count),
        [shape((64, width + 128)), shape((64, width))],
        [SM] + [VM] * 3,
        [VM] * 2,
    )(where, ids, x, t)


def stack_body(width, own, one, two, three, out):
    n = own.shape[0]
    for k, ref in enumerate((own, one, two, three)):
        spot = pl.ds(k * n, n)
        out[spot, : 4 * width] = swapped(ref[:, : 4 * width], width, k)
        if out.shape[1] > 4 * width:
            out[spot, 4 * width :] = ref[:, 4 * width :]


def stack(pieces, width):
    n, cols = pieces[0].shape
    return call(
        functools.partial(stack_body, width), shape((4 * n, cols)), [VM] * 4, VM
    )(*pieces)


def first_sum_body(mine, got, one, three, keep):
    n = one.shape[0]

    def piece(k):
        spot = pl.ds(k * n, n)
        return mine[spot, :] + got[spot, :].astype(F32)

    three[...] = piece(3).astype(BF)
    one[...] = piece(1).astype(BF)
    keep[:n, :] = piece(0)
    keep[n:, :] = piece(2)


def first_sum(mine, got):
    n, width = mine.shape
    n //= 4
    return call(
        first_sum_body, [shape((n, width))] * 2 + [shape((2 * n, width), F32)], [VM] * 2, [VM] * 3
    )(mine, got)


def second_sum_body(width, keep, three, out):
    n = out.shape[0]
    out[...] = (keep[n:, :] + swapped(three[...].astype(F32), width, 1)).astype(BF)


def second_sum(keep, three, width):
    return call(functools.partial(second_sum_body, width), shape(three.shape), [VM] * 2, VM)(keep, three)


def last_sum(width, keep, one, two):
    n = one.shape[0]
    return keep[:n, :] + swapped(one[...].astype(F32), width, 1) + swapped(two[...].astype(F32), width, 2)


def mean_scale(value):
    return lax.rsqrt(jnp.mean(value * value, axis=-1, keepdims=True) + EPS)


def back_norm(grad, value, gain):
    scale = mean_scale(value)
    unit = value * scale
    scaled = grad * gain
    return unit, scale * (scaled - unit * jnp.mean(scaled * unit, axis=-1, keepdims=True))


def after_attn_body(width, keep, one, two, x_own, gain, middle, n_own, total):
    branch = last_sum(width, keep, one, two)
    value = x_own[:, : 4 * width].astype(F32) + branch
    middle[...] = value
    n_own[...] = (value * mean_scale(value) * gain[1:2, :]).astype(BF)
    total[...] = jnp.full(total.shape, jnp.sum(branch * branch), F32)


def after_mlp_body(width, count, where_ref, keep, one, two, middle, target, d_own, out, total):
    branch = last_sum(width, keep, one, two)
    stream = middle[...] + branch
    d_own[...] = (stream - target[...].astype(F32)).astype(BF)
    out[...] = relative(stream, where_ref[1], count).astype(BF)
    total[0:8, :] = jnp.full((8, 128), jnp.sum(stream * stream), F32)
    total[8:16, :] = jnp.full((8, 128), jnp.sum(branch * branch), F32)


def after_feed_back_body(width, keep, one, two, middle, d_own, gain, d_middle, a_own, gain_grad):
    grad = last_sum(width, keep, one, two)
    unit, back = back_norm(grad, middle[...], gain[1:2, :])
    value = d_own[...].astype(F32) + back
    d_middle[...] = value
    a_own[...] = value.astype(BF)
    gain_grad[...] = jnp.sum(grad * unit, axis=0, keepdims=True)


def after_all_body(width, count, where_ref, keep, one, two, x_own, d_middle, gain, out):
    grad = last_sum(width, keep, one, two)
    unit, back = back_norm(grad, x_own[:, : 4 * width].astype(F32), gain[0:1, :])
    out[...] = relative(d_middle[...] + back, where_ref[1], count).astype(BF)


def spread_rows_body(spots, p0, p1, p2, p3, out):
    n = p0.shape[0]
    for i, ref in enumerate((p0, p1, p2, p3)):
        out[pl.ds(pl.multiple_of(spots[i], 64), n), :] = ref[...]


def spread_rows(spots, pieces):
    n, width = pieces[0].shape
    return call(spread_rows_body, shape((4 * n, width)), [SM] + [VM] * 4, VM)(spots, *pieces)


def rotated(value, cosine, sine):
    half = HEAD_DIM // 2
    a, b = value[:, :half], value[:, half:]
    return jnp.concatenate([a * cosine - b * sine, b * cosine + a * sine], axis=1)


def project_body(qw, x_mine, x_theirs, cosine, sine, *refs):
    w = refs[:16]
    first, q_ref, kv_ref, gains, row_ids = refs[16:21]
    store, sem = refs[21:]
    waits = [fetch(w[8 * i : 8 * i + 8], store.at[i], sem, 8 * i) for i in range(2)]
    rows = x_mine.shape[0]
    width = first.shape[1]
    step = width // 4
    ids = jnp.concatenate([x_mine[:, width:], x_theirs[:, width:]], axis=0).astype(F32)
    row_ids[...] = ids.T[0:8, :]
    waits[0]()
    spot = 480 - 384
    for p in range(4):
        tail = store[0, pl.ds(p * step, step), 384:512].astype(F32).T
        gains[:, pl.ds(p * step, step)] = tail[spot : spot + 8]
    gain = gains[0:1, :]
    for i, ref in enumerate((x_mine, x_theirs)):
        x = ref[:, :width].astype(F32)
        first[pl.ds(i * rows, rows), :] = (x * mean_scale(x) * gain).astype(BF)
    cos, sin = cosine[...], sine[...]
    queries, keys, values = [], [], []
    for i in range(2):
        if i:
            waits[1]()
        out = dot(first[...], store[i])
        for start in range(0, qw, HEAD_DIM):
            queries.append(rotated(out[:, start : start + HEAD_DIM], cos, sin))
        keys.append(rotated(out[:, qw : qw + HEAD_DIM], cos, sin))
        values.append(out[:, qw + HEAD_DIM : qw + 2 * HEAD_DIM])
    q_ref[...] = jnp.concatenate(queries, axis=1).astype(BF)
    kv_ref[...] = jnp.concatenate(keys + values + [ids[:, :64]], axis=1).astype(BF)


def project(x_mine, x_theirs, cosine, sine, w, qw):
    rows, width = x_mine.shape
    width -= 128
    return call(
        functools.partial(project_body, qw),
        [
            shape((2 * rows, width)),
            shape((2 * rows, 2 * qw)),
            shape((2 * rows, 384)),
            shape((8, width), F32),
            shape((8, 2 * rows), F32),
        ],
        [VM] * 4 + [ANY] * 16,
        [VM] * 5,
        [pltpu.VMEM((2, width, 512), BF), pltpu.SemaphoreType.DMA((16,))],
    )(x_mine, x_theirs, cosine, sine, *w)


def out_sides(partial, mine, theirs):
    n = mine.shape[0]
    mine[...] = partial[:n]
    theirs[...] = partial[n:].astype(theirs.dtype)


def each(count, step, start):
    if count <= 2:
        for s in range(count):
            start = step(s, start)
        return start
    return lax.fori_loop(0, count, step, start)


def reader(kvs, rows):
    def read(s, lane):
        if len(kvs) > 1:
            return kvs[s][:, lane]
        return kvs[0][pl.ds(pl.multiple_of(s * rows, rows), rows), lane]

    return read


def lanes(i):
    return pl.ds(i * HEAD_DIM, HEAD_DIM)


ID_LANE = pl.ds(4 * HEAD_DIM, 1)


def attend_body(sides, q_ref, row_ids, *refs):
    arrays = sides if sides <= 2 else 1
    kvs, refs = refs[:arrays], refs[arrays:]
    w = refs[:16]
    mixed = refs[16:18]
    lse, mine, theirs = refs[18:21]
    store, sem = refs[21:]
    waits = [fetch(w[8 * i : 8 * i + 8], store.at[i], sem, 8 * i) for i in range(2)]
    rows = q_ref.shape[0]
    qw = q_ref.shape[1] // 2
    ids = row_ids[0:1, :]
    read = reader(kvs, rows)

    def look(s):
        return read(s, ID_LANE).astype(F32) <= ids

    looks = [look(s) for s in range(sides)] if sides <= 2 else None
    lse[...] = jnp.zeros_like(lse)
    head = 0
    c = FACTOR * LOG2E
    for i in range(2):
        outs = []
        for start in range(i * qw, (i + 1) * qw, HEAD_DIM):
            q = q_ref[:, start : start + HEAD_DIM]

            def score(s):
                seen = looks[s] if looks else look(s)
                return jnp.where(seen, dot(read(s, lanes(i)), q, LAST), -1e30)

            scores = [score(s) for s in range(sides)] if sides <= 2 else None

            def highest(s, top):
                value = scores[s] if scores else score(s)
                return jnp.maximum(top, jnp.max(value, axis=0, keepdims=True))

            top = each(sides, highest, jnp.full((1, rows), -1e30, F32))

            def gathered(s, carry):
                total, out = carry
                value = scores[s] if scores else score(s)
                p = jnp.exp2(value * c - top * c)
                total = total + jnp.sum(p, axis=0, keepdims=True)
                return total, out + dot(read(s, lanes(2 + i)), p.astype(BF), ROWS)

            nothing = (jnp.zeros((1, rows), F32), jnp.zeros((HEAD_DIM, rows), F32))
            total, out = each(sides, gathered, nothing)
            outs.append(out / total)
            lse[head : head + 1, :] = top * c + jnp.log2(total)
            head += 1
        fill = jnp.zeros((512 - 320 - qw, rows), F32)
        tall = jnp.concatenate([jnp.zeros((320, rows), F32)] + outs + [fill], axis=0)
        mixed[i][...] = tall.T.astype(BF)
    for i in range(2):
        waits[i]()
    partial = dot(mixed[0][...], store[0], LAST) + dot(mixed[1][...], store[1], LAST)
    out_sides(partial, mine, theirs)


def attend(q, kvs, row_ids, w, sides):
    rows = q.shape[0]
    width = 8 * w[0].shape[0]
    return call(
        functools.partial(attend_body, sides),
        [shape((rows, 512))] * 2
        + [shape((8, rows), F32), shape((rows // 2, width), F32), shape((rows // 2, width))],
        [VM] * (2 + len(kvs)) + [ANY] * 16,
        [VM] * 5,
        [pltpu.VMEM((2, width, 512), BF), pltpu.SemaphoreType.DMA((16,))],
    )(q, row_ids, *kvs, *w)


def padded(value, width):
    return jnp.concatenate([value, jnp.zeros((value.shape[0], width - value.shape[1]), value.dtype)], axis=1)


def feed_body(fw, n_mine, n_theirs, *refs):
    w = refs[:16]
    hidden, slope, silu = refs[16:18], refs[18:20], refs[20:22]
    mine, theirs = refs[22:24]
    store, sem = refs[24:]
    waits = [fetch(w[8 * i : 8 * i + 8], store.at[i], sem, 8 * i) for i in range(2)]
    rows = n_mine.shape[0]
    for i in range(2):
        waits[i]()
        for side, ref in enumerate((n_mine, n_theirs)):
            out = dot(ref[...], store[i, :, : 2 * fw])
            gate, upper = out[:, :fw], out[:, fw:]
            sigma = jax.nn.sigmoid(gate)
            act = gate * sigma
            spot = pl.ds(side * rows, rows)
            hidden[i][spot, :] = padded(act * upper, 512).astype(BF)
            slope[i][spot, :] = padded(upper * (sigma + act * (1.0 - sigma)), 512).astype(BF)
            silu[i][spot, :] = padded(act, 512).astype(BF)
    for side, ref in ((1, theirs), (0, mine)):
        spot = pl.ds(side * rows, rows)
        ref[...] = (
            dot(hidden[0][spot, :], store[0, :, 2 * fw :], LAST)
            + dot(hidden[1][spot, :], store[1, :, 2 * fw :], LAST)
        ).astype(ref.dtype)


def feed(n_mine, n_theirs, w, fw):
    rows, width = n_mine.shape
    return call(
        functools.partial(feed_body, fw),
        [shape((2 * rows, 512))] * 6 + [shape((rows, width), F32), shape((rows, width))],
        [VM] * 2 + [ANY] * 16,
        [VM] * 8,
        [pltpu.VMEM((2, width, 2 * fw + 512), BF), pltpu.SemaphoreType.DMA((16,))],
    )(n_mine, n_theirs, *w)


def feed_back_body(fw, d_mine, d_theirs, *refs):
    slope, silu = refs[:2], refs[2:4]
    w = refs[4:20]
    d_gu = refs[20:22]
    mine, theirs = refs[22:24]
    store, sem = refs[24:]
    waits = [fetch(w[8 * i : 8 * i + 8], store.at[i], sem, 8 * i) for i in range(2)]
    rows = d_mine.shape[0]
    for i in range(2):
        waits[i]()
        for side, ref in enumerate((d_mine, d_theirs)):
            spot = pl.ds(side * rows, rows)
            out = dot(ref[...], store[i, :, 2 * fw :])
            a = (out * slope[i][spot, :].astype(F32))[:, :fw]
            b = (out * silu[i][spot, :].astype(F32))[:, :fw]
            d_gu[i][spot, :] = jnp.concatenate([a, b], axis=1).astype(BF)
    for side, ref in ((1, theirs), (0, mine)):
        spot = pl.ds(side * rows, rows)
        ref[...] = (
            dot(d_gu[0][spot, :], store[0, :, : 2 * fw], LAST)
            + dot(d_gu[1][spot, :], store[1, :, : 2 * fw], LAST)
        ).astype(ref.dtype)


def feed_back(d_mine, d_theirs, slope, silu, w, fw):
    rows, width = d_mine.shape
    return call(
        functools.partial(feed_back_body, fw),
        [shape((2 * rows, 2 * fw))] * 2 + [shape((rows, width), F32), shape((rows, width))],
        [VM] * 6 + [ANY] * 16,
        [VM] * 4,
        [pltpu.VMEM((2, width, 2 * fw + 512), BF), pltpu.SemaphoreType.DMA((16,))],
    )(d_mine, d_theirs, *slope, *silu, *w)


def send_out(store, outs, sem, p, i, copies):
    step = outs[0].shape[0]
    for side in range(2):
        n = 8 * i + 2 * p + side
        spot = store.at[4 * i + p, pl.ds(side * step, step)]
        copies.append(pltpu.make_async_copy(spot, outs[n], sem.at[n]))
        copies[-1].start()


def weight_grad_body(left_mine, left_theirs, *refs):
    right = refs[:2]
    outs = refs[2:18]
    store, sem = refs[18:]
    rows = left_mine.shape[0]
    step = 2 * outs[0].shape[0]
    copies = []
    for p in range(4):
        spot = pl.ds(p * step, step)
        for i in range(2):
            value = dot(left_mine[:, spot], right[i][:rows, :], ROWS)
            value += dot(left_theirs[:, spot], right[i][rows:, :], ROWS)
            store[4 * i + p] = value.astype(BF)
            send_out(store, outs, sem, p, i, copies)
    for c in copies:
        c.wait()


def weight_grad(left_mine, left_theirs, right):
    rows, width = left_mine.shape
    cols = right[0].shape[1]
    step = width // 8
    return call(
        weight_grad_body,
        [shape((step, cols))] * 16,
        [VM] * 4,
        [ANY] * 16,
        [pltpu.VMEM((8, 2 * step, cols), BF), pltpu.SemaphoreType.DMA((16,))],
    )(left_mine, left_theirs, *right)


def attend_back_body(sides, d_mine, d_theirs, q_ref, row_ids, lse, cosine, sine, *refs):
    arrays = sides if sides <= 2 else 1
    kvs, refs = refs[:arrays], refs[arrays:]
    w = refs[:16]
    dq_ref, own_ref, send_ref = refs[16:19]
    store, mix, d_kv, sem = refs[19:]
    waits = [fetch(w[8 * i : 8 * i + 8], store.at[i], sem, 8 * i) for i in range(2)]
    rows = q_ref.shape[0]
    half = rows // 2
    qw = q_ref.shape[1] // 2
    for i in range(2):
        waits[i]()
        for side, ref in enumerate((d_mine, d_theirs)):
            mix[i, pl.ds(side * half, half), :] = dot(ref[...], store[i])[:, 320 : 320 + qw].astype(BF)
    ids = row_ids[0:1, :]
    read = reader(kvs, rows)

    def look(s):
        return read(s, ID_LANE).astype(F32) <= ids

    looks = [look(s) for s in range(sides)] if sides <= 2 else None
    d_q = []
    c = FACTOR * LOG2E
    head = 0
    for i in range(2):
        for start in range(0, qw, HEAD_DIM):
            q = q_ref[:, i * qw + start : i * qw + start + HEAD_DIM]
            dm = mix[i, :, start : start + HEAD_DIM]
            level = lse[head : head + 1, :]
            head += 1

            def pair(s):
                seen = looks[s] if looks else look(s)
                p = jnp.where(seen, jnp.exp2(dot(read(s, lanes(i)), q, LAST) * c - level), 0.0)
                return p, dot(read(s, lanes(2 + i)), dm, LAST)

            held = [pair(s) for s in range(sides)] if sides <= 2 else None

            def weigh(s, delta):
                p, dp = held[s] if held else pair(s)
                return delta + jnp.sum(p * dp, axis=0, keepdims=True)

            delta = each(sides, weigh, jnp.zeros((1, rows), F32))

            def grads(s, out):
                p, dp = held[s] if held else pair(s)
                ds = (p * (dp - delta)).astype(BF)
                d_value = dot(p.astype(BF), dm)
                d_key = dot(ds, q)
                if start == 0:
                    d_kv[2 + i, s] = d_value
                    d_kv[i, s] = d_key
                else:
                    d_kv[2 + i, s] += d_value
                    d_kv[i, s] += d_key
                return out + dot(read(s, lanes(i)), ds, ROWS)

            d_q.append(each(sides, grads, jnp.zeros((HEAD_DIM, rows), F32)))
    tall = jnp.concatenate(d_q + [jnp.zeros((512 - 4 * HEAD_DIM, rows), F32)], axis=0).T * FACTOR
    cos, sin = cosine[...], sine[...]
    dq_ref[...] = jnp.concatenate(
        [rotated(tall[:, h * HEAD_DIM : (h + 1) * HEAD_DIM], cos, -sin) for h in range(4)], axis=1
    ).astype(BF)
    for s in range(sides):
        value = jnp.concatenate([d_kv[0, s] * FACTOR, d_kv[1, s] * FACTOR, d_kv[2, s], d_kv[3, s]], axis=1)
        if s == 0:
            own_ref[...] = value
        else:
            send_ref[pl.ds((s - 1) * rows, rows), :] = value.astype(BF)


def attend_back(d_mine, d_theirs, q, kvs, row_ids, lse, cosine, sine, w, sides):
    rows = q.shape[0]
    width = d_mine.shape[1]
    cols = 4 * HEAD_DIM
    return call(
        functools.partial(attend_back_body, sides),
        [shape(q.shape), shape((rows, cols), F32), shape(((sides - 1) * rows, cols))],
        [VM] * (7 + len(kvs)) + [ANY] * 16,
        [VM] * 3,
        [
            pltpu.VMEM((2, width, 512), BF),
            pltpu.VMEM((2, rows, q.shape[1] // 2), BF),
            pltpu.VMEM((4, sides, rows, HEAD_DIM), F32),
            pltpu.SemaphoreType.DMA((16,)),
        ],
    )(d_mine, d_theirs, q, row_ids, lse, cosine, sine, *kvs, *w)


def project_back_body(x_mine, x_theirs, dq_ref, own_ref, got_ref, cosine, sine, *refs):
    w = refs[:16]
    d_qkv = refs[16:18]
    mine, theirs, gain_ref = refs[18:21]
    store, sem = refs[21:]
    waits = [fetch(w[8 * i : 8 * i + 8], store.at[i], sem, 8 * i) for i in range(2)]
    qw = dq_ref.shape[1] // 2
    cos, sin = cosine[...], sine[...]
    d_kv = own_ref[...] + got_ref[...].astype(F32)
    d_q = dq_ref[...].astype(F32)
    rows = d_q.shape[0]
    for i in range(2):
        d_k = rotated(d_kv[:, i * HEAD_DIM : (i + 1) * HEAD_DIM], cos, -sin)
        d_v = d_kv[:, (2 + i) * HEAD_DIM : (3 + i) * HEAD_DIM]
        d_qkv[i][...] = padded(
            jnp.concatenate([d_q[:, i * qw : (i + 1) * qw], d_k, d_v], axis=1), 512
        ).astype(BF)
    for i in range(2):
        waits[i]()
    half = rows // 2
    width = mine.shape[1]
    total = 0.0
    for side, ref, x_ref in ((1, theirs, x_theirs), (0, mine, x_mine)):
        spot = pl.ds(side * half, half)
        part = dot(d_qkv[0][spot, :], store[0], LAST) + dot(d_qkv[1][spot, :], store[1], LAST)
        ref[...] = part.astype(ref.dtype)
        x = x_ref[:, :width].astype(F32)
        total = total + jnp.sum(part * (x * mean_scale(x)), axis=0, keepdims=True)
    gain_ref[...] = total


def project_back(x_mine, x_theirs, dq, own, got, cosine, sine, w):
    rows, width = x_mine.shape
    width -= 128
    return call(
        project_back_body,
        [shape((2 * rows, 512))] * 2 + [shape((rows, width), F32), shape((rows, width)), shape((1, width), F32)],
        [VM] * 7 + [ANY] * 16,
        [VM] * 5,
        [pltpu.VMEM((2, width, 512), BF), pltpu.SemaphoreType.DMA((16,))],
    )(x_mine, x_theirs, dq, own, got, cosine, sine, *w)


def attn_grad_body(first, d_mine, d_theirs, gain_one, gain_two, sum_attn, sums, *refs):
    d_qkv, mixed = refs[:2], refs[2:4]
    outs = refs[4:20]
    store, sem = refs[20:]
    half = d_mine.shape[0]
    step = 2 * outs[0].shape[0]
    copies = []
    lane = lax.broadcasted_iota(jnp.int32, (1, 128), 1)
    tail = jnp.where(lane == 98, sums[0:1, :], 0.0)
    tail = jnp.where(lane == 99, sum_attn[0:1, :], tail)
    tail = jnp.where(lane == 100, sums[8:9, :], tail)
    for p in range(4):
        spot = pl.ds(p * step, step)
        tall = jnp.concatenate(
            [
                jnp.zeros((96, step), F32),
                gain_one[:, spot],
                gain_two[:, spot],
                jnp.zeros((30, step), F32),
            ],
            axis=0,
        ).T
        for i in range(2):
            value = dot(first[:, spot], d_qkv[i][...], ROWS)
            value += dot(d_mine[:, spot], mixed[i][:half, :], ROWS)
            value += dot(d_theirs[:, spot], mixed[i][half:, :], ROWS)
            store[4 * i + p, :, :384] = value[:, :384].astype(BF)
            store[4 * i + p, :, 384:] = (value[:, 384:] + tall + tail).astype(BF)
            send_out(store, outs, sem, p, i, copies)
    for c in copies:
        c.wait()


def attn_grad(first, d_mine, d_theirs, gain_one, gain_two, sum_attn, sums, d_qkv, mixed):
    rows, width = first.shape
    step = width // 8
    return call(
        attn_grad_body,
        [shape((step, 512))] * 16,
        [VM] * 11,
        [ANY] * 16,
        [pltpu.VMEM((8, 2 * step, 512), BF), pltpu.SemaphoreType.DMA((16,))],
    )(first, d_mine, d_theirs, gain_one, gain_two, sum_attn, sums, *d_qkv, *mixed)


def hold(values, *others):
    values = list(values)
    got = lax.optimization_barrier(tuple(values) + tuple(others))
    return list(got[: len(values)])


class Place:
    def __init__(self):
        self.count = lax.axis_size("seq")
        self.inner = self.count // PARTS
        s = lax.axis_index("seq")
        m = lax.axis_index("mp")
        self.s = s
        self.z = s // self.inner
        self.y = s % self.inner
        self.x = m // 2
        self.c = m % 2
        self.zs = self.z.reshape(1).astype(jnp.int32)
        self.bits = []
        b = 1
        while b < self.inner:
            self.bits.append(b)
            b *= 2

    def hop_z(self, v, k):
        return hop(v, "seq", k * self.inner)

    def hop_y(self, v, b):
        return hop(v, "seq", b)

    def hop_x(self, v):
        return hop(v, "mp", 2)

    def hop_c(self, v):
        return hop(v, "mp", 1)

    def low_y(self, v):
        for b in self.bits[:-1]:
            v = jnp.concatenate([v, self.hop_y(v, b)], 0)
        return v

    def far_y(self, v):
        return self.hop_y(v, self.bits[-1])

    def spread(self, k, v):
        if k % 2 == 0:
            v = self.low_y(v)
            w = self.far_y(v)
            return (v, w), (self.hop_x(v), self.hop_x(w))
        u = self.low_y(self.hop_x(v))
        v = self.low_y(v)
        return (v, self.far_y(v)), (u, self.far_y(u))

    def add(self, own, got):
        return (own.astype(F32) + got.astype(F32)).astype(BF)

    def collect_y(self, own, far):
        value = self.add(own, self.far_y(far))
        for b in reversed(self.bits[:-1]):
            n = value.shape[0] // 2
            value = self.add(value[:n], self.hop_y(value[n:], b))
        return value

    def collect(self, k, own, other):
        if k % 2 == 0:
            v, w = [self.add(a, self.hop_x(b)) for a, b in zip(own, other)]
            return self.collect_y(v, w)
        u = self.collect_y(*other)
        return self.add(self.collect_y(*own), self.hop_x(u))

    def gather(self, own, width):
        one = self.hop_z(own, 1)
        two = self.hop_z(own, 2)
        three = self.hop_z(two, 1)
        mine = stack([own, one, two, three], width)
        return mine, self.hop_c(mine)

    def scatter(self, mine, theirs, width):
        one, three, keep = first_sum(mine, self.hop_c(theirs))
        three = self.hop_z(three, 1)
        two = self.hop_z(second_sum(keep, three, width), 2)
        one = self.hop_z(one, 1)
        return keep, one, two


def tables(place):
    half = HEAD_DIM // 2
    freq = THETA ** (-(jnp.arange(half, dtype=F32) * 2.0 / HEAD_DIM))
    angle = place[:, None] * freq[None, :]
    return (jnp.cos(angle), jnp.sin(angle))


def on_device(
    inputs,
    targets,
    seq_ids,
    block_ids,
    attn_gain,
    mlp_gain,
    w_query,
    w_key,
    w_value,
    w_out,
    w_gate,
    w_up,
    w_down,
):
    at = Place()
    inner = at.inner
    full = inputs.shape[1]
    width = full // PARTS
    half_span = SPAN // 2
    kw = w_key.shape[1] // 2
    qw = w_query.shape[1] // PARTS
    fw = w_gate.shape[1] // PARTS
    row_f32 = shape((half_span, full), F32)
    row_bf = shape((half_span, full))

    off = jnp.where(seq_ids[0] == at.x, 0, SPAN)
    where = jnp.stack([off + at.c * half_span, at.s]).astype(jnp.int32)
    spots = [
        (off if xr == 0 else SPAN - off) + (at.c ^ cr) * half_span for xr in range(2) for cr in range(2)
    ]
    spots = jnp.stack(spots).astype(jnp.int32)

    def all_rows(own):
        across = at.hop_x(own)
        return spread_rows(spots, [own, at.hop_c(own), across, at.hop_c(across)])

    rows = 2 * PARTS * half_span
    count = jnp.arange(rows, dtype=jnp.int32)
    zz = at.z ^ ((count // half_span) % PARTS)
    cc = at.c ^ (count // (half_span * PARTS))
    place = ((zz * inner + at.y) * SPAN + cc * half_span + count % half_span).astype(F32)
    cosine, sine = tables(place)

    gains = jnp.stack([attn_gain, mlp_gain], -1)
    takes = [(qw, 1), (kw, 2), (kw, 2), (qw, 1), (2, 4)]
    piece = pack(at.zs, [w_query, w_key, w_value, w_out, gains], takes, 512)
    x_own, t_own = own_rows(where, block_ids.reshape(-1, 1), inputs, targets, at.count)

    def spread_all(got):
        w = [at.spread(k, got[k]) for k in range(PARTS)]
        return [v for i in range(2) for k in range(PARTS) for v in w[k][i]]

    got_qo = [piece[0]] + [at.hop_z(piece[k], k) for k in range(1, PARTS)]
    w_qo = spread_all(got_qo)
    x_mine, x_theirs = at.gather(x_own, width)

    piece = pack(at.zs, [w_gate, w_up, w_down], [(fw, 1)] * 3, 2 * fw + 512)
    piece = hold(piece, *got_qo, x_mine)
    got = [piece[0]] + [at.hop_z(piece[k], k) for k in range(1, PARTS)]
    w_ff = spread_all(got)

    first, query, kv, gain, row_ids = project(x_mine, x_theirs, cosine, sine, w_qo, qw)
    kvs = [kv]
    for b in at.bits:
        kvs = kvs + [at.hop_y(v, b) for v in kvs]
    if inner > 2:
        kvs = [jnp.concatenate(kvs, 0)]
    mixed_a, mixed_b, lse, mine, theirs = attend(query, kvs, row_ids, w_qo, inner)
    left = at.scatter(mine, theirs, width)
    middle, n_own, sum_attn = call(
        functools.partial(after_attn_body, width),
        [row_f32, row_bf, shape((8, 128), F32)],
        [VM] * 5,
        [VM] * 3,
    )(*left, x_own, gain)
    n_mine, n_theirs = at.gather(n_own, width)
    out = feed(n_mine, n_theirs, w_ff, fw)
    hidden, slope, silu, (mine, theirs) = out[:2], out[2:4], out[4:6], out[6:]
    left = at.scatter(mine, theirs, width)
    d_own, layer_own, sums = call(
        functools.partial(after_mlp_body, width, at.count),
        [row_bf, row_bf, shape((16, 128), F32)],
        [SM] + [VM] * 5,
        [VM] * 3,
    )(where, *left, middle, t_own)

    d_mine, d_theirs = at.gather(d_own, width)
    grad_d = weight_grad(d_mine, d_theirs, hidden)
    d_mine, d_theirs, *_ = hold([d_mine, d_theirs], grad_d[0])
    out = feed_back(d_mine, d_theirs, slope, silu, w_ff, fw)
    d_gu, (mine, theirs) = out[:2], out[2:]
    left = at.scatter(mine, theirs, width)
    grad_gu = weight_grad(n_mine, n_theirs, d_gu)
    d_middle, a_own, grad_gain_two = call(
        functools.partial(after_feed_back_body, width),
        [row_f32, row_bf, shape((1, full), F32)],
        [VM] * 6,
        [VM] * 3,
    )(*left, middle, d_own, gain)
    a_mine, a_theirs = at.gather(a_own, width)
    d_query, d_kv, sent = attend_back(
        a_mine, a_theirs, query, kvs, row_ids, lse, cosine, sine, w_qo, inner
    )
    if inner > 2:
        sent = jnp.concatenate([d_kv, sent.astype(F32)], 0)
        for b in reversed(at.bits[1:]):
            n = sent.shape[0] // 2
            sent = sent[:n] + at.hop_y(sent[n:].astype(BF), b).astype(F32)
        d_kv, sent = sent[:rows], sent[rows:].astype(BF)
    sent = at.hop_y(sent, at.bits[0])
    out = project_back(x_mine, x_theirs, d_query, d_kv, sent, cosine, sine, w_qo)
    d_qkv, mine, theirs, grad_gain_one = out[:2], out[2], out[3], out[4]
    left = at.scatter(mine, theirs, width)
    grad_qo = attn_grad(
        first, a_mine, a_theirs, grad_gain_one, grad_gain_two, sum_attn, sums, d_qkv, (mixed_a, mixed_b)
    )
    (input_own,) = call(
        functools.partial(after_all_body, width, at.count),
        [row_bf],
        [SM] + [VM] * 6,
        [VM],
    )(where, *left, x_own, d_middle, gain)

    layer_out = all_rows(layer_own)
    input_grad = all_rows(input_own)

    def arrive(grads):
        got = []
        for k in reversed(range(PARTS)):
            own, other = grads[2 * k : 2 * k + 2], grads[8 + 2 * k : 10 + 2 * k]
            v = at.collect(k, own, other)
            got.append(at.hop_z(v, k) if k else v)
        return got[::-1]

    (g_down,) = unpack(at.zs, arrive(grad_d), [(0, fw, 1)])
    g_gate, g_up = unpack(at.zs, arrive(grad_gu), [(0, fw, 1), (fw, fw, 1)])
    takes = [(0, qw, 1), (qw, kw, 2), (qw + kw, kw, 2), (qw + 2 * kw, qw, 1)]
    got_qo = arrive(grad_qo)
    g_query, g_key, g_value, g_out = unpack(at.zs, got_qo, takes)
    tails = sum(p[:, 384:512].astype(F32) for p in got_qo)
    tails = tails + at.hop_c(tails)
    entries = inputs.shape[0] * lax.axis_size("seq") * inputs.shape[1]
    rms = jnp.sqrt(tails[0, 98:101] / entries + EPS)
    return (
        layer_out,
        input_grad,
        g_query,
        g_key,
        g_value,
        g_out,
        g_gate,
        g_up,
        g_down,
        tails[:, 96],
        tails[:, 97],
        rms[0],
        rms[1],
        rms[2],
    )


def solution(mesh):
    return jax.shard_map(
        on_device,
        mesh=mesh,
        in_specs=(
            P("seq", None),
            P("seq", None),
            P("seq"),
            P("seq"),
            P("seq"),
            P("seq"),
            P("seq", "mp"),
            P("seq", "mp"),
            P("seq", "mp"),
            P("seq", "mp"),
            P("seq", "mp"),
            P("seq", "mp"),
            P("seq", "mp"),
        ),
        out_specs=(
            P("seq", None),
            P("seq", None),
            P("seq", "mp"),
            P("seq", "mp"),
            P("seq", "mp"),
            P("seq", "mp"),
            P("seq", "mp"),
            P("seq", "mp"),
            P("seq", "mp"),
            P("seq"),
            P("seq"),
            P(),
            P(),
            P(),
        ),
        check_vma=False,
    )
```

time: 834 us -> 833 us (level); the launches traced: 818 us -> 827 us
  Pallas kernels: 138 us -> 175 us
  other arithmetic: 50 us -> 13.4 us
  starting transfers between devices: 135 us -> 153 us
    pallas_call x9 -> x22, Pallas kernels: 42.1 us -> 77.5 us  [the longest x2 15.3 us: weight_grad(): call(weight_grad_body, [shape((step, cols))] * 16, [VM] * 4, [ANY] * 16,...]
    ppermute x102 -> x116, starting transfers between devices: 135 us -> 153 us  [hop(): return lax.ppermute(value, axis, [(i, i ^ k) for i in range(size)])]
    convert_element_type x12 -> x24, other arithmetic: 24.1 us -> 9.96 us  [add(): return (own.astype(F32) + got.astype(F32)).astype(BF)]
    convert_element_type x13 -> x0, other arithmetic: 9.71 us -> none  [the longest x4 5.81 us: scatter(): one = self.hop_z(piece(1).astype(BF), 1)]
    unnamed x153 -> x238, local copies, waits for them, and re-layouts: 17.9 us -> 24.5 us
    ppermute x102 -> x116, waiting for transfers between devices: 458 us -> 455 us  [hop(): return lax.ppermute(value, axis, [(i, i ^ k) for i in range(size)])]
  transfers between devices with their start and end apart: 102 -> 116, of which waited for: 56 -> 53; matrix products, arithmetic and copies ran while one was open for 7% -> 2% of each run, Pallas kernels for 11% -> 12%
where the time goes in v3:
time: 833 us; the launch traced here: 827 us
  waiting for transfers between devices  455 us (55%)
  Pallas kernels  175 us (21%)
  starting transfers between devices  153 us (18%)
  local copies, waits for them, and re-layouts  29.5 us (4%)
  other arithmetic  13.4 us (2%)
    ppermute x116, waiting for transfers between devices, hop(): return lax.ppermute(value, axis, [(i, i ^ k) for i in range(size)])  455 us
    ppermute x116, starting transfers between devices, hop(): return lax.ppermute(value, axis, [(i, i ^ k) for i in range(size)])  153 us
    unnamed x238, local copies, waits for them, and re-layouts  24.5 us
  transfers between devices with their start and end apart: 116, of which 53 were waited for; matrix products, arithmetic and copies ran while one was open for 2% of the time, Pallas kernels for 12%

profile of v3, /device:TPU:0, one launch (start us, length us, event | category | flops | bytes accessed | tf_op | source)
XLA Modules:
  0.0 827.5 jit_solution(11293769771723725178)
XLA Ops:
  13.1 14.2 %collective-permute-done.1.two = bf16[64,2688]{1,0:T(8,128)(2,1)S(1)} collective-permute-done((bf16[64,2688]{1,0:T(8,128)(2,1)}, bf16[64,2688]{1,0:T(8,128)(2,1)S(1)}, u32[]{:S(2)}, u32[]{:S(2)}) %collective-permute-start.1) | collective-permute-done | bytes 344096 | tf_op jit(solution)/shard_map/ppermute | solution.py:47
  28.1 8.4 %collective-permute-done.2.three = bf16[64,2688]{1,0:T(8,128)(2,1)S(1)} collective-permute-done((bf16[64,2688]{1,0:T(8,128)(2,1)S(1)}, bf16[64,2688]{1,0:T(8,128)(2,1)S(1)}, u32[]{:S(2)}, u32[]{:S(2)}) %collective-permute-start.2) | collective-permute-done | bytes 344096 | tf_op jit(solution)/shard_map/ppermute | solution.py:47
  51.7 10.7 %collective-permute-done.5.refs_2_.refs_4_ = bf16[320,512]{1,0:T(8,128)(2,1)S(1)} collective-permute-done((bf16[320,512]{1,0:T(8,128)(2,1)}, bf16[320,512]{1,0:T(8,128)(2,1)S(1)}, u32[]{:S(2)}, u32[]{:S(2)}) %collective-permute-start.5) | collective-permute-done | bytes 327712 | tf_op jit(solution)/shard_map/ppermute | solution.py:47
  63.7 9.2 %collective-permute-done.7.refs_4_.refs_6_ = bf16[320,512]{1,0:T(8,128)(2,1)S(1)} collective-permute-done((bf16[320,512]{1,0:T(8,128)(2,1)}, bf16[320,512]{1,0:T(8,128)(2,1)S(1)}, u32[]{:S(2)}, u32[]{:S(2)}) %collective-permute-start.7) | collective-permute-done | bytes 327712 | tf_op jit(solution)/shard_map/ppermute | solution.py:47
  78.0 5.5 collective-permute-done.13.refs_10_.refs_12_
  92.3 5.4 collective-permute-done.12.refs_9_.refs_11_
  112.5 9.8 %shard_map.239 = (bf16[512,2560]{1,0:T(8,128)(2,1)}, bf16[512,320]{1,0:T(8,128)(2,1)}, bf16[512,384]{1,0:T(8,128)(2,1)}, f32[8,2560]{1,0:T(8,128)}, f32[8,512]{1,0:T(8,128)}) custom-call(bf16[256,2688]{1,0:T(8,128)(2,1)} %shard_map.237.x_mine, bf16[256,2688]{1,0:T(8,128)(2,1)} %copy-done, f32[512,40]{1,0:T(8,128)} %get-tuple-element.301.cosine, ...), custom_call_target="tpu_custom_call" | custom-call | tf_op jit(solution)/shard_map/pallas_call | solution.py:311
  123.3 7.0 collective-permute-done.19.refs_1_
  131.1 10.2 %shard_map.240 = (bf16[512,512]{1,0:T(8,128)(2,1)}, bf16[512,512]{1,0:T(8,128)(2,1)}, f32[8,512]{1,0:T(8,128)}, f32[256,2560]{1,0:T(8,128)}, bf16[256,2560]{1,0:T(8,128)(2,1)}) custom-call(bf16[512,320]{1,0:T(8,128)(2,1)} %get-tuple-element.140.q_ref, f32[8,512]{1,0:T(8,128)} %get-tuple-element.141.row_ids, bf16[512,384]{1,0:T(8,128)(2,1)} %get-tuple-element.142.refs_0_, ...), custom_call_target="tpu_custom_call" | custom-call | tf_op jit(solution)/shard_map/pallas_call | solution.py:417
  141.4 5.1 shard_map.245
  146.5 8.3 %collective-permute-start.29 = (bf16[320,1408]{1,0:T(8,128)(2,1)}, bf16[320,1408]{1,0:T(8,128)(2,1)S(1)}, u32[]{:S(2)}, u32[]{:S(2)}) collective-permute-start(bf16[320,1408]{1,0:T(8,128)(2,1)} %get-tuple-element.155), channel_id=1, source_target_pairs={{0,8},{4,12},{8,0},{12,4},{16,24},{20,28},{24,16},{28,20},{1,9},{5... | collective-permute-start | bytes 2703368 | tf_op jit(solution)/shard_map/ppermute | solution.py:47
  163.8 38.4 %collective-permute-done.22.three = bf16[64,2560]{1,0:T(8,128)(2,1)S(1)} collective-permute-done((bf16[64,2560]{1,0:T(8,128)(2,1)}, bf16[64,2560]{1,0:T(8,128)(2,1)S(1)}, u32[]{:S(2)}, u32[]{:S(2)}) %collective-permute-start.22) | collective-permute-done | bytes 327712 | tf_op jit(solution)/shard_map/ppermute | solution.py:47
  206.7 21.6 %collective-permute-done.21.one = bf16[64,2560]{1,0:T(8,128)(2,1)S(1)} collective-permute-done((bf16[64,2560]{1,0:T(8,128)(2,1)}, bf16[64,2560]{1,0:T(8,128)(2,1)S(1)}, u32[]{:S(2)}, u32[]{:S(2)}) %collective-permute-start.21) | collective-permute-done | bytes 327712 | tf_op jit(solution)/shard_map/ppermute | solution.py:47
  229.8 24.8 %collective-permute-done.23.two = bf16[64,2560]{1,0:T(8,128)(2,1)S(1)} collective-permute-done((bf16[64,2560]{1,0:T(8,128)(2,1)}, bf16[64,2560]{1,0:T(8,128)(2,1)S(1)}, u32[]{:S(2)}, u32[]{:S(2)}) %collective-permute-start.23) | collective-permute-done | bytes 327712 | tf_op jit(solution)/shard_map/ppermute | solution.py:47
  262.8 12.2 %collective-permute-done.25.two = bf16[64,2560]{1,0:T(8,128)(2,1)S(1)} collective-permute-done((bf16[64,2560]{1,0:T(8,128)(2,1)}, bf16[64,2560]{1,0:T(8,128)(2,1)S(1)}, u32[]{:S(2)}, u32[]{:S(2)}) %collective-permute-start.25) | collective-permute-done | bytes 327712 | tf_op jit(solution)/shard_map/ppermute | solution.py:47
  278.2 6.4 collective-permute-done.26.three
  288.1 10.0 %collective-permute-done.41.refs_14_.refs_18_ = bf16[320,1408]{1,0:T(8,128)(2,1)} collective-permute-done((bf16[320,1408]{1,0:T(8,128)(2,1)S(1)}, bf16[320,1408]{1,0:T(8,128)(2,1)}, u32[]{:S(2)}, u32[]{:S(2)}) %collective-permute-start.41) | collective-permute-done | bytes 901152 | tf_op jit(solution)/shard_map/ppermute | solution.py:47
  302.7 17.8 %collective-permute-done.34.refs_7_.refs_11_ = bf16[320,1408]{1,0:T(8,128)(2,1)} collective-permute-done((bf16[320,1408]{1,0:T(8,128)(2,1)S(1)}, bf16[320,1408]{1,0:T(8,128)(2,1)}, u32[]{:S(2)}, u32[]{:S(2)}) %collective-permute-start.34) | collective-permute-done | bytes 901152 | tf_op jit(solution)/shard_map/ppermute | solution.py:47
  323.0 13.6 %collective-permute-done.39.refs_12_.refs_16_ = bf16[320,1408]{1,0:T(8,128)(2,1)S(1)} collective-permute-done((bf16[320,1408]{1,0:T(8,128)(2,1)S(1)}, bf16[320,1408]{1,0:T(8,128)(2,1)S(1)}, u32[]{:S(2)}, u32[]{:S(2)}) %collective-permute-start.39) | collective-permute-done | bytes 901152 | tf_op jit(solution)/shard_map/ppermute | solution.py:47
  339.6 15.3 %collective-permute-done.40.refs_13_.refs_17_ = bf16[320,1408]{1,0:T(8,128)(2,1)S(1)} collective-permute-done((bf16[320,1408]{1,0:T(8,128)(2,1)S(1)}, bf16[320,1408]{1,0:T(8,128)(2,1)S(1)}, u32[]{:S(2)}, u32[]{:S(2)}) %collective-permute-start.40) | collective-permute-done | bytes 901152 | tf_op jit(solution)/shard_map/ppermute | solution.py:47
  359.4 15.4 %shard_map.246 = (bf16[512,512]{1,0:T(8,128)(2,1)}, bf16[512,512]{1,0:T(8,128)(2,1)}, bf16[512,512]{1,0:T(8,128)(2,1)}, bf16[512,512]{1,0:T(8,128)(2,1)}, bf16[5...) custom-call(bf16[256,2560]{1,0:T(8,128)(2,1)} %shard_map.244.n_mine.left_mine, ...), custom_call_target="tpu_custom_call" | custom-call | tf_op jit(solution)/shard_map/pallas_call | solution.py:459
  384.6 8.7 %collective-permute-done.45.three = bf16[64,2560]{1,0:T(8,128)(2,1)S(1)} collective-permute-done((bf16[64,2560]{1,0:T(8,128)(2,1)}, bf16[64,2560]{1,0:T(8,128)(2,1)S(1)}, u32[]{:S(2)}, u32[]{:S(2)}) %collective-permute-start.45) | collective-permute-done | bytes 327712 | tf_op jit(solution)/shard_map/ppermute | solution.py:47
  402.5 10.2 %collective-permute-done.46.two = bf16[64,2560]{1,0:T(8,128)(2,1)S(1)} collective-permute-done((bf16[64,2560]{1,0:T(8,128)(2,1)}, bf16[64,2560]{1,0:T(8,128)(2,1)S(1)}, u32[]{:S(2)}, u32[]{:S(2)}) %collective-permute-start.46) | collective-permute-done | bytes 327712 | tf_op jit(solution)/shard_map/ppermute | solution.py:47
  419.4 13.0 %collective-permute-done.51.two = bf16[64,2560]{1,0:T(8,128)(2,1)S(1)} collective-permute-done((bf16[64,2560]{1,0:T(8,128)(2,1)}, bf16[64,2560]{1,0:T(8,128)(2,1)S(1)}, u32[]{:S(2)}, u32[]{:S(2)}) %collective-permute-start.51) | collective-permute-done | bytes 327712 | tf_op jit(solution)/shard_map/ppermute | solution.py:47
  432.6 9.4 %collective-permute-done.52.three = bf16[64,2560]{1,0:T(8,128)(2,1)S(1)} collective-permute-done((bf16[64,2560]{1,0:T(8,128)(2,1)S(1)}, bf16[64,2560]{1,0:T(8,128)(2,1)S(1)}, u32[]{:S(2)}, u32[]{:S(2)}) %collective-permute-start.52) | collective-permute-done | bytes 327712 | tf_op jit(solution)/shard_map/ppermute | solution.py:47
  449.5 5.9 shard_map.252
  455.5 16.2 %shard_map.253 = (bf16[512,896]{1,0:T(8,128)(2,1)}, bf16[512,896]{1,0:T(8,128)(2,1)}, f32[256,2560]{1,0:T(8,128)}, bf16[256,2560]{1,0:T(8,128)(2,1)}) custom-call(bf16[256,2560]{1,0:T(8,128)(2,1)} %shard_map.251.left_mine.d_mine, bf16[256,2560]{1,0:T(8,128)(2,1)} %copy-done.12, bf16[512,512]{1,0:T(8,128)(2,1)} %get-tuple-element.172.refs_0_, ...), custom_call_target="tpu_custom_call" | custom-call | tf_op jit(solution)/shard_map/pallas_call | solution.py:494
  481.4 8.7 %collective-permute-done.56.three = bf16[64,2560]{1,0:T(8,128)(2,1)S(1)} collective-permute-done((bf16[64,2560]{1,0:T(8,128)(2,1)}, bf16[64,2560]{1,0:T(8,128)(2,1)S(1)}, u32[]{:S(2)}, u32[]{:S(2)}) %collective-permute-start.56) | collective-permute-done | bytes 327712 | tf_op jit(solution)/shard_map/ppermute | solution.py:47
  497.2 12.0 %collective-permute-done.57.two = bf16[64,2560]{1,0:T(8,128)(2,1)S(1)} collective-permute-done((bf16[64,2560]{1,0:T(8,128)(2,1)}, bf16[64,2560]{1,0:T(8,128)(2,1)S(1)}, u32[]{:S(2)}, u32[]{:S(2)}) %collective-permute-start.57) | collective-permute-done | bytes 327712 | tf_op jit(solution)/shard_map/ppermute | solution.py:47
  517.7 10.4 %collective-permute-done.59.two = bf16[64,2560]{1,0:T(8,128)(2,1)S(1)} collective-permute-done((bf16[64,2560]{1,0:T(8,128)(2,1)}, bf16[64,2560]{1,0:T(8,128)(2,1)S(1)}, u32[]{:S(2)}, u32[]{:S(2)}) %collective-permute-start.59) | collective-permute-done | bytes 327712 | tf_op jit(solution)/shard_map/ppermute | solution.py:47
  533.5 9.3 %shard_map.266 = (bf16[320,896]{1,0:T(8,128)(2,1)}, bf16[320,896]{1,0:T(8,128)(2,1)}, bf16[320,896]{1,0:T(8,128)(2,1)}, bf16[320,896]{1,0:T(8,128)(2,1)}, bf16[3...) custom-call(bf16[256,2560]{1,0:T(8,128)(2,1)} %shard_map.244.n_mine., ...), custom_call_target="tpu_custom_call" | custom-call | tf_op jit(solution)/shard_map/pallas_call | solution.py:534
  561.0 10.5 %collective-permute-done.103 = bf16[320,512]{1,0:T(8,128)(2,1)S(1)} collective-permute-done((bf16[320,512]{1,0:T(8,128)(2,1)S(1)}, bf16[320,512]{1,0:T(8,128)(2,1)S(1)}, u32[]{:S(2)}, u32[]{:S(2)}) %collective-permute-start.103) | collective-permute-done | bytes 327712 | tf_op jit(solution)/shard_map/ppermute | solution.py:47
  575.0 4.4 collective-permute-done.100
  591.2 15.3 %shard_map.258 = (bf16[512,320]{1,0:T(8,128)(2,1)}, f32[512,320]{1,0:T(8,128)}, bf16[512,320]{1,0:T(8,128)(2,1)}) custom-call(bf16[256,2560]{1,0:T(8,128)(2,1)} %shard_map.257.d_mine, bf16[256,2560]{1,0:T(8,128)(2,1)} %copy-done.14, bf16[512,320]{1,0:T(8,128)(2,1)} %get-tuple-element.140.q_ref, f32[8,512]{1,0:T(8,128)} %get-tuple-element.141.row_ids, ...), custom_call_target="tpu_custom_call" | custom-call | tf_op jit(solution)/shard_map/pallas_call | solution.py:618
  621.8 10.5 %shard_map.259 = (bf16[512,512]{1,0:T(8,128)(2,1)}, bf16[512,512]{1,0:T(8,128)(2,1)}, f32[256,2560]{1,0:T(8,128)}, bf16[256,2560]{1,0:T(8,128)(2,1)}, f32[1,2560]{1,0:T(1,128)}) custom-call(bf16[256,2688]{1,0:T(8,128)(2,1)} %shard_map.237.x_mine, bf16[256,2688]{1,0:T(8,128)(2,1)} %copy-done, bf16[512,320]{1,0:T(8,128)(2,1)} %get-tuple-element.183.dq_ref, ...), custom_call_target="tpu_custom_call" | custom-call | tf_op jit(solution)/shard_map/pallas_call | solution.py:666
  632.2 4.6 collective-permute-done.110.refs_2_
  642.3 10.0 %shard_map.264 = (bf16[320,512]{1,0:T(8,128)(2,1)}, bf16[320,512]{1,0:T(8,128)(2,1)}, bf16[320,512]{1,0:T(8,128)(2,1)}, bf16[320,512]{1,0:T(8,128)(2,1)}, bf16[3...) custom-call(bf16[512,2560]{1,0:T(8,128)(2,1)} %get-tuple-element.192, ...), custom_call_target="tpu_custom_call" | custom-call | tf_op jit(solution)/shard_map/pallas_call | solution.py:711
  657.6 5.1 collective-permute-done.82
  664.2 12.8 %collective-permute-done.78 = bf16[320,512]{1,0:T(8,128)(2,1)S(1)} collective-permute-done((bf16[320,512]{1,0:T(8,128)(2,1)S(1)}, bf16[320,512]{1,0:T(8,128)(2,1)S(1)}, u32[]{:S(2)}, u32[]{:S(2)}) %collective-permute-start.78) | collective-permute-done | bytes 327712 | tf_op jit(solution)/shard_map/ppermute | solution.py:47
  690.6 5.8 collective-permute-done.71
  696.4 8.0 collective-permute-start.65
  717.5 6.7 collective-permute-start.80
  725.4 7.0 collective-permute-start.66
  733.7 5.6 collective-permute-start.76
  739.5 12.0 %collective-permute-done.80.refs_2_ = bf16[320,512]{1,0:T(8,128)(2,1)S(1)} collective-permute-done((bf16[320,512]{1,0:T(8,128)(2,1)S(1)}, bf16[320,512]{1,0:T(8,128)(2,1)S(1)}, u32[]{:S(2)}, u32[]{:S(2)}) %collective-permute-start.80) | collective-permute-done | bytes 327712 | tf_op jit(solution)/shard_map/ppermute | solution.py:47
  754.0 29.0 %collective-permute-done.66.two = bf16[64,2560]{1,0:T(8,128)(2,1)S(1)} collective-permute-done((bf16[64,2560]{1,0:T(8,128)(2,1)}, bf16[64,2560]{1,0:T(8,128)(2,1)S(1)}, u32[]{:S(2)}, u32[]{:S(2)}) %collective-permute-start.66) | collective-permute-done | bytes 327712 | tf_op jit(solution)/shard_map/ppermute | solution.py:47
  789.2 17.6 %collective-permute-done.95.refs_2_ = bf16[320,896]{1,0:T(8,128)(2,1)S(1)} collective-permute-done((bf16[320,896]{1,0:T(8,128)(2,1)S(1)}, bf16[320,896]{1,0:T(8,128)(2,1)S(1)}, u32[]{:S(2)}, u32[]{:S(2)}) %collective-permute-start.95) | collective-permute-done | bytes 573472 | tf_op jit(solution)/shard_map/ppermute | solution.py:47
  809.4 4.6 shard_map.267
  (495 shorter events, 282.2 us)
Async XLA Ops:
  39.7 71.7 %collective-permute-start.3 = (bf16[256,2688]{1,0:T(8,128)(2,1)}, bf16[256,2688]{1,0:T(8,128)(2,1)S(1)}, u32[]{:S(2)}, u32[]{:S(2)}) collective-permute-start(bf16[256,2688]{1,0:T(8,128)(2,1)} %shard_map.237.x_mine), channel_id=1, source_target_pairs={{0,1},{1,0},{2,3},{3,2},{4,5},{5,4},{6,7},{7,6},{8,9},{9,8},{10,11... | collective-permute-start | bytes 4128776 | tf_op jit(solution)/shard_map/ppermute | solution.py:47
  46.9 26.0 %collective-permute-start.7 = (bf16[320,512]{1,0:T(8,128)(2,1)}, bf16[320,512]{1,0:T(8,128)(2,1)S(1)}, u32[]{:S(2)}, u32[]{:S(2)}) collective-permute-start(bf16[320,512]{1,0:T(8,128)(2,1)} %get-tuple-element.138), channel_id=1, source_target_pairs={{0,16},{4,20},{8,24},{12,28},{16,0},{20,4},{24,8},{28,12},{1,17},{... | collective-permute-start | bytes 983048 | tf_op jit(solution)/shard_map/ppermute | solution.py:47
  50.2 25.8 %collective-permute-start.4 = (bf16[320,512]{1,0:T(8,128)(2,1)}, bf16[320,512]{1,0:T(8,128)(2,1)S(1)}, u32[]{:S(2)}, u32[]{:S(2)}) collective-permute-start(bf16[320,512]{1,0:T(8,128)(2,1)} %get-tuple-element.136.refs_0_.refs_2_), channel_id=1, source_target_pairs={{0,4},{4,0},{8,12},{12,8},{16,20},{20,16},{24,28},{28,24},{1,5},{5... | collective-permute-start | bytes 983048 | tf_op jit(solution)/shard_map/ppermute | solution.py:47
  146.5 58.6 %collective-permute-start.29 = (bf16[320,1408]{1,0:T(8,128)(2,1)}, bf16[320,1408]{1,0:T(8,128)(2,1)S(1)}, u32[]{:S(2)}, u32[]{:S(2)}) collective-permute-start(bf16[320,1408]{1,0:T(8,128)(2,1)} %get-tuple-element.155), channel_id=1, source_target_pairs={{0,8},{4,12},{8,0},{12,4},{16,24},{20,28},{24,16},{28,20},{1,9},{5... | collective-permute-start | bytes 2703368 | tf_op jit(solution)/shard_map/ppermute | solution.py:47
  159.4 42.8 %collective-permute-start.22 = (bf16[64,2560]{1,0:T(8,128)(2,1)}, bf16[64,2560]{1,0:T(8,128)(2,1)S(1)}, u32[]{:S(2)}, u32[]{:S(2)}) collective-permute-start(bf16[64,2560]{1,0:T(8,128)(2,1)} %get-tuple-element.147), channel_id=1, source_target_pairs={{0,8},{4,12},{8,0},{12,4},{16,24},{20,28},{24,16},{28,20},{1,9},{5... | collective-permute-start | bytes 983048 | tf_op jit(solution)/shard_map/ppermute | solution.py:47
  159.4 99.5 %collective-permute-start.31 = (bf16[320,1408]{1,0:T(8,128)(2,1)}, bf16[320,1408]{1,0:T(8,128)(2,1)S(1)}, u32[]{:S(2)}, u32[]{:S(2)}) collective-permute-start(bf16[320,1408]{1,0:T(8,128)(2,1)} %get-tuple-element.156), channel_id=1, source_target_pairs={{0,16},{4,20},{8,24},{12,28},{16,0},{20,4},{24,8},{28,12},{1,17},{... | collective-permute-start | bytes 2703368 | tf_op jit(solution)/shard_map/ppermute | solution.py:47
  161.7 97.3 %collective-permute-start.33 = (bf16[320,1408]{1,0:T(8,128)(2,1)S(1)}, bf16[320,1408]{1,0:T(8,128)(2,1)S(1)}, u32[]{:S(2)}, u32[]{:S(2)}) collective-permute-start(bf16[320,1408]{1,0:T(8,128)(2,1)S(1)} %copy-done.106), channel_id=1, source_target_pairs={{0,24},{4,28},{8,16},{12,20},{16,8},{20,12},{24,0},{28,4},{1,25},{... | collective-permute-start | bytes 2703368 | tf_op jit(solution)/shard_map/ppermute | solution.py:47
  163.8 64.6 %collective-permute-start.21 = (bf16[64,2560]{1,0:T(8,128)(2,1)}, bf16[64,2560]{1,0:T(8,128)(2,1)S(1)}, u32[]{:S(2)}, u32[]{:S(2)}) collective-permute-start(bf16[64,2560]{1,0:T(8,128)(2,1)} %get-tuple-element.146), channel_id=1, source_target_pairs={{0,8},{4,12},{8,0},{12,4},{16,24},{20,28},{24,16},{28,20},{1,9},{5... | collective-permute-start | bytes 983048 | tf_op jit(solution)/shard_map/ppermute | solution.py:47
  205.1 49.6 %collective-permute-start.23 = (bf16[64,2560]{1,0:T(8,128)(2,1)}, bf16[64,2560]{1,0:T(8,128)(2,1)S(1)}, u32[]{:S(2)}, u32[]{:S(2)}) collective-permute-start(bf16[64,2560]{1,0:T(8,128)(2,1)} %shard_map.242), channel_id=1, source_target_pairs={{0,16},{4,20},{8,24},{12,28},{16,0},{20,4},{24,8},{28,12},{1,17},{... | collective-permute-start | bytes 983048 | tf_op jit(solution)/shard_map/ppermute | solution.py:47
  205.1 55.5 %collective-permute-start.28 = (bf16[320,1408]{1,0:T(8,128)(2,1)S(1)}, bf16[320,1408]{1,0:T(8,128)(2,1)S(1)}, u32[]{:S(2)}, u32[]{:S(2)}) collective-permute-start(bf16[320,1408]{1,0:T(8,128)(2,1)S(1)} %copy-done.15), channel_id=1, source_target_pairs={{0,4},{4,0},{8,12},{12,8},{16,20},{20,16},{24,28},{28,24},{1,5},{5... | collective-permute-start | bytes 2703368 | tf_op jit(solution)/shard_map/ppermute | solution.py:47
  228.3 46.7 %collective-permute-start.35 = (bf16[320,1408]{1,0:T(8,128)(2,1)S(1)}, bf16[320,1408]{1,0:T(8,128)(2,1)S(1)}, u32[]{:S(2)}, u32[]{:S(2)}) collective-permute-start(bf16[320,1408]{1,0:T(8,128)(2,1)S(1)} %copy-done.15), channel_id=1, source_target_pairs={{0,2},{1,3},{2,0},{3,1},{4,6},{5,7},{6,4},{7,5},{8,10},{9,11},{10,... | collective-permute-start | bytes 2703368 | tf_op jit(solution)/shard_map/ppermute | solution.py:47
  259.0 29.0 %collective-permute-start.32 = (bf16[320,1408]{1,0:T(8,128)(2,1)S(1)}, bf16[320,1408]{1,0:T(8,128)(2,1)S(1)}, u32[]{:S(2)}, u32[]{:S(2)}) collective-permute-start(bf16[320,1408]{1,0:T(8,128)(2,1)S(1)} %collective-permute-done.31.refs_4_.refs_8_), channel_id=1, source_target_pairs={{0,4},{4,0},{8,12},{12,8},{16,20},{20,16},{24,28},{28,24},{1,5},{5... | collective-permute-start | bytes 2703368 | tf_op jit(solution)/shard_map/ppermute | solution.py:47
  276.1 25.0 %collective-permute-start.30 = (bf16[320,1408]{1,0:T(8,128)(2,1)S(1)}, bf16[320,1408]{1,0:T(8,128)(2,1)}, u32[]{:S(2)}, u32[]{:S(2)}) collective-permute-start(bf16[320,1408]{1,0:T(8,128)(2,1)S(1)} %collective-permute-done.29.refs_2_.refs_6_), channel_id=1, source_target_pairs={{0,4},{4,0},{8,12},{12,8},{16,20},{20,16},{24,28},{28,24},{1,5},{5... | collective-permute-start | bytes 2703368 | tf_op jit(solution)/shard_map/ppermute | solution.py:47
  277.7 42.8 %collective-permute-start.34 = (bf16[320,1408]{1,0:T(8,128)(2,1)S(1)}, bf16[320,1408]{1,0:T(8,128)(2,1)}, u32[]{:S(2)}, u32[]{:S(2)}) collective-permute-start(bf16[320,1408]{1,0:T(8,128)(2,1)S(1)} %collective-permute-done.33.refs_6_.refs_10_), channel_id=1, source_target_pairs={{0,4},{4,0},{8,12},{12,8},{16,20},{20,16},{24,28},{28,24},{1,5},{5... | collective-permute-start | bytes 2703368 | tf_op jit(solution)/shard_map/ppermute | solution.py:47
  284.6 36.8 %collective-permute-start.36 = (bf16[320,1408]{1,0:T(8,128)(2,1)S(1)}, bf16[320,1408]{1,0:T(8,128)(2,1)}, u32[]{:S(2)}, u32[]{:S(2)}) collective-permute-start(bf16[320,1408]{1,0:T(8,128)(2,1)S(1)} %collective-permute-done.28.refs_1_.refs_5_), channel_id=1, source_target_pairs={{0,2},{1,3},{2,0},{3,1},{4,6},{5,7},{6,4},{7,5},{8,10},{9,11},{10,... | collective-permute-start | bytes 2703368 | tf_op jit(solution)/shard_map/ppermute | solution.py:47
  288.0 70.3 %collective-permute-start.27 = (bf16[256,2560]{1,0:T(8,128)(2,1)}, bf16[256,2560]{1,0:T(8,128)(2,1)S(1)}, u32[]{:S(2)}, u32[]{:S(2)}) collective-permute-start(bf16[256,2560]{1,0:T(8,128)(2,1)} %shard_map.244.n_mine.left_mine), channel_id=1, source_target_pairs={{0,1},{1,0},{2,3},{3,2},{4,5},{5,4},{6,7},{7,6},{8,9},{9,8},{10,11... | collective-permute-start | bytes 3932168 | tf_op jit(solution)/shard_map/ppermute | solution.py:47
  298.1 38.5 %collective-permute-start.39 = (bf16[320,1408]{1,0:T(8,128)(2,1)S(1)}, bf16[320,1408]{1,0:T(8,128)(2,1)S(1)}, u32[]{:S(2)}, u32[]{:S(2)}) collective-permute-start(bf16[320,1408]{1,0:T(8,128)(2,1)S(1)} %collective-permute-done.31.refs_4_.refs_8_), channel_id=1, source_target_pairs={{0,2},{1,3},{2,0},{3,1},{4,6},{5,7},{6,4},{7,5},{8,10},{9,11},{10,... | collective-permute-start | bytes 2703368 | tf_op jit(solution)/shard_map/ppermute | solution.py:47
  301.1 38.5 %collective-permute-start.38 = (bf16[320,1408]{1,0:T(8,128)(2,1)S(1)}, bf16[320,1408]{1,0:T(8,128)(2,1)S(1)}, u32[]{:S(2)}, u32[]{:S(2)}) collective-permute-start(bf16[320,1408]{1,0:T(8,128)(2,1)S(1)} %collective-permute-done.37.refs_10_.refs_14_), channel_id=1, source_target_pairs={{0,4},{4,0},{8,12},{12,8},{16,20},{20,16},{24,28},{28,24},{1,5},{5... | collective-permute-start | bytes 2703368 | tf_op jit(solution)/shard_map/ppermute | solution.py:47
  320.4 34.5 %collective-permute-start.40 = (bf16[320,1408]{1,0:T(8,128)(2,1)S(1)}, bf16[320,1408]{1,0:T(8,128)(2,1)S(1)}, u32[]{:S(2)}, u32[]{:S(2)}) collective-permute-start(bf16[320,1408]{1,0:T(8,128)(2,1)S(1)} %collective-permute-done.32.refs_5_.refs_9_), channel_id=1, source_target_pairs={{0,2},{1,3},{2,0},{3,1},{4,6},{5,7},{6,4},{7,5},{8,10},{9,11},{10,... | collective-permute-start | bytes 2703368 | tf_op jit(solution)/shard_map/ppermute | solution.py:47
  321.4 35.9 %collective-permute-start.42 = (bf16[320,1408]{1,0:T(8,128)(2,1)}, bf16[320,1408]{1,0:T(8,128)(2,1)S(1)}, u32[]{:S(2)}, u32[]{:S(2)}) collective-permute-start(bf16[320,1408]{1,0:T(8,128)(2,1)} %collective-permute-done.41.refs_14_.refs_18_), channel_id=1, source_target_pairs={{0,4},{4,0},{8,12},{12,8},{16,20},{20,16},{24,28},{28,24},{1,5},{5... | collective-permute-start | bytes 2703368 | tf_op jit(solution)/shard_map/ppermute | solution.py:47
  513.3 29.5 %collective-permute-start.112 = (bf16[320,512]{1,0:T(8,128)(2,1)S(1)}, bf16[320,512]{1,0:T(8,128)(2,1)S(1)}, u32[]{:S(2)}, u32[]{:S(2)}) collective-permute-start(bf16[320,512]{1,0:T(8,128)(2,1)S(1)} %copy-done.114), channel_id=1, source_target_pairs={{0,4},{4,0},{8,12},{12,8},{16,20},{20,16},{24,28},{28,24},{1,5},{5... | collective-permute-start | bytes 983048 | tf_op jit(solution)/shard_map/ppermute | solution.py:47
  514.8 28.7 %collective-permute-start.58 = (bf16[64,2560]{1,0:T(8,128)(2,1)}, bf16[64,2560]{1,0:T(8,128)(2,1)S(1)}, u32[]{:S(2)}, u32[]{:S(2)}) collective-permute-start(bf16[64,2560]{1,0:T(8,128)(2,1)} %get-tuple-element.181.own), channel_id=1, source_target_pairs={{0,8},{4,12},{8,0},{12,4},{16,24},{20,28},{24,16},{28,20},{1,9},{5... | collective-permute-start | bytes 983048 | tf_op jit(solution)/shard_map/ppermute | solution.py:47
  516.8 31.9 %collective-permute-start.108 = (bf16[320,512]{1,0:T(8,128)(2,1)}, bf16[320,512]{1,0:T(8,128)(2,1)S(1)}, u32[]{:S(2)}, u32[]{:S(2)}) collective-permute-start(bf16[320,512]{1,0:T(8,128)(2,1)} %get-tuple-element.251), channel_id=1, source_target_pairs={{0,2},{1,3},{2,0},{3,1},{4,6},{5,7},{6,4},{7,5},{8,10},{9,11},{10,... | collective-permute-start | bytes 983048 | tf_op jit(solution)/shard_map/ppermute | solution.py:47
  544.7 27.8 %collective-permute-start.97 = (bf16[320,896]{1,0:T(8,128)(2,1)}, bf16[320,896]{1,0:T(8,128)(2,1)S(1)}, u32[]{:S(2)}, u32[]{:S(2)}) collective-permute-start(bf16[320,896]{1,0:T(8,128)(2,1)} %get-tuple-element.238), channel_id=1, source_target_pairs={{0,4},{4,0},{8,12},{12,8},{16,20},{20,16},{24,28},{28,24},{1,5},{5... | collective-permute-start | bytes 1720328 | tf_op jit(solution)/shard_map/ppermute | solution.py:47
  548.7 40.1 %collective-permute-start.61 = (bf16[256,2560]{1,0:T(8,128)(2,1)}, bf16[256,2560]{1,0:T(8,128)(2,1)S(1)}, u32[]{:S(2)}, u32[]{:S(2)}) collective-permute-start(bf16[256,2560]{1,0:T(8,128)(2,1)} %shard_map.257.d_mine), channel_id=1, source_target_pairs={{0,1},{1,0},{2,3},{3,2},{4,5},{5,4},{6,7},{7,6},{8,9},{9,8},{10,11... | collective-permute-start | bytes 3932168 | tf_op jit(solution)/shard_map/ppermute | solution.py:47
  573.3 33.2 %collective-permute-start.96 = (bf16[320,896]{1,0:T(8,128)(2,1)}, bf16[320,896]{1,0:T(8,128)(2,1)S(1)}, u32[]{:S(2)}, u32[]{:S(2)}) collective-permute-start(bf16[320,896]{1,0:T(8,128)(2,1)} %get-tuple-element.236), channel_id=1, source_target_pairs={{0,4},{4,0},{8,12},{12,8},{16,20},{20,16},{24,28},{28,24},{1,5},{5... | collective-permute-start | bytes 1720328 | tf_op jit(solution)/shard_map/ppermute | solution.py:47
  579.3 30.0 %collective-permute-start.89 = (bf16[320,896]{1,0:T(8,128)(2,1)}, bf16[320,896]{1,0:T(8,128)(2,1)S(1)}, u32[]{:S(2)}, u32[]{:S(2)}) collective-permute-start(bf16[320,896]{1,0:T(8,128)(2,1)} %get-tuple-element.230), channel_id=1, source_target_pairs={{0,4},{4,0},{8,12},{12,8},{16,20},{20,16},{24,28},{28,24},{1,5},{5... | collective-permute-start | bytes 1720328 | tf_op jit(solution)/shard_map/ppermute | solution.py:47
  585.9 24.6 %collective-permute-start.86 = (bf16[320,896]{1,0:T(8,128)(2,1)}, bf16[320,896]{1,0:T(8,128)(2,1)S(1)}, u32[]{:S(2)}, u32[]{:S(2)}) collective-permute-start(bf16[320,896]{1,0:T(8,128)(2,1)} %get-tuple-element.226), channel_id=1, source_target_pairs={{0,2},{1,3},{2,0},{3,1},{4,6},{5,7},{6,4},{7,5},{8,10},{9,11},{10,... | collective-permute-start | bytes 1720328 | tf_op jit(solution)/shard_map/ppermute | solution.py:47
  588.8 26.0 %collective-permute-start.102 = (bf16[320,512]{1,0:T(8,128)(2,1)S(1)}, bf16[320,512]{1,0:T(8,128)(2,1)S(1)}, u32[]{:S(2)}, u32[]{:S(2)}) collective-permute-start(bf16[320,512]{1,0:T(8,128)(2,1)S(1)} %add_convert_fusion.22), channel_id=1, source_target_pairs={{0,4},{4,0},{8,12},{12,8},{16,20},{20,16},{24,28},{28,24},{1,5},{5... | collective-permute-start | bytes 983048 | tf_op jit(solution)/shard_map/ppermute | solution.py:47
  609.4 42.9 %collective-permute-start.98 = (bf16[320,896]{1,0:T(8,128)(2,1)S(1)}, bf16[320,896]{1,0:T(8,128)(2,1)S(1)}, u32[]{:S(2)}, u32[]{:S(2)}) collective-permute-start(bf16[320,896]{1,0:T(8,128)(2,1)S(1)} %add_convert_fusion.1), channel_id=1, source_target_pairs={{0,2},{1,3},{2,0},{3,1},{4,6},{5,7},{6,4},{7,5},{8,10},{9,11},{10,... | collective-permute-start | bytes 1720328 | tf_op jit(solution)/shard_map/ppermute | solution.py:47
  610.5 26.3 %collective-permute-start.110 = (bf16[320,512]{1,0:T(8,128)(2,1)}, bf16[320,512]{1,0:T(8,128)(2,1)S(1)}, u32[]{:S(2)}, u32[]{:S(2)}) collective-permute-start(bf16[320,512]{1,0:T(8,128)(2,1)} %add_convert_fusion.15), channel_id=1, source_target_pairs={{0,16},{4,20},{8,24},{12,28},{16,0},{20,4},{24,8},{28,12},{1,17},{... | collective-permute-start | bytes 983048 | tf_op jit(solution)/shard_map/ppermute | solution.py:47
  620.0 33.4 %collective-permute-start.92 = (bf16[320,896]{1,0:T(8,128)(2,1)}, bf16[320,896]{1,0:T(8,128)(2,1)S(1)}, u32[]{:S(2)}, u32[]{:S(2)}) collective-permute-start(bf16[320,896]{1,0:T(8,128)(2,1)} %get-tuple-element.232), channel_id=1, source_target_pairs={{0,2},{1,3},{2,0},{3,1},{4,6},{5,7},{6,4},{7,5},{8,10},{9,11},{10,... | collective-permute-start | bytes 1720328 | tf_op jit(solution)/shard_map/ppermute | solution.py:47
  621.0 34.2 %collective-permute-start.94 = (bf16[320,896]{1,0:T(8,128)(2,1)S(1)}, bf16[320,896]{1,0:T(8,128)(2,1)S(1)}, u32[]{:S(2)}, u32[]{:S(2)}) collective-permute-start(bf16[320,896]{1,0:T(8,128)(2,1)S(1)} %add_convert_fusion.4), channel_id=1, source_target_pairs={{0,4},{4,0},{8,12},{12,8},{16,20},{20,16},{24,28},{28,24},{1,5},{5... | collective-permute-start | bytes 1720328 | tf_op jit(solution)/shard_map/ppermute | solution.py:47
  638.1 42.4 %collective-permute-start.63 = (bf16[256,2560]{1,0:T(8,128)(2,1)}, bf16[256,2560]{1,0:T(8,128)(2,1)S(1)}, u32[]{:S(2)}, u32[]{:S(2)}) collective-permute-start(bf16[256,2560]{1,0:T(8,128)(2,1)} %get-tuple-element.187), channel_id=1, source_target_pairs={{0,1},{1,0},{2,3},{3,2},{4,5},{5,4},{6,7},{7,6},{8,9},{9,8},{10,11... | collective-permute-start | bytes 3932168 | tf_op jit(solution)/shard_map/ppermute | solution.py:47
  656.5 32.8 %collective-permute-start.90 = (bf16[320,896]{1,0:T(8,128)(2,1)S(1)}, bf16[320,896]{1,0:T(8,128)(2,1)S(1)}, u32[]{:S(2)}, u32[]{:S(2)}) collective-permute-start(bf16[320,896]{1,0:T(8,128)(2,1)S(1)} %add_convert_fusion.7), channel_id=1, source_target_pairs={{0,2},{1,3},{2,0},{3,1},{4,6},{5,7},{6,4},{7,5},{8,10},{9,11},{10,... | collective-permute-start | bytes 1720328 | tf_op jit(solution)/shard_map/ppermute | solution.py:47
  678.2 28.1 %collective-permute-start.81 = (bf16[320,512]{1,0:T(8,128)(2,1)}, bf16[320,512]{1,0:T(8,128)(2,1)S(1)}, u32[]{:S(2)}, u32[]{:S(2)}) collective-permute-start(bf16[320,512]{1,0:T(8,128)(2,1)} %get-tuple-element.214), channel_id=1, source_target_pairs={{0,4},{4,0},{8,12},{12,8},{16,20},{20,16},{24,28},{28,24},{1,5},{5... | collective-permute-start | bytes 983048 | tf_op jit(solution)/shard_map/ppermute | solution.py:47
  679.5 27.4 %collective-permute-start.77 = (bf16[320,512]{1,0:T(8,128)(2,1)}, bf16[320,512]{1,0:T(8,128)(2,1)S(1)}, u32[]{:S(2)}, u32[]{:S(2)}) collective-permute-start(bf16[320,512]{1,0:T(8,128)(2,1)} %get-tuple-element.210), channel_id=1, source_target_pairs={{0,2},{1,3},{2,0},{3,1},{4,6},{5,7},{6,4},{7,5},{8,10},{9,11},{10,... | collective-permute-start | bytes 983048 | tf_op jit(solution)/shard_map/ppermute | solution.py:47
  680.5 29.9 %collective-permute-start.83 = (bf16[320,512]{1,0:T(8,128)(2,1)}, bf16[320,512]{1,0:T(8,128)(2,1)S(1)}, u32[]{:S(2)}, u32[]{:S(2)}) collective-permute-start(bf16[320,512]{1,0:T(8,128)(2,1)} %add_convert_fusion.25), channel_id=1, source_target_pairs={{0,2},{1,3},{2,0},{3,1},{4,6},{5,7},{6,4},{7,5},{8,10},{9,11},{10,... | collective-permute-start | bytes 983048 | tf_op jit(solution)/shard_map/ppermute | solution.py:47
  717.5 33.9 %collective-permute-start.80 = (bf16[320,512]{1,0:T(8,128)(2,1)S(1)}, bf16[320,512]{1,0:T(8,128)(2,1)S(1)}, u32[]{:S(2)}, u32[]{:S(2)}) collective-permute-start(bf16[320,512]{1,0:T(8,128)(2,1)S(1)} %add_convert_fusion.27), channel_id=1, source_target_pairs={{0,16},{4,20},{8,24},{12,28},{16,0},{20,4},{24,8},{28,12},{1,17},{... | collective-permute-start | bytes 983048 | tf_op jit(solution)/shard_map/ppermute | solution.py:47
  724.2 29.7 %collective-permute-start.64 = (bf16[64,2560]{1,0:T(8,128)(2,1)}, bf16[64,2560]{1,0:T(8,128)(2,1)S(1)}, u32[]{:S(2)}, u32[]{:S(2)}) collective-permute-start(bf16[64,2560]{1,0:T(8,128)(2,1)} %get-tuple-element.189), channel_id=1, source_target_pairs={{0,8},{4,12},{8,0},{12,4},{16,24},{20,28},{24,16},{28,20},{1,9},{5... | collective-permute-start | bytes 983048 | tf_op jit(solution)/shard_map/ppermute | solution.py:47
  725.4 57.6 %collective-permute-start.66 = (bf16[64,2560]{1,0:T(8,128)(2,1)}, bf16[64,2560]{1,0:T(8,128)(2,1)S(1)}, u32[]{:S(2)}, u32[]{:S(2)}) collective-permute-start(bf16[64,2560]{1,0:T(8,128)(2,1)} %shard_map.261), channel_id=1, source_target_pairs={{0,16},{4,20},{8,24},{12,28},{16,0},{20,4},{24,8},{28,12},{1,17},{... | collective-permute-start | bytes 983048 | tf_op jit(solution)/shard_map/ppermute | solution.py:47
  732.5 55.6 %collective-permute-start.87 = (bf16[320,896]{1,0:T(8,128)(2,1)S(1)}, bf16[320,896]{1,0:T(8,128)(2,1)S(1)}, u32[]{:S(2)}, u32[]{:S(2)}) collective-permute-start(bf16[320,896]{1,0:T(8,128)(2,1)S(1)} %add_convert_fusion.10), channel_id=1, source_target_pairs={{0,4},{4,0},{8,12},{12,8},{16,20},{20,16},{24,28},{28,24},{1,5},{5... | collective-permute-start | bytes 1720328 | tf_op jit(solution)/shard_map/ppermute | solution.py:47
  733.7 53.3 %collective-permute-start.76 = (bf16[320,512]{1,0:T(8,128)(2,1)S(1)}, bf16[320,512]{1,0:T(8,128)(2,1)S(1)}, u32[]{:S(2)}, u32[]{:S(2)}) collective-permute-start(bf16[320,512]{1,0:T(8,128)(2,1)S(1)} %add_convert_fusion.30), channel_id=1, source_target_pairs={{0,8},{4,12},{8,0},{12,4},{16,24},{20,28},{24,16},{28,20},{1,9},{5... | collective-permute-start | bytes 983048 | tf_op jit(solution)/shard_map/ppermute | solution.py:47
  751.4 37.8 %collective-permute-start.99 = (bf16[320,896]{1,0:T(8,128)(2,1)S(1)}, bf16[320,896]{1,0:T(8,128)(2,1)S(1)}, u32[]{:S(2)}, u32[]{:S(2)}) collective-permute-start(bf16[320,896]{1,0:T(8,128)(2,1)S(1)} %add_convert_fusion), channel_id=1, source_target_pairs={{0,24},{4,28},{8,16},{12,20},{16,8},{20,12},{24,0},{28,4},{1,25},{... | collective-permute-start | bytes 1720328 | tf_op jit(solution)/shard_map/ppermute | solution.py:47
  754.0 52.8 %collective-permute-start.95 = (bf16[320,896]{1,0:T(8,128)(2,1)S(1)}, bf16[320,896]{1,0:T(8,128)(2,1)S(1)}, u32[]{:S(2)}, u32[]{:S(2)}) collective-permute-start(bf16[320,896]{1,0:T(8,128)(2,1)S(1)} %add_convert_fusion.3), channel_id=1, source_target_pairs={{0,16},{4,20},{8,24},{12,28},{16,0},{20,4},{24,8},{28,12},{1,17},{... | collective-permute-start | bytes 1720328 | tf_op jit(solution)/shard_map/ppermute | solution.py:47
  783.0 25.6 %collective-permute-start.91 = (bf16[320,896]{1,0:T(8,128)(2,1)S(1)}, bf16[320,896]{1,0:T(8,128)(2,1)S(1)}, u32[]{:S(2)}, u32[]{:S(2)}) collective-permute-start(bf16[320,896]{1,0:T(8,128)(2,1)S(1)} %add_convert_fusion.6), channel_id=1, source_target_pairs={{0,8},{4,12},{8,0},{12,4},{16,24},{20,28},{24,16},{28,20},{1,9},{5... | collective-permute-start | bytes 1720328 | tf_op jit(solution)/shard_map/ppermute | solution.py:47
  786.9 34.4 %collective-permute-start.68 = (bf16[64,2560]{1,0:T(8,128)(2,1)}, bf16[64,2560]{1,0:T(8,128)(2,1)S(1)}, u32[]{:S(2)}, u32[]{:S(2)}) collective-permute-start(bf16[64,2560]{1,0:T(8,128)(2,1)} %shard_map.262.p0), channel_id=1, source_target_pairs={{0,2},{1,3},{2,0},{3,1},{4,6},{5,7},{6,4},{7,5},{8,10},{9,11},{10,... | collective-permute-start | bytes 983048 | tf_op jit(solution)/shard_map/ppermute | solution.py:47
  788.1 33.1 %collective-permute-start.115 = (f32[320,128]{1,0:T(8,128)S(1)}, f32[320,128]{1,0:T(8,128)S(1)}, u32[]{:S(2)}, u32[]{:S(2)}) collective-permute-start(f32[320,128]{1,0:T(8,128)S(1)} %convert_add_fusion), channel_id=1, source_target_pairs={{0,1},{1,0},{2,3},{3,2},{4,5},{5,4},{6,7},{7,6},{8,9},{9,8},{10,11... | collective-permute-start | bytes 491528 | tf_op jit(solution)/shard_map/ppermute | solution.py:47
  (185 other events, 2730.3 us)

commit v4 on v3

v4 whole, which is shorter than its diff:
```python
import functools

import jax
import jax.numpy as jnp
from jax import lax
from jax.experimental import pallas as pl
from jax.experimental.pallas import tpu as pltpu
from jax.sharding import Mesh
from jax.sharding import PartitionSpec as P

HEAD_DIM = 80
SPAN = 128
EPS = 1e-05
THETA = 1000000.0
PARTS = 4
BF = jnp.bfloat16
F32 = jnp.float32
FACTOR = HEAD_DIM**-0.5
LOG2E = 1.4426950408889634
LIMIT = 56 * 1024 * 1024

PLAIN = (((1,), (0,)), ((), ()))
LAST = (((1,), (1,)), ((), ()))
ROWS = (((0,), (0,)), ((), ()))

VM = pl.BlockSpec(memory_space=pltpu.VMEM)
SM = pl.BlockSpec(memory_space=pltpu.SMEM)
ANY = pl.BlockSpec(memory_space=pl.ANY)


def shape(dims, kind=BF):
    return jax.ShapeDtypeStruct(tuple(dims), kind)


def call(body, outs, in_specs, out_specs, scratch=(), cost=2):
    return pl.pallas_call(
        body,
        out_shape=outs,
        in_specs=in_specs,
        out_specs=out_specs,
        scratch_shapes=list(scratch),
        compiler_params=pltpu.CompilerParams(vmem_limit_bytes=LIMIT),
        cost_estimate=pl.CostEstimate(flops=cost * 10**9, bytes_accessed=0, transcendentals=0),
    )


AXES = ("z", "y", "x", "c")


def hop(value, axis, k):
    size = lax.axis_size(axis)
    return lax.ppermute(value, axis, [(i, i ^ k) for i in range(size)])


def dot(left, right, dims=PLAIN):
    return lax.dot_general(left, right, dims, preferred_element_type=F32)


def joined(values, width):
    values = [v.astype(F32) for v in values]
    have = sum(v.shape[1] for v in values)
    if have < width:
        values.append(jnp.zeros((values[0].shape[0], width - have), F32))
    return jnp.concatenate(values, axis=1).astype(BF)


def pack_body(takes, width, cut, z_ref, *refs):
    count = len(takes)
    ins, outs = refs[:count], refs[count:]
    for k in range(PARTS):
        part = z_ref[0] ^ k
        for j in range(PARTS):

            @pl.when(part == j)
            def _():
                values = [ref[:, pl.ds(step * (j // share), step)] for ref, (step, share) in zip(ins, takes)]
                value = joined(values, width)
                if cut and k >= 2:
                    outs[k][...] = value[:, :cut]
                    outs[k + 2][...] = value[:, cut:]
                else:
                    outs[k][...] = value


def pack(z, arrays, takes, width, cut=None):
    depth = arrays[0].shape[0]
    outs = [shape((depth, width))] * PARTS
    if cut:
        outs = outs[:2] + [shape((depth, cut))] * 2 + [shape((depth, width - cut))] * 2
    return call(
        functools.partial(pack_body, takes, width, cut),
        outs,
        [SM] + [VM] * len(arrays),
        [VM] * len(outs),
    )(z, *arrays)


def pack_attn_body(z_ref, wq, wk, wv, wo, gain_one, gain_two, *outs):
    depth, width = outs[0].shape
    kw = wk.shape[0] // 2
    qw = wq.shape[1] // PARTS
    narrow = jnp.concatenate([wk[...].astype(F32), wv[...].astype(F32)], axis=0)
    gains = jnp.concatenate([gain_one[...], gain_two[...]], axis=0).astype(F32)
    fill = jnp.zeros((128 - (4 * kw + 2) % 128, depth), F32)
    tall = jnp.concatenate([narrow, gains, fill], axis=0).T
    for k in range(PARTS):
        part = z_ref[0] ^ k
        for j in range(PARTS):

            @pl.when(part == j)
            def _():
                spot = pl.ds(qw * j, qw)
                h = j // 2
                values = [
                    wq[:, spot],
                    tall[:, kw * h : kw * h + kw],
                    tall[:, kw * (h + 2) : kw * (h + 3)],
                    wo[:, spot],
                    tall[:, 4 * kw : 4 * kw + 2],
                ]
                outs[k][...] = joined(values, width)


def pack_attn(z, wq, wk, wv, wo, gain_one, gain_two, width):
    depth = wq.shape[0]
    return call(
        pack_attn_body, [shape((depth, width))] * PARTS, [SM] + [VM] * 6, [VM] * PARTS
    )(z, wq, wk.T, wv.T, wo, gain_one.reshape(1, -1), gain_two.reshape(1, -1))


def unpack_body(takes, cut, z_ref, *refs):
    count = PARTS + 2 if cut else PARTS
    ins, outs = refs[:count], refs[count:]
    for ref, (start, step, share) in zip(outs, takes):
        if share == 2:
            ref[...] = jnp.zeros_like(ref)
    for k in range(PARTS):
        part = z_ref[0] ^ k
        for j in range(PARTS):

            @pl.when(part == j)
            def _():
                for ref, (start, step, share) in zip(outs, takes):
                    late = cut and k >= 2 and start >= cut
                    piece = ins[k + 2] if late else ins[k]
                    value = piece[:, pl.ds(start - cut if late else start, step)].astype(F32)
                    spot = pl.ds(step * (j // share), step)
                    if share == 1:
                        ref[:, spot] = value
                    else:
                        ref[:, spot] += value


def unpack(z, pieces, takes, cut=None):
    depth = pieces[0].shape[0]
    return call(
        functools.partial(unpack_body, takes, cut),
        [shape((depth, step * PARTS // share), F32) for start, step, share in takes],
        [SM] + [VM] * len(pieces),
        [VM] * len(takes),
        cost=4,
    )(z, *pieces)


def spot_of(pos, k, j, inner, depth):
    return pl.ds(pl.multiple_of(((pos[1] ^ k) * inner + (pos[2] ^ j)) * depth, 16), depth)


def piece_copies(pos, inner, pieces, store, sem, i, back=False):
    half = inner // 2
    depth = store.shape[1] // (PARTS * inner)
    copies = []
    for k in range(PARTS):
        for j in range(inner):
            ends = (
                pieces[2 * k + j // half].at[pl.ds((j % half) * depth, depth)],
                store.at[i, spot_of(pos, k, j, inner, depth)],
            )
            n = (i * PARTS + k) * inner + j
            copies.append(pltpu.make_async_copy(*(ends[::-1] if back else ends), sem.at[n]))
    return copies


def fetch(pos, inner, pieces, store, sem):
    copies = [piece_copies(pos, inner, pieces[8 * i : 8 * i + 8], store, sem, i) for i in range(2)]
    return start_all(copies)


def start_all(copies):
    for half in copies:
        for c in half:
            c.start()

    def wait(i):
        for c in copies[i]:
            c.wait()

    return wait


def own_rows_body(pos, ids, x_ref, t_ref, x_out, t_out, tall):
    spot = pl.ds(pl.multiple_of(pos[0], 64), 64)
    width = x_ref.shape[1]
    tall[...] = jnp.broadcast_to(ids[...].astype(F32), tall.shape[::-1]).T
    x_out[:, :width] = x_ref[spot, :]
    x_out[:, width:] = tall[spot, :].astype(BF)
    t_out[...] = t_ref[spot, :]


def own_rows(pos, ids, x, t):
    rows, width = x.shape
    return call(
        own_rows_body,
        [shape((64, width + 128)), shape((64, width))],
        [SM] + [VM] * 3,
        [VM] * 2,
        [pltpu.VMEM((rows, 128), F32)],
    )(pos, ids, x, t)


def stack_body(own, one, two, three, out):
    n = own.shape[0]
    for k, ref in enumerate((own, one, two, three)):
        out[pl.ds(k * n, n), :] = ref[...]


def stack(pieces):
    n, cols = pieces[0].shape
    return call(stack_body, shape((4 * n, cols)), [VM] * 4, VM)(*pieces)


def first_sum_body(mine, got, one, three, keep):
    n = one.shape[0]

    def piece(k):
        spot = pl.ds(k * n, n)
        return mine[spot, :] + got[spot, :].astype(F32)

    three[...] = piece(3).astype(BF)
    one[...] = piece(1).astype(BF)
    keep[:n, :] = piece(0)
    keep[n:, :] = piece(2)


def first_sum(mine, got):
    n, width = mine.shape
    n //= 4
    return call(
        first_sum_body, [shape((n, width))] * 2 + [shape((2 * n, width), F32)], [VM] * 2, [VM] * 3
    )(mine, got)


def second_sum_body(keep, three, out):
    n = out.shape[0]
    out[...] = (keep[n:, :] + three[...].astype(F32)).astype(BF)


def second_sum(keep, three):
    return call(second_sum_body, shape(three.shape), [VM] * 2, VM)(keep, three)


def last_sum(keep, one, two):
    n = one.shape[0]
    return keep[:n, :] + one[...].astype(F32) + two[...].astype(F32)


def mean_scale(value):
    return lax.rsqrt(jnp.mean(value * value, axis=-1, keepdims=True) + EPS)


def back_norm(grad, value, gain):
    scale = mean_scale(value)
    unit = value * scale
    scaled = grad * gain
    return unit, scale * (scaled - unit * jnp.mean(scaled * unit, axis=-1, keepdims=True))


def after_attn_body(keep, one, two, x_own, gain, middle, n_own, total):
    branch = last_sum(keep, one, two)
    value = x_own[:, : branch.shape[1]].astype(F32) + branch
    middle[...] = value
    n_own[...] = (value * mean_scale(value) * gain[1:2, :]).astype(BF)
    total[...] = jnp.full(total.shape, jnp.sum(branch * branch), F32)


def after_mlp_body(keep, one, two, middle, target, d_own, out, total):
    branch = last_sum(keep, one, two)
    stream = middle[...] + branch
    d_own[...] = (stream - target[...].astype(F32)).astype(BF)
    out[...] = stream.astype(BF)
    total[0:8, :] = jnp.full((8, 128), jnp.sum(stream * stream), F32)
    total[8:16, :] = jnp.full((8, 128), jnp.sum(branch * branch), F32)


def after_feed_back_body(keep, one, two, middle, d_own, gain, d_middle, a_own, gain_grad):
    grad = last_sum(keep, one, two)
    unit, back = back_norm(grad, middle[...], gain[1:2, :])
    value = d_own[...].astype(F32) + back
    d_middle[...] = value
    a_own[...] = value.astype(BF)
    gain_grad[...] = jnp.sum(grad * unit, axis=0, keepdims=True)


def after_all_body(keep, one, two, x_own, d_middle, gain, out):
    grad = last_sum(keep, one, two)
    unit, back = back_norm(grad, x_own[:, : grad.shape[1]].astype(F32), gain[0:1, :])
    out[...] = (d_middle[...] + back).astype(BF)


def spread_rows_body(spots, p0, p1, p2, p3, out):
    n = p0.shape[0]
    for i, ref in enumerate((p0, p1, p2, p3)):
        out[pl.ds(pl.multiple_of(spots[i], 64), n), :] = ref[...]


def spread_rows(spots, pieces):
    n, width = pieces[0].shape
    return call(spread_rows_body, shape((4 * n, width)), [SM] + [VM] * 4, VM)(spots, *pieces)


def rotated(value, cosine, sine):
    half = HEAD_DIM // 2
    a, b = value[:, :half], value[:, half:]
    return jnp.concatenate([a * cosine - b * sine, b * cosine + a * sine], axis=1)


def project_body(qw, inner, pos, x_mine, x_theirs, cosine, sine, *refs):
    w = refs[:16]
    first, q_ref, kv_ref, gains, row_ids = refs[16:21]
    store, sem = refs[21:]
    wait = fetch(pos, inner, w, store, sem)
    width = first.shape[1]
    step = width // 4
    ids = jnp.concatenate([x_mine[:, width:], x_theirs[:, width:]], axis=0).astype(F32)
    row_ids[...] = ids.T[0:8, :]
    wait(0)
    spot = 480 - 384
    for p in range(4):
        tail = store[0, pl.ds(p * step, step), 384:512].astype(F32).T
        gains[:, pl.ds(p * step, step)] = tail[spot : spot + 8]
    gain = gains[0:1, :]
    rows = x_mine.shape[0]
    for i, ref in enumerate((x_mine, x_theirs)):
        value = ref[:, :width].astype(F32)
        first[pl.ds(i * rows, rows), :] = (value * mean_scale(value) * gain).astype(BF)
    cos, sin = cosine[...], sine[...]
    queries, keys, values = [], [], []
    for i in range(2):
        if i:
            wait(1)
        out = dot(first[...], store[i])
        for start in range(0, qw, HEAD_DIM):
            queries.append(rotated(out[:, start : start + HEAD_DIM], cos, sin))
        keys.append(rotated(out[:, qw : qw + HEAD_DIM], cos, sin))
        values.append(out[:, qw + HEAD_DIM : qw + 2 * HEAD_DIM])
    q_ref[...] = jnp.concatenate(queries, axis=1).astype(BF)
    kv_ref[...] = jnp.concatenate(keys + values + [ids[:, :64]], axis=1).astype(BF)


def sems(inner):
    return pltpu.SemaphoreType.DMA((2 * PARTS * inner,))


def project(pos, x_mine, x_theirs, cosine, sine, w, qw, inner):
    rows, width = x_mine.shape
    rows *= 2
    width -= 128
    return call(
        functools.partial(project_body, qw, inner),
        [
            shape((rows, width)),
            shape((rows, 2 * qw)),
            shape((rows, 384)),
            shape((8, width), F32),
            shape((8, rows), F32),
        ],
        [SM] + [VM] * 4 + [ANY] * 16,
        [VM] * 5,
        [pltpu.VMEM((2, width, 512), BF), sems(inner)],
        cost=12,
    )(pos, x_mine, x_theirs, cosine, sine, *w)


def out_sides(partial, mine, theirs):
    n = mine.shape[0]
    mine[...] = partial[:n]
    theirs[...] = partial[n:].astype(theirs.dtype)


def each(count, step, start):
    if count <= 2:
        for s in range(count):
            start = step(s, start)
        return start
    return lax.fori_loop(0, count, step, start)


def reader(kvs, rows):
    def read(s, lane):
        if len(kvs) > 1:
            return kvs[s][:, lane]
        return kvs[0][pl.ds(pl.multiple_of(s * rows, rows), rows), lane]

    return read


def lanes(i):
    return pl.ds(i * HEAD_DIM, HEAD_DIM)


ID_LANE = pl.ds(4 * HEAD_DIM, 1)


def attend_body(sides, pos, q_ref, row_ids, *refs):
    arrays = sides if sides <= 2 else 1
    kvs, refs = refs[:arrays], refs[arrays:]
    w = refs[:16]
    mixed = refs[16:18]
    lse, mine, theirs = refs[18:21]
    store, sem = refs[21:]
    wait = fetch(pos, sides, w, store, sem)
    rows = q_ref.shape[0]
    qw = q_ref.shape[1] // 2
    ids = row_ids[0:1, :]
    read = reader(kvs, rows)

    def look(s):
        return read(s, ID_LANE).astype(F32) <= ids

    looks = [look(s) for s in range(sides)] if sides <= 2 else None
    lse[...] = jnp.zeros_like(lse)
    head = 0
    c = FACTOR * LOG2E
    for i in range(2):
        outs = []
        for start in range(i * qw, (i + 1) * qw, HEAD_DIM):
            q = q_ref[:, start : start + HEAD_DIM]

            def score(s):
                seen = looks[s] if looks else look(s)
                return jnp.where(seen, dot(read(s, lanes(i)), q, LAST), -1e30)

            scores = [score(s) for s in range(sides)] if sides <= 2 else None

            def highest(s, top):
                value = scores[s] if scores else score(s)
                return jnp.maximum(top, jnp.max(value, axis=0, keepdims=True))

            top = each(sides, highest, jnp.full((1, rows), -1e30, F32))

            def gathered(s, carry):
                total, out = carry
                value = scores[s] if scores else score(s)
                p = jnp.exp2(value * c - top * c)
                total = total + jnp.sum(p, axis=0, keepdims=True)
                return total, out + dot(read(s, lanes(2 + i)), p.astype(BF), ROWS)

            nothing = (jnp.zeros((1, rows), F32), jnp.zeros((HEAD_DIM, rows), F32))
            total, out = each(sides, gathered, nothing)
            outs.append(out / total)
            lse[head : head + 1, :] = top * c + jnp.log2(total)
            head += 1
        fill = jnp.zeros((512 - 320 - qw, rows), F32)
        tall = jnp.concatenate([jnp.zeros((320, rows), F32)] + outs + [fill], axis=0)
        mixed[i][...] = tall.T.astype(BF)
    for i in range(2):
        wait(i)
    partial = dot(mixed[0][...], store[0], LAST) + dot(mixed[1][...], store[1], LAST)
    out_sides(partial, mine, theirs)


def attend(pos, q, kvs, row_ids, w, sides):
    rows = q.shape[0]
    width = 8 * w[0].shape[0]
    return call(
        functools.partial(attend_body, sides),
        [shape((rows, 512))] * 2
        + [shape((8, rows), F32), shape((rows // 2, width), F32), shape((rows // 2, width))],
        [SM] + [VM] * (2 + len(kvs)) + [ANY] * 16,
        [VM] * 5,
        [pltpu.VMEM((2, width, 512), BF), sems(sides)],
        cost=12,
    )(pos, q, row_ids, *kvs, *w)


def padded(value, width):
    return jnp.concatenate([value, jnp.zeros((value.shape[0], width - value.shape[1]), value.dtype)], axis=1)


def block_copies(pos, inner, arrays, store, sem, i):
    depth = arrays[0].shape[1] // 2
    copies = []
    for k in range(PARTS):
        for j in range(inner):
            n = k * inner + j
            spot = arrays[k // 2].at[j * 2 + (pos[3] ^ i), pl.ds((k % 2) * depth, depth)]
            to = store.at[i, pl.ds(pl.multiple_of(((pos[1] ^ k) * inner + j) * depth, 16), depth)]
            copies.append(pltpu.make_async_copy(spot, to, sem.at[i * PARTS * inner + n]))
    return copies


def feed_body(fw, inner, pos, n_mine, n_theirs, near, far, *refs):
    hidden, slope, silu = refs[0:2], refs[2:4], refs[4:6]
    mine, theirs = refs[6:8]
    rows_in, store, sem = refs[8:]
    wait = start_all([block_copies(pos, inner, (near, far), store, sem, i) for i in range(2)])
    rows = n_mine.shape[0]
    rows_in[:rows, :] = n_mine[...]
    rows_in[rows:, :] = n_theirs[...]
    for i in range(2):
        wait(i)
        out = dot(rows_in[...], store[i, :, : 2 * fw])
        gate, upper = out[:, :fw], out[:, fw:]
        sigma = jax.nn.sigmoid(gate)
        act = gate * sigma
        hidden[i][...] = padded(act * upper, 512).astype(BF)
        slope[i][...] = padded(upper * (sigma + act * (1.0 - sigma)), 512).astype(BF)
        silu[i][...] = padded(act, 512).astype(BF)
    out_sides(
        dot(hidden[0][...], store[0, :, 2 * fw :], LAST)
        + dot(hidden[1][...], store[1, :, 2 * fw :], LAST),
        mine,
        theirs,
    )


def feed(pos, n_mine, n_theirs, w, fw, inner):
    rows, width = n_mine.shape
    return call(
        functools.partial(feed_body, fw, inner),
        [shape((2 * rows, 512))] * 6 + [shape((rows, width), F32), shape((rows, width))],
        [SM] + [VM] * 2 + [ANY] * 2,
        [VM] * 8,
        [pltpu.VMEM((2 * rows, width), BF), pltpu.VMEM((2, width, 2 * fw + 512), BF), sems(inner)],
        cost=18,
    )(pos, n_mine, n_theirs, *w)


def feed_back_body(fw, inner, pos, d_mine, d_theirs, *refs):
    slope, silu = refs[:2], refs[2:4]
    blocks = refs[4:6]
    d_gu = refs[6:8]
    mine, theirs = refs[8:10]
    rows_in, store, sem = refs[10:]
    wait = start_all([block_copies(pos, inner, blocks, store, sem, i) for i in range(2)])
    rows = d_mine.shape[0]
    rows_in[:rows, :] = d_mine[...]
    rows_in[rows:, :] = d_theirs[...]
    for i in range(2):
        wait(i)
        out = dot(rows_in[...], store[i, :, 2 * fw :])
        a = (out * slope[i][...].astype(F32))[:, :fw]
        b = (out * silu[i][...].astype(F32))[:, :fw]
        d_gu[i][...] = jnp.concatenate([a, b], axis=1).astype(BF)
    out_sides(
        dot(d_gu[0][...], store[0, :, : 2 * fw], LAST)
        + dot(d_gu[1][...], store[1, :, : 2 * fw], LAST),
        mine,
        theirs,
    )


def feed_back(pos, d_mine, d_theirs, slope, silu, w, fw, inner):
    rows, width = d_mine.shape
    return call(
        functools.partial(feed_back_body, fw, inner),
        [shape((2 * rows, 2 * fw))] * 2 + [shape((rows, width), F32), shape((rows, width))],
        [SM] + [VM] * 6 + [ANY] * 2,
        [VM] * 4,
        [pltpu.VMEM((2 * rows, width), BF), pltpu.VMEM((2, width, 2 * fw + 512), BF), sems(inner)],
        cost=16,
    )(pos, d_mine, d_theirs, *slope, *silu, *w)


def features(pos, k, step):
    return pl.ds(pl.multiple_of((pos[1] ^ k) * step, 128), step)


def feed_grad_body(inner, pair, pos, n_mine, n_theirs, d_mine, d_theirs, *refs):
    d_gu, hidden = refs[:2], refs[2:4]
    out, store, sem = refs[4:]
    rows = n_mine.shape[0]
    step = store.shape[1] // 2
    depth = step // inner
    cut = d_gu[0].shape[1]
    copies = []
    for p in range(2):
        spot = features(pos, 2 * pair + p, step)
        to = pl.ds(p * step, step)
        for i in range(2):
            value = dot(n_mine[:, spot], d_gu[i][:rows, :], ROWS)
            value += dot(n_theirs[:, spot], d_gu[i][rows:, :], ROWS)
            store[i, to, :cut] = value.astype(BF)
            value = dot(d_mine[:, spot], hidden[i][:rows, :], ROWS)
            value += dot(d_theirs[:, spot], hidden[i][rows:, :], ROWS)
            store[i, to, cut:] = value.astype(BF)
            for j in range(inner):
                n = p * inner + j
                copies.append(
                    pltpu.make_async_copy(
                        store.at[i, pl.ds(n * depth, depth)],
                        out.at[j * 2 + (pos[3] ^ i), pl.ds(p * depth, depth)],
                        sem.at[i * 2 * inner + n],
                    )
                )
                copies[-1].start()
    for c in copies:
        c.wait()


def feed_grad(pos, n_all, d_all, d_gu, hidden, inner, pair):
    rows, width = n_all[0].shape
    cols = d_gu[0].shape[1] + hidden[0].shape[1]
    return call(
        functools.partial(feed_grad_body, inner, pair),
        shape((inner * 2, width // (2 * inner), cols)),
        [SM] + [VM] * 8,
        ANY,
        [pltpu.VMEM((2, width // 2, cols), BF), pltpu.SemaphoreType.DMA((4 * inner,))],
        cost=9,
    )(pos, *n_all, *d_all, *d_gu, *hidden)


def attend_back_body(sides, pos, d_mine, d_theirs, q_ref, row_ids, lse, cosine, sine, *refs):
    arrays = sides if sides <= 2 else 1
    kvs, refs = refs[:arrays], refs[arrays:]
    w = refs[:16]
    dq_ref, own_ref, send_ref = refs[16:19]
    store, mix, d_kv, sem = refs[19:]
    wait = fetch(pos, sides, w, store, sem)
    rows = q_ref.shape[0]
    half = rows // 2
    qw = q_ref.shape[1] // 2
    for i in range(2):
        wait(i)
        for side, ref in enumerate((d_mine, d_theirs)):
            mix[i, pl.ds(side * half, half), :] = dot(ref[...], store[i])[:, 320 : 320 + qw].astype(BF)
    ids = row_ids[0:1, :]
    read = reader(kvs, rows)

    def look(s):
        return read(s, ID_LANE).astype(F32) <= ids

    looks = [look(s) for s in range(sides)] if sides <= 2 else None
    d_q = []
    c = FACTOR * LOG2E
    head = 0
    for i in range(2):
        for start in range(0, qw, HEAD_DIM):
            q = q_ref[:, i * qw + start : i * qw + start + HEAD_DIM]
            dm = mix[i, :, start : start + HEAD_DIM]
            level = lse[head : head + 1, :]
            head += 1

            def pair(s):
                seen = looks[s] if looks else look(s)
                p = jnp.where(seen, jnp.exp2(dot(read(s, lanes(i)), q, LAST) * c - level), 0.0)
                return p, dot(read(s, lanes(2 + i)), dm, LAST)

            held = [pair(s) for s in range(sides)] if sides <= 2 else None

            def weigh(s, delta):
                p, dp = held[s] if held else pair(s)
                return delta + jnp.sum(p * dp, axis=0, keepdims=True)

            delta = each(sides, weigh, jnp.zeros((1, rows), F32))

            def grads(s, out):
                p, dp = held[s] if held else pair(s)
                ds = (p * (dp - delta)).astype(BF)
                d_value = dot(p.astype(BF), dm)
                d_key = dot(ds, q)
                if start == 0:
                    d_kv[2 + i, s] = d_value
                    d_kv[i, s] = d_key
                else:
                    d_kv[2 + i, s] += d_value
                    d_kv[i, s] += d_key
                return out + dot(read(s, lanes(i)), ds, ROWS)

            d_q.append(each(sides, grads, jnp.zeros((HEAD_DIM, rows), F32)))
    tall = jnp.concatenate(d_q + [jnp.zeros((512 - 4 * HEAD_DIM, rows), F32)], axis=0).T * FACTOR
    cos, sin = cosine[...], sine[...]
    dq_ref[...] = jnp.concatenate(
        [rotated(tall[:, h * HEAD_DIM : (h + 1) * HEAD_DIM], cos, -sin) for h in range(4)], axis=1
    ).astype(BF)
    for s in range(sides):
        value = jnp.concatenate([d_kv[0, s] * FACTOR, d_kv[1, s] * FACTOR, d_kv[2, s], d_kv[3, s]], axis=1)
        if s == 0:
            own_ref[...] = value
        else:
            send_ref[pl.ds((s - 1) * rows, rows), :] = value.astype(BF)


def attend_back(pos, d_mine, d_theirs, q, kvs, row_ids, lse, cosine, sine, w, sides):
    rows = q.shape[0]
    width = d_mine.shape[1]
    cols = 4 * HEAD_DIM
    return call(
        functools.partial(attend_back_body, sides),
        [shape(q.shape), shape((rows, cols), F32), shape(((sides - 1) * rows, cols))],
        [SM] + [VM] * (7 + len(kvs)) + [ANY] * 16,
        [VM] * 3,
        [
            pltpu.VMEM((2, width, 512), BF),
            pltpu.VMEM((2, rows, q.shape[1] // 2), BF),
            pltpu.VMEM((4, sides, rows, HEAD_DIM), F32),
            sems(sides),
        ],
        cost=18,
    )(pos, d_mine, d_theirs, q, row_ids, lse, cosine, sine, *kvs, *w)


def split_body(dq_ref, own_ref, got_ref, cosine, sine, *d_qkv):
    qw = dq_ref.shape[1] // 2
    cos, sin = cosine[...], sine[...]
    d_kv = own_ref[...] + got_ref[...].astype(F32)
    d_q = dq_ref[...].astype(F32)
    for i in range(2):
        d_k = rotated(d_kv[:, i * HEAD_DIM : (i + 1) * HEAD_DIM], cos, -sin)
        d_v = d_kv[:, (2 + i) * HEAD_DIM : (3 + i) * HEAD_DIM]
        d_qkv[i][...] = padded(
            jnp.concatenate([d_q[:, i * qw : (i + 1) * qw], d_k, d_v], axis=1), 512
        ).astype(BF)


def split_grads(dq, own, got, cosine, sine):
    rows = dq.shape[0]
    return call(split_body, [shape((rows, 512))] * 2, [VM] * 5, [VM] * 2)(dq, own, got, cosine, sine)


def project_back_body(inner, pos, x_mine, x_theirs, d_a, d_b, *refs):
    w = refs[:16]
    mine, theirs, gain_ref = refs[16:19]
    store, sem = refs[19:]
    wait = fetch(pos, inner, w, store, sem)
    for i in range(2):
        wait(i)
    half, width = mine.shape
    total = 0.0
    for side, ref, x_ref in ((1, theirs, x_theirs), (0, mine, x_mine)):
        spot = pl.ds(side * half, half)
        part = dot(d_a[spot, :], store[0], LAST) + dot(d_b[spot, :], store[1], LAST)
        ref[...] = part.astype(ref.dtype)
        x = x_ref[:, :width].astype(F32)
        total = total + jnp.sum(part * (x * mean_scale(x)), axis=0, keepdims=True)
    gain_ref[...] = jnp.broadcast_to(total, gain_ref.shape)


def project_back(pos, x_mine, x_theirs, d_qkv, w, inner):
    rows, width = x_mine.shape
    width -= 128
    return call(
        functools.partial(project_back_body, inner),
        [shape((rows, width), F32), shape((rows, width)), shape((8, width), F32)],
        [SM] + [VM] * 4 + [ANY] * 16,
        [VM] * 3,
        [pltpu.VMEM((2, width, 512), BF), sems(inner)],
        cost=10,
    )(pos, x_mine, x_theirs, *d_qkv, *w)


def attn_grad_body(inner, pos, first, d_mine, d_theirs, *refs):
    d_qkv, mixed = refs[:2], refs[2:4]
    outs = refs[4:20]
    store, sem = refs[20:]
    half = d_mine.shape[0]
    step = store.shape[1] // PARTS
    copies = [piece_copies(pos, inner, outs[8 * i : 8 * i + 8], store, sem, i, True) for i in range(2)]
    for k in (3, 2, 1, 0):
        spot = features(pos, k, step)
        for i in range(2):
            value = dot(first[:, spot], d_qkv[i][...], ROWS)
            value += dot(d_mine[:, spot], mixed[i][:half, :], ROWS)
            value += dot(d_theirs[:, spot], mixed[i][half:, :], ROWS)
            store[i, spot, :] = value.astype(BF)
            for c in copies[i][k * inner : (k + 1) * inner]:
                c.start()
    for i in range(2):
        for c in copies[i]:
            c.wait()


def attn_grad(pos, first, d_mine, d_theirs, d_qkv, mixed, inner):
    rows, width = first.shape
    return call(
        functools.partial(attn_grad_body, inner),
        [shape((width // 8, 512))] * 16,
        [SM] + [VM] * 7,
        [ANY] * 16,
        [pltpu.VMEM((2, width, 512), BF), sems(inner)],
        cost=10,
    )(pos, first, d_mine, d_theirs, *d_qkv, *mixed)


def tail_body(gain_one, gain_two, sum_attn, sums, out):
    width = gain_two.shape[1]
    out[:, :width] = jnp.concatenate(
        [gain_one[0:1, :], gain_two[...], jnp.zeros((6, width), F32)], axis=0
    )
    lane = lax.broadcasted_iota(jnp.int32, (8, 128), 1)
    tail = jnp.where(lane == 0, sums[0:8, :], 0.0)
    tail = jnp.where(lane == 1, sum_attn[...], tail)
    out[:, width:] = jnp.where(lane == 2, sums[8:16, :], tail)


def tail_rows(gain_one, gain_two, sum_attn, sums):
    width = gain_two.shape[1]
    return call(tail_body, shape((8, width + 128), F32), [VM] * 4, VM)(gain_one, gain_two, sum_attn, sums)


class Live:
    def fence(self):
        names = sorted(self.__dict__)
        leaves, tree = jax.tree.flatten([self.__dict__[n] for n in names])
        leaves = lax.optimization_barrier(tuple(leaves))
        self.__dict__.update(zip(names, jax.tree.unflatten(tree, leaves)))


class Place:
    def __init__(self):
        self.inner = lax.axis_size("y")
        self.count = PARTS * self.inner
        self.z, self.y, self.x, self.c = [lax.axis_index(name) for name in AXES]
        self.s = self.z * self.inner + self.y
        self.zs = self.z.reshape(1).astype(jnp.int32)
        self.bits = []
        b = 1
        while b < self.inner:
            self.bits.append(b)
            b *= 2

    def hop_z(self, v, k):
        return hop(v, "z", k)

    def hop_y(self, v, b):
        return hop(v, "y", b)

    def hop_x(self, v):
        return hop(v, "x", 1)

    def hop_c(self, v):
        return hop(v, "c", 1)

    def low_y(self, v):
        for b in self.bits[:-1]:
            v = jnp.concatenate([v, self.hop_y(v, b)], 0)
        return v

    def far_y(self, v):
        return self.hop_y(v, self.bits[-1])

    def add(self, own, got):
        return (own.astype(F32) + got.astype(F32)).astype(BF)

    def sum_y(self, own, far):
        value = self.add(own, self.far_y(far))
        for b in reversed(self.bits[:-1]):
            n = value.shape[0] // 2
            value = self.add(value[:n], self.hop_y(value[n:], b))
        return value

    def sum_x(self, own, other):
        return self.add(own, self.hop_x(other))

    def gather(self, own):
        one = self.hop_z(own, 1)
        two = self.hop_z(own, 2)
        three = self.hop_z(two, 1)
        mine = stack([own, one, two, three])
        return [mine, self.hop_c(mine)]

    def scatter(self, mine, theirs):
        one, three, keep = first_sum(mine, self.hop_c(theirs))
        two = second_sum(keep, self.hop_z(three, 1))
        return keep, self.hop_z(one, 1), self.hop_z(two, 2)


def tables(place):
    half = HEAD_DIM // 2
    freq = THETA ** (-(jnp.arange(half, dtype=F32) * 2.0 / HEAD_DIM))
    angle = place[:, None] * freq[None, :]
    return (jnp.cos(angle), jnp.sin(angle))


def on_device(
    inputs,
    targets,
    seq_ids,
    block_ids,
    attn_gain,
    mlp_gain,
    w_query,
    w_key,
    w_value,
    w_out,
    w_gate,
    w_up,
    w_down,
):
    at = Place()
    inner = at.inner
    full = inputs.shape[1]
    half_span = SPAN // 2
    kw = w_key.shape[1] // 2
    qw = w_query.shape[1] // PARTS
    fw = w_gate.shape[1] // PARTS
    row_f32 = shape((half_span, full), F32)
    row_bf = shape((half_span, full))

    off = jnp.where(seq_ids[0] == at.x, 0, SPAN)
    pos = jnp.stack([off + at.c * half_span, at.z, at.y, at.x, at.c]).astype(jnp.int32)
    spots = [
        (off if xr == 0 else SPAN - off) + (at.c ^ cr) * half_span for xr in range(2) for cr in range(2)
    ]
    spots = jnp.stack(spots).astype(jnp.int32)

    def all_rows(own):
        across = at.hop_x(own)
        return spread_rows(spots, [own, at.hop_c(own), across, at.hop_c(across)])

    rows = 2 * PARTS * half_span
    count = jnp.arange(rows, dtype=jnp.int32)
    zz = at.z ^ ((count // half_span) % PARTS)
    cc = at.c ^ (count // (half_span * PARTS))
    place = ((zz * inner + at.y) * SPAN + cc * half_span + count % half_span).astype(F32)
    cosine, sine = tables(place)

    def listed(w):
        return [v for i in range(2) for k in range(PARTS) for v in w[k][i]]

    def pieces(grads):
        return [(grads[2 * k : 2 * k + 2], grads[8 + 2 * k : 10 + 2 * k]) for k in range(PARTS)]

    def first_x(g):
        return [at.sum_x(a, b) for a, b in zip(*g)]

    def first_y(g):
        return [at.sum_y(*side) for side in g]

    def gather_blocks(pair):
        return lax.all_gather(pair, ("y", "x"), axis=0)

    def scatter_blocks(blocks):
        blocks = blocks.reshape(-1, blocks.shape[-1])
        got = lax.psum_scatter(blocks, ("y", "x"), scatter_dimension=0, tiled=True)
        n = got.shape[0] // 2
        return [got[:n], got[n:]]

    hop_x, hop_z, low_y, far_y = at.hop_x, at.hop_z, at.low_y, at.far_y
    live = Live()
    live.w = [w_gate, w_up, w_down]
    live.rows = [inputs, targets]
    live.qo = pack_attn(at.zs, w_query, w_key, w_value, w_out, attn_gain, mlp_gain, 512)
    live.fence()

    q = live.qo
    z = [q[0]] + [hop_z(q[k], k) for k in range(1, PARTS)]
    live.x_own, live.t_own = own_rows(pos, block_ids.reshape(1, -1), *live.rows)
    live.g = list(pack(at.zs, live.w, [(fw, 1)] * 3, 2 * fw + 512, 2 * fw))
    del live.w, live.rows
    live.g[1] = hop_z(live.g[1], 1)
    v = low_y(z[0])
    w = far_y(v)
    q0 = ((v, w), (hop_x(v), hop_x(w)))
    u, v = low_y(hop_x(z[1])), low_y(z[1])
    q1 = ((v, far_y(v)), (u, far_y(u)))
    live.qo, live.z = [q0, q1], z[2:]
    live.fence()

    near = gather_blocks(jnp.concatenate(live.g[:2], 0))
    v = low_y(live.z[0])
    w = far_y(v)
    q2 = ((v, w), (hop_x(v), hop_x(w)))
    u, v = low_y(hop_x(live.z[1])), low_y(live.z[1])
    q3 = ((v, far_y(v)), (u, far_y(u)))
    one, two = hop_z(live.x_own, 1), hop_z(live.x_own, 2)
    live.x_all = [stack([live.x_own, one, two, hop_z(two, 1)])]
    live.w_qo = listed(live.qo + [q2, q3])
    live.g[2] = hop_z(live.g[2], 2)
    del live.z, live.qo
    live.fence()

    live.x_all = [live.x_all[0], at.hop_c(live.x_all[0])]
    live.first, live.query, kv, live.gain, live.row_ids = project(
        pos, *live.x_all, cosine, sine, live.w_qo, qw, inner
    )
    live.kvs = [kv]
    live.g[4], live.g[5] = hop_z(live.g[4], 2), hop_z(live.g[5], 3)
    live.fence()

    kvs = live.kvs
    for b in at.bits:
        kvs = kvs + [at.hop_y(v, b) for v in kvs]
    if inner > 2:
        kvs = [jnp.concatenate(kvs, 0)]
    live.kvs = kvs
    mixed_a, mixed_b, live.lse, live.mine, live.theirs = attend(
        pos, live.query, kvs, live.row_ids, live.w_qo, inner
    )
    live.mixed = (mixed_a, mixed_b)
    live.g[3] = hop_z(live.g[3], 3)
    live.fence()

    two = [jnp.concatenate([live.g[k], live.g[k + 2]], 1) for k in (2, 3)]
    far = gather_blocks(jnp.concatenate(two, 0))
    del live.g
    live.middle, n_own, live.sum_attn = call(
        after_attn_body,
        [row_f32, row_bf, shape((8, 128), F32)],
        [VM] * 5,
        [VM] * 3,
    )(*at.scatter(live.mine, live.theirs), live.x_own, live.gain)
    live.n_all = at.gather(n_own)
    del live.mine, live.theirs
    live.fence()

    live.w_ff = [near, far]
    out = feed(pos, *live.n_all, live.w_ff, fw, inner)
    live.hidden, live.slope, live.silu, (mine, theirs) = out[:2], out[2:4], out[4:6], out[6:]
    live.d_own, live.layer_own, live.sums = call(
        after_mlp_body,
        [row_bf, row_bf, shape((16, 128), F32)],
        [VM] * 5,
        [VM] * 3,
    )(*at.scatter(mine, theirs), live.middle, live.t_own)
    del live.t_own
    live.d_all = at.gather(live.d_own)
    live.fence()


    out = feed_back(pos, *live.d_all, live.slope, live.silu, live.w_ff, fw, inner)
    live.d_gu, live.mine, live.theirs = out[:2], out[2], out[3]
    del live.slope, live.silu, live.w_ff
    live.fence()

    one, three, keep = first_sum(live.mine, at.hop_c(live.theirs))
    live.left = [keep, one, second_sum(keep, hop_z(three, 1))]
    del live.mine, live.theirs
    live.far = feed_grad(pos, live.n_all, live.d_all, live.d_gu, live.hidden, inner, 1)
    live.fence()

    far = scatter_blocks(live.far)
    keep, one, two = live.left
    live.d_middle, live.a_own, live.grad_gain_two = call(
        after_feed_back_body,
        [row_f32, row_bf, shape((1, full), F32)],
        [VM] * 6,
        [VM] * 3,
    )(keep, hop_z(one, 1), hop_z(two, 2), live.middle, live.d_own, live.gain)
    del live.middle, live.d_own, live.left, live.far
    live.near = feed_grad(pos, live.n_all, live.d_all, live.d_gu, live.hidden, inner, 0)
    del live.n_all, live.d_all, live.d_gu, live.hidden
    live.fence()

    near = scatter_blocks(live.near)
    del live.near
    live.a_all = at.gather(live.a_own)
    del live.a_own
    live.fence()

    live.d_query, live.d_kv, live.sent = attend_back(
        pos, *live.a_all, live.query, live.kvs, live.row_ids, live.lse, cosine, sine, live.w_qo, inner
    )
    del live.query, live.kvs, live.row_ids, live.lse
    live.fence()

    d_kv, sent = live.d_kv, live.sent
    if inner > 2:
        sent = jnp.concatenate([d_kv, sent.astype(F32)], 0)
        for b in reversed(at.bits[1:]):
            n = sent.shape[0] // 2
            sent = sent[:n] + at.hop_y(sent[n:].astype(BF), b).astype(F32)
        d_kv, sent = sent[:rows], sent[rows:].astype(BF)
    sent = at.hop_y(sent, at.bits[0])
    live.d_qkv = split_grads(live.d_query, d_kv, sent, cosine, sine)
    live.mine, live.theirs, live.gain_one = project_back(pos, *live.x_all, live.d_qkv, live.w_qo, inner)
    del live.d_kv, live.sent, live.d_query, live.w_qo, live.x_all
    live.far3 = [far[1][:, : 2 * fw], hop_z(far[1][:, 2 * fw :], 3)]
    live.fence()

    one, three, keep = first_sum(live.mine, at.hop_c(live.theirs))
    live.left = [keep, one, second_sum(keep, hop_z(three, 1))]
    live.grad_qo = pieces(attn_grad(pos, live.first, *live.a_all, live.d_qkv, live.mixed, inner))
    del live.first, live.a_all, live.mixed, live.mine, live.theirs, live.d_qkv
    live.far3[0] = hop_z(live.far3[0], 3)
    live.fence()

    q = live.grad_qo
    live.tails = tail_rows(live.gain_one, live.grad_gain_two, live.sum_attn, live.sums)
    del live.gain_one, live.grad_gain_two, live.sum_attn, live.sums
    keep, one, two = live.left
    (live.input_own,) = call(
        after_all_body,
        [row_bf],
        [VM] * 6,
        [VM],
    )(keep, hop_z(one, 1), hop_z(two, 2), live.x_own, live.d_middle, live.gain)
    del live.left, live.x_own, live.d_middle
    q[3], q[2] = first_y(q[3]), first_x(q[2])
    live.fence()

    q = live.grad_qo
    live.far2 = [hop_z(far[0][:, : 2 * fw], 2), far[0][:, 2 * fw :]]
    q[3], q[2] = at.sum_x(*q[3]), at.sum_y(*q[2])
    q[1], q[0] = first_y(q[1]), first_x(q[0])
    live.input_grad = all_rows(live.input_own)
    del live.input_own
    tails = live.tails + at.hop_c(live.tails)
    live.tails = tails + at.hop_x(tails)
    live.fence()

    q = live.grad_qo
    q[3] = hop_z(q[3], 3)
    live.far2[1] = hop_z(live.far2[1], 2)
    q[1], q[0] = at.sum_x(*q[1]), at.sum_y(*q[0])
    live.near = [near[0], hop_z(near[1], 1)]
    tails = live.tails
    for b in at.bits:
        tails = tails + at.hop_y(tails, b)
    live.tails = tails + at.hop_z(tails, 1)
    live.fence()

    q = live.grad_qo
    q[2], q[1] = hop_z(q[2], 2), hop_z(q[1], 1)
    tails = live.tails + at.hop_z(live.tails, 2)
    layer_out, input_grad = all_rows(live.layer_own), live.input_grad
    live.g = live.near + [live.far2[0], live.far3[0], live.far2[1], live.far3[1]]
    g_gate, g_up, g_down = unpack(at.zs, live.g, [(i * fw, fw, 1) for i in range(3)], 2 * fw)
    takes = [(0, qw, 1), (qw, kw, 2), (qw + kw, kw, 2), (qw + 2 * kw, qw, 1)]
    g_query, g_key, g_value, g_out = unpack(at.zs, q, takes)
    depth = w_query.shape[0]
    own_gains = lax.dynamic_slice_in_dim(tails[:2, :full], at.s * depth, depth, 1)
    entries = inputs.shape[0] * at.count * inputs.shape[1]
    rms = jnp.sqrt(tails[0, full : full + 3] / entries + EPS)
    return (
        layer_out,
        input_grad,
        g_query,
        g_key,
        g_value,
        g_out,
        g_gate,
        g_up,
        g_down,
        own_gains[0],
        own_gains[1],
        rms[0],
        rms[1],
        rms[2],
    )


def solution(mesh):
    devices = mesh.devices.reshape(PARTS, -1, 2, mesh.devices.shape[1] // 2)
    seq, mp = ("z", "y"), ("x", "c")
    rows, single, block = P(seq, None), P(seq), P(seq, mp)
    return jax.shard_map(
        on_device,
        mesh=Mesh(devices, AXES),
        in_specs=(rows, rows, single, single, single, single) + (block,) * 7,
        out_specs=(rows, rows) + (block,) * 7 + (single, single, P(), P(), P()),
        check_vma=False,
    )
```

time: 833 us -> 710 us (0.85)
  waiting for transfers between devices: 455 us -> 317 us
  starting transfers between devices: 153 us -> 133 us
  between operations: 2.56 us -> 15.5 us
  local copies, waits for them, and re-layouts: 29.5 us -> 40.6 us
    ppermute x116 -> x85, waiting for transfers between devices: 455 us -> 313 us  [hop(): return lax.ppermute(value, axis, [(i, i ^ k) for i in range(size)])]
    ppermute x116 -> x85, starting transfers between devices: 153 us -> 133 us  [hop(): return lax.ppermute(value, axis, [(i, i ^ k) for i in range(size)])]
    unnamed x238 -> x182, local copies, waits for them, and re-layouts: 24.5 us -> 31.8 us
    pallas_call x25 -> x26, Pallas kernels: 130 us -> 137 us  [the longest x2 19.1 us: feed_grad(): call(functools.partial(feed_grad_body, inner, pair), shape((inner * 2, wi...]
  transfers between devices with their start and end apart: 116 -> 89, of which waited for: 53 -> 50; matrix products, arithmetic and copies ran while one was open for 2% -> 3% of each run, Pallas kernels for 12% -> 18%
where the time goes in v4:
time: 710 us; the launch traced here: 703 us
  waiting for transfers between devices  317 us (45%)
  Pallas kernels  183 us (26%)
  starting transfers between devices  133 us (19%)
  local copies, waits for them, and re-layouts  40.6 us (6%)
  between operations  15.5 us (2%)
  other arithmetic  13 us (2%)
    ppermute x85, waiting for transfers between devices, hop(): return lax.ppermute(value, axis, [(i, i ^ k) for i in range(size)])  313 us
    ppermute x85, starting transfers between devices, hop(): return lax.ppermute(value, axis, [(i, i ^ k) for i in range(size)])  133 us
    unnamed x182, local copies, waits for them, and re-layouts  31.8 us
    pallas_call x2, Pallas kernels, feed_grad(): call(functools.partial(feed_grad_body, inner, pair), shape((inner * 2, wi...  19.1 us
    pallas_call x1, Pallas kernels, feed_back(): call(functools.partial(feed_back_body, fw, inner), [shape((2 * rows, 2 *...  17 us
    pallas_call x1, Pallas kernels, attend_back(): call(functools.partial(attend_back_body, sides), [shape(q.shape), shape((...  15.9 us
    pallas_call x1, Pallas kernels, feed(): call(functools.partial(feed_body, fw, inner), [shape((2 * rows, 512))] *...  15.8 us
  transfers between devices with their start and end apart: 89, of which 50 were waited for; matrix products, arithmetic and copies ran while one was open for 3% of the time, Pallas kernels for 18%

profile of v4, /device:TPU:0, one launch (start us, length us, event | category | flops | bytes accessed | tf_op | source)
XLA Modules:
  0.0 702.6 jit_solution(14294331067218548742)
XLA Ops:
  16.1 4.7 shard_map.237
  30.0 3.7 collective-permute-start.9
  35.2 15.6 %collective-permute-done.8.refs_4_.refs_6_ = bf16[320,512]{1,0:T(8,128)(2,1)S(1)} collective-permute-done((bf16[320,512]{1,0:T(8,128)(2,1)S(1)}, bf16[320,512]{1,0:T(8,128)(2,1)S(1)}, u32[]{:S(2)}, u32[]{:S(2)}) %collective-permute-start.8) | collective-permute-done | bytes 327712 | tf_op jit(solution)/shard_map/ppermute | solution.py:52
  61.6 3.8 collective-permute-done.7.refs_11_.refs_13_
  71.3 12.2 %collective-permute-done.18.two = bf16[64,2688]{1,0:T(8,128)(2,1)S(1)} collective-permute-done((bf16[64,2688]{1,0:T(8,128)(2,1)S(1)}, bf16[64,2688]{1,0:T(8,128)(2,1)S(1)}, u32[]{:S(2)}, u32[]{:S(2)}) %collective-permute-start.18) | collective-permute-done | bytes 344096 | tf_op jit(solution)/shard_map/ppermute | solution.py:52
  90.1 10.5 %collective-permute-done.11.refs_5_.refs_7_ = bf16[320,512]{1,0:T(8,128)(2,1)S(1)} collective-permute-done((bf16[320,512]{1,0:T(8,128)(2,1)S(1)}, bf16[320,512]{1,0:T(8,128)(2,1)S(1)}, u32[]{:S(2)}, u32[]{:S(2)}) %collective-permute-start.11) | collective-permute-done | bytes 327712 | tf_op jit(solution)/shard_map/ppermute | solution.py:52
  107.3 7.0 collective-permute-done.12.refs_7_.refs_9_
  114.3 7.9 %collective-permute-done.14.refs_13_.refs_15_ = bf16[320,512]{1,0:T(8,128)(2,1)S(1)} collective-permute-done((bf16[320,512]{1,0:T(8,128)(2,1)S(1)}, bf16[320,512]{1,0:T(8,128)(2,1)S(1)}, u32[]{:S(2)}, u32[]{:S(2)}) %collective-permute-start.14) | collective-permute-done | bytes 327712 | tf_op jit(solution)/shard_map/ppermute | solution.py:52
  130.7 9.8 %shard_map.240 = (bf16[512,2560]{1,0:T(8,128)(2,1)}, bf16[512,320]{1,0:T(8,128)(2,1)}, bf16[512,384]{1,0:T(8,128)(2,1)}, f32[8,2560]{1,0:T(8,128)}, f32[8,512]{1,0:T(8,128)}) custom-call(s32[5]{0:T(128)} %stack.40.pos, bf16[256,2688]{1,0:T(8,128)(2,1)} %shard_map.239.x_mine, bf16[256,2688]{1,0:T(8,128)(2,1)} %copy-done.12, ...), custom_call_target="tpu_custom_call" | custom-call | flops 12000000000 | tf_op jit(solution)/shard_map/pallas_call | solution.py:368
  140.6 10.1 %collective-permute-done.21 = bf16[320,512]{1,0:T(8,128)(2,1)S(1)} collective-permute-done((bf16[320,512]{1,0:T(8,128)(2,1)S(1)}, bf16[320,512]{1,0:T(8,128)(2,1)S(1)}, u32[]{:S(2)}, u32[]{:S(2)}) %collective-permute-start.21) | collective-permute-done | bytes 327712 | tf_op jit(solution)/shard_map/ppermute | solution.py:52
  154.3 13.2 %collective-permute-done.24.refs_1_ = bf16[512,384]{1,0:T(8,128)(2,1)S(1)} collective-permute-done((bf16[512,384]{1,0:T(8,128)(2,1)}, bf16[512,384]{1,0:T(8,128)(2,1)S(1)}, u32[]{:S(2)}, u32[]{:S(2)}) %collective-permute-start.24) | collective-permute-done | bytes 393248 | tf_op jit(solution)/shard_map/ppermute | solution.py:52
  168.3 11.4 %shard_map.241 = (bf16[512,512]{1,0:T(8,128)(2,1)}, bf16[512,512]{1,0:T(8,128)(2,1)}, f32[8,512]{1,0:T(8,128)}, f32[256,2560]{1,0:T(8,128)}, bf16[256,2560]{1,0:T(8,128)(2,1)}) custom-call(s32[5]{0:T(128)} %stack.40.pos, bf16[512,320]{1,0:T(8,128)(2,1)} %get-tuple-element.942.q_ref, f32[8,512]{1,0:T(8,128)} %get-tuple-element.943.row_ids, ...), custom_call_target="tpu_custom_call" | custom-call | flops 12000000000 | tf_op jit(solution)/shard_map/pallas_call | solution.py:475
  189.9 14.0 %collective-permute-start.27 = (bf16[64,2560]{1,0:T(8,128)(2,1)}, bf16[64,2560]{1,0:T(8,128)(2,1)S(1)}, u32[]{:S(2)}, u32[]{:S(2)}) collective-permute-start(bf16[64,2560]{1,0:T(8,128)(2,1)} %get-tuple-element.684), channel_id=1, source_target_pairs={{0,8},{8,0},{16,24},{24,16},{1,9},{9,1},{17,25},{25,17},{2,10},{10... | collective-permute-start | bytes 983048 | tf_op jit(solution)/shard_map/ppermute | solution.py:52
  203.9 8.7 %collective-permute-done.27.three = bf16[64,2560]{1,0:T(8,128)(2,1)S(1)} collective-permute-done((bf16[64,2560]{1,0:T(8,128)(2,1)}, bf16[64,2560]{1,0:T(8,128)(2,1)S(1)}, u32[]{:S(2)}, u32[]{:S(2)}) %collective-permute-start.27) | collective-permute-done | bytes 327712 | tf_op jit(solution)/shard_map/ppermute | solution.py:52
  215.4 4.4 collective-permute-start.28
  219.8 13.7 %collective-permute-done.28.two = bf16[64,2560]{1,0:T(8,128)(2,1)S(1)} collective-permute-done((bf16[64,2560]{1,0:T(8,128)(2,1)}, bf16[64,2560]{1,0:T(8,128)(2,1)S(1)}, u32[]{:S(2)}, u32[]{:S(2)}) %collective-permute-start.28) | collective-permute-done | bytes 327712 | tf_op jit(solution)/shard_map/ppermute | solution.py:52
  240.2 12.6 %collective-permute-done.30.two = bf16[64,2560]{1,0:T(8,128)(2,1)S(1)} collective-permute-done((bf16[64,2560]{1,0:T(8,128)(2,1)}, bf16[64,2560]{1,0:T(8,128)(2,1)S(1)}, u32[]{:S(2)}, u32[]{:S(2)}) %collective-permute-start.30) | collective-permute-done | bytes 327712 | tf_op jit(solution)/shard_map/ppermute | solution.py:52
  252.9 8.3 %collective-permute-done.31.three = bf16[64,2560]{1,0:T(8,128)(2,1)S(1)} collective-permute-done((bf16[64,2560]{1,0:T(8,128)(2,1)S(1)}, bf16[64,2560]{1,0:T(8,128)(2,1)S(1)}, u32[]{:S(2)}, u32[]{:S(2)}) %collective-permute-start.31) | collective-permute-done | bytes 327712 | tf_op jit(solution)/shard_map/ppermute | solution.py:52
  267.6 3.7 all-gather.7.cloned.1.call-done
  271.3 15.8 %shard_map.246 = (bf16[512,512]{1,0:T(8,128)(2,1)}, bf16[512,512]{1,0:T(8,128)(2,1)}, bf16[512,512]{1,0:T(8,128)(2,1)}, bf16[512,512]{1,0:T(8,128)(2,1)}, bf16[5...) custom-call(s32[5]{0:T(128)} %stack.40.pos, ...), custom_call_target="tpu_custom_call" | custom-call | flops 17999998976 | tf_op jit(solution)/shard_map/pallas_call | solution.py:529
  296.9 8.7 %collective-permute-done.35.three = bf16[64,2560]{1,0:T(8,128)(2,1)S(1)} collective-permute-done((bf16[64,2560]{1,0:T(8,128)(2,1)}, bf16[64,2560]{1,0:T(8,128)(2,1)S(1)}, u32[]{:S(2)}, u32[]{:S(2)}) %collective-permute-start.35) | collective-permute-done | bytes 327712 | tf_op jit(solution)/shard_map/ppermute | solution.py:52
  311.0 4.0 collective-permute-done.34.one
  314.9 9.9 %collective-permute-done.36.two = bf16[64,2560]{1,0:T(8,128)(2,1)S(1)} collective-permute-done((bf16[64,2560]{1,0:T(8,128)(2,1)}, bf16[64,2560]{1,0:T(8,128)(2,1)S(1)}, u32[]{:S(2)}, u32[]{:S(2)}) %collective-permute-start.36) | collective-permute-done | bytes 327712 | tf_op jit(solution)/shard_map/ppermute | solution.py:52
  328.5 3.8 collective-permute-start.37
  332.4 11.8 %collective-permute-done.38.two = bf16[64,2560]{1,0:T(8,128)(2,1)S(1)} collective-permute-done((bf16[64,2560]{1,0:T(8,128)(2,1)}, bf16[64,2560]{1,0:T(8,128)(2,1)S(1)}, u32[]{:S(2)}, u32[]{:S(2)}) %collective-permute-start.38) | collective-permute-done | bytes 327712 | tf_op jit(solution)/shard_map/ppermute | solution.py:52
  344.3 7.7 %collective-permute-done.39.three = bf16[64,2560]{1,0:T(8,128)(2,1)S(1)} collective-permute-done((bf16[64,2560]{1,0:T(8,128)(2,1)S(1)}, bf16[64,2560]{1,0:T(8,128)(2,1)S(1)}, u32[]{:S(2)}, u32[]{:S(2)}) %collective-permute-start.39) | collective-permute-done | bytes 327712 | tf_op jit(solution)/shard_map/ppermute | solution.py:52
  359.4 17.0 %shard_map.251 = (bf16[512,896]{1,0:T(8,128)(2,1)}, bf16[512,896]{1,0:T(8,128)(2,1)}, f32[256,2560]{1,0:T(8,128)}, bf16[256,2560]{1,0:T(8,128)(2,1)}) custom-call(s32[5]{0:T(128)} %stack.40.pos, bf16[256,2560]{1,0:T(8,128)(2,1)} %shard_map.250.d_mine, bf16[256,2560]{1,0:T(8,128)(2,1)} %copy-done.15, bf16[512,512]{1,0:T(8,128)(2,1)} %get-tuple-element.765.refs_0_, ...), custom_call_target="tpu_custom_call" | custom-call | flops 16000000000 | tf_op jit(solution)/shard_map/pallas_call | solution.py:565
  384.6 9.0 %shard_map.252 = bf16[4,640,1408]{2,1,0:T(8,128)(2,1)} custom-call(s32[5]{0:T(128)} %stack.40.pos, bf16[256,2560]{1,0:T(8,128)(2,1)} %shard_map.245.n_mine, bf16[256,2560]{1,0:T(8,128)(2,1)} %copy-done.13, bf16[256,2560]{1,0:T(8,128)(2,1)} %shard_map.250.d_mine, bf16[256,2560]{1,0:T(8,128)(2,1)} %copy-done.15, bf16[512,896]{1,0:T(8,128)(2,1)} %get-tuple-element.879.refs_0_, ...), custom_call_target="tpu_custom_call" | custom-call | flops 8999999488 | tf_op jit(solution)/shard_map/pallas_call | solution.py:614
  401.3 10.1 %shard_map.256 = bf16[4,640,1408]{2,1,0:T(8,128)(2,1)} custom-call(s32[5]{0:T(128)} %stack.40.pos, bf16[256,2560]{1,0:T(8,128)(2,1)} %shard_map.245.n_mine, bf16[256,2560]{1,0:T(8,128)(2,1)} %copy-done.13, bf16[256,2560]{1,0:T(8,128)(2,1)} %shard_map.250.d_mine, bf16[256,2560]{1,0:T(8,128)(2,1)} %copy-done.15, bf16[512,896]{1,0:T(8,128)(2,1)} %get-tuple-element.879.refs_0_, ...), custom_call_target="tpu_custom_call" | custom-call | flops 8999999488 | tf_op jit(solution)/shard_map/pallas_call | solution.py:614
  415.5 3.6 shard_map.255
  424.7 11.0 %collective-permute-done.47.two = bf16[64,2560]{1,0:T(8,128)(2,1)S(1)} collective-permute-done((bf16[64,2560]{1,0:T(8,128)(2,1)S(1)}, bf16[64,2560]{1,0:T(8,128)(2,1)S(1)}, u32[]{:S(2)}, u32[]{:S(2)}) %collective-permute-start.47) | collective-permute-done | bytes 327712 | tf_op jit(solution)/shard_map/ppermute | solution.py:52
  435.7 7.3 %collective-permute-done.48.three = bf16[64,2560]{1,0:T(8,128)(2,1)S(1)} collective-permute-done((bf16[64,2560]{1,0:T(8,128)(2,1)S(1)}, bf16[64,2560]{1,0:T(8,128)(2,1)S(1)}, u32[]{:S(2)}, u32[]{:S(2)}) %collective-permute-start.48) | collective-permute-done | bytes 327712 | tf_op jit(solution)/shard_map/ppermute | solution.py:52
  450.5 15.9 %shard_map.258 = (bf16[512,320]{1,0:T(8,128)(2,1)}, f32[512,320]{1,0:T(8,128)}, bf16[512,320]{1,0:T(8,128)(2,1)}) custom-call(s32[5]{0:T(128)} %stack.40.pos, bf16[256,2560]{1,0:T(8,128)(2,1)} %shard_map.257.d_mine, bf16[256,2560]{1,0:T(8,128)(2,1)} %copy-done.14, bf16[512,320]{1,0:T(8,128)(2,1)} %get-tuple-element.942.q_ref, ...), custom_call_target="tpu_custom_call" | custom-call | flops 17999998976 | tf_op jit(solution)/shard_map/pallas_call | solution.py:699
  468.0 12.8 %collective-permute-done.50.got_ref = bf16[512,320]{1,0:T(8,128)(2,1)S(1)} collective-permute-done((bf16[512,320]{1,0:T(8,128)(2,1)}, bf16[512,320]{1,0:T(8,128)(2,1)S(1)}, u32[]{:S(2)}, u32[]{:S(2)}) %collective-permute-start.50) | collective-permute-done | bytes 327712 | tf_op jit(solution)/shard_map/ppermute | solution.py:52
  489.6 9.5 %shard_map.260 = (f32[256,2560]{1,0:T(8,128)}, bf16[256,2560]{1,0:T(8,128)(2,1)}, f32[8,2560]{1,0:T(8,128)}) custom-call(s32[5]{0:T(128)} %stack.40.pos, bf16[256,2688]{1,0:T(8,128)(2,1)} %shard_map.239.x_mine, bf16[256,2688]{1,0:T(8,128)(2,1)} %copy-done.12, bf16[512,512]{1,0:T(8,128)(2,1)} %get-tuple-element.1025.d_a.refs_0_, ...), custom_call_target="tpu_custom_call" | custom-call | flops 10000000000 | tf_op jit(solution)/shard_map/pallas_call | solution.py:753
  508.4 4.3 collective-permute-start.54
  512.6 9.8 %shard_map.261 = (bf16[320,512]{1,0:T(8,128)(2,1)}, bf16[320,512]{1,0:T(8,128)(2,1)}, bf16[320,512]{1,0:T(8,128)(2,1)}, bf16[320,512]{1,0:T(8,128)(2,1)}, bf16[3...) custom-call(s32[5]{0:T(128)} %stack.40.pos, ...), custom_call_target="tpu_custom_call" | custom-call | flops 10000000000 | tf_op jit(solution)/shard_map/pallas_call | solution.py:786
  537.3 5.4 collective-permute-done.55
  544.8 11.3 %collective-permute-done.56 = bf16[320,512]{1,0:T(8,128)(2,1)S(1)} collective-permute-done((bf16[320,512]{1,0:T(8,128)(2,1)}, bf16[320,512]{1,0:T(8,128)(2,1)S(1)}, u32[]{:S(2)}, u32[]{:S(2)}) %collective-permute-start.56) | collective-permute-done | bytes 327712 | tf_op jit(solution)/shard_map/ppermute | solution.py:52
  574.0 10.5 %collective-permute-done.71 = f32[8,2688]{1,0:T(8,128)S(1)} collective-permute-done((f32[8,2688]{1,0:T(8,128)S(1)}, f32[8,2688]{1,0:T(8,128)S(1)}, u32[]{:S(2)}, u32[]{:S(2)}) %collective-permute-start.71) | collective-permute-done | bytes 86048 | tf_op jit(solution)/shard_map/ppermute | solution.py:52
  589.6 5.8 collective-permute-done.63
  597.2 5.1 collective-permute-done.64
  615.9 9.6 %collective-permute-done.77 = f32[8,2688]{1,0:T(8,128)S(1)} collective-permute-done((f32[8,2688]{1,0:T(8,128)S(1)}, f32[8,2688]{1,0:T(8,128)S(1)}, u32[]{:S(2)}, u32[]{:S(2)}) %collective-permute-start.77) | collective-permute-done | bytes 86048 | tf_op jit(solution)/shard_map/ppermute | solution.py:52
  631.9 3.6 collective-permute-start.75
  637.7 15.9 %collective-permute-done.72.refs_4_ = bf16[320,512]{1,0:T(8,128)(2,1)S(1)} collective-permute-done((bf16[320,512]{1,0:T(8,128)(2,1)S(1)}, bf16[320,512]{1,0:T(8,128)(2,1)S(1)}, u32[]{:S(2)}, u32[]{:S(2)}) %collective-permute-start.72) | collective-permute-done | bytes 327712 | tf_op jit(solution)/shard_map/ppermute | solution.py:52
  654.4 6.2 collective-permute-start.82
  663.5 5.8 shard_map.269
  669.3 12.5 %collective-permute-done.84 = f32[8,2688]{1,0:T(8,128)S(1)} collective-permute-done((f32[8,2688]{1,0:T(8,128)S(1)}, f32[8,2688]{1,0:T(8,128)S(1)}, u32[]{:S(2)}, u32[]{:S(2)}) %collective-permute-start.84) | collective-permute-done | bytes 86048 | tf_op jit(solution)/shard_map/ppermute | solution.py:52
  (384 shorter events, 248.5 us)
Async XLA Ops:
  7.2 260.4 %all-gather.5.cloned.1.call-start = ((), (), s32[]{:S(2)}) async-start(), calls=%async_computation.4 | async-start | bytes 9011200 | tf_op jit(solution)/shard_map/all_gather | solution.py:942
  20.8 40.8 %collective-permute-start = (bf16[320,1408]{1,0:T(8,128)(2,1)}, bf16[320,1408]{1,0:T(8,128)(2,1)S(1)}, u32[]{:S(2)}, u32[]{:S(2)}) collective-permute-start(bf16[320,1408]{1,0:T(8,128)(2,1)} %get-tuple-element.582), channel_id=1, source_target_pairs={{0,8},{8,0},{16,24},{24,16},{1,9},{9,1},{17,25},{25,17},{2,10},{10... | collective-permute-start | bytes 2703368 | tf_op jit(solution)/shard_map/ppermute | solution.py:52
  24.3 26.5 %collective-permute-start.8 = (bf16[320,512]{1,0:T(8,128)(2,1)S(1)}, bf16[320,512]{1,0:T(8,128)(2,1)S(1)}, u32[]{:S(2)}, u32[]{:S(2)}) collective-permute-start(bf16[320,512]{1,0:T(8,128)(2,1)S(1)} %copy-done.60), channel_id=1, source_target_pairs={{0,16},{8,24},{16,0},{24,8},{1,17},{9,25},{17,1},{25,9},{2,18},{10... | collective-permute-start | bytes 983048 | tf_op jit(solution)/shard_map/ppermute | solution.py:52
  26.8 25.5 %collective-permute-start.6 = (bf16[320,512]{1,0:T(8,128)(2,1)S(1)}, bf16[320,512]{1,0:T(8,128)(2,1)S(1)}, u32[]{:S(2)}, u32[]{:S(2)}) collective-permute-start(bf16[320,512]{1,0:T(8,128)(2,1)S(1)} %collective-permute-done.4.refs_2_.refs_4_), channel_id=1, source_target_pairs={{0,2},{2,0},{1,3},{3,1},{4,6},{6,4},{5,7},{7,5},{8,10},{10,8},{9,1... | collective-permute-start | bytes 983048 | tf_op jit(solution)/shard_map/ppermute | solution.py:52
  30.0 29.5 %collective-permute-start.9 = (bf16[320,512]{1,0:T(8,128)(2,1)}, bf16[320,512]{1,0:T(8,128)(2,1)S(1)}, u32[]{:S(2)}, u32[]{:S(2)}) collective-permute-start(bf16[320,512]{1,0:T(8,128)(2,1)} %get-tuple-element.594), channel_id=1, source_target_pairs={{0,24},{8,16},{16,8},{24,0},{1,25},{9,17},{17,9},{25,1},{2,26},{10... | collective-permute-start | bytes 983048 | tf_op jit(solution)/shard_map/ppermute | solution.py:52
  33.7 25.9 %collective-permute-start.3 = (bf16[320,512]{1,0:T(8,128)(2,1)S(1)}, bf16[320,512]{1,0:T(8,128)(2,1)S(1)}, u32[]{:S(2)}, u32[]{:S(2)}) collective-permute-start(bf16[320,512]{1,0:T(8,128)(2,1)S(1)} %collective-permute-done.1.refs_1_.refs_3_), channel_id=1, source_target_pairs={{0,2},{2,0},{1,3},{3,1},{4,6},{6,4},{5,7},{7,5},{8,10},{10,8},{9,1... | collective-permute-start | bytes 983048 | tf_op jit(solution)/shard_map/ppermute | solution.py:52
  66.8 204.5 %all-gather.7.cloned.1.call-start = ((), (), s32[]{:S(2)}) async-start(), calls=%async_computation.5 | async-start | bytes 9011200 | tf_op jit(solution)/shard_map/all_gather | solution.py:942
  71.1 32.5 %collective-permute-start.17 = (bf16[64,2688]{1,0:T(8,128)(2,1)S(1)}, bf16[64,2688]{1,0:T(8,128)(2,1)S(1)}, u32[]{:S(2)}, u32[]{:S(2)}) collective-permute-start(bf16[64,2688]{1,0:T(8,128)(2,1)S(1)} %copy-done.27), channel_id=1, source_target_pairs={{0,8},{8,0},{16,24},{24,16},{1,9},{9,1},{17,25},{25,17},{2,10},{10... | collective-permute-start | bytes 1032200 | tf_op jit(solution)/shard_map/ppermute | solution.py:52
  83.6 20.5 %collective-permute-start.19 = (bf16[64,2688]{1,0:T(8,128)(2,1)S(1)}, bf16[64,2688]{1,0:T(8,128)(2,1)S(1)}, u32[]{:S(2)}, u32[]{:S(2)}) collective-permute-start(bf16[64,2688]{1,0:T(8,128)(2,1)S(1)} %collective-permute-done.18.two), channel_id=1, source_target_pairs={{0,8},{8,0},{16,24},{24,16},{1,9},{9,1},{17,25},{25,17},{2,10},{10... | collective-permute-start | bytes 1032200 | tf_op jit(solution)/shard_map/ppermute | solution.py:52
  83.6 16.9 %collective-permute-start.11 = (bf16[320,512]{1,0:T(8,128)(2,1)S(1)}, bf16[320,512]{1,0:T(8,128)(2,1)S(1)}, u32[]{:S(2)}, u32[]{:S(2)}) collective-permute-start(bf16[320,512]{1,0:T(8,128)(2,1)S(1)} %copy-done.36), channel_id=1, source_target_pairs={{0,4},{4,0},{1,5},{5,1},{2,6},{6,2},{3,7},{7,3},{8,12},{12,8},{9,1... | collective-permute-start | bytes 983048 | tf_op jit(solution)/shard_map/ppermute | solution.py:52
  85.2 16.9 %collective-permute-start.15 = (bf16[320,512]{1,0:T(8,128)(2,1)S(1)}, bf16[320,512]{1,0:T(8,128)(2,1)S(1)}, u32[]{:S(2)}, u32[]{:S(2)}) collective-permute-start(bf16[320,512]{1,0:T(8,128)(2,1)S(1)} %copy-done.39), channel_id=1, source_target_pairs={{0,2},{2,0},{1,3},{3,1},{4,6},{6,4},{5,7},{7,5},{8,10},{10,8},{9,1... | collective-permute-start | bytes 983048 | tf_op jit(solution)/shard_map/ppermute | solution.py:52
  86.7 27.7 %collective-permute-start.10 = (bf16[320,896]{1,0:T(8,128)(2,1)S(1)}, bf16[320,896]{1,0:T(8,128)(2,1)S(1)}, u32[]{:S(2)}, u32[]{:S(2)}) collective-permute-start(bf16[320,896]{1,0:T(8,128)(2,1)S(1)} %copy-done.24), channel_id=1, source_target_pairs={{0,16},{8,24},{16,0},{24,8},{1,17},{9,25},{17,1},{25,9},{2,18},{10... | collective-permute-start | bytes 1720328 | tf_op jit(solution)/shard_map/ppermute | solution.py:52
  103.6 18.6 %collective-permute-start.14 = (bf16[320,512]{1,0:T(8,128)(2,1)S(1)}, bf16[320,512]{1,0:T(8,128)(2,1)S(1)}, u32[]{:S(2)}, u32[]{:S(2)}) collective-permute-start(bf16[320,512]{1,0:T(8,128)(2,1)S(1)} %collective-permute-done.11.refs_5_.refs_7_), channel_id=1, source_target_pairs={{0,2},{2,0},{1,3},{3,1},{4,6},{6,4},{5,7},{7,5},{8,10},{10,8},{9,1... | collective-permute-start | bytes 983048 | tf_op jit(solution)/shard_map/ppermute | solution.py:52
  104.1 19.0 %collective-permute-start.16 = (bf16[320,512]{1,0:T(8,128)(2,1)S(1)}, bf16[320,512]{1,0:T(8,128)(2,1)S(1)}, u32[]{:S(2)}, u32[]{:S(2)}) collective-permute-start(bf16[320,512]{1,0:T(8,128)(2,1)S(1)} %collective-permute-done.15.refs_14_.refs_16_), channel_id=1, source_target_pairs={{0,4},{4,0},{1,5},{5,1},{2,6},{6,2},{3,7},{7,3},{8,12},{12,8},{9,1... | collective-permute-start | bytes 983048 | tf_op jit(solution)/shard_map/ppermute | solution.py:52
  125.2 25.4 %collective-permute-start.21 = (bf16[320,512]{1,0:T(8,128)(2,1)S(1)}, bf16[320,512]{1,0:T(8,128)(2,1)S(1)}, u32[]{:S(2)}, u32[]{:S(2)}) collective-permute-start(bf16[320,512]{1,0:T(8,128)(2,1)S(1)} %copy-done.49), channel_id=1, source_target_pairs={{0,16},{8,24},{16,0},{24,8},{1,17},{9,25},{17,1},{25,9},{2,18},{10... | collective-permute-start | bytes 983048 | tf_op jit(solution)/shard_map/ppermute | solution.py:52
  127.6 23.0 %collective-permute-start.22 = (bf16[320,512]{1,0:T(8,128)(2,1)S(1)}, bf16[320,512]{1,0:T(8,128)(2,1)S(1)}, u32[]{:S(2)}, u32[]{:S(2)}) collective-permute-start(bf16[320,512]{1,0:T(8,128)(2,1)S(1)} %copy-done.48), channel_id=1, source_target_pairs={{0,24},{8,16},{16,8},{24,0},{1,25},{9,17},{17,9},{25,1},{2,26},{10... | collective-permute-start | bytes 983048 | tf_op jit(solution)/shard_map/ppermute | solution.py:52
  150.7 16.8 %collective-permute-start.24 = (bf16[512,384]{1,0:T(8,128)(2,1)}, bf16[512,384]{1,0:T(8,128)(2,1)S(1)}, u32[]{:S(2)}, u32[]{:S(2)}) collective-permute-start(bf16[512,384]{1,0:T(8,128)(2,1)} %get-tuple-element.945.refs_0_), channel_id=1, source_target_pairs={{0,4},{4,0},{1,5},{5,1},{2,6},{6,2},{3,7},{7,3},{8,12},{12,8},{9,1... | collective-permute-start | bytes 1179656 | tf_op jit(solution)/shard_map/ppermute | solution.py:52
  151.3 28.4 %collective-permute-start.23 = (bf16[320,896]{1,0:T(8,128)(2,1)S(1)}, bf16[320,896]{1,0:T(8,128)(2,1)S(1)}, u32[]{:S(2)}, u32[]{:S(2)}) collective-permute-start(bf16[320,896]{1,0:T(8,128)(2,1)S(1)} %copy-done.23), channel_id=1, source_target_pairs={{0,24},{8,16},{16,8},{24,0},{1,25},{9,17},{17,9},{25,1},{2,26},{10... | collective-permute-start | bytes 1720328 | tf_op jit(solution)/shard_map/ppermute | solution.py:52
  181.1 304.0 %reduce-scatter.3.cloned.1.call-start = ((), (), s32[]{:S(2)}) async-start(), calls=%async_computation.2 | async-start | bytes 9011200 | tf_op jit(solution)/shard_map/reduce_scatter | solution.py:946
  189.9 22.7 %collective-permute-start.27 = (bf16[64,2560]{1,0:T(8,128)(2,1)}, bf16[64,2560]{1,0:T(8,128)(2,1)S(1)}, u32[]{:S(2)}, u32[]{:S(2)}) collective-permute-start(bf16[64,2560]{1,0:T(8,128)(2,1)} %get-tuple-element.684), channel_id=1, source_target_pairs={{0,8},{8,0},{16,24},{24,16},{1,9},{9,1},{17,25},{25,17},{2,10},{10... | collective-permute-start | bytes 983048 | tf_op jit(solution)/shard_map/ppermute | solution.py:52
  203.8 15.9 %collective-permute-start.26 = (bf16[64,2560]{1,0:T(8,128)(2,1)}, bf16[64,2560]{1,0:T(8,128)(2,1)S(1)}, u32[]{:S(2)}, u32[]{:S(2)}) collective-permute-start(bf16[64,2560]{1,0:T(8,128)(2,1)} %get-tuple-element.683), channel_id=1, source_target_pairs={{0,8},{8,0},{16,24},{24,16},{1,9},{9,1},{17,25},{25,17},{2,10},{10... | collective-permute-start | bytes 983048 | tf_op jit(solution)/shard_map/ppermute | solution.py:52
  215.4 18.0 %collective-permute-start.28 = (bf16[64,2560]{1,0:T(8,128)(2,1)}, bf16[64,2560]{1,0:T(8,128)(2,1)S(1)}, u32[]{:S(2)}, u32[]{:S(2)}) collective-permute-start(bf16[64,2560]{1,0:T(8,128)(2,1)} %shard_map.243), channel_id=1, source_target_pairs={{0,16},{8,24},{16,0},{24,8},{1,17},{9,25},{17,1},{25,9},{2,18},{10... | collective-permute-start | bytes 983048 | tf_op jit(solution)/shard_map/ppermute | solution.py:52
  237.0 15.9 %collective-permute-start.29 = (bf16[64,2560]{1,0:T(8,128)(2,1)}, bf16[64,2560]{1,0:T(8,128)(2,1)S(1)}, u32[]{:S(2)}, u32[]{:S(2)}) collective-permute-start(bf16[64,2560]{1,0:T(8,128)(2,1)} %get-tuple-element.689.own), channel_id=1, source_target_pairs={{0,8},{8,0},{16,24},{24,16},{1,9},{9,1},{17,25},{25,17},{2,10},{10... | collective-permute-start | bytes 983048 | tf_op jit(solution)/shard_map/ppermute | solution.py:52
  296.4 18.5 %collective-permute-start.34 = (bf16[64,2560]{1,0:T(8,128)(2,1)}, bf16[64,2560]{1,0:T(8,128)(2,1)S(1)}, u32[]{:S(2)}, u32[]{:S(2)}) collective-permute-start(bf16[64,2560]{1,0:T(8,128)(2,1)} %get-tuple-element.721), channel_id=1, source_target_pairs={{0,8},{8,0},{16,24},{24,16},{1,9},{9,1},{17,25},{25,17},{2,10},{10... | collective-permute-start | bytes 983048 | tf_op jit(solution)/shard_map/ppermute | solution.py:52
  308.6 16.3 %collective-permute-start.36 = (bf16[64,2560]{1,0:T(8,128)(2,1)}, bf16[64,2560]{1,0:T(8,128)(2,1)S(1)}, u32[]{:S(2)}, u32[]{:S(2)}) collective-permute-start(bf16[64,2560]{1,0:T(8,128)(2,1)} %shard_map.248), channel_id=1, source_target_pairs={{0,16},{8,24},{16,0},{24,8},{1,17},{9,25},{17,1},{25,9},{2,18},{10... | collective-permute-start | bytes 983048 | tf_op jit(solution)/shard_map/ppermute | solution.py:52
  397.1 172.3 %reduce-scatter.5.cloned.1.call-start = ((), (), s32[]{:S(2)}) async-start(), calls=%async_computation.3 | async-start | bytes 9011200 | tf_op jit(solution)/shard_map/reduce_scatter | solution.py:946
  398.1 15.9 %collective-permute-start.44 = (bf16[64,2560]{1,0:T(8,128)(2,1)S(1)}, bf16[64,2560]{1,0:T(8,128)(2,1)S(1)}, u32[]{:S(2)}, u32[]{:S(2)}) collective-permute-start(bf16[64,2560]{1,0:T(8,128)(2,1)S(1)} %copy-done.62), channel_id=1, source_target_pairs={{0,8},{8,0},{16,24},{24,16},{1,9},{9,1},{17,25},{25,17},{2,10},{10... | collective-permute-start | bytes 983048 | tf_op jit(solution)/shard_map/ppermute | solution.py:52
  500.8 27.3 %collective-permute-start.52 = (bf16[320,896]{1,0:T(8,128)(2,1)S(1)}, bf16[320,896]{1,0:T(8,128)(2,1)S(1)}, u32[]{:S(2)}, u32[]{:S(2)}) collective-permute-start(bf16[320,896]{1,0:T(8,128)(2,1)S(1)} %get-tuple-element.1017), channel_id=1, source_target_pairs={{0,24},{8,16},{16,8},{24,0},{1,25},{9,17},{17,9},{25,1},{2,26},{10... | collective-permute-start | bytes 1720328 | tf_op jit(solution)/shard_map/ppermute | solution.py:52
  508.4 16.8 %collective-permute-start.54 = (bf16[64,2560]{1,0:T(8,128)(2,1)}, bf16[64,2560]{1,0:T(8,128)(2,1)S(1)}, u32[]{:S(2)}, u32[]{:S(2)}) collective-permute-start(bf16[64,2560]{1,0:T(8,128)(2,1)} %get-tuple-element.1050), channel_id=1, source_target_pairs={{0,8},{8,0},{16,24},{24,16},{1,9},{9,1},{17,25},{25,17},{2,10},{10... | collective-permute-start | bytes 983048 | tf_op jit(solution)/shard_map/ppermute | solution.py:52
  530.3 25.8 %collective-permute-start.56 = (bf16[320,512]{1,0:T(8,128)(2,1)}, bf16[320,512]{1,0:T(8,128)(2,1)S(1)}, u32[]{:S(2)}, u32[]{:S(2)}) collective-permute-start(bf16[320,512]{1,0:T(8,128)(2,1)} %get-tuple-element.1068), channel_id=1, source_target_pairs={{0,2},{2,0},{1,3},{3,1},{4,6},{6,4},{5,7},{7,5},{8,10},{10,8},{9,1... | collective-permute-start | bytes 983048 | tf_op jit(solution)/shard_map/ppermute | solution.py:52
  530.9 30.7 %collective-permute-start.57 = (bf16[320,512]{1,0:T(8,128)(2,1)}, bf16[320,512]{1,0:T(8,128)(2,1)S(1)}, u32[]{:S(2)}, u32[]{:S(2)}) collective-permute-start(bf16[320,512]{1,0:T(8,128)(2,1)} %get-tuple-element.1070), channel_id=1, source_target_pairs={{0,4},{4,0},{1,5},{5,1},{2,6},{6,2},{3,7},{7,3},{8,12},{12,8},{9,1... | collective-permute-start | bytes 983048 | tf_op jit(solution)/shard_map/ppermute | solution.py:52
  531.2 30.5 %collective-permute-start.58 = (bf16[320,512]{1,0:T(8,128)(2,1)S(1)}, bf16[320,512]{1,0:T(8,128)(2,1)S(1)}, u32[]{:S(2)}, u32[]{:S(2)}) collective-permute-start(bf16[320,512]{1,0:T(8,128)(2,1)S(1)} %copy-done.51), channel_id=1, source_target_pairs={{0,4},{4,0},{1,5},{5,1},{2,6},{6,2},{3,7},{7,3},{8,12},{12,8},{9,1... | collective-permute-start | bytes 983048 | tf_op jit(solution)/shard_map/ppermute | solution.py:52
  532.9 24.0 %collective-permute-start.59 = (bf16[64,2560]{1,0:T(8,128)(2,1)}, bf16[64,2560]{1,0:T(8,128)(2,1)S(1)}, u32[]{:S(2)}, u32[]{:S(2)}) collective-permute-start(bf16[64,2560]{1,0:T(8,128)(2,1)} %get-tuple-element.1074), channel_id=1, source_target_pairs={{0,8},{8,0},{16,24},{24,16},{1,9},{9,1},{17,25},{25,17},{2,10},{10... | collective-permute-start | bytes 983048 | tf_op jit(solution)/shard_map/ppermute | solution.py:52
  563.1 50.7 %collective-permute-start.43 = (bf16[320,896]{1,0:T(8,128)(2,1)S(1)}, bf16[320,896]{1,0:T(8,128)(2,1)}, u32[]{:S(2)}, u32[]{:S(2)}) collective-permute-start(bf16[320,896]{1,0:T(8,128)(2,1)S(1)} %get-tuple-element.1155), channel_id=1, source_target_pairs={{0,16},{8,24},{16,0},{24,8},{1,17},{9,25},{17,1},{25,9},{2,18},{10... | collective-permute-start | bytes 1720328 | tf_op jit(solution)/shard_map/ppermute | solution.py:52
  564.9 19.6 %collective-permute-start.61 = (bf16[320,512]{1,0:T(8,128)(2,1)}, bf16[320,512]{1,0:T(8,128)(2,1)}, u32[]{:S(2)}, u32[]{:S(2)}) collective-permute-start(bf16[320,512]{1,0:T(8,128)(2,1)} %get-tuple-element.1086), channel_id=1, source_target_pairs={{0,2},{2,0},{1,3},{3,1},{4,6},{6,4},{5,7},{7,5},{8,10},{10,8},{9,1... | collective-permute-start | bytes 983048 | tf_op jit(solution)/shard_map/ppermute | solution.py:52
  567.3 20.4 %collective-permute-start.62 = (bf16[320,512]{1,0:T(8,128)(2,1)}, bf16[320,512]{1,0:T(8,128)(2,1)}, u32[]{:S(2)}, u32[]{:S(2)}) collective-permute-start(bf16[320,512]{1,0:T(8,128)(2,1)} %get-tuple-element.1088), channel_id=1, source_target_pairs={{0,2},{2,0},{1,3},{3,1},{4,6},{6,4},{5,7},{7,5},{8,10},{10,8},{9,1... | collective-permute-start | bytes 983048 | tf_op jit(solution)/shard_map/ppermute | solution.py:52
  567.4 17.1 %collective-permute-start.71 = (f32[8,2688]{1,0:T(8,128)S(1)}, f32[8,2688]{1,0:T(8,128)S(1)}, u32[]{:S(2)}, u32[]{:S(2)}) collective-permute-start(f32[8,2688]{1,0:T(8,128)S(1)} %add.150), channel_id=1, source_target_pairs={{0,2},{2,0},{1,3},{3,1},{4,6},{6,4},{5,7},{7,5},{8,10},{10,8},{9,1... | collective-permute-start | bytes 258056 | tf_op jit(solution)/shard_map/ppermute | solution.py:52
  572.0 65.7 %collective-permute-start.76 = (bf16[320,1408]{1,0:T(8,128)(2,1)S(1)}, bf16[320,1408]{1,0:T(8,128)(2,1)}, u32[]{:S(2)}, u32[]{:S(2)}) collective-permute-start(bf16[320,1408]{1,0:T(8,128)(2,1)S(1)} %get-tuple-element.1150), channel_id=1, source_target_pairs={{0,8},{8,0},{16,24},{24,16},{1,9},{9,1},{17,25},{25,17},{2,10},{10... | collective-permute-start | bytes 2703368 | tf_op jit(solution)/shard_map/ppermute | solution.py:52
  584.5 17.8 %collective-permute-start.64 = (bf16[320,512]{1,0:T(8,128)(2,1)}, bf16[320,512]{1,0:T(8,128)(2,1)S(1)}, u32[]{:S(2)}, u32[]{:S(2)}) collective-permute-start(bf16[320,512]{1,0:T(8,128)(2,1)} %get-tuple-element.1092), channel_id=1, source_target_pairs={{0,4},{4,0},{1,5},{5,1},{2,6},{6,2},{3,7},{7,3},{8,12},{12,8},{9,1... | collective-permute-start | bytes 983048 | tf_op jit(solution)/shard_map/ppermute | solution.py:52
  587.7 20.5 %collective-permute-start.65 = (bf16[320,512]{1,0:T(8,128)(2,1)}, bf16[320,512]{1,0:T(8,128)(2,1)S(1)}, u32[]{:S(2)}, u32[]{:S(2)}) collective-permute-start(bf16[320,512]{1,0:T(8,128)(2,1)} %add_convert_fusion.10), channel_id=1, source_target_pairs={{0,4},{4,0},{1,5},{5,1},{2,6},{6,2},{3,7},{7,3},{8,12},{12,8},{9,1... | collective-permute-start | bytes 983048 | tf_op jit(solution)/shard_map/ppermute | solution.py:52
  613.8 21.7 %collective-permute-start.73 = (bf16[320,512]{1,0:T(8,128)(2,1)}, bf16[320,512]{1,0:T(8,128)(2,1)S(1)}, u32[]{:S(2)}, u32[]{:S(2)}) collective-permute-start(bf16[320,512]{1,0:T(8,128)(2,1)} %add_convert_fusion.6), channel_id=1, source_target_pairs={{0,4},{4,0},{1,5},{5,1},{2,6},{6,2},{3,7},{7,3},{8,12},{12,8},{9,1... | collective-permute-start | bytes 983048 | tf_op jit(solution)/shard_map/ppermute | solution.py:52
  629.6 24.0 %collective-permute-start.72 = (bf16[320,512]{1,0:T(8,128)(2,1)S(1)}, bf16[320,512]{1,0:T(8,128)(2,1)S(1)}, u32[]{:S(2)}, u32[]{:S(2)}) collective-permute-start(bf16[320,512]{1,0:T(8,128)(2,1)S(1)} %get-tuple-element.1101), channel_id=1, source_target_pairs={{0,16},{8,24},{16,0},{24,8},{1,17},{9,25},{17,1},{25,9},{2,18},{10... | collective-permute-start | bytes 983048 | tf_op jit(solution)/shard_map/ppermute | solution.py:52
  631.9 21.7 %collective-permute-start.75 = (bf16[320,512]{1,0:T(8,128)(2,1)S(1)}, bf16[320,512]{1,0:T(8,128)(2,1)S(1)}, u32[]{:S(2)}, u32[]{:S(2)}) collective-permute-start(bf16[320,512]{1,0:T(8,128)(2,1)S(1)} %add_convert_fusion.2), channel_id=1, source_target_pairs={{0,24},{8,16},{16,8},{24,0},{1,25},{9,17},{17,9},{25,1},{2,26},{10... | collective-permute-start | bytes 983048 | tf_op jit(solution)/shard_map/ppermute | solution.py:52
  653.6 38.2 %collective-permute-start.79 = (bf16[64,2560]{1,0:T(8,128)(2,1)}, bf16[64,2560]{1,0:T(8,128)(2,1)S(1)}, u32[]{:S(2)}, u32[]{:S(2)}) collective-permute-start(bf16[64,2560]{1,0:T(8,128)(2,1)} %get-tuple-element.1114.p0), channel_id=1, source_target_pairs={{0,1},{1,0},{2,3},{3,2},{4,5},{5,4},{6,7},{7,6},{8,9},{9,8},{10,11... | collective-permute-start | bytes 983048 | tf_op jit(solution)/shard_map/ppermute | solution.py:52
  653.7 29.5 %collective-permute-start.80 = (bf16[64,2560]{1,0:T(8,128)(2,1)}, bf16[64,2560]{1,0:T(8,128)(2,1)S(1)}, u32[]{:S(2)}, u32[]{:S(2)}) collective-permute-start(bf16[64,2560]{1,0:T(8,128)(2,1)} %get-tuple-element.1114.p0), channel_id=1, source_target_pairs={{0,2},{2,0},{1,3},{3,1},{4,6},{6,4},{5,7},{7,5},{8,10},{10,8},{9,1... | collective-permute-start | bytes 983048 | tf_op jit(solution)/shard_map/ppermute | solution.py:52
  654.4 28.7 %collective-permute-start.82 = (bf16[320,512]{1,0:T(8,128)(2,1)S(1)}, bf16[320,512]{1,0:T(8,128)(2,1)S(1)}, u32[]{:S(2)}, u32[]{:S(2)}) collective-permute-start(bf16[320,512]{1,0:T(8,128)(2,1)S(1)} %add_convert_fusion), channel_id=1, source_target_pairs={{0,8},{8,0},{16,24},{24,16},{1,9},{9,1},{17,25},{25,17},{2,10},{10... | collective-permute-start | bytes 983048 | tf_op jit(solution)/shard_map/ppermute | solution.py:52
  660.6 22.6 %collective-permute-start.83 = (bf16[320,512]{1,0:T(8,128)(2,1)S(1)}, bf16[320,512]{1,0:T(8,128)(2,1)S(1)}, u32[]{:S(2)}, u32[]{:S(2)}) collective-permute-start(bf16[320,512]{1,0:T(8,128)(2,1)S(1)} %add_convert_fusion.3), channel_id=1, source_target_pairs={{0,16},{8,24},{16,0},{24,8},{1,17},{9,25},{17,1},{25,9},{2,18},{10... | collective-permute-start | bytes 983048 | tf_op jit(solution)/shard_map/ppermute | solution.py:52
  661.6 20.2 %collective-permute-start.84 = (f32[8,2688]{1,0:T(8,128)S(1)}, f32[8,2688]{1,0:T(8,128)S(1)}, u32[]{:S(2)}, u32[]{:S(2)}) collective-permute-start(f32[8,2688]{1,0:T(8,128)S(1)} %add.155), channel_id=1, source_target_pairs={{0,16},{8,24},{16,0},{24,8},{1,17},{9,25},{17,1},{25,9},{2,18},{10... | collective-permute-start | bytes 258056 | tf_op jit(solution)/shard_map/ppermute | solution.py:52
  (131 other events, 1257.4 us)
Sparse Core Ops, SparseCore 0:
  66.9 98.2 all-gather.4
  181.2 90.0 all-gather.6
  397.3 79.8 reduce-scatter.2
  480.1 88.4 reduce-scatter.4

commit v5 on v4

v5 whole, which is shorter than its diff:
```python
import functools

import jax
import jax.numpy as jnp
from jax import lax
from jax.experimental import pallas as pl
from jax.experimental.pallas import tpu as pltpu
from jax.sharding import Mesh
from jax.sharding import PartitionSpec as P

HEAD_DIM = 80
SPAN = 128
EPS = 1e-05
THETA = 1000000.0
PARTS = 4
BF = jnp.bfloat16
F32 = jnp.float32
FACTOR = HEAD_DIM**-0.5
LOG2E = 1.4426950408889634
LIMIT = 56 * 1024 * 1024

PLAIN = (((1,), (0,)), ((), ()))
LAST = (((1,), (1,)), ((), ()))
ROWS = (((0,), (0,)), ((), ()))

VM = pl.BlockSpec(memory_space=pltpu.VMEM)
SM = pl.BlockSpec(memory_space=pltpu.SMEM)
ANY = pl.BlockSpec(memory_space=pl.ANY)


def shape(dims, kind=BF):
    return jax.ShapeDtypeStruct(tuple(dims), kind)


def call(body, outs, in_specs, out_specs, scratch=(), cost=2):
    return pl.pallas_call(
        body,
        out_shape=outs,
        in_specs=in_specs,
        out_specs=out_specs,
        scratch_shapes=list(scratch),
        compiler_params=pltpu.CompilerParams(vmem_limit_bytes=LIMIT),
        cost_estimate=pl.CostEstimate(flops=cost * 10**9, bytes_accessed=0, transcendentals=0),
    )


AXES = ("z", "y", "x", "c")


def hop(value, axis, k):
    size = lax.axis_size(axis)
    return lax.ppermute(value, axis, [(i, i ^ k) for i in range(size)])


def dot(left, right, dims=PLAIN):
    return lax.dot_general(left, right, dims, preferred_element_type=F32)


def joined(values, width):
    values = [v.astype(F32) for v in values]
    have = sum(v.shape[1] for v in values)
    if have < width:
        values.append(jnp.zeros((values[0].shape[0], width - have), F32))
    return jnp.concatenate(values, axis=1).astype(BF)


def pack_body(takes, width, cut, z_ref, *refs):
    count = len(takes)
    ins, outs = refs[:count], refs[count:]
    for k in range(PARTS):
        part = z_ref[0] ^ k
        for j in range(PARTS):

            @pl.when(part == j)
            def _():
                values = [ref[:, pl.ds(step * (j // share), step)] for ref, (step, share) in zip(ins, takes)]
                value = joined(values, width)
                if cut and k >= 2:
                    outs[k][...] = value[:, :cut]
                    outs[k + 2][...] = value[:, cut:]
                else:
                    outs[k][...] = value


def pack(z, arrays, takes, width, cut=None):
    depth = arrays[0].shape[0]
    outs = [shape((depth, width))] * PARTS
    if cut:
        outs = outs[:2] + [shape((depth, cut))] * 2 + [shape((depth, width - cut))] * 2
    return call(
        functools.partial(pack_body, takes, width, cut),
        outs,
        [SM] + [VM] * len(arrays),
        [VM] * len(outs),
    )(z, *arrays)


def pack_attn_body(z_ref, wq, wk, wv, wo, gain_one, gain_two, *outs):
    depth, width = outs[0].shape
    kw = wk.shape[0] // 2
    qw = wq.shape[1] // PARTS
    narrow = jnp.concatenate([wk[...].astype(F32), wv[...].astype(F32)], axis=0)
    gains = jnp.concatenate([gain_one[...], gain_two[...]], axis=0).astype(F32)
    fill = jnp.zeros((128 - (4 * kw + 2) % 128, depth), F32)
    tall = jnp.concatenate([narrow, gains, fill], axis=0).T
    for k in range(PARTS):
        part = z_ref[0] ^ k
        for j in range(PARTS):

            @pl.when(part == j)
            def _():
                spot = pl.ds(qw * j, qw)
                h = j // 2
                values = [
                    wq[:, spot],
                    tall[:, kw * h : kw * h + kw],
                    tall[:, kw * (h + 2) : kw * (h + 3)],
                    wo[:, spot],
                    tall[:, 4 * kw : 4 * kw + 2],
                ]
                outs[k][...] = joined(values, width)


def pack_attn(z, wq, wk, wv, wo, gain_one, gain_two, width):
    depth = wq.shape[0]
    return call(
        pack_attn_body, [shape((depth, width))] * PARTS, [SM] + [VM] * 6, [VM] * PARTS
    )(z, wq, wk.T, wv.T, wo, gain_one.reshape(1, -1), gain_two.reshape(1, -1))


def unpack_body(takes, z_ref, *refs):
    ins, outs = refs[:PARTS], refs[PARTS:]
    for ref, (start, step, share) in zip(outs, takes):
        if share == 2:
            ref[...] = jnp.zeros_like(ref)
    depth = ins[0].shape[0]
    for k in range(PARTS):
        part = z_ref[0] ^ k
        flat = None
        if any(share == 2 for start, step, share in takes):
            first = min(start for start, step, share in takes if share == 2)
            last = max(start + step for start, step, share in takes if share == 2)
            fill = jnp.zeros((depth, -(last - first) % 128), F32)
            flat = jnp.concatenate([ins[k][:, pl.ds(first, last - first)].astype(F32), fill], axis=1).T
        for j in range(PARTS):

            @pl.when(part == j)
            def _():
                for ref, (start, step, share) in zip(outs, takes):
                    spot = pl.ds(step * (j // share), step)
                    if share == 1:
                        ref[:, spot] = ins[k][:, pl.ds(start, step)].astype(F32)
                    else:
                        ref[spot, :] += flat[start - first : start - first + step]


def unpack(z, pieces, takes):
    depth = pieces[0].shape[0]
    dims = [(depth, step * PARTS // share) for start, step, share in takes]
    dims = [d[::-1] if take[2] == 2 else d for d, take in zip(dims, takes)]
    return call(
        functools.partial(unpack_body, takes),
        [shape(d, F32) for d in dims],
        [SM] + [VM] * PARTS,
        [VM] * len(takes),
        cost=4,
    )(z, *pieces)


def spot_of(pos, k, j, inner, depth):
    return pl.ds(pl.multiple_of(((pos[1] ^ k) * inner + (pos[2] ^ j)) * depth, 16), depth)


def piece_copies(pos, inner, pieces, store, sem, i, back=False):
    half = inner // 2
    depth = store.shape[1] // (PARTS * inner)
    copies = []
    for k in range(PARTS):
        for j in range(inner):
            ends = (
                pieces[2 * k + j // half].at[pl.ds((j % half) * depth, depth)],
                store.at[i, spot_of(pos, k, j, inner, depth)],
            )
            n = (i * PARTS + k) * inner + j
            copies.append(pltpu.make_async_copy(*(ends[::-1] if back else ends), sem.at[n]))
    return copies


def fetch(pos, inner, pieces, store, sem):
    copies = [piece_copies(pos, inner, pieces[8 * i : 8 * i + 8], store, sem, i) for i in range(2)]
    return start_all(copies)


def start_all(copies):
    for half in copies:
        for c in half:
            c.start()

    def wait(i):
        for c in copies[i]:
            c.wait()

    return wait


def own_rows_body(pos, ids, x_ref, t_ref, x_out, t_out, tall):
    spot = pl.ds(pl.multiple_of(pos[0], 64), 64)
    width = x_ref.shape[1]
    tall[...] = jnp.broadcast_to(ids[...].astype(F32), tall.shape[::-1]).T
    x_out[:, :width] = x_ref[spot, :]
    x_out[:, width:] = tall[spot, :].astype(BF)
    t_out[...] = t_ref[spot, :]


def own_rows(pos, ids, x, t):
    rows, width = x.shape
    return call(
        own_rows_body,
        [shape((64, width + 128)), shape((64, width))],
        [SM] + [VM] * 3,
        [VM] * 2,
        [pltpu.VMEM((rows, 128), F32)],
    )(pos, ids, x, t)


def join_rows(pieces, out):
    n = pieces[0].shape[0]
    for i, ref in enumerate(pieces):
        out[pl.ds(i * n, n), :] = ref[:, : out.shape[1]]


def first_sum_body(mine, got, three):
    three[...] = (mine[...].astype(F32) + got[...].astype(F32)).astype(BF)


def first_sum(mine, got):
    return call(first_sum_body, shape(mine.shape), [VM] * 2, VM)(mine, got)


def second_sum_body(mine_one, got_one, mine_two, got_two, three, one, two):
    one[...] = (mine_one[...].astype(F32) + got_one[...].astype(F32)).astype(BF)
    two[...] = (mine_two[...].astype(F32) + got_two[...].astype(F32) + three[...].astype(F32)).astype(BF)


def second_sum(mine, got, three):
    return call(second_sum_body, [shape(three.shape)] * 2, [VM] * 5, [VM] * 2)(
        mine[1], got[1], mine[2], got[2], three
    )


def last_sum(parts):
    return functools.reduce(jnp.add, [ref[...].astype(F32) for ref in parts])


def mean_scale(value):
    return lax.rsqrt(jnp.mean(value * value, axis=-1, keepdims=True) + EPS)


def back_norm(grad, value, gain):
    scale = mean_scale(value)
    unit = value * scale
    scaled = grad * gain
    return unit, scale * (scaled - unit * jnp.mean(scaled * unit, axis=-1, keepdims=True))


def after_attn_body(mine, got, one, two, x_own, gain, middle, n_own, total):
    branch = last_sum((mine, got, one, two))
    value = x_own[:, : branch.shape[1]].astype(F32) + branch
    middle[...] = value
    n_own[...] = (value * mean_scale(value) * gain[1:2, :]).astype(BF)
    total[...] = jnp.full(total.shape, jnp.sum(branch * branch), F32)


def after_mlp_body(mine, got, one, two, middle, target, d_own, out, total):
    branch = last_sum((mine, got, one, two))
    stream = middle[...] + branch
    d_own[...] = (stream - target[...].astype(F32)).astype(BF)
    out[...] = stream.astype(BF)
    total[0:8, :] = jnp.full((8, 128), jnp.sum(stream * stream), F32)
    total[8:16, :] = jnp.full((8, 128), jnp.sum(branch * branch), F32)


def after_feed_back_body(mine, got, one, two, middle, d_own, gain, d_middle, a_own, gain_grad):
    grad = last_sum((mine, got, one, two))
    unit, back = back_norm(grad, middle[...], gain[1:2, :])
    value = d_own[...].astype(F32) + back
    d_middle[...] = value
    a_own[...] = value.astype(BF)
    gain_grad[...] = jnp.sum(grad * unit, axis=0, keepdims=True)


def after_all_body(mine, got, one, two, x_own, d_middle, gain, out):
    grad = last_sum((mine, got, one, two))
    unit, back = back_norm(grad, x_own[:, : grad.shape[1]].astype(F32), gain[0:1, :])
    out[...] = (d_middle[...] + back).astype(BF)


def spread_rows_body(spots, p0, p1, p2, p3, out):
    n = p0.shape[0]
    for i, ref in enumerate((p0, p1, p2, p3)):
        out[pl.ds(pl.multiple_of(spots[i], 64), n), :] = ref[...]


def spread_rows(spots, pieces):
    n, width = pieces[0].shape
    return call(spread_rows_body, shape((4 * n, width)), [SM] + [VM] * 4, VM)(spots, *pieces)


def rotated(value, cosine, sine):
    half = HEAD_DIM // 2
    a, b = value[:, :half], value[:, half:]
    return jnp.concatenate([a * cosine - b * sine, b * cosine + a * sine], axis=1)


def project_body(qw, inner, pos, cosine, sine, *refs):
    x, w = refs[:8], refs[8:24]
    first, q_ref, kv_ref, gains, row_ids = refs[24:29]
    store, sem = refs[29:]
    wait = fetch(pos, inner, w, store, sem)
    width = first.shape[1]
    step = width // 4
    ids = jnp.concatenate([ref[:, width:] for ref in x], axis=0).astype(F32)
    row_ids[...] = ids.T[0:8, :]
    wait(0)
    spot = 480 - 384
    for p in range(4):
        tail = store[0, pl.ds(p * step, step), 384:512].astype(F32).T
        gains[:, pl.ds(p * step, step)] = tail[spot : spot + 8]
    gain = gains[0:1, :]
    rows = x[0].shape[0]
    for i, ref in enumerate(x):
        value = ref[:, :width].astype(F32)
        first[pl.ds(i * rows, rows), :] = (value * mean_scale(value) * gain).astype(BF)
    cos, sin = cosine[...], sine[...]
    queries, keys, values = [], [], []
    for i in range(2):
        if i:
            wait(1)
        out = dot(first[...], store[i])
        for start in range(0, qw, HEAD_DIM):
            queries.append(rotated(out[:, start : start + HEAD_DIM], cos, sin))
        keys.append(rotated(out[:, qw : qw + HEAD_DIM], cos, sin))
        values.append(out[:, qw + HEAD_DIM : qw + 2 * HEAD_DIM])
    q_ref[...] = jnp.concatenate(queries, axis=1).astype(BF)
    kv_ref[...] = jnp.concatenate(keys + values + [ids[:, :64]], axis=1).astype(BF)


def sems(inner):
    return pltpu.SemaphoreType.DMA((2 * (PARTS + 1) * inner,))


def project(pos, x, cosine, sine, w, qw, inner):
    rows, width = x[0].shape
    rows *= 8
    width -= 128
    return call(
        functools.partial(project_body, qw, inner),
        [
            shape((rows, width)),
            shape((rows, 2 * qw)),
            shape((rows, 384)),
            shape((8, width), F32),
            shape((8, rows), F32),
        ],
        [SM] + [VM] * 10 + [ANY] * 16,
        [VM] * 5,
        [pltpu.VMEM((2, width, 512), BF), sems(inner)],
        cost=12,
    )(pos, cosine, sine, *x, *w)


def out_rows(partial, outs):
    n = outs[0].shape[0]
    for i, ref in enumerate(outs):
        ref[...] = partial[i * n : (i + 1) * n].astype(ref.dtype)


def each(count, step, start):
    if count <= 2:
        for s in range(count):
            start = step(s, start)
        return start
    return lax.fori_loop(0, count, step, start)


def reader(kvs, rows):
    def read(s, lane):
        if len(kvs) > 1:
            return kvs[s][:, lane]
        return kvs[0][pl.ds(pl.multiple_of(s * rows, rows), rows), lane]

    return read


def lanes(i):
    return pl.ds(i * HEAD_DIM, HEAD_DIM)


ID_LANE = pl.ds(4 * HEAD_DIM, 1)


def attend_body(sides, pos, q_ref, row_ids, *refs):
    arrays = sides if sides <= 2 else 1
    kvs, refs = refs[:arrays], refs[arrays:]
    w = refs[:16]
    mixed = refs[16:18]
    lse, sides_out = refs[18], refs[19:27]
    store, sem = refs[27:]
    wait = fetch(pos, sides, w, store, sem)
    rows = q_ref.shape[0]
    qw = q_ref.shape[1] // 2
    ids = row_ids[0:1, :]
    read = reader(kvs, rows)

    def look(s):
        return read(s, ID_LANE).astype(F32) <= ids

    looks = [look(s) for s in range(sides)] if sides <= 2 else None
    lse[...] = jnp.zeros_like(lse)
    head = 0
    c = FACTOR * LOG2E
    for i in range(2):
        outs = []
        for start in range(i * qw, (i + 1) * qw, HEAD_DIM):
            q = q_ref[:, start : start + HEAD_DIM]

            def score(s):
                seen = looks[s] if looks else look(s)
                return jnp.where(seen, dot(read(s, lanes(i)), q, LAST), -1e30)

            scores = [score(s) for s in range(sides)] if sides <= 2 else None

            def highest(s, top):
                value = scores[s] if scores else score(s)
                return jnp.maximum(top, jnp.max(value, axis=0, keepdims=True))

            top = each(sides, highest, jnp.full((1, rows), -1e30, F32))

            def gathered(s, carry):
                total, out = carry
                value = scores[s] if scores else score(s)
                p = jnp.exp2(value * c - top * c)
                total = total + jnp.sum(p, axis=0, keepdims=True)
                return total, out + dot(read(s, lanes(2 + i)), p.astype(BF), ROWS)

            nothing = (jnp.zeros((1, rows), F32), jnp.zeros((HEAD_DIM, rows), F32))
            total, out = each(sides, gathered, nothing)
            outs.append(out / total)
            lse[head : head + 1, :] = top * c + jnp.log2(total)
            head += 1
        fill = jnp.zeros((512 - 320 - qw, rows), F32)
        tall = jnp.concatenate([jnp.zeros((320, rows), F32)] + outs + [fill], axis=0)
        mixed[i][...] = tall.T.astype(BF)
    for i in range(2):
        wait(i)
    partial = dot(mixed[0][...], store[0], LAST) + dot(mixed[1][...], store[1], LAST)
    out_rows(partial, sides_out)


def attend(pos, q, kvs, row_ids, w, sides):
    rows = q.shape[0]
    width = 8 * w[0].shape[0]
    return call(
        functools.partial(attend_body, sides),
        [shape((rows, 512))] * 2
        + [shape((8, rows), F32)]
        + [shape((rows // 8, width))] * 8,
        [SM] + [VM] * (2 + len(kvs)) + [ANY] * 16,
        [VM] * 11,
        [pltpu.VMEM((2, width, 512), BF), sems(sides)],
        cost=12,
    )(pos, q, row_ids, *kvs, *w)


def padded(value, width):
    return jnp.concatenate([value, jnp.zeros((value.shape[0], width - value.shape[1]), value.dtype)], axis=1)


def block_copies(pos, inner, arrays, store, sem, i):
    depth = arrays[1].shape[1]
    half = inner // 2
    cut = arrays[2].shape[1]
    copies = []
    for k in range(PARTS):
        for j in range(inner):
            n = (i * PARTS + k) * inner + j
            if k < 3:
                spot = arrays[k // 2].at[j * 2 + (pos[3] ^ i), pl.ds(depth if k == 1 else 0, depth)]
                to = store.at[i, pl.ds(pl.multiple_of(((pos[1] ^ k) * inner + j) * depth, 16), depth)]
                copies.append(pltpu.make_async_copy(spot, to, sem.at[n]))
                continue
            for late in range(2):
                piece = arrays[2 + 4 * late + 2 * i + j // half]
                lane = pl.ds(cut * late, piece.shape[1])
                to = store.at[i, spot_of(pos, k, j, inner, depth), lane]
                spot = piece.at[pl.ds((j % half) * depth, depth)]
                copies.append(
                    pltpu.make_async_copy(spot, to, sem.at[2 * PARTS * inner + i * inner + j] if late else sem.at[n])
                )
    return copies


def feed_body(fw, inner, pos, *refs):
    n, blocks = refs[:8], refs[8:18]
    hidden, slope, silu = refs[18:20], refs[20:22], refs[22:24]
    rows_in, outs = refs[24], refs[25:33]
    store, sem = refs[33:]
    wait = start_all([block_copies(pos, inner, blocks, store, sem, i) for i in range(2)])
    join_rows(n, rows_in)
    for i in range(2):
        wait(i)
        out = dot(rows_in[...], store[i, :, : 2 * fw])
        gate, upper = out[:, :fw], out[:, fw:]
        sigma = jax.nn.sigmoid(gate)
        act = gate * sigma
        hidden[i][...] = padded(act * upper, 512).astype(BF)
        slope[i][...] = padded(upper * (sigma + act * (1.0 - sigma)), 512).astype(BF)
        silu[i][...] = padded(act, 512).astype(BF)
    out_rows(
        dot(hidden[0][...], store[0, :, 2 * fw :], LAST)
        + dot(hidden[1][...], store[1, :, 2 * fw :], LAST),
        outs,
    )


def feed(pos, n, w, fw, inner):
    rows, width = n[0].shape
    return call(
        functools.partial(feed_body, fw, inner),
        [shape((8 * rows, 512))] * 6 + [shape((8 * rows, width))] + [shape((rows, width))] * 8,
        [SM] + [VM] * 8 + [ANY] * 10,
        [VM] * 15,
        [pltpu.VMEM((2, width, 2 * fw + 512), BF), sems(inner)],
        cost=18,
    )(pos, *n, *w)


def feed_back_body(fw, inner, pos, rows_in, *refs):
    slope, silu = refs[0:2], refs[2:4]
    blocks = refs[4:14]
    d_gu, outs = refs[14:16], refs[16:24]
    store, sem = refs[24:]
    wait = start_all([block_copies(pos, inner, blocks, store, sem, i) for i in range(2)])
    for i in range(2):
        wait(i)
        out = dot(rows_in[...], store[i, :, 2 * fw :])
        a = (out * slope[i][...].astype(F32))[:, :fw]
        b = (out * silu[i][...].astype(F32))[:, :fw]
        d_gu[i][...] = jnp.concatenate([a, b], axis=1).astype(BF)
    out_rows(
        dot(d_gu[0][...], store[0, :, : 2 * fw], LAST)
        + dot(d_gu[1][...], store[1, :, : 2 * fw], LAST),
        outs,
    )


def feed_back(pos, d, slope, silu, w, fw, inner):
    rows, width = d.shape
    return call(
        functools.partial(feed_back_body, fw, inner),
        [shape((rows, 2 * fw))] * 2 + [shape((rows // 8, width))] * 8,
        [SM] + [VM] * 5 + [ANY] * 10,
        [VM] * 10,
        [pltpu.VMEM((2, width, 2 * fw + 512), BF), sems(inner)],
        cost=16,
    )(pos, d, *slope, *silu, *w)


def features(pos, k, step):
    return pl.ds(pl.multiple_of((pos[1] ^ k) * step, 128), step)


def block_grad_body(inner, parts, pos, left, right_a, right_b, out, store, sem):
    step = store.shape[1] // len(parts)
    depth = step // inner
    copies = []
    for p, k in enumerate(parts):
        spot = features(pos, k, step)
        for i, right in enumerate((right_a, right_b)):
            store[i, pl.ds(p * step, step), :] = dot(left[:, spot], right[...], ROWS).astype(BF)
            for j in range(inner):
                n = p * inner + j
                copies.append(
                    pltpu.make_async_copy(
                        store.at[i, pl.ds(n * depth, depth)],
                        out.at[j * 2 + (pos[3] ^ i), pl.ds(p * depth, depth)],
                        sem.at[i * len(parts) * inner + n],
                    )
                )
                copies[-1].start()
    for c in copies:
        c.wait()


def down_grad_body(inner, pos, *refs):
    pieces, right, out, rows_in, store, sem = refs[:8], refs[8:10], *refs[10:]
    join_rows(pieces, rows_in)
    block_grad_body(inner, range(PARTS), pos, rows_in, *right, out, store, sem)


def down_grad(pos, pieces, right, inner):
    rows, width = pieces[0].shape
    rows *= 8
    cols = right[0].shape[1]
    return call(
        functools.partial(down_grad_body, inner),
        [shape((inner * 2, width // inner, cols)), shape((rows, width))],
        [SM] + [VM] * 10,
        [ANY, VM],
        [pltpu.VMEM((2, width, cols), BF), sems(inner)],
        cost=7,
    )(pos, *pieces, *right)


def block_grad(pos, left, right, inner, parts):
    rows, width = left.shape
    cols = right[0].shape[1]
    held = width // PARTS * len(parts)
    return call(
        functools.partial(block_grad_body, inner, parts),
        shape((inner * 2, held // inner, cols)),
        [SM] + [VM] * 3,
        ANY,
        [pltpu.VMEM((2, held, cols), BF), sems(inner)],
        cost=7,
    )(pos, left, *right)


def attend_back_body(sides, pos, q_ref, row_ids, lse, cosine, sine, *refs):
    arrays = sides if sides <= 2 else 1
    d, refs = refs[:8], refs[8:]
    kvs, refs = refs[:arrays], refs[arrays:]
    w = refs[:16]
    dq_ref, own_ref, send_ref, rows_in = refs[16:20]
    store, mix, d_kv, sem = refs[20:]
    join_rows(d, rows_in)
    wait = fetch(pos, sides, w, store, sem)
    rows = q_ref.shape[0]
    qw = q_ref.shape[1] // 2
    for i in range(2):
        wait(i)
        mix[i] = dot(rows_in[...], store[i])[:, 320 : 320 + qw].astype(BF)
    ids = row_ids[0:1, :]
    read = reader(kvs, rows)

    def look(s):
        return read(s, ID_LANE).astype(F32) <= ids

    looks = [look(s) for s in range(sides)] if sides <= 2 else None
    d_q = []
    c = FACTOR * LOG2E
    head = 0
    for i in range(2):
        for start in range(0, qw, HEAD_DIM):
            q = q_ref[:, i * qw + start : i * qw + start + HEAD_DIM]
            dm = mix[i, :, start : start + HEAD_DIM]
            level = lse[head : head + 1, :]
            head += 1

            def pair(s):
                seen = looks[s] if looks else look(s)
                p = jnp.where(seen, jnp.exp2(dot(read(s, lanes(i)), q, LAST) * c - level), 0.0)
                return p, dot(read(s, lanes(2 + i)), dm, LAST)

            held = [pair(s) for s in range(sides)] if sides <= 2 else None

            def weigh(s, delta):
                p, dp = held[s] if held else pair(s)
                return delta + jnp.sum(p * dp, axis=0, keepdims=True)

            delta = each(sides, weigh, jnp.zeros((1, rows), F32))

            def grads(s, out):
                p, dp = held[s] if held else pair(s)
                ds = (p * (dp - delta)).astype(BF)
                d_value = dot(p.astype(BF), dm)
                d_key = dot(ds, q)
                if start == 0:
                    d_kv[2 + i, s] = d_value
                    d_kv[i, s] = d_key
                else:
                    d_kv[2 + i, s] += d_value
                    d_kv[i, s] += d_key
                return out + dot(read(s, lanes(i)), ds, ROWS)

            d_q.append(each(sides, grads, jnp.zeros((HEAD_DIM, rows), F32)))
    tall = jnp.concatenate(d_q + [jnp.zeros((512 - 4 * HEAD_DIM, rows), F32)], axis=0).T * FACTOR
    cos, sin = cosine[...], sine[...]
    dq_ref[...] = jnp.concatenate(
        [rotated(tall[:, h * HEAD_DIM : (h + 1) * HEAD_DIM], cos, -sin) for h in range(4)], axis=1
    ).astype(BF)
    for s in range(sides):
        value = jnp.concatenate([d_kv[0, s] * FACTOR, d_kv[1, s] * FACTOR, d_kv[2, s], d_kv[3, s]], axis=1)
        if s == 0:
            own_ref[...] = value
        else:
            send_ref[pl.ds((s - 1) * rows, rows), :] = value.astype(BF)


def attend_back(pos, d, q, kvs, row_ids, lse, cosine, sine, w, sides):
    rows = q.shape[0]
    width = d[0].shape[1]
    cols = 4 * HEAD_DIM
    return call(
        functools.partial(attend_back_body, sides),
        [shape(q.shape), shape((rows, cols), F32), shape(((sides - 1) * rows, cols)), shape((rows, width))],
        [SM] + [VM] * (13 + len(kvs)) + [ANY] * 16,
        [VM] * 4,
        [
            pltpu.VMEM((2, width, 512), BF),
            pltpu.VMEM((2, rows, q.shape[1] // 2), BF),
            pltpu.VMEM((4, sides, rows, HEAD_DIM), F32),
            sems(sides),
        ],
        cost=18,
    )(pos, q, row_ids, lse, cosine, sine, *d, *kvs, *w)


def split_body(dq_ref, own_ref, got_ref, cosine, sine, *d_qkv):
    qw = dq_ref.shape[1] // 2
    cos, sin = cosine[...], sine[...]
    d_kv = own_ref[...] + got_ref[...].astype(F32)
    d_q = dq_ref[...].astype(F32)
    for i in range(2):
        d_k = rotated(d_kv[:, i * HEAD_DIM : (i + 1) * HEAD_DIM], cos, -sin)
        d_v = d_kv[:, (2 + i) * HEAD_DIM : (3 + i) * HEAD_DIM]
        d_qkv[i][...] = padded(
            jnp.concatenate([d_q[:, i * qw : (i + 1) * qw], d_k, d_v], axis=1), 512
        ).astype(BF)


def split_grads(dq, own, got, cosine, sine):
    rows = dq.shape[0]
    return call(split_body, [shape((rows, 512))] * 2, [VM] * 5, [VM] * 2)(dq, own, got, cosine, sine)


def project_back_body(inner, pos, d_a, d_b, *refs):
    w, outs = refs[:16], refs[16:24]
    store, sem = refs[24:]
    wait = fetch(pos, inner, w, store, sem)
    for i in range(2):
        wait(i)
    out_rows(dot(d_a[...], store[0], LAST) + dot(d_b[...], store[1], LAST), outs)


def project_back(pos, d_qkv, w, inner):
    rows = d_qkv[0].shape[0] // 8
    width = 8 * w[0].shape[0]
    return call(
        functools.partial(project_back_body, inner),
        [shape((rows, width))] * 8,
        [SM] + [VM] * 2 + [ANY] * 16,
        [VM] * 8,
        [pltpu.VMEM((2, width, 512), BF), sems(inner)],
        cost=8,
    )(pos, *d_qkv, *w)


def pair_copies(pos, inner, outs, store, sem, i):
    half = inner // 2
    depth = store.shape[1] // (PARTS * inner)
    copies = []
    for k in range(PARTS):
        for j in range(inner):
            spot = ((k % 2) * half + j % half) * depth
            to = outs[2 * (k // 2) + j // half].at[pl.ds(spot, depth)]
            n = (i * PARTS + k) * inner + j
            copies.append(
                pltpu.make_async_copy(store.at[i, spot_of(pos, k, j, inner, depth)], to, sem.at[n])
            )
    return copies


def attn_grad_body(inner, pos, first, d_all, gain_two, sum_attn, sums, *refs):
    d_qkv, mixed = refs[:2], refs[2:4]
    w, outs = refs[4:20], refs[20:28]
    held, store, sem, out_sem = refs[28:]
    wait = fetch(pos, inner, w, held, sem)
    step = store.shape[1] // PARTS
    copies = [pair_copies(pos, inner, outs[4 * i : 4 * i + 4], store, out_sem, i) for i in range(2)]
    lane = lax.broadcasted_iota(jnp.int32, (1, 128), 1)
    tail = jnp.where(lane == 98, sums[0:1, :], 0.0)
    tail = jnp.where(lane == 99, sum_attn[0:1, :], tail)
    tail = jnp.where(lane == 100, sums[8:9, :], tail)
    wait(0)
    wait(1)
    for k in (3, 2, 1, 0):
        spot = features(pos, k, step)
        rows = [jnp.zeros((97, step), F32), gain_two[0:1, spot], jnp.zeros((30, step), F32)]
        tall = jnp.concatenate(rows, axis=0).T + tail
        values = [dot(first[:, spot], d_qkv[i][...], ROWS) for i in range(2)]
        gain = 0.0
        for i in range(2):
            gain = gain + jnp.sum(values[i] * held[i, spot, :].astype(F32), axis=1, keepdims=True)
        gain = gain / held[0, spot, 480:481].astype(F32)
        tall = tall + jnp.where(lane == 96, gain, 0.0)
        for i in range(2):
            value = values[i] + dot(d_all[:, spot], mixed[i][...], ROWS)
            store[i, spot, :384] = value[:, :384].astype(BF)
            store[i, spot, 384:] = (value[:, 384:] + tall).astype(BF)
            for c in copies[i][k * inner : (k + 1) * inner]:
                c.start()
    for i in range(2):
        for c in copies[i]:
            c.wait()


def attn_grad(pos, first, d_all, gain_two, sum_attn, sums, d_qkv, mixed, w, inner):
    rows, width = first.shape
    return call(
        functools.partial(attn_grad_body, inner),
        [shape((width // 4, 512))] * 8,
        [SM] + [VM] * 9 + [ANY] * 16,
        [ANY] * 8,
        [pltpu.VMEM((2, width, 512), BF), pltpu.VMEM((2, width, 512), BF), sems(inner), sems(inner)],
        cost=12,
    )(pos, first, d_all, gain_two, sum_attn, sums, *d_qkv, *mixed, *w)


def hold(values, *others):
    got = lax.optimization_barrier(tuple(values) + tuple(others))
    return list(got[: len(values)])


class Live:
    def fence(self):
        names = sorted(self.__dict__)
        leaves, tree = jax.tree.flatten([self.__dict__[n] for n in names])
        leaves = lax.optimization_barrier(tuple(leaves))
        self.__dict__.update(zip(names, jax.tree.unflatten(tree, leaves)))


class Place:
    def __init__(self):
        self.inner = lax.axis_size("y")
        self.count = PARTS * self.inner
        self.z, self.y, self.x, self.c = [lax.axis_index(name) for name in AXES]
        self.s = self.z * self.inner + self.y
        self.zs = self.z.reshape(1).astype(jnp.int32)
        self.bits = []
        b = 1
        while b < self.inner:
            self.bits.append(b)
            b *= 2

    def hop_z(self, v, k):
        return hop(v, "z", k)

    def hop_y(self, v, b):
        return hop(v, "y", b)

    def hop_x(self, v):
        return hop(v, "x", 1)

    def hop_c(self, v):
        return hop(v, "c", 1)

    def low_y(self, v):
        for b in self.bits[:-1]:
            v = jnp.concatenate([v, self.hop_y(v, b)], 0)
        return v

    def far_y(self, v):
        return self.hop_y(v, self.bits[-1])

    def add(self, own, got):
        return (own.astype(F32) + got.astype(F32)).astype(BF)

    def sum_y(self, own, far):
        value = self.add(own, self.far_y(far))
        for b in reversed(self.bits[:-1]):
            n = value.shape[0] // 2
            value = self.add(value[:n], self.hop_y(value[n:], b))
        return value

    def sum_x(self, own, other):
        return self.add(own, self.hop_x(other))

    def gather(self, own):
        mine = [own, self.hop_z(own, 1), self.hop_z(own, 2)]
        mine.append(self.hop_z(mine[2], 1))
        return mine + [self.hop_c(v) for v in mine]

    def scatter_one(self, outs):
        mine = list(outs[:4])
        got = [self.hop_c(v) for v in outs[4:]]
        one, two = second_sum(mine, got, self.hop_z(first_sum(mine[3], got[3]), 1))
        return [mine[0], got[0], one, two]

    def scatter_two(self, left):
        return left[0], left[1], self.hop_z(left[2], 1), self.hop_z(left[3], 2)

    def scatter(self, outs):
        return self.scatter_two(self.scatter_one(outs))


def tables(place):
    half = HEAD_DIM // 2
    freq = THETA ** (-(jnp.arange(half, dtype=F32) * 2.0 / HEAD_DIM))
    angle = place[:, None] * freq[None, :]
    return (jnp.cos(angle), jnp.sin(angle))


def on_device(
    inputs,
    targets,
    seq_ids,
    block_ids,
    attn_gain,
    mlp_gain,
    w_query,
    w_key,
    w_value,
    w_out,
    w_gate,
    w_up,
    w_down,
):
    at = Place()
    inner = at.inner
    full = inputs.shape[1]
    half_span = SPAN // 2
    kw = w_key.shape[1] // 2
    qw = w_query.shape[1] // PARTS
    fw = w_gate.shape[1] // PARTS
    row_f32 = shape((half_span, full), F32)
    row_bf = shape((half_span, full))

    off = jnp.where(seq_ids[0] == at.x, 0, SPAN)
    pos = jnp.stack([off + at.c * half_span, at.z, at.y, at.x, at.c]).astype(jnp.int32)
    spots = [
        (off if xr == 0 else SPAN - off) + (at.c ^ cr) * half_span for xr in range(2) for cr in range(2)
    ]
    spots = jnp.stack(spots).astype(jnp.int32)

    def all_rows(own):
        across = at.hop_x(own)
        return [own, at.hop_c(own), across, at.hop_c(across)]

    rows = 2 * PARTS * half_span
    count = jnp.arange(rows, dtype=jnp.int32)
    zz = at.z ^ ((count // half_span) % PARTS)
    cc = at.c ^ (count // (half_span * PARTS))
    place = ((zz * inner + at.y) * SPAN + cc * half_span + count % half_span).astype(F32)
    cosine, sine = tables(place)

    def listed(w):
        return [v for i in range(2) for k in range(PARTS) for v in w[k][i]]

    def gather_blocks(pair):
        return lax.all_gather(pair, ("y", "x"), axis=0)

    def scatter_blocks(blocks, count):
        blocks = blocks.reshape(-1, blocks.shape[-1])
        got = lax.psum_scatter(blocks, ("y", "x"), scatter_dimension=0, tiled=True)
        n = got.shape[0] // count
        return [got[k * n : (k + 1) * n] for k in range(count)]

    hop_x, hop_z, low_y, far_y = at.hop_x, at.hop_z, at.low_y, at.far_y
    live = Live()
    live.w = [w_gate, w_up, w_down]
    live.rows = [inputs, targets]
    live.qo = pack_attn(at.zs, w_query, w_key, w_value, w_out, attn_gain, mlp_gain, 512)
    live.fence()

    q = live.qo
    z = [q[0]] + [hop_z(q[k], k) for k in range(1, PARTS)]
    live.x_own, live.t_own = own_rows(pos, block_ids.reshape(1, -1), *live.rows)
    live.g = list(pack(at.zs, live.w, [(fw, 1)] * 3, 2 * fw + 512, 2 * fw))
    del live.w, live.rows
    live.g[1] = hop_z(hold([live.g[1]], z[1])[0], 1)
    v = low_y(z[0])
    w = far_y(v)
    live.q0 = (v, w, hop_x(v))
    live.q1 = (low_y(z[1]), low_y(hop_x(z[1])))
    live.z = z[2:]
    live.fence()

    near = gather_blocks(jnp.concatenate(live.g[:2], 0))
    v, w, u = live.q0
    q0 = ((v, w), (u, hop_x(w)))
    v, u = live.q1
    q1 = ((v, far_y(v)), (u, far_y(u)))
    v = low_y(live.z[0])
    w = far_y(v)
    q2 = ((v, w), (hop_x(v), hop_x(w)))
    u, v = low_y(hop_x(live.z[1])), low_y(live.z[1])
    q3 = ((v, far_y(v)), (u, far_y(u)))
    live.x_all = at.gather(live.x_own)
    live.w_qo = listed([q0, q1, q2, q3])
    live.g[2] = hop_z(live.g[2], 2)
    del live.z, live.q0, live.q1
    live.fence()

    live.first, live.query, kv, live.gain, live.row_ids = project(
        pos, live.x_all, cosine, sine, live.w_qo, qw, inner
    )
    live.kvs = [kv]
    live.g[4] = hop_z(live.g[4], 2)
    live.fence()

    g2 = gather_blocks(jnp.concatenate([live.g[2], live.g[4]], 1))

    kvs = live.kvs
    for b in at.bits:
        kvs = kvs + [at.hop_y(v, b) for v in kvs]
    if inner > 2:
        kvs = [jnp.concatenate(kvs, 0)]
    live.kvs = kvs
    mixed_a, mixed_b, live.lse, *live.outs = attend(
        pos, live.query, kvs, live.row_ids, live.w_qo, inner
    )
    live.mixed = (mixed_a, mixed_b)
    live.g[3] = hop_z(live.g[3], 3)
    live.w_near = near
    live.fence()

    live.left = at.scatter_one(live.outs)
    live.g[5] = hop_z(live.g[5], 3)
    v = low_y(live.g[3])
    live.g3 = (v, far_y(v), low_y(hop_x(live.g[3])))
    del live.outs
    live.fence()

    v, w, u = live.g3
    live.g3 = [v, w, u, far_y(u)]
    v = low_y(live.g[5])
    w = far_y(v)
    live.g3 += [v, w, hop_x(v), hop_x(w)]
    del live.g
    live.middle, n_own, live.sum_attn = call(
        after_attn_body,
        [row_f32, row_bf, shape((8, 128), F32)],
        [VM] * 6,
        [VM] * 3,
    )(*at.scatter_two(live.left), live.x_own, live.gain)
    live.n_all = at.gather(n_own)
    live.w_two = g2
    del live.left
    live.fence()

    live.w_ff = [live.w_near, live.w_two, *live.g3]
    del live.w_near, live.w_two, live.g3
    out = feed(pos, live.n_all, live.w_ff, fw, inner)
    live.hidden, live.slope, live.silu = out[:2], out[2:4], out[4:6]
    live.n_all, outs = out[6], out[7:]
    live.d_own, live.layer_own, live.sums = call(
        after_mlp_body,
        [row_bf, row_bf, shape((16, 128), F32)],
        [VM] * 6,
        [VM] * 3,
    )(*at.scatter(outs), live.middle, live.t_own)
    del live.t_own
    live.fence()

    live.d_rows = at.gather(live.d_own)
    live.layer_out = all_rows(live.layer_own)
    del live.layer_own
    live.fence()


    live.grad_d, live.d_rows = down_grad(pos, live.d_rows, live.hidden, inner)
    live.fence()

    d = scatter_blocks(live.grad_d, 4)
    out = feed_back(pos, live.d_rows, live.slope, live.silu, live.w_ff, fw, inner)
    live.d_gu, live.outs = out[:2], out[2:]
    del live.slope, live.silu, live.w_ff, live.d_rows, live.hidden, live.grad_d
    live.fence()

    live.left = at.scatter_one(live.outs)
    del live.outs
    live.far = block_grad(pos, live.n_all, live.d_gu, inner, (2, 3))
    live.fence()

    far = scatter_blocks(live.far, 2)
    live.d_middle, live.a_own, live.grad_gain_two = call(
        after_feed_back_body,
        [row_f32, row_bf, shape((1, full), F32)],
        [VM] * 7,
        [VM] * 3,
    )(*at.scatter_two(live.left), live.middle, live.d_own, live.gain)
    del live.middle, live.d_own, live.left, live.far
    live.near = block_grad(pos, live.n_all, live.d_gu, inner, (0, 1))
    del live.n_all, live.d_gu
    live.fence()

    near = scatter_blocks(live.near, 2)
    live.a_all = at.gather(live.a_own)
    del live.a_own, live.near
    live.fence()

    live.d_query, live.d_kv, live.sent, live.a_all = attend_back(
        pos, live.a_all, live.query, live.kvs, live.row_ids, live.lse, cosine, sine, live.w_qo, inner
    )
    del live.query, live.kvs, live.row_ids, live.lse
    live.d = [d[0], hop_z(d[1], 1), d[2], hop_z(d[3], 3)]
    live.fence()

    d_kv, sent = live.d_kv, live.sent
    if inner > 2:
        sent = jnp.concatenate([d_kv, sent.astype(F32)], 0)
        for b in reversed(at.bits[1:]):
            n = sent.shape[0] // 2
            sent = sent[:n] + at.hop_y(sent[n:].astype(BF), b).astype(F32)
        d_kv, sent = sent[:rows], sent[rows:].astype(BF)
    sent = at.hop_y(sent, at.bits[0])
    live.d_qkv = split_grads(live.d_query, d_kv, sent, cosine, sine)
    live.d[2] = hop_z(live.d[2], 2)
    del live.d_kv, live.sent, live.d_query
    live.fence()

    tails = (live.grad_gain_two, live.sum_attn, live.sums)
    q = attn_grad(pos, live.first, live.a_all, *tails, live.d_qkv, live.mixed, live.w_qo, inner)
    live.q_near, live.q_far = (q[0:2], q[4:6]), (q[2:4], q[6:8])
    live.far3 = hop_z(far[1], 3)
    del live.first, live.a_all, live.mixed
    del live.grad_gain_two, live.sum_attn, live.sums
    live.fence()

    live.left = at.scatter_one(project_back(pos, live.d_qkv, live.w_qo, inner))
    del live.d_qkv, live.w_qo
    q_near, q_far = live.q_near, live.q_far
    del live.q_near, live.q_far
    (a, b), (c, d) = q_far
    q_far = at.sum_y(at.sum_x(a, c), at.sum_x(b, d))
    q_near = at.sum_x(*[at.sum_y(*side) for side in q_near])
    far2 = hop_z(far[0], 2)
    live.fence()

    (live.input_own,) = call(
        after_all_body,
        [row_bf],
        [VM] * 7,
        [VM],
    )(*at.scatter_two(live.left), live.x_own, live.d_middle, live.gain)
    del live.left, live.x_own, live.d_middle
    live.q_near, live.q_far, live.far2 = q_near, q_far, far2
    (live.g_down,) = unpack(at.zs, live.d, [(0, fw, 1)])
    live.layer_out = spread_rows(spots, live.layer_out)
    del live.d
    live.fence()

    near_own, near_one = hold(near, live.input_own)
    live.g = [near_own, hop_z(near_one, 1), live.far2, live.far3]
    live.input_grad = all_rows(live.input_own)
    del live.far2, live.far3, live.input_own
    n = live.q_far.shape[0] // 2
    live.q = [live.q_near[:n], live.q_near[n:], hop_z(live.q_far[:n], 2), hop_z(live.q_far[n:], 3)]
    del live.q_near, live.q_far
    live.fence()

    q = live.q
    q[1] = hop_z(q[1], 1)
    layer_out, input_grad = live.layer_out, spread_rows(spots, live.input_grad)
    g_gate, g_up = unpack(at.zs, live.g, [(0, fw, 1), (fw, fw, 1)])
    g_down = live.g_down
    takes = [(0, qw, 1), (qw, kw, 2), (qw + kw, kw, 2), (qw + 2 * kw, qw, 1)]
    g_query, g_key, g_value, g_out = unpack(at.zs, q, takes)
    g_key, g_value = g_key.T, g_value.T
    tails = sum(p[:, 384:512].astype(F32) for p in q)
    tails = tails + at.hop_c(tails)
    entries = inputs.shape[0] * at.count * inputs.shape[1]
    rms = jnp.sqrt(tails[0, 98:101] / entries + EPS)
    return (
        layer_out,
        input_grad,
        g_query,
        g_key,
        g_value,
        g_out,
        g_gate,
        g_up,
        g_down,
        tails[:, 96],
        tails[:, 97],
        rms[0],
        rms[1],
        rms[2],
    )


def solution(mesh):
    devices = mesh.devices.reshape(PARTS, -1, 2, mesh.devices.shape[1] // 2)
    seq, mp = ("z", "y"), ("x", "c")
    rows, single, block = P(seq, None), P(seq), P(seq, mp)
    return jax.shard_map(
        on_device,
        mesh=Mesh(devices, AXES),
        in_specs=(rows, rows, single, single, single, single) + (block,) * 7,
        out_specs=(rows, rows) + (block,) * 7 + (single, single, P(), P(), P()),
        check_vma=False,
    )
```

time: 710 us -> 645 us (0.908)
  starting transfers between devices: 133 us -> 106 us
  Pallas kernels: 183 us -> 170 us
  local copies, waits for them, and re-layouts: 40.6 us -> 29.9 us
  other arithmetic: 13 us -> 5.76 us
    ppermute x85 -> x106, starting transfers between devices: 133 us -> 105 us  [hop(): return lax.ppermute(value, axis, [(i, i ^ k) for i in range(size)])]
    ppermute x85 -> x106, waiting for transfers between devices: 313 us -> 289 us  [hop(): return lax.ppermute(value, axis, [(i, i ^ k) for i in range(size)])]
    reduce_scatter x2 -> x3, waiting for transfers between devices: 0.01 us -> 21.5 us  [scatter_blocks(): got = lax.psum_scatter(blocks, ('y', 'x'), scatter_dimension=0, tiled=True)]
    unnamed x182 -> x240, local copies, waits for them, and re-layouts: 31.8 us -> 19.2 us
    pallas_call x24 -> x21, Pallas kernels: 123 us -> 112 us  [the longest x1 16.9 us: feed_back(): call(functools.partial(feed_back_body, fw, inner), [shape((rows, 2 * fw))...]
  transfers between devices with their start and end apart: 89 -> 111, of which waited for: 50 -> 48; matrix products, arithmetic and copies ran while one was open for 3% -> 2% of each run, Pallas kernels for 18% -> 22%
where the time goes in v5:
time: 645 us; the launch traced here: 639 us
  waiting for transfers between devices  311 us (48%)
  Pallas kernels  170 us (26%)
  starting transfers between devices  106 us (16%)
  local copies, waits for them, and re-layouts  29.9 us (5%)
  between operations  15.9 us (2%)
    ppermute x106, waiting for transfers between devices, hop(): return lax.ppermute(value, axis, [(i, i ^ k) for i in range(size)])  289 us
    ppermute x106, starting transfers between devices, hop(): return lax.ppermute(value, axis, [(i, i ^ k) for i in range(size)])  105 us
    reduce_scatter x3, waiting for transfers between devices, scatter_blocks(): got = lax.psum_scatter(blocks, ('y', 'x'), scatter_dimension=0, tiled=True)  21.5 us
    unnamed x240, local copies, waits for them, and re-layouts  19.2 us
    pallas_call x1, Pallas kernels, feed_back(): call(functools.partial(feed_back_body, fw, inner), [shape((rows, 2 * fw))...  16.9 us
    pallas_call x1, Pallas kernels, feed(): call(functools.partial(feed_body, fw, inner), [shape((8 * rows, 512))] *...  15.8 us
    pallas_call x1, Pallas kernels, attend_back(): call(functools.partial(attend_back_body, sides), [shape(q.shape), shape((...  15.4 us
    pallas_call x1, Pallas kernels, attn_grad(): call(functools.partial(attn_grad_body, inner), [shape((width // 4, 512))]...  13.5 us
  transfers between devices with their start and end apart: 111, of which 48 were waited for; matrix products, arithmetic and copies ran while one was open for 2% of the time, Pallas kernels for 22%

profile of v5, /device:TPU:0, one launch (start us, length us, event | category | flops | bytes accessed | tf_op | source)
XLA Modules:
  0.0 638.6 jit_solution(6426868951272929846)
XLA Ops:
  16.1 4.6 shard_map.237
  31.6 21.8 %collective-permute-done.5.refs_12_.refs_6_.refs_14_.refs_8_.refs_4_ = bf16[320,512]{1,0:T(8,128)(2,1)} collective-permute-done((bf16[320,512]{1,0:T(8,128)(2,1)S(1)}, bf16[320,512]{1,0:T(8,128)(2,1)}, u32[]{:S(2)}, u32[]{:S(2)}) %collective-permute-start.5) | collective-permute-done | bytes 327712 | tf_op jit(solution)/shard_map/ppermute | solution.py:52
  71.2 4.0 collective-permute-done.12.refs_19_.refs_13_.refs_21_.refs_15_.refs_11_
  80.5 8.1 %collective-permute-done.8.refs_11_.refs_5_.refs_13_.refs_7_.refs_3_ = bf16[320,512]{1,0:T(8,128)(2,1)S(1)} collective-permute-done((bf16[320,512]{1,0:T(8,128)(2,1)S(1)}, bf16[320,512]{1,0:T(8,128)(2,1)S(1)}, u32[]{:S(2)}, u32[]{:S(2)}) %collective-permute-start.8) | collective-permute-done | bytes 327712 | tf_op jit(solution)/shard_map/ppermute | solution.py:52
  92.0 9.0 %collective-permute-done.10.refs_15_.refs_9_.refs_17_.refs_11_.refs_7_ = bf16[320,512]{1,0:T(8,128)(2,1)S(1)} collective-permute-done((bf16[320,512]{1,0:T(8,128)(2,1)S(1)}, bf16[320,512]{1,0:T(8,128)(2,1)S(1)}, u32[]{:S(2)}, u32[]{:S(2)}) %collective-permute-start.10) | collective-permute-done | bytes 327712 | tf_op jit(solution)/shard_map/ppermute | solution.py:52
  105.6 8.2 %collective-permute-done.9.refs_13_.refs_7_.refs_15_.refs_9_.refs_5_ = bf16[320,512]{1,0:T(8,128)(2,1)S(1)} collective-permute-done((bf16[320,512]{1,0:T(8,128)(2,1)}, bf16[320,512]{1,0:T(8,128)(2,1)S(1)}, u32[]{:S(2)}, u32[]{:S(2)}) %collective-permute-start.9) | collective-permute-done | bytes 327712 | tf_op jit(solution)/shard_map/ppermute | solution.py:52
  119.0 8.7 %collective-permute-done.16.refs_23_.refs_17_.refs_25_.refs_19_.refs_15_ = bf16[320,512]{1,0:T(8,128)(2,1)S(1)} collective-permute-done((bf16[320,512]{1,0:T(8,128)(2,1)S(1)}, bf16[320,512]{1,0:T(8,128)(2,1)S(1)}, u32[]{:S(2)}, u32[]{:S(2)}) %collective-permute-start.16) | collective-permute-done | bytes 327712 | tf_op jit(solution)/shard_map/ppermute | solution.py:52
  130.8 9.8 %shard_map.239 = (bf16[512,2560]{1,0:T(8,128)(2,1)}, bf16[512,320]{1,0:T(8,128)(2,1)}, bf16[512,384]{1,0:T(8,128)(2,1)}, f32[8,2560]{1,0:T(8,128)}, f32[8,512]{1,0:T(8,128)}) custom-call(s32[5]{0:T(128)} %stack.36.pos, f32[512,40]{1,0:T(8,128)} %get-tuple-element.1645.cosine, f32[512,40]{1,0:T(8,128)} %get-tuple-element.1644.sine, ...), custom_call_target="tpu_custom_call" | custom-call | flops 12000000000 | tf_op jit(solution)/shard_map/pallas_call | solution.py:356
  140.6 6.6 %collective-permute-done.24 = bf16[320,512]{1,0:T(8,128)(2,1)S(1)} collective-permute-done((bf16[320,512]{1,0:T(8,128)(2,1)S(1)}, bf16[320,512]{1,0:T(8,128)(2,1)S(1)}, u32[]{:S(2)}, u32[]{:S(2)}) %collective-permute-start.24) | collective-permute-done | bytes 327712 | tf_op jit(solution)/shard_map/ppermute | solution.py:52
  148.7 4.1 collective-permute-start.25
  152.8 12.0 %collective-permute-done.26.refs_1_.refs_9_ = bf16[512,384]{1,0:T(8,128)(2,1)S(1)} collective-permute-done((bf16[512,384]{1,0:T(8,128)(2,1)S(1)}, bf16[512,384]{1,0:T(8,128)(2,1)S(1)}, u32[]{:S(2)}, u32[]{:S(2)}) %collective-permute-start.26) | collective-permute-done | bytes 393248 | tf_op jit(solution)/shard_map/ppermute | solution.py:52
  165.5 10.6 %shard_map.240 = (bf16[512,512]{1,0:T(8,128)(2,1)}, bf16[512,512]{1,0:T(8,128)(2,1)}, f32[8,512]{1,0:T(8,128)}, bf16[64,2560]{1,0:T(8,128)(2,1)}, bf16[64,2560]{...) custom-call(s32[5]{0:T(128)} %stack.36.pos, ...), custom_call_target="tpu_custom_call" | custom-call | flops 12000000000 | tf_op jit(solution)/shard_map/pallas_call | solution.py:463
  185.2 8.5 %collective-permute-done.34.three = bf16[64,2560]{1,0:T(8,128)(2,1)S(1)} collective-permute-done((bf16[64,2560]{1,0:T(8,128)(2,1)}, bf16[64,2560]{1,0:T(8,128)(2,1)S(1)}, u32[]{:S(2)}, u32[]{:S(2)}) %collective-permute-start.34) | collective-permute-done | bytes 327712 | tf_op jit(solution)/shard_map/ppermute | solution.py:52
  196.8 3.6 collective-permute-done.27.refs_14_.refs_10_
  206.5 12.5 %collective-permute-done.39.one = bf16[64,2560]{1,0:T(8,128)(2,1)S(1)} collective-permute-done((bf16[64,2560]{1,0:T(8,128)(2,1)}, bf16[64,2560]{1,0:T(8,128)(2,1)S(1)}, u32[]{:S(2)}, u32[]{:S(2)}) %collective-permute-start.39) | collective-permute-done | bytes 327712 | tf_op jit(solution)/shard_map/ppermute | solution.py:52
  230.3 9.7 %collective-permute-done.42.refs_2_ = bf16[64,2560]{1,0:T(8,128)(2,1)S(1)} collective-permute-done((bf16[64,2560]{1,0:T(8,128)(2,1)}, bf16[64,2560]{1,0:T(8,128)(2,1)S(1)}, u32[]{:S(2)}, u32[]{:S(2)}) %collective-permute-start.42) | collective-permute-done | bytes 327712 | tf_op jit(solution)/shard_map/ppermute | solution.py:52
  240.1 6.0 collective-permute-done.36.refs_15_.refs_11_
  248.4 6.3 collective-permute-done.38.refs_17_.refs_13_
  255.7 15.8 %shard_map.244 = (bf16[512,512]{1,0:T(8,128)(2,1)}, bf16[512,512]{1,0:T(8,128)(2,1)}, bf16[512,512]{1,0:T(8,128)(2,1)}, bf16[512,512]{1,0:T(8,128)(2,1)}, bf16[5...) custom-call(s32[5]{0:T(128)} %stack.36.pos, ...), custom_call_target="tpu_custom_call" | custom-call | flops 17999998976 | tf_op jit(solution)/shard_map/pallas_call | solution.py:528
  276.8 9.1 %collective-permute-done.52.three = bf16[64,2560]{1,0:T(8,128)(2,1)S(1)} collective-permute-done((bf16[64,2560]{1,0:T(8,128)(2,1)}, bf16[64,2560]{1,0:T(8,128)(2,1)S(1)}, u32[]{:S(2)}, u32[]{:S(2)}) %collective-permute-start.52) | collective-permute-done | bytes 327712 | tf_op jit(solution)/shard_map/ppermute | solution.py:52
  289.8 3.6 collective-permute-start.54
  293.4 11.8 %collective-permute-done.53.one = bf16[64,2560]{1,0:T(8,128)(2,1)S(1)} collective-permute-done((bf16[64,2560]{1,0:T(8,128)(2,1)}, bf16[64,2560]{1,0:T(8,128)(2,1)S(1)}, u32[]{:S(2)}, u32[]{:S(2)}) %collective-permute-start.53) | collective-permute-done | bytes 327712 | tf_op jit(solution)/shard_map/ppermute | solution.py:52
  311.7 4.0 collective-permute-start.55
  315.7 9.3 %collective-permute-done.56.refs_2_ = bf16[64,2560]{1,0:T(8,128)(2,1)S(1)} collective-permute-done((bf16[64,2560]{1,0:T(8,128)(2,1)}, bf16[64,2560]{1,0:T(8,128)(2,1)S(1)}, u32[]{:S(2)}, u32[]{:S(2)}) %collective-permute-start.56) | collective-permute-done | bytes 327712 | tf_op jit(solution)/shard_map/ppermute | solution.py:52
  328.8 6.8 %collective-permute-done.57.refs_3_ = bf16[64,2560]{1,0:T(8,128)(2,1)S(1)} collective-permute-done((bf16[64,2560]{1,0:T(8,128)(2,1)S(1)}, bf16[64,2560]{1,0:T(8,128)(2,1)S(1)}, u32[]{:S(2)}, u32[]{:S(2)}) %collective-permute-start.57) | collective-permute-done | bytes 327712 | tf_op jit(solution)/shard_map/ppermute | solution.py:52
  338.1 7.6 %shard_map.248 = (bf16[4,1280,512]{2,1,0:T(8,128)(2,1)}, bf16[512,2560]{1,0:T(8,128)(2,1)}) custom-call(s32[5]{0:T(128)} %stack.36.pos, bf16[64,2560]{1,0:T(8,128)(2,1)} %get-tuple-element.1331.refs_0_.d_own, bf16[64,2560]{1,0:T(8,128)(2,1)} %copy-done.80, bf16[64,2560]{1,0:T(8,128)(2,1)} %copy-done.72, bf16[64,2560]{1,0:T(8,128)(2,1)} %copy-done.84, ...), custom_call_target="tpu_custom_call" | custom-call | flops 7000000000 | tf_op jit(solution)/shard_map/pallas_call | solution.py:605
  345.9 16.9 %shard_map.249 = (bf16[512,896]{1,0:T(8,128)(2,1)}, bf16[512,896]{1,0:T(8,128)(2,1)}, bf16[64,2560]{1,0:T(8,128)(2,1)}, bf16[64,2560]{1,0:T(8,128)(2,1)}, bf16[6...) custom-call(s32[5]{0:T(128)} %stack.36.pos, ...), custom_call_target="tpu_custom_call" | custom-call | flops 16000000000 | tf_op jit(solution)/shard_map/pallas_call | solution.py:559
  367.4 6.4 shard_map.250
  373.8 3.9 collective-permute-done.69.three
  382.1 4.3 collective-permute-start.71
  386.4 6.4 %shard_map.254 = bf16[4,640,896]{2,1,0:T(8,128)(2,1)} custom-call(s32[5]{0:T(128)} %stack.36.pos, bf16[512,2560]{1,0:T(8,128)(2,1)} %get-tuple-element.1346.left, bf16[512,896]{1,0:T(8,128)(2,1)} %get-tuple-element.1347.right_a, bf16[512,896]{1,0:T(8,128)(2,1)} %get-tuple-element.1348.right_b), custom_call_target="tpu_custom_call" | custom-call | flops 7000000000 | tf_op jit(solution)/shard_map/pallas_call | solution.py:619
  392.8 5.5 collective-permute-done.70.one
  404.6 4.1 collective-permute-start.73
  408.7 11.8 %collective-permute-done.74.refs_2_ = bf16[64,2560]{1,0:T(8,128)(2,1)S(1)} collective-permute-done((bf16[64,2560]{1,0:T(8,128)(2,1)S(1)}, bf16[64,2560]{1,0:T(8,128)(2,1)S(1)}, u32[]{:S(2)}, u32[]{:S(2)}) %collective-permute-start.74) | collective-permute-done | bytes 327712 | tf_op jit(solution)/shard_map/ppermute | solution.py:52
  421.1 7.4 %collective-permute-done.75.refs_3_ = bf16[64,2560]{1,0:T(8,128)(2,1)S(1)} collective-permute-done((bf16[64,2560]{1,0:T(8,128)(2,1)S(1)}, bf16[64,2560]{1,0:T(8,128)(2,1)S(1)}, u32[]{:S(2)}, u32[]{:S(2)}) %collective-permute-start.75) | collective-permute-done | bytes 327712 | tf_op jit(solution)/shard_map/ppermute | solution.py:52
  436.4 15.4 %shard_map.255 = (bf16[512,320]{1,0:T(8,128)(2,1)}, f32[512,320]{1,0:T(8,128)}, bf16[512,320]{1,0:T(8,128)(2,1)}, bf16[512,2560]{1,0:T(8,128)(2,1)}) custom-call(s32[5]{0:T(128)} %stack.36.pos, bf16[512,320]{1,0:T(8,128)(2,1)} %get-tuple-element.1407.q_ref, f32[8,512]{1,0:T(8,128)} %get-tuple-element.1408.row_ids, f32[8,512]{1,0:T(8,128)} %get-tuple-element.1409.lse, ...), custom_call_target="tpu_custom_call" | custom-call | flops 17999998976 | tf_op jit(solution)/shard_map/pallas_call | solution.py:704
  453.1 21.5 %reduce-scatter.6.cloned.1.call-done = bf16[640,896]{1,0:T(8,128)(2,1)} async-done(((bf16[2560,896]{1,0:T(8,128)(2,1)}), bf16[640,896]{1,0:T(8,128)(2,1)}) %reduce-scatter.6.cloned.1.call-update) | async-done | bytes 1146896 | tf_op jit(solution)/shard_map/reduce_scatter | solution.py:955
  479.5 3.5 shard_map.256
  483.1 13.5 %shard_map.257 = (bf16[640,512]{1,0:T(8,128)(2,1)}, bf16[640,512]{1,0:T(8,128)(2,1)}, bf16[640,512]{1,0:T(8,128)(2,1)}, bf16[640,512]{1,0:T(8,128)(2,1)}, bf16[6...) custom-call(s32[5]{0:T(128)} %stack.36.pos, ...), custom_call_target="tpu_custom_call" | custom-call | flops 12000000000 | tf_op jit(solution)/shard_map/pallas_call | solution.py:810
  497.5 8.2 %shard_map.258 = (bf16[64,2560]{1,0:T(8,128)(2,1)}, bf16[64,2560]{1,0:T(8,128)(2,1)}, bf16[64,2560]{1,0:T(8,128)(2,1)}, bf16[64,2560]{1,0:T(8,128)(2,1)}, bf16[6...) custom-call(s32[5]{0:T(128)} %stack.36.pos, ...), custom_call_target="tpu_custom_call" | custom-call | flops 8000000000 | tf_op jit(solution)/shard_map/pallas_call | solution.py:749
  510.4 8.6 %collective-permute-start.89 = (bf16[64,2560]{1,0:T(8,128)(2,1)}, bf16[64,2560]{1,0:T(8,128)(2,1)}, u32[]{:S(2)}, u32[]{:S(2)}) collective-permute-start(bf16[64,2560]{1,0:T(8,128)(2,1)} %shard_map.259), channel_id=1, source_target_pairs={{0,8},{8,0},{16,24},{24,16},{1,9},{9,1},{17,25},{25,17},{2,10},{10... | collective-permute-start | bytes 983048 | tf_op jit(solution)/shard_map/ppermute | solution.py:52
  535.3 8.0 %collective-permute-done.96 = bf16[640,512]{1,0:T(8,128)(2,1)S(1)} collective-permute-done((bf16[640,512]{1,0:T(8,128)(2,1)S(1)}, bf16[640,512]{1,0:T(8,128)(2,1)S(1)}, u32[]{:S(2)}, u32[]{:S(2)}) %collective-permute-start.96) | collective-permute-done | bytes 655392 | tf_op jit(solution)/shard_map/ppermute | solution.py:52
  546.0 22.0 %collective-permute-done.91.two = bf16[64,2560]{1,0:T(8,128)(2,1)S(1)} collective-permute-done((bf16[64,2560]{1,0:T(8,128)(2,1)S(1)}, bf16[64,2560]{1,0:T(8,128)(2,1)S(1)}, u32[]{:S(2)}, u32[]{:S(2)}) %collective-permute-start.91) | collective-permute-done | bytes 327712 | tf_op jit(solution)/shard_map/ppermute | solution.py:52
  571.6 4.9 collective-permute-done.94
  589.7 17.7 %collective-permute-done.103.refs_3_ = bf16[320,512]{1,0:T(8,128)(2,1)S(1)} collective-permute-done((bf16[320,512]{1,0:T(8,128)(2,1)S(1)}, bf16[320,512]{1,0:T(8,128)(2,1)S(1)}, u32[]{:S(2)}, u32[]{:S(2)}) %collective-permute-start.103) | collective-permute-done | bytes 327712 | tf_op jit(solution)/shard_map/ppermute | solution.py:52
  607.4 9.0 %collective-permute-done.102.refs_2_ = bf16[320,512]{1,0:T(8,128)(2,1)S(1)} collective-permute-done((bf16[320,512]{1,0:T(8,128)(2,1)S(1)}, bf16[320,512]{1,0:T(8,128)(2,1)S(1)}, u32[]{:S(2)}, u32[]{:S(2)}) %collective-permute-start.102) | collective-permute-done | bytes 327712 | tf_op jit(solution)/shard_map/ppermute | solution.py:52
  619.6 4.4 shard_map.266
  626.2 4.1 shard_map.265
  (474 shorter events, 193.3 us)
Async XLA Ops:
  7.2 169.0 %all-gather.5.cloned.1.call-start = ((), (), s32[]{:S(2)}) async-start(), calls=%async_computation.6 | async-start | bytes 9011200 | tf_op jit(solution)/shard_map/all_gather | solution.py:951
  24.1 37.4 %collective-permute-start.1 = (bf16[320,1408]{1,0:T(8,128)(2,1)}, bf16[320,1408]{1,0:T(8,128)(2,1)S(1)}, u32[]{:S(2)}, u32[]{:S(2)}) collective-permute-start(bf16[320,1408]{1,0:T(8,128)(2,1)} %get-tuple-element.832), channel_id=1, source_target_pairs={{0,8},{8,0},{16,24},{24,16},{1,9},{9,1},{17,25},{25,17},{2,10},{10... | collective-permute-start | bytes 2703368 | tf_op jit(solution)/shard_map/ppermute | solution.py:52
  25.8 27.7 %collective-permute-start.5 = (bf16[320,512]{1,0:T(8,128)(2,1)S(1)}, bf16[320,512]{1,0:T(8,128)(2,1)}, u32[]{:S(2)}, u32[]{:S(2)}) collective-permute-start(bf16[320,512]{1,0:T(8,128)(2,1)S(1)} %copy-done.93), channel_id=1, source_target_pairs={{0,16},{8,24},{16,0},{24,8},{1,17},{9,25},{17,1},{25,9},{2,18},{10... | collective-permute-start | bytes 983048 | tf_op jit(solution)/shard_map/ppermute | solution.py:52
  28.4 33.0 %collective-permute-start.6 = (bf16[320,512]{1,0:T(8,128)(2,1)S(1)}, bf16[320,512]{1,0:T(8,128)(2,1)S(1)}, u32[]{:S(2)}, u32[]{:S(2)}) collective-permute-start(bf16[320,512]{1,0:T(8,128)(2,1)S(1)} %copy-done.67), channel_id=1, source_target_pairs={{0,24},{8,16},{16,8},{24,0},{1,25},{9,17},{17,9},{25,1},{2,26},{10... | collective-permute-start | bytes 983048 | tf_op jit(solution)/shard_map/ppermute | solution.py:52
  28.5 32.9 %collective-permute-start.3 = (bf16[320,512]{1,0:T(8,128)(2,1)S(1)}, bf16[320,512]{1,0:T(8,128)(2,1)S(1)}, u32[]{:S(2)}, u32[]{:S(2)}) collective-permute-start(bf16[320,512]{1,0:T(8,128)(2,1)S(1)} %copy-done.32), channel_id=1, source_target_pairs={{0,2},{2,0},{1,3},{3,1},{4,6},{6,4},{5,7},{7,5},{8,10},{10,8},{9,1... | collective-permute-start | bytes 983048 | tf_op jit(solution)/shard_map/ppermute | solution.py:52
  30.1 31.3 %collective-permute-start.2 = (bf16[320,512]{1,0:T(8,128)(2,1)S(1)}, bf16[320,512]{1,0:T(8,128)(2,1)S(1)}, u32[]{:S(2)}, u32[]{:S(2)}) collective-permute-start(bf16[320,512]{1,0:T(8,128)(2,1)S(1)} %copy-done.32), channel_id=1, source_target_pairs={{0,4},{4,0},{1,5},{5,1},{2,6},{6,2},{3,7},{7,3},{8,12},{12,8},{9,1... | collective-permute-start | bytes 983048 | tf_op jit(solution)/shard_map/ppermute | solution.py:52
  63.6 184.8 %all-gather.7.cloned.1.call-start = ((), (), s32[]{:S(2)}) async-start(), calls=%async_computation.7 | async-start | bytes 4505600 | tf_op jit(solution)/shard_map/all_gather | solution.py:951
  67.5 21.0 %collective-permute-start.8 = (bf16[320,512]{1,0:T(8,128)(2,1)S(1)}, bf16[320,512]{1,0:T(8,128)(2,1)S(1)}, u32[]{:S(2)}, u32[]{:S(2)}) collective-permute-start(bf16[320,512]{1,0:T(8,128)(2,1)S(1)} %collective-permute-done.refs_10_.refs_4_.refs_12_.refs_6_.refs_2_), channel_id=1, source_target_pairs={{0,4},{4,0},{1,5},{5,1},{2,6},{6,2},{3,7},{7,3},{8,12},{12,8},{9,1... | collective-permute-start | bytes 983048 | tf_op jit(solution)/shard_map/ppermute | solution.py:52
  68.0 33.6 %collective-permute-start.18 = (bf16[64,2688]{1,0:T(8,128)(2,1)S(1)}, bf16[64,2688]{1,0:T(8,128)(2,1)S(1)}, u32[]{:S(2)}, u32[]{:S(2)}) collective-permute-start(bf16[64,2688]{1,0:T(8,128)(2,1)S(1)} %copy-done.24), channel_id=1, source_target_pairs={{0,16},{8,24},{16,0},{24,8},{1,17},{9,25},{17,1},{25,9},{2,18},{10... | collective-permute-start | bytes 1032200 | tf_op jit(solution)/shard_map/ppermute | solution.py:52
  70.6 21.4 %collective-permute-start.15 = (bf16[320,512]{1,0:T(8,128)(2,1)S(1)}, bf16[320,512]{1,0:T(8,128)(2,1)S(1)}, u32[]{:S(2)}, u32[]{:S(2)}) collective-permute-start(bf16[320,512]{1,0:T(8,128)(2,1)S(1)} %collective-permute-done.6.refs_14_.refs_8_.refs_16_.refs_10_.refs_6_), channel_id=1, source_target_pairs={{0,2},{2,0},{1,3},{3,1},{4,6},{6,4},{5,7},{7,5},{8,10},{10,8},{9,1... | collective-permute-start | bytes 983048 | tf_op jit(solution)/shard_map/ppermute | solution.py:52
  75.2 25.9 %collective-permute-start.10 = (bf16[320,512]{1,0:T(8,128)(2,1)S(1)}, bf16[320,512]{1,0:T(8,128)(2,1)S(1)}, u32[]{:S(2)}, u32[]{:S(2)}) collective-permute-start(bf16[320,512]{1,0:T(8,128)(2,1)S(1)} %collective-permute-done.6.refs_14_.refs_8_.refs_16_.refs_10_.refs_6_), channel_id=1, source_target_pairs={{0,4},{4,0},{1,5},{5,1},{2,6},{6,2},{3,7},{7,3},{8,12},{12,8},{9,1... | collective-permute-start | bytes 983048 | tf_op jit(solution)/shard_map/ppermute | solution.py:52
  78.0 25.1 %collective-permute-start.13 = (bf16[320,512]{1,0:T(8,128)(2,1)}, bf16[320,512]{1,0:T(8,128)(2,1)S(1)}, u32[]{:S(2)}, u32[]{:S(2)}) collective-permute-start(bf16[320,512]{1,0:T(8,128)(2,1)} %collective-permute-done.5.refs_12_.refs_6_.refs_14_.refs_8_.refs_4_), channel_id=1, source_target_pairs={{0,2},{2,0},{1,3},{3,1},{4,6},{6,4},{5,7},{7,5},{8,10},{10,8},{9,1... | collective-permute-start | bytes 983048 | tf_op jit(solution)/shard_map/ppermute | solution.py:52
  88.5 28.1 %collective-permute-start.7 = (bf16[320,896]{1,0:T(8,128)(2,1)S(1)}, bf16[320,896]{1,0:T(8,128)(2,1)S(1)}, u32[]{:S(2)}, u32[]{:S(2)}) collective-permute-start(bf16[320,896]{1,0:T(8,128)(2,1)S(1)} %copy-done.18), channel_id=1, source_target_pairs={{0,16},{8,24},{16,0},{24,8},{1,17},{9,25},{17,1},{25,9},{2,18},{10... | collective-permute-start | bytes 1720328 | tf_op jit(solution)/shard_map/ppermute | solution.py:52
  92.0 23.6 %collective-permute-start.20 = (bf16[64,2688]{1,0:T(8,128)(2,1)S(1)}, bf16[64,2688]{1,0:T(8,128)(2,1)S(1)}, u32[]{:S(2)}, u32[]{:S(2)}) collective-permute-start(bf16[64,2688]{1,0:T(8,128)(2,1)S(1)} %copy-done.24), channel_id=1, source_target_pairs={{0,1},{1,0},{2,3},{3,2},{4,5},{5,4},{6,7},{7,6},{8,9},{9,8},{10,11... | collective-permute-start | bytes 1032200 | tf_op jit(solution)/shard_map/ppermute | solution.py:52
  129.7 17.5 %collective-permute-start.24 = (bf16[320,512]{1,0:T(8,128)(2,1)S(1)}, bf16[320,512]{1,0:T(8,128)(2,1)S(1)}, u32[]{:S(2)}, u32[]{:S(2)}) collective-permute-start(bf16[320,512]{1,0:T(8,128)(2,1)S(1)} %copy-done.56), channel_id=1, source_target_pairs={{0,16},{8,24},{16,0},{24,8},{1,17},{9,25},{17,1},{25,9},{2,18},{10... | collective-permute-start | bytes 983048 | tf_op jit(solution)/shard_map/ppermute | solution.py:52
  148.2 282.7 %reduce-scatter.8.cloned.1.call-start = ((), (), s32[]{:S(2)}) async-start(), calls=%async_computation.5 | async-start | bytes 6553600 | tf_op jit(solution)/shard_map/reduce_scatter | solution.py:955
  148.7 27.5 %collective-permute-start.25 = (bf16[320,896]{1,0:T(8,128)(2,1)S(1)}, bf16[320,896]{1,0:T(8,128)(2,1)S(1)}, u32[]{:S(2)}, u32[]{:S(2)}) collective-permute-start(bf16[320,896]{1,0:T(8,128)(2,1)S(1)} %copy-done.17), channel_id=1, source_target_pairs={{0,24},{8,16},{16,8},{24,0},{1,25},{9,17},{17,9},{25,1},{2,26},{10... | collective-permute-start | bytes 1720328 | tf_op jit(solution)/shard_map/ppermute | solution.py:52
  176.3 25.8 %collective-permute-start.29 = (bf16[320,896]{1,0:T(8,128)(2,1)S(1)}, bf16[320,896]{1,0:T(8,128)(2,1)S(1)}, u32[]{:S(2)}, u32[]{:S(2)}) collective-permute-start(bf16[320,896]{1,0:T(8,128)(2,1)S(1)} %collective-permute-done.25.refs_10_.refs_6_), channel_id=1, source_target_pairs={{0,2},{2,0},{1,3},{3,1},{4,6},{6,4},{5,7},{7,5},{8,10},{10,8},{9,1... | collective-permute-start | bytes 1720328 | tf_op jit(solution)/shard_map/ppermute | solution.py:52
  179.4 23.2 %collective-permute-start.28 = (bf16[320,896]{1,0:T(8,128)(2,1)S(1)}, bf16[320,896]{1,0:T(8,128)(2,1)S(1)}, u32[]{:S(2)}, u32[]{:S(2)}) collective-permute-start(bf16[320,896]{1,0:T(8,128)(2,1)S(1)} %collective-permute-done.25.refs_10_.refs_6_), channel_id=1, source_target_pairs={{0,4},{4,0},{1,5},{5,1},{2,6},{6,2},{3,7},{7,3},{8,12},{12,8},{9,1... | collective-permute-start | bytes 1720328 | tf_op jit(solution)/shard_map/ppermute | solution.py:52
  183.5 16.9 %collective-permute-start.27 = (bf16[320,512]{1,0:T(8,128)(2,1)S(1)}, bf16[320,512]{1,0:T(8,128)(2,1)S(1)}, u32[]{:S(2)}, u32[]{:S(2)}) collective-permute-start(bf16[320,512]{1,0:T(8,128)(2,1)S(1)} %copy-done.52), channel_id=1, source_target_pairs={{0,24},{8,16},{16,8},{24,0},{1,25},{9,17},{17,9},{25,1},{2,26},{10... | collective-permute-start | bytes 983048 | tf_op jit(solution)/shard_map/ppermute | solution.py:52
  203.8 17.4 %collective-permute-start.40 = (bf16[64,2560]{1,0:T(8,128)(2,1)}, bf16[64,2560]{1,0:T(8,128)(2,1)S(1)}, u32[]{:S(2)}, u32[]{:S(2)}) collective-permute-start(bf16[64,2560]{1,0:T(8,128)(2,1)} %get-tuple-element.1016), channel_id=1, source_target_pairs={{0,16},{8,24},{16,0},{24,8},{1,17},{9,25},{17,1},{25,9},{2,18},{10... | collective-permute-start | bytes 983048 | tf_op jit(solution)/shard_map/ppermute | solution.py:52
  224.8 22.8 %collective-permute-start.35 = (bf16[320,896]{1,0:T(8,128)(2,1)S(1)}, bf16[320,896]{1,0:T(8,128)(2,1)S(1)}, u32[]{:S(2)}, u32[]{:S(2)}) collective-permute-start(bf16[320,896]{1,0:T(8,128)(2,1)S(1)} %collective-permute-done.29.refs_12_.refs_8_), channel_id=1, source_target_pairs={{0,4},{4,0},{1,5},{5,1},{2,6},{6,2},{3,7},{7,3},{8,12},{12,8},{9,1... | collective-permute-start | bytes 1720328 | tf_op jit(solution)/shard_map/ppermute | solution.py:52
  226.1 20.1 %collective-permute-start.36 = (bf16[320,512]{1,0:T(8,128)(2,1)S(1)}, bf16[320,512]{1,0:T(8,128)(2,1)S(1)}, u32[]{:S(2)}, u32[]{:S(2)}) collective-permute-start(bf16[320,512]{1,0:T(8,128)(2,1)S(1)} %collective-permute-done.27.refs_14_.refs_10_), channel_id=1, source_target_pairs={{0,4},{4,0},{1,5},{5,1},{2,6},{6,2},{3,7},{7,3},{8,12},{12,8},{9,1... | collective-permute-start | bytes 983048 | tf_op jit(solution)/shard_map/ppermute | solution.py:52
  227.7 20.0 %collective-permute-start.41 = (bf16[64,2560]{1,0:T(8,128)(2,1)}, bf16[64,2560]{1,0:T(8,128)(2,1)S(1)}, u32[]{:S(2)}, u32[]{:S(2)}) collective-permute-start(bf16[64,2560]{1,0:T(8,128)(2,1)} %get-tuple-element.1043.refs_0_), channel_id=1, source_target_pairs={{0,8},{8,0},{16,24},{24,16},{1,9},{9,1},{17,25},{25,17},{2,10},{10... | collective-permute-start | bytes 983048 | tf_op jit(solution)/shard_map/ppermute | solution.py:52
  276.8 16.6 %collective-permute-start.48 = (bf16[64,2560]{1,0:T(8,128)(2,1)S(1)}, bf16[64,2560]{1,0:T(8,128)(2,1)S(1)}, u32[]{:S(2)}, u32[]{:S(2)}) collective-permute-start(bf16[64,2560]{1,0:T(8,128)(2,1)S(1)} %copy-done.71), channel_id=1, source_target_pairs={{0,1},{1,0},{2,3},{3,2},{4,5},{5,4},{6,7},{7,6},{8,9},{9,8},{10,11... | collective-permute-start | bytes 983048 | tf_op jit(solution)/shard_map/ppermute | solution.py:52
  311.7 17.1 %collective-permute-start.55 = (bf16[64,2560]{1,0:T(8,128)(2,1)}, bf16[64,2560]{1,0:T(8,128)(2,1)S(1)}, u32[]{:S(2)}, u32[]{:S(2)}) collective-permute-start(bf16[64,2560]{1,0:T(8,128)(2,1)} %get-tuple-element.1331.refs_0_.d_own), channel_id=1, source_target_pairs={{0,8},{8,0},{16,24},{24,16},{1,9},{9,1},{17,25},{25,17},{2,10},{10... | collective-permute-start | bytes 983048 | tf_op jit(solution)/shard_map/ppermute | solution.py:52
  345.7 128.9 %reduce-scatter.6.cloned.1.call-start = ((), (), s32[]{:S(2)}) async-start(), calls=%async_computation.4 | async-start | bytes 5734400 | tf_op jit(solution)/shard_map/reduce_scatter | solution.py:955
  363.3 17.4 %collective-permute-start.65 = (bf16[64,2560]{1,0:T(8,128)(2,1)}, bf16[64,2560]{1,0:T(8,128)(2,1)S(1)}, u32[]{:S(2)}, u32[]{:S(2)}) collective-permute-start(bf16[64,2560]{1,0:T(8,128)(2,1)} %get-tuple-element.1292), channel_id=1, source_target_pairs={{0,1},{1,0},{2,3},{3,2},{4,5},{5,4},{6,7},{7,6},{8,9},{9,8},{10,11... | collective-permute-start | bytes 983048 | tf_op jit(solution)/shard_map/ppermute | solution.py:52
  381.4 200.3 %reduce-scatter.4.cloned.1.call-start = ((), (), s32[]{:S(2)}) async-start(), calls=%async_computation.3 | async-start | bytes 5734400 | tf_op jit(solution)/shard_map/reduce_scatter | solution.py:955
  403.9 16.6 %collective-permute-start.74 = (bf16[64,2560]{1,0:T(8,128)(2,1)S(1)}, bf16[64,2560]{1,0:T(8,128)(2,1)S(1)}, u32[]{:S(2)}, u32[]{:S(2)}) collective-permute-start(bf16[64,2560]{1,0:T(8,128)(2,1)S(1)} %copy-done.63), channel_id=1, source_target_pairs={{0,16},{8,24},{16,0},{24,8},{1,17},{9,25},{17,1},{25,9},{2,18},{10... | collective-permute-start | bytes 983048 | tf_op jit(solution)/shard_map/ppermute | solution.py:52
  433.0 18.8 %collective-permute-start.81 = (bf16[320,512]{1,0:T(8,128)(2,1)S(1)}, bf16[320,512]{1,0:T(8,128)(2,1)S(1)}, u32[]{:S(2)}, u32[]{:S(2)}) collective-permute-start(bf16[320,512]{1,0:T(8,128)(2,1)S(1)} %get-tuple-element.1632), channel_id=1, source_target_pairs={{0,24},{8,16},{16,8},{24,0},{1,25},{9,17},{17,9},{25,1},{2,26},{10... | collective-permute-start | bytes 983048 | tf_op jit(solution)/shard_map/ppermute | solution.py:52
  451.9 26.9 %collective-permute-start.83 = (bf16[512,320]{1,0:T(8,128)(2,1)}, bf16[512,320]{1,0:T(8,128)(2,1)S(1)}, u32[]{:S(2)}, u32[]{:S(2)}) collective-permute-start(bf16[512,320]{1,0:T(8,128)(2,1)} %get-tuple-element.1462), channel_id=1, source_target_pairs={{0,4},{4,0},{1,5},{5,1},{2,6},{6,2},{3,7},{7,3},{8,12},{12,8},{9,1... | collective-permute-start | bytes 983048 | tf_op jit(solution)/shard_map/ppermute | solution.py:52
  452.4 30.7 %collective-permute-start.82 = (bf16[320,512]{1,0:T(8,128)(2,1)S(1)}, bf16[320,512]{1,0:T(8,128)(2,1)S(1)}, u32[]{:S(2)}, u32[]{:S(2)}) collective-permute-start(bf16[320,512]{1,0:T(8,128)(2,1)S(1)} %get-tuple-element.1457), channel_id=1, source_target_pairs={{0,16},{8,24},{16,0},{24,8},{1,17},{9,25},{17,1},{25,9},{2,18},{10... | collective-permute-start | bytes 983048 | tf_op jit(solution)/shard_map/ppermute | solution.py:52
  475.9 20.7 %collective-permute-start.84 = (bf16[320,896]{1,0:T(8,128)(2,1)S(1)}, bf16[320,896]{1,0:T(8,128)(2,1)S(1)}, u32[]{:S(2)}, u32[]{:S(2)}) collective-permute-start(bf16[320,896]{1,0:T(8,128)(2,1)S(1)} %get-tuple-element.1636), channel_id=1, source_target_pairs={{0,24},{8,16},{16,8},{24,0},{1,25},{9,17},{17,9},{25,1},{2,26},{10... | collective-permute-start | bytes 1720328 | tf_op jit(solution)/shard_map/ppermute | solution.py:52
  496.6 26.7 %collective-permute-start.93 = (bf16[640,512]{1,0:T(8,128)(2,1)}, bf16[640,512]{1,0:T(8,128)(2,1)S(1)}, u32[]{:S(2)}, u32[]{:S(2)}) collective-permute-start(bf16[640,512]{1,0:T(8,128)(2,1)} %get-tuple-element.1596), channel_id=1, source_target_pairs={{0,2},{2,0},{1,3},{3,1},{4,6},{6,4},{5,7},{7,5},{8,10},{10,8},{9,1... | collective-permute-start | bytes 1966088 | tf_op jit(solution)/shard_map/ppermute | solution.py:52
  505.8 17.7 %collective-permute-start.86 = (bf16[64,2560]{1,0:T(8,128)(2,1)}, bf16[64,2560]{1,0:T(8,128)(2,1)S(1)}, u32[]{:S(2)}, u32[]{:S(2)}) collective-permute-start(bf16[64,2560]{1,0:T(8,128)(2,1)} %get-tuple-element.1569), channel_id=1, source_target_pairs={{0,1},{1,0},{2,3},{3,2},{4,5},{5,4},{6,7},{7,6},{8,9},{9,8},{10,11... | collective-permute-start | bytes 983048 | tf_op jit(solution)/shard_map/ppermute | solution.py:52
  506.3 17.6 %collective-permute-start.87 = (bf16[64,2560]{1,0:T(8,128)(2,1)}, bf16[64,2560]{1,0:T(8,128)(2,1)S(1)}, u32[]{:S(2)}, u32[]{:S(2)}) collective-permute-start(bf16[64,2560]{1,0:T(8,128)(2,1)} %get-tuple-element.1571), channel_id=1, source_target_pairs={{0,1},{1,0},{2,3},{3,2},{4,5},{5,4},{6,7},{7,6},{8,9},{9,8},{10,11... | collective-permute-start | bytes 983048 | tf_op jit(solution)/shard_map/ppermute | solution.py:52
  510.4 16.9 %collective-permute-start.89 = (bf16[64,2560]{1,0:T(8,128)(2,1)}, bf16[64,2560]{1,0:T(8,128)(2,1)}, u32[]{:S(2)}, u32[]{:S(2)}) collective-permute-start(bf16[64,2560]{1,0:T(8,128)(2,1)} %shard_map.259), channel_id=1, source_target_pairs={{0,8},{8,0},{16,24},{24,16},{1,9},{9,1},{17,25},{25,17},{2,10},{10... | collective-permute-start | bytes 983048 | tf_op jit(solution)/shard_map/ppermute | solution.py:52
  519.6 23.7 %collective-permute-start.96 = (bf16[640,512]{1,0:T(8,128)(2,1)S(1)}, bf16[640,512]{1,0:T(8,128)(2,1)S(1)}, u32[]{:S(2)}, u32[]{:S(2)}) collective-permute-start(bf16[640,512]{1,0:T(8,128)(2,1)S(1)} %copy-done.11), channel_id=1, source_target_pairs={{0,4},{4,0},{1,5},{5,1},{2,6},{6,2},{3,7},{7,3},{8,12},{12,8},{9,1... | collective-permute-start | bytes 1966088 | tf_op jit(solution)/shard_map/ppermute | solution.py:52
  523.5 48.1 %collective-permute-start.92 = (bf16[640,512]{1,0:T(8,128)(2,1)S(1)}, bf16[640,512]{1,0:T(8,128)(2,1)S(1)}, u32[]{:S(2)}, u32[]{:S(2)}) collective-permute-start(bf16[640,512]{1,0:T(8,128)(2,1)S(1)} %copy-done.10), channel_id=1, source_target_pairs={{0,2},{2,0},{1,3},{3,1},{4,6},{6,4},{5,7},{7,5},{8,10},{10,8},{9,1... | collective-permute-start | bytes 1966088 | tf_op jit(solution)/shard_map/ppermute | solution.py:52
  523.9 52.8 %collective-permute-start.95 = (bf16[640,512]{1,0:T(8,128)(2,1)S(1)}, bf16[640,512]{1,0:T(8,128)(2,1)S(1)}, u32[]{:S(2)}, u32[]{:S(2)}) collective-permute-start(bf16[640,512]{1,0:T(8,128)(2,1)S(1)} %copy-done.9), channel_id=1, source_target_pairs={{0,4},{4,0},{1,5},{5,1},{2,6},{6,2},{3,7},{7,3},{8,12},{12,8},{9,1... | collective-permute-start | bytes 1966088 | tf_op jit(solution)/shard_map/ppermute | solution.py:52
  527.3 49.1 %collective-permute-start.94 = (bf16[640,512]{1,0:T(8,128)(2,1)S(1)}, bf16[640,512]{1,0:T(8,128)(2,1)S(1)}, u32[]{:S(2)}, u32[]{:S(2)}) collective-permute-start(bf16[640,512]{1,0:T(8,128)(2,1)S(1)} %add_convert_fusion.4), channel_id=1, source_target_pairs={{0,4},{4,0},{1,5},{5,1},{2,6},{6,2},{3,7},{7,3},{8,12},{12,8},{9,1... | collective-permute-start | bytes 1966088 | tf_op jit(solution)/shard_map/ppermute | solution.py:52
  543.3 24.7 %collective-permute-start.91 = (bf16[64,2560]{1,0:T(8,128)(2,1)S(1)}, bf16[64,2560]{1,0:T(8,128)(2,1)S(1)}, u32[]{:S(2)}, u32[]{:S(2)}) collective-permute-start(bf16[64,2560]{1,0:T(8,128)(2,1)S(1)} %copy-done.92), channel_id=1, source_target_pairs={{0,16},{8,24},{16,0},{24,8},{1,17},{9,25},{17,1},{25,9},{2,18},{10... | collective-permute-start | bytes 983048 | tf_op jit(solution)/shard_map/ppermute | solution.py:52
  543.5 33.3 %collective-permute-start.97 = (bf16[640,512]{1,0:T(8,128)(2,1)S(1)}, bf16[640,512]{1,0:T(8,128)(2,1)S(1)}, u32[]{:S(2)}, u32[]{:S(2)}) collective-permute-start(bf16[640,512]{1,0:T(8,128)(2,1)S(1)} %add_convert_fusion.1), channel_id=1, source_target_pairs={{0,2},{2,0},{1,3},{3,1},{4,6},{6,4},{5,7},{7,5},{8,10},{10,8},{9,1... | collective-permute-start | bytes 1966088 | tf_op jit(solution)/shard_map/ppermute | solution.py:52
  583.8 32.5 %collective-permute-start.98 = (bf16[320,896]{1,0:T(8,128)(2,1)S(1)}, bf16[320,896]{1,0:T(8,128)(2,1)S(1)}, u32[]{:S(2)}, u32[]{:S(2)}) collective-permute-start(bf16[320,896]{1,0:T(8,128)(2,1)S(1)} %get-tuple-element.1603), channel_id=1, source_target_pairs={{0,8},{8,0},{16,24},{24,16},{1,9},{9,1},{17,25},{25,17},{2,10},{10... | collective-permute-start | bytes 1720328 | tf_op jit(solution)/shard_map/ppermute | solution.py:52
  583.9 23.5 %collective-permute-start.103 = (bf16[320,512]{1,0:T(8,128)(2,1)S(1)}, bf16[320,512]{1,0:T(8,128)(2,1)S(1)}, u32[]{:S(2)}, u32[]{:S(2)}) collective-permute-start(bf16[320,512]{1,0:T(8,128)(2,1)S(1)} %get-tuple-element.1640), channel_id=1, source_target_pairs={{0,24},{8,16},{16,8},{24,0},{1,25},{9,17},{17,9},{25,1},{2,26},{10... | collective-permute-start | bytes 983048 | tf_op jit(solution)/shard_map/ppermute | solution.py:52
  586.5 29.8 %collective-permute-start.102 = (bf16[320,512]{1,0:T(8,128)(2,1)S(1)}, bf16[320,512]{1,0:T(8,128)(2,1)S(1)}, u32[]{:S(2)}, u32[]{:S(2)}) collective-permute-start(bf16[320,512]{1,0:T(8,128)(2,1)S(1)} %get-tuple-element.1641), channel_id=1, source_target_pairs={{0,16},{8,24},{16,0},{24,8},{1,17},{9,25},{17,1},{25,9},{2,18},{10... | collective-permute-start | bytes 983048 | tf_op jit(solution)/shard_map/ppermute | solution.py:52
  589.6 26.8 %collective-permute-start.101 = (bf16[64,2560]{1,0:T(8,128)(2,1)S(1)}, bf16[64,2560]{1,0:T(8,128)(2,1)S(1)}, u32[]{:S(2)}, u32[]{:S(2)}) collective-permute-start(bf16[64,2560]{1,0:T(8,128)(2,1)S(1)} %collective-permute-done.100.p2), channel_id=1, source_target_pairs={{0,1},{1,0},{2,3},{3,2},{4,5},{5,4},{6,7},{7,6},{8,9},{9,8},{10,11... | collective-permute-start | bytes 983048 | tf_op jit(solution)/shard_map/ppermute | solution.py:52
  (183 other events, 1919.4 us)
Sparse Core Ops, SparseCore 0:
  63.7 104.3 all-gather.4
  170.5 57.1 all-gather.6
  345.8 61.4 reduce-scatter.7
  410.2 64.2 reduce-scatter.5
  477.5 79.8 reduce-scatter.3

commit v6 on v5

--- a/solution.py
+++ b/solution.py
@@ -171,23 +171,23 @@
     return pl.ds(pl.multiple_of(((pos[1] ^ k) * inner + (pos[2] ^ j)) * depth, 16), depth)
 
 
-def piece_copies(pos, inner, pieces, store, sem, i, back=False):
+def piece_copies(pos, inner, pieces, store, sem, i, lanes):
     half = inner // 2
     depth = store.shape[1] // (PARTS * inner)
     copies = []
     for k in range(PARTS):
         for j in range(inner):
-            ends = (
-                pieces[2 * k + j // half].at[pl.ds((j % half) * depth, depth)],
-                store.at[i, spot_of(pos, k, j, inner, depth)],
+            piece = pieces[2 * k + j // half].at[pl.ds((j % half) * depth, depth), lanes]
+            n = (i * PARTS + k) * inner + j
+            copies.append(
+                pltpu.make_async_copy(piece, store.at[i, spot_of(pos, k, j, inner, depth)], sem.at[n])
             )
-            n = (i * PARTS + k) * inner + j
-            copies.append(pltpu.make_async_copy(*(ends[::-1] if back else ends), sem.at[n]))
     return copies
 
 
-def fetch(pos, inner, pieces, store, sem):
-    copies = [piece_copies(pos, inner, pieces[8 * i : 8 * i + 8], store, sem, i) for i in range(2)]
+def fetch(pos, inner, pieces, store, sem, start=0):
+    lanes = pl.ds(start, store.shape[2])
+    copies = [piece_copies(pos, inner, pieces[8 * i : 8 * i + 8], store, sem, i, lanes) for i in range(2)]
     return start_all(copies)
 
 
@@ -237,19 +237,22 @@
     return call(first_sum_body, shape(mine.shape), [VM] * 2, VM)(mine, got)
 
 
-def second_sum_body(mine_one, got_one, mine_two, got_two, three, one, two):
-    one[...] = (mine_one[...].astype(F32) + got_one[...].astype(F32)).astype(BF)
-    two[...] = (mine_two[...].astype(F32) + got_two[...].astype(F32) + three[...].astype(F32)).astype(BF)
+def second_sum_body(mine_one, mine_two, got, three, one, two):
+    n = one.shape[0]
+    one[...] = (mine_one[...].astype(F32) + got[pl.ds(n, n), :].astype(F32)).astype(BF)
+    value = mine_two[...].astype(F32) + got[pl.ds(2 * n, n), :].astype(F32)
+    two[...] = (value + three[...].astype(F32)).astype(BF)
 
 
 def second_sum(mine, got, three):
-    return call(second_sum_body, [shape(three.shape)] * 2, [VM] * 5, [VM] * 2)(
-        mine[1], got[1], mine[2], got[2], three
+    return call(second_sum_body, [shape(three.shape)] * 2, [VM] * 4, [VM] * 2)(
+        mine[1], mine[2], got, three
     )
 
 
-def last_sum(parts):
-    return functools.reduce(jnp.add, [ref[...].astype(F32) for ref in parts])
+def last_sum(mine, got, one, two):
+    first = mine[...].astype(F32) + got[pl.ds(0, mine.shape[0]), :].astype(F32)
+    return first + one[...].astype(F32) + two[...].astype(F32)
 
 
 def mean_scale(value):
@@ -264,7 +267,7 @@
 
 
 def after_attn_body(mine, got, one, two, x_own, gain, middle, n_own, total):
-    branch = last_sum((mine, got, one, two))
+    branch = last_sum(mine, got, one, two)
     value = x_own[:, : branch.shape[1]].astype(F32) + branch
     middle[...] = value
     n_own[...] = (value * mean_scale(value) * gain[1:2, :]).astype(BF)
@@ -272,7 +275,7 @@
 
 
 def after_mlp_body(mine, got, one, two, middle, target, d_own, out, total):
-    branch = last_sum((mine, got, one, two))
+    branch = last_sum(mine, got, one, two)
     stream = middle[...] + branch
     d_own[...] = (stream - target[...].astype(F32)).astype(BF)
     out[...] = stream.astype(BF)
@@ -281,7 +284,7 @@
 
 
 def after_feed_back_body(mine, got, one, two, middle, d_own, gain, d_middle, a_own, gain_grad):
-    grad = last_sum((mine, got, one, two))
+    grad = last_sum(mine, got, one, two)
     unit, back = back_norm(grad, middle[...], gain[1:2, :])
     value = d_own[...].astype(F32) + back
     d_middle[...] = value
@@ -290,7 +293,7 @@
 
 
 def after_all_body(mine, got, one, two, x_own, d_middle, gain, out):
-    grad = last_sum((mine, got, one, two))
+    grad = last_sum(mine, got, one, two)
     unit, back = back_norm(grad, x_own[:, : grad.shape[1]].astype(F32), gain[0:1, :])
     out[...] = (d_middle[...] + back).astype(BF)
 
@@ -336,7 +339,7 @@
     for i in range(2):
         if i:
             wait(1)
-        out = dot(first[...], store[i])
+        out = dot(first[...], store[i, :, :384])
         for start in range(0, qw, HEAD_DIM):
             queries.append(rotated(out[:, start : start + HEAD_DIM], cos, sin))
         keys.append(rotated(out[:, qw : qw + HEAD_DIM], cos, sin))
@@ -346,7 +349,7 @@
 
 
 def sems(inner):
-    return pltpu.SemaphoreType.DMA((2 * (PARTS + 1) * inner,))
+    return pltpu.SemaphoreType.DMA((2 * PARTS * inner,))
 
 
 def project(pos, x, cosine, sine, w, qw, inner):
@@ -371,8 +374,13 @@
 
 def out_rows(partial, outs):
     n = outs[0].shape[0]
-    for i, ref in enumerate(outs):
-        ref[...] = partial[i * n : (i + 1) * n].astype(ref.dtype)
+    spots = [(i * n, n) for i in range(4)] + [(7 * n, n), (4 * n, 3 * n)]
+    for (start, size), ref in zip(spots, outs):
+        ref[...] = partial[start : start + size].astype(ref.dtype)
+
+
+def row_shapes(rows, width):
+    return [shape((rows, width))] * 5 + [shape((3 * rows, width))]
 
 
 def each(count, step, start):
@@ -404,9 +412,9 @@
     kvs, refs = refs[:arrays], refs[arrays:]
     w = refs[:16]
     mixed = refs[16:18]
-    lse, sides_out = refs[18], refs[19:27]
-    store, sem = refs[27:]
-    wait = fetch(pos, sides, w, store, sem)
+    lse, sides_out = refs[18], refs[19:25]
+    store, sem = refs[25:]
+    wait = fetch(pos, sides, w, store, sem, 256)
     rows = q_ref.shape[0]
     qw = q_ref.shape[1] // 2
     ids = row_ids[0:1, :]
@@ -449,7 +457,7 @@
             lse[head : head + 1, :] = top * c + jnp.log2(total)
             head += 1
         fill = jnp.zeros((512 - 320 - qw, rows), F32)
-        tall = jnp.concatenate([jnp.zeros((320, rows), F32)] + outs + [fill], axis=0)
+        tall = jnp.concatenate([jnp.zeros((64, rows), F32)] + outs + [fill], axis=0)
         mixed[i][...] = tall.T.astype(BF)
     for i in range(2):
         wait(i)
@@ -462,12 +470,12 @@
     width = 8 * w[0].shape[0]
     return call(
         functools.partial(attend_body, sides),
-        [shape((rows, 512))] * 2
+        [shape((rows, 256))] * 2
         + [shape((8, rows), F32)]
-        + [shape((rows // 8, width))] * 8,
+        + row_shapes(rows // 8, width),
         [SM] + [VM] * (2 + len(kvs)) + [ANY] * 16,
-        [VM] * 11,
-        [pltpu.VMEM((2, width, 512), BF), sems(sides)],
+        [VM] * 9,
+        [pltpu.VMEM((2, width, 256), BF), sems(sides)],
         cost=12,
     )(pos, q, row_ids, *kvs, *w)
 
@@ -480,57 +488,71 @@
     depth = arrays[1].shape[1]
     half = inner // 2
     cut = arrays[2].shape[1]
-    copies = []
+    copies = [[], []]
     for k in range(PARTS):
         for j in range(inner):
             n = (i * PARTS + k) * inner + j
             if k < 3:
-                spot = arrays[k // 2].at[j * 2 + (pos[3] ^ i), pl.ds(depth if k == 1 else 0, depth)]
-                to = store.at[i, pl.ds(pl.multiple_of(((pos[1] ^ k) * inner + j) * depth, 16), depth)]
-                copies.append(pltpu.make_async_copy(spot, to, sem.at[n]))
+                row = pl.ds(pl.multiple_of(((pos[1] ^ k) * inner + j) * depth, 16), depth)
+                for late in range(2):
+                    lane = pl.ds(cut, store.shape[2] - cut) if late else pl.ds(0, cut)
+                    spot = arrays[k // 2].at[j * 2 + (pos[3] ^ i), pl.ds(depth if k == 1 else 0, depth), lane]
+                    to = store.at[i, row, lane]
+                    copies[late].append(pltpu.make_async_copy(spot, to, sem.at[late, n]))
                 continue
             for late in range(2):
                 piece = arrays[2 + 4 * late + 2 * i + j // half]
                 lane = pl.ds(cut * late, piece.shape[1])
                 to = store.at[i, spot_of(pos, k, j, inner, depth), lane]
                 spot = piece.at[pl.ds((j % half) * depth, depth)]
-                copies.append(
-                    pltpu.make_async_copy(spot, to, sem.at[2 * PARTS * inner + i * inner + j] if late else sem.at[n])
-                )
+                copies[late].append(pltpu.make_async_copy(spot, to, sem.at[late, n]))
     return copies
 
 
 def feed_body(fw, inner, pos, *refs):
     n, blocks = refs[:8], refs[8:18]
     hidden, slope, silu = refs[18:20], refs[20:22], refs[22:24]
-    rows_in, outs = refs[24], refs[25:33]
-    store, sem = refs[33:]
-    wait = start_all([block_copies(pos, inner, blocks, store, sem, i) for i in range(2)])
+    rows_out, outs = refs[24], refs[25:31]
+    rows_in, kept, store, sem, out_sem = refs[31:]
+    copies = [block_copies(pos, inner, blocks, store, sem, i) for i in range(2)]
+    wait = start_all([copies[0][0], copies[1][0], copies[0][1] + copies[1][1]])
     join_rows(n, rows_in)
+    saves = [pltpu.make_async_copy(rows_in, rows_out, out_sem.at[6])]
+    saves[0].start()
     for i in range(2):
         wait(i)
         out = dot(rows_in[...], store[i, :, : 2 * fw])
         gate, upper = out[:, :fw], out[:, fw:]
         sigma = jax.nn.sigmoid(gate)
         act = gate * sigma
-        hidden[i][...] = padded(act * upper, 512).astype(BF)
-        slope[i][...] = padded(upper * (sigma + act * (1.0 - sigma)), 512).astype(BF)
-        silu[i][...] = padded(act, 512).astype(BF)
+        values = (act * upper, upper * (sigma + act * (1.0 - sigma)), act)
+        for n, (value, to) in enumerate(zip(values, (hidden, slope, silu))):
+            kept[2 * n + i] = padded(value, 512).astype(BF)
+            saves.append(pltpu.make_async_copy(kept.at[2 * n + i], to[i], out_sem.at[2 * n + i]))
+            saves[-1].start()
+    wait(2)
     out_rows(
-        dot(hidden[0][...], store[0, :, 2 * fw :], LAST)
-        + dot(hidden[1][...], store[1, :, 2 * fw :], LAST),
+        dot(kept[0], store[0, :, 2 * fw :], LAST) + dot(kept[1], store[1, :, 2 * fw :], LAST),
         outs,
     )
+    for c in saves:
+        c.wait()
 
 
 def feed(pos, n, w, fw, inner):
     rows, width = n[0].shape
     return call(
         functools.partial(feed_body, fw, inner),
-        [shape((8 * rows, 512))] * 6 + [shape((8 * rows, width))] + [shape((rows, width))] * 8,
+        [shape((8 * rows, 512))] * 6 + [shape((8 * rows, width))] + row_shapes(rows, width),
         [SM] + [VM] * 8 + [ANY] * 10,
-        [VM] * 15,
-        [pltpu.VMEM((2, width, 2 * fw + 512), BF), sems(inner)],
+        [ANY] * 7 + [VM] * 6,
+        [
+            pltpu.VMEM((8 * rows, width), BF),
+            pltpu.VMEM((6, 8 * rows, 512), BF),
+            pltpu.VMEM((2, width, 2 * fw + 512), BF),
+            pltpu.SemaphoreType.DMA((2, 2 * PARTS * inner)),
+            pltpu.SemaphoreType.DMA((7,)),
+        ],
         cost=18,
     )(pos, *n, *w)
 
@@ -538,30 +560,41 @@
 def feed_back_body(fw, inner, pos, rows_in, *refs):
     slope, silu = refs[0:2], refs[2:4]
     blocks = refs[4:14]
-    d_gu, outs = refs[14:16], refs[16:24]
-    store, sem = refs[24:]
-    wait = start_all([block_copies(pos, inner, blocks, store, sem, i) for i in range(2)])
+    d_gu, outs = refs[14:16], refs[16:22]
+    kept, store, sem, out_sem = refs[22:]
+    copies = [block_copies(pos, inner, blocks, store, sem, i) for i in range(2)]
+    wait = start_all([copies[0][1], copies[1][1], copies[0][0] + copies[1][0]])
+    saves = []
     for i in range(2):
         wait(i)
         out = dot(rows_in[...], store[i, :, 2 * fw :])
         a = (out * slope[i][...].astype(F32))[:, :fw]
         b = (out * silu[i][...].astype(F32))[:, :fw]
-        d_gu[i][...] = jnp.concatenate([a, b], axis=1).astype(BF)
+        kept[i] = jnp.concatenate([a, b], axis=1).astype(BF)
+        saves.append(pltpu.make_async_copy(kept.at[i], d_gu[i], out_sem.at[i]))
+        saves[-1].start()
+    wait(2)
     out_rows(
-        dot(d_gu[0][...], store[0, :, : 2 * fw], LAST)
-        + dot(d_gu[1][...], store[1, :, : 2 * fw], LAST),
+        dot(kept[0], store[0, :, : 2 * fw], LAST) + dot(kept[1], store[1, :, : 2 * fw], LAST),
         outs,
     )
+    for c in saves:
+        c.wait()
 
 
 def feed_back(pos, d, slope, silu, w, fw, inner):
     rows, width = d.shape
     return call(
         functools.partial(feed_back_body, fw, inner),
-        [shape((rows, 2 * fw))] * 2 + [shape((rows // 8, width))] * 8,
+        [shape((rows, 2 * fw))] * 2 + row_shapes(rows // 8, width),
         [SM] + [VM] * 5 + [ANY] * 10,
-        [VM] * 10,
-        [pltpu.VMEM((2, width, 2 * fw + 512), BF), sems(inner)],
+        [ANY] * 2 + [VM] * 6,
+        [
+            pltpu.VMEM((2, rows, 2 * fw), BF),
+            pltpu.VMEM((2, width, 2 * fw + 512), BF),
+            pltpu.SemaphoreType.DMA((2, 2 * PARTS * inner)),
+            pltpu.SemaphoreType.DMA((2,)),
+        ],
         cost=16,
     )(pos, d, *slope, *silu, *w)
 
@@ -634,12 +667,12 @@
     dq_ref, own_ref, send_ref, rows_in = refs[16:20]
     store, mix, d_kv, sem = refs[20:]
     join_rows(d, rows_in)
-    wait = fetch(pos, sides, w, store, sem)
+    wait = fetch(pos, sides, w, store, sem, 256)
     rows = q_ref.shape[0]
     qw = q_ref.shape[1] // 2
     for i in range(2):
         wait(i)
-        mix[i] = dot(rows_in[...], store[i])[:, 320 : 320 + qw].astype(BF)
+        mix[i] = dot(rows_in[...], store[i])[:, 64 : 64 + qw].astype(BF)
     ids = row_ids[0:1, :]
     read = reader(kvs, rows)
 
@@ -707,7 +740,7 @@
         [SM] + [VM] * (13 + len(kvs)) + [ANY] * 16,
         [VM] * 4,
         [
-            pltpu.VMEM((2, width, 512), BF),
+            pltpu.VMEM((2, width, 256), BF),
             pltpu.VMEM((2, rows, q.shape[1] // 2), BF),
             pltpu.VMEM((4, sides, rows, HEAD_DIM), F32),
             sems(sides),
@@ -725,18 +758,18 @@
         d_k = rotated(d_kv[:, i * HEAD_DIM : (i + 1) * HEAD_DIM], cos, -sin)
         d_v = d_kv[:, (2 + i) * HEAD_DIM : (3 + i) * HEAD_DIM]
         d_qkv[i][...] = padded(
-            jnp.concatenate([d_q[:, i * qw : (i + 1) * qw], d_k, d_v], axis=1), 512
+            jnp.concatenate([d_q[:, i * qw : (i + 1) * qw], d_k, d_v], axis=1), 384
         ).astype(BF)
 
 
 def split_grads(dq, own, got, cosine, sine):
     rows = dq.shape[0]
-    return call(split_body, [shape((rows, 512))] * 2, [VM] * 5, [VM] * 2)(dq, own, got, cosine, sine)
+    return call(split_body, [shape((rows, 384))] * 2, [VM] * 5, [VM] * 2)(dq, own, got, cosine, sine)
 
 
 def project_back_body(inner, pos, d_a, d_b, *refs):
-    w, outs = refs[:16], refs[16:24]
-    store, sem = refs[24:]
+    w, outs = refs[:16], refs[16:22]
+    store, sem = refs[22:]
     wait = fetch(pos, inner, w, store, sem)
     for i in range(2):
         wait(i)
@@ -748,22 +781,24 @@
     width = 8 * w[0].shape[0]
     return call(
         functools.partial(project_back_body, inner),
-        [shape((rows, width))] * 8,
+        row_shapes(rows, width),
         [SM] + [VM] * 2 + [ANY] * 16,
-        [VM] * 8,
-        [pltpu.VMEM((2, width, 512), BF), sems(inner)],
+        [VM] * 6,
+        [pltpu.VMEM((2, width, 384), BF), sems(inner)],
         cost=8,
     )(pos, *d_qkv, *w)
 
 
-def pair_copies(pos, inner, outs, store, sem, i):
+def pair_copies(pos, inner, far, near, store, sem, i):
     half = inner // 2
     depth = store.shape[1] // (PARTS * inner)
     copies = []
     for k in range(PARTS):
         for j in range(inner):
-            spot = ((k % 2) * half + j % half) * depth
-            to = outs[2 * (k // 2) + j // half].at[pl.ds(spot, depth)]
+            if k >= 2:
+                to = far[j // half].at[pl.ds(((k % 2) * half + j % half) * depth, depth)]
+            else:
+                to = near.at[(pos[2] ^ j) * 2 + (pos[3] ^ i), pl.ds(k * depth, depth)]
             n = (i * PARTS + k) * inner + j
             copies.append(
                 pltpu.make_async_copy(store.at[i, spot_of(pos, k, j, inner, depth)], to, sem.at[n])
@@ -773,31 +808,33 @@
 
 def attn_grad_body(inner, pos, first, d_all, gain_two, sum_attn, sums, *refs):
     d_qkv, mixed = refs[:2], refs[2:4]
-    w, outs = refs[4:20], refs[20:28]
-    held, store, sem, out_sem = refs[28:]
+    w, outs, near = refs[4:20], refs[20:24], refs[24]
+    held, store, sem, out_sem = refs[25:]
     wait = fetch(pos, inner, w, held, sem)
     step = store.shape[1] // PARTS
-    copies = [pair_copies(pos, inner, outs[4 * i : 4 * i + 4], store, out_sem, i) for i in range(2)]
+    copies = [pair_copies(pos, inner, outs[2 * i : 2 * i + 2], near, store, out_sem, i) for i in range(2)]
     lane = lax.broadcasted_iota(jnp.int32, (1, 128), 1)
     tail = jnp.where(lane == 98, sums[0:1, :], 0.0)
     tail = jnp.where(lane == 99, sum_attn[0:1, :], tail)
     tail = jnp.where(lane == 100, sums[8:9, :], tail)
-    wait(0)
-    wait(1)
     for k in (3, 2, 1, 0):
         spot = features(pos, k, step)
         rows = [jnp.zeros((97, step), F32), gain_two[0:1, spot], jnp.zeros((30, step), F32)]
         tall = jnp.concatenate(rows, axis=0).T + tail
         values = [dot(first[:, spot], d_qkv[i][...], ROWS) for i in range(2)]
+        others = [dot(d_all[:, spot], mixed[i][...], ROWS) for i in range(2)]
+        if k == 3:
+            wait(0)
+            wait(1)
         gain = 0.0
         for i in range(2):
-            gain = gain + jnp.sum(values[i] * held[i, spot, :].astype(F32), axis=1, keepdims=True)
+            gain = gain + jnp.sum(values[i] * held[i, spot, :384].astype(F32), axis=1, keepdims=True)
         gain = gain / held[0, spot, 480:481].astype(F32)
         tall = tall + jnp.where(lane == 96, gain, 0.0)
         for i in range(2):
-            value = values[i] + dot(d_all[:, spot], mixed[i][...], ROWS)
-            store[i, spot, :384] = value[:, :384].astype(BF)
-            store[i, spot, 384:] = (value[:, 384:] + tall).astype(BF)
+            store[i, spot, :256] = values[i][:, :256].astype(BF)
+            store[i, spot, 256:384] = (values[i][:, 256:] + others[i][:, :128]).astype(BF)
+            store[i, spot, 384:] = (others[i][:, 128:] + tall).astype(BF)
             for c in copies[i][k * inner : (k + 1) * inner]:
                 c.start()
     for i in range(2):
@@ -809,9 +846,9 @@
     rows, width = first.shape
     return call(
         functools.partial(attn_grad_body, inner),
-        [shape((width // 4, 512))] * 8,
+        [shape((width // 4, 512))] * 4 + [shape((inner * 2, width // (2 * inner), 512))],
         [SM] + [VM] * 9 + [ANY] * 16,
-        [ANY] * 8,
+        [ANY] * 5,
         [pltpu.VMEM((2, width, 512), BF), pltpu.VMEM((2, width, 512), BF), sems(inner), sems(inner)],
         cost=12,
     )(pos, first, d_all, gain_two, sum_attn, sums, *d_qkv, *mixed, *w)
@@ -866,6 +903,10 @@
     def add(self, own, got):
         return (own.astype(F32) + got.astype(F32)).astype(BF)
 
+    def halves(self, own, got):
+        n = own.shape[0] // 2
+        return [self.add(own[:n], got[:n]), self.add(own[n:], got[n:])]
+
     def sum_y(self, own, far):
         value = self.add(own, self.far_y(far))
         for b in reversed(self.bits[:-1]):
@@ -883,9 +924,9 @@
 
     def scatter_one(self, outs):
         mine = list(outs[:4])
-        got = [self.hop_c(v) for v in outs[4:]]
-        one, two = second_sum(mine, got, self.hop_z(first_sum(mine[3], got[3]), 1))
-        return [mine[0], got[0], one, two]
+        last, rest = [self.hop_c(v) for v in outs[4:]]
+        one, two = second_sum(mine, rest, self.hop_z(first_sum(mine[3], last), 1))
+        return [mine[0], rest, one, two]
 
     def scatter_two(self, left):
         return left[0], left[1], self.hop_z(left[2], 1), self.hop_z(left[3], 2)
@@ -1112,7 +1153,7 @@
 
     tails = (live.grad_gain_two, live.sum_attn, live.sums)
     q = attn_grad(pos, live.first, live.a_all, *tails, live.d_qkv, live.mixed, live.w_qo, inner)
-    live.q_near, live.q_far = (q[0:2], q[4:6]), (q[2:4], q[6:8])
+    live.q_far, live.q_near = (q[0:2], q[2:4]), q[4]
     live.far3 = hop_z(far[1], 3)
     del live.first, live.a_all, live.mixed
     del live.grad_gain_two, live.sum_attn, live.sums
@@ -1120,11 +1161,14 @@
 
     live.left = at.scatter_one(project_back(pos, live.d_qkv, live.w_qo, inner))
     del live.d_qkv, live.w_qo
-    q_near, q_far = live.q_near, live.q_far
+    q_near, q_far = scatter_blocks(live.q_near, 2), live.q_far
     del live.q_near, live.q_far
     (a, b), (c, d) = q_far
-    q_far = at.sum_y(at.sum_x(a, c), at.sum_x(b, d))
-    q_near = at.sum_x(*[at.sum_y(*side) for side in q_near])
+    q_far, last = at.sum_x(a, c), at.sum_x(b, d)
+    if inner == 2:
+        q_far = at.halves(q_far, at.far_y(last))
+    else:
+        q_far = jnp.split(at.sum_y(q_far, last), 2)
     far2 = hop_z(far[0], 2)
     live.fence()
 
@@ -1135,7 +1179,7 @@
         [VM],
     )(*at.scatter_two(live.left), live.x_own, live.d_middle, live.gain)
     del live.left, live.x_own, live.d_middle
-    live.q_near, live.q_far, live.far2 = q_near, q_far, far2
+    live.q_far, live.far2 = q_far, far2
     (live.g_down,) = unpack(at.zs, live.d, [(0, fw, 1)])
     live.layer_out = spread_rows(spots, live.layer_out)
     del live.d
@@ -1145,13 +1189,12 @@
     live.g = [near_own, hop_z(near_one, 1), live.far2, live.far3]
     live.input_grad = all_rows(live.input_own)
     del live.far2, live.far3, live.input_own
-    n = live.q_far.shape[0] // 2
-    live.q = [live.q_near[:n], live.q_near[n:], hop_z(live.q_far[:n], 2), hop_z(live.q_far[n:], 3)]
-    del live.q_near, live.q_far
-    live.fence()
-
-    q = live.q
-    q[1] = hop_z(q[1], 1)
+    live.q = [hop_z(live.q_far[0], 2), hop_z(live.q_far[1], 3)]
+    del live.q_far
+    live.fence()
+
+    q_near = hold(q_near, live.q[0])
+    q = [q_near[0], hop_z(q_near[1], 1), *live.q]
     layer_out, input_grad = live.layer_out, spread_rows(spots, live.input_grad)
     g_gate, g_up = unpack(at.zs, live.g, [(0, fw, 1), (fw, fw, 1)])
     g_down = live.g_down

time: 645 us -> 638 us (0.989)
  waiting for transfers between devices: 311 us -> 303 us
    ppermute x106 -> x95, waiting for transfers between devices: 289 us -> 282 us  [hop(): return lax.ppermute(value, axis, [(i, i ^ k) for i in range(size)])]
    unnamed x240 -> x204, local copies, waits for them, and re-layouts: 19.2 us -> 23.4 us
    ppermute x106 -> x95, starting transfers between devices: 105 us -> 102 us  [hop(): return lax.ppermute(value, axis, [(i, i ^ k) for i in range(size)])]
    reduce_scatter x3 -> x4, waiting for transfers between devices: 21.5 us -> 21.3 us  [scatter_blocks(): got = lax.psum_scatter(blocks, ('y', 'x'), scatter_dimension=0, tiled=True)]
  transfers between devices with their start and end apart: 111 -> 101, of which waited for: 48 -> 50; matrix products, arithmetic and copies ran while one was open for 2% -> 2% of each run, Pallas kernels for 22% -> 21%
where the time goes in v6:
time: 638 us; the launch traced here: 631 us
  waiting for transfers between devices  303 us (47%)
  Pallas kernels  168 us (26%)
  starting transfers between devices  103 us (16%)
  local copies, waits for them, and re-layouts  35.3 us (6%)
  between operations  16.2 us (3%)
    ppermute x95, waiting for transfers between devices, hop(): return lax.ppermute(value, axis, [(i, i ^ k) for i in range(size)])  282 us
    ppermute x95, starting transfers between devices, hop(): return lax.ppermute(value, axis, [(i, i ^ k) for i in range(size)])  102 us
    unnamed x204, local copies, waits for them, and re-layouts  23.4 us
    reduce_scatter x4, waiting for transfers between devices, scatter_blocks(): got = lax.psum_scatter(blocks, ('y', 'x'), scatter_dimension=0, tiled=True)  21.3 us
    pallas_call x1, Pallas kernels, feed(): call(functools.partial(feed_body, fw, inner), [shape((8 * rows, 512))] *...  16.5 us
    pallas_call x1, Pallas kernels, feed_back(): call(functools.partial(feed_back_body, fw, inner), [shape((rows, 2 * fw))...  16.2 us
    pallas_call x1, Pallas kernels, attend_back(): call(functools.partial(attend_back_body, sides), [shape(q.shape), shape((...  14.8 us
  transfers between devices with their start and end apart: 101, of which 50 were waited for; matrix products, arithmetic and copies ran while one was open for 2% of the time, Pallas kernels for 21%

profile of v6, /device:TPU:0, one launch (start us, length us, event | category | flops | bytes accessed | tf_op | source)
XLA Modules:
  0.0 631.1 jit_solution(3277618484756375752)
XLA Ops:
  16.1 4.6 shard_map.237
  31.6 21.9 %collective-permute-done.5.refs_12_.refs_6_.refs_14_.refs_8_.refs_4_ = bf16[320,512]{1,0:T(8,128)(2,1)S(1)} collective-permute-done((bf16[320,512]{1,0:T(8,128)(2,1)S(1)}, bf16[320,512]{1,0:T(8,128)(2,1)S(1)}, u32[]{:S(2)}, u32[]{:S(2)}) %collective-permute-start.5) | collective-permute-done | bytes 327712 | tf_op jit(solution)/shard_map/ppermute | solution.py:52
  71.1 4.3 collective-permute-done.12.refs_19_.refs_13_.refs_21_.refs_15_.refs_11_
  80.9 8.1 %collective-permute-done.8.refs_11_.refs_5_.refs_13_.refs_7_.refs_3_ = bf16[320,512]{1,0:T(8,128)(2,1)S(1)} collective-permute-done((bf16[320,512]{1,0:T(8,128)(2,1)S(1)}, bf16[320,512]{1,0:T(8,128)(2,1)S(1)}, u32[]{:S(2)}, u32[]{:S(2)}) %collective-permute-start.8) | collective-permute-done | bytes 327712 | tf_op jit(solution)/shard_map/ppermute | solution.py:52
  89.0 3.5 collective-permute-done.15.refs_22_.refs_16_.refs_24_.refs_18_.refs_14_
  92.5 9.1 %collective-permute-done.10.refs_15_.refs_9_.refs_17_.refs_11_.refs_7_ = bf16[320,512]{1,0:T(8,128)(2,1)S(1)} collective-permute-done((bf16[320,512]{1,0:T(8,128)(2,1)S(1)}, bf16[320,512]{1,0:T(8,128)(2,1)S(1)}, u32[]{:S(2)}, u32[]{:S(2)}) %collective-permute-start.10) | collective-permute-done | bytes 327712 | tf_op jit(solution)/shard_map/ppermute | solution.py:52
  106.2 7.6 %collective-permute-done.9.refs_13_.refs_7_.refs_15_.refs_9_.refs_5_ = bf16[320,512]{1,0:T(8,128)(2,1)S(1)} collective-permute-done((bf16[320,512]{1,0:T(8,128)(2,1)S(1)}, bf16[320,512]{1,0:T(8,128)(2,1)S(1)}, u32[]{:S(2)}, u32[]{:S(2)}) %collective-permute-start.9) | collective-permute-done | bytes 327712 | tf_op jit(solution)/shard_map/ppermute | solution.py:52
  119.4 8.4 %collective-permute-done.16.refs_23_.refs_17_.refs_25_.refs_19_.refs_15_ = bf16[320,512]{1,0:T(8,128)(2,1)S(1)} collective-permute-done((bf16[320,512]{1,0:T(8,128)(2,1)S(1)}, bf16[320,512]{1,0:T(8,128)(2,1)S(1)}, u32[]{:S(2)}, u32[]{:S(2)}) %collective-permute-start.16) | collective-permute-done | bytes 327712 | tf_op jit(solution)/shard_map/ppermute | solution.py:52
  130.7 9.8 %shard_map.239 = (bf16[512,2560]{1,0:T(8,128)(2,1)}, bf16[512,320]{1,0:T(8,128)(2,1)}, bf16[512,384]{1,0:T(8,128)(2,1)}, f32[8,2560]{1,0:T(8,128)}, f32[8,512]{1,0:T(8,128)}) custom-call(s32[5]{0:T(128)} %stack.36.pos, f32[512,40]{1,0:T(8,128)} %get-tuple-element.1609.cosine, f32[512,40]{1,0:T(8,128)} %get-tuple-element.1608.sine, ...), custom_call_target="tpu_custom_call" | custom-call | flops 12000000000 | tf_op jit(solution)/shard_map/pallas_call | solution.py:359
  140.5 9.1 %collective-permute-done.24 = bf16[320,512]{1,0:T(8,128)(2,1)S(1)} collective-permute-done((bf16[320,512]{1,0:T(8,128)(2,1)}, bf16[320,512]{1,0:T(8,128)(2,1)S(1)}, u32[]{:S(2)}, u32[]{:S(2)}) %collective-permute-start.24) | collective-permute-done | bytes 327712 | tf_op jit(solution)/shard_map/ppermute | solution.py:52
  153.3 13.8 %collective-permute-done.26.refs_1_.refs_9_ = bf16[512,384]{1,0:T(8,128)(2,1)S(1)} collective-permute-done((bf16[512,384]{1,0:T(8,128)(2,1)S(1)}, bf16[512,384]{1,0:T(8,128)(2,1)S(1)}, u32[]{:S(2)}, u32[]{:S(2)}) %collective-permute-start.26) | collective-permute-done | bytes 393248 | tf_op jit(solution)/shard_map/ppermute | solution.py:52
  167.9 9.2 %shard_map.240 = (bf16[512,256]{1,0:T(8,128)(2,1)}, bf16[512,256]{1,0:T(8,128)(2,1)}, f32[8,512]{1,0:T(8,128)}, bf16[64,2560]{1,0:T(8,128)(2,1)}, bf16[64,2560]{...) custom-call(s32[5]{0:T(128)} %stack.36.pos, ...), custom_call_target="tpu_custom_call" | custom-call | flops 12000000000 | tf_op jit(solution)/shard_map/pallas_call | solution.py:471
  185.3 7.6 %collective-permute-done.32.three = bf16[64,2560]{1,0:T(8,128)(2,1)S(1)} collective-permute-done((bf16[64,2560]{1,0:T(8,128)(2,1)}, bf16[64,2560]{1,0:T(8,128)(2,1)S(1)}, u32[]{:S(2)}, u32[]{:S(2)}) %collective-permute-start.32) | collective-permute-done | bytes 327712 | tf_op jit(solution)/shard_map/ppermute | solution.py:52
  197.0 3.6 collective-permute-done.27.refs_14_.refs_10_
  203.1 3.9 collective-permute-start.38
  207.0 11.5 %collective-permute-done.37.one = bf16[64,2560]{1,0:T(8,128)(2,1)S(1)} collective-permute-done((bf16[64,2560]{1,0:T(8,128)(2,1)}, bf16[64,2560]{1,0:T(8,128)(2,1)S(1)}, u32[]{:S(2)}, u32[]{:S(2)}) %collective-permute-start.37) | collective-permute-done | bytes 327712 | tf_op jit(solution)/shard_map/ppermute | solution.py:52
  229.1 10.3 %collective-permute-done.40.refs_2_ = bf16[64,2560]{1,0:T(8,128)(2,1)S(1)} collective-permute-done((bf16[64,2560]{1,0:T(8,128)(2,1)}, bf16[64,2560]{1,0:T(8,128)(2,1)S(1)}, u32[]{:S(2)}, u32[]{:S(2)}) %collective-permute-start.40) | collective-permute-done | bytes 327712 | tf_op jit(solution)/shard_map/ppermute | solution.py:52
  239.5 7.1 %collective-permute-done.34.refs_15_.refs_11_ = bf16[320,512]{1,0:T(8,128)(2,1)S(1)} collective-permute-done((bf16[320,512]{1,0:T(8,128)(2,1)S(1)}, bf16[320,512]{1,0:T(8,128)(2,1)S(1)}, u32[]{:S(2)}, u32[]{:S(2)}) %collective-permute-start.34) | collective-permute-done | bytes 327712 | tf_op jit(solution)/shard_map/ppermute | solution.py:52
  249.0 6.4 %collective-permute-done.36.refs_17_.refs_13_ = bf16[320,512]{1,0:T(8,128)(2,1)S(1)} collective-permute-done((bf16[320,512]{1,0:T(8,128)(2,1)S(1)}, bf16[320,512]{1,0:T(8,128)(2,1)S(1)}, u32[]{:S(2)}, u32[]{:S(2)}) %collective-permute-start.36) | collective-permute-done | bytes 327712 | tf_op jit(solution)/shard_map/ppermute | solution.py:52
  256.3 16.5 %shard_map.244 = (bf16[512,512]{1,0:T(8,128)(2,1)}, bf16[512,512]{1,0:T(8,128)(2,1)}, bf16[512,512]{1,0:T(8,128)(2,1)}, bf16[512,512]{1,0:T(8,128)(2,1)}, bf16[5...) custom-call(s32[5]{0:T(128)} %stack.36.pos, ...), custom_call_target="tpu_custom_call" | custom-call | flops 17999998976 | tf_op jit(solution)/shard_map/pallas_call | solution.py:544
  280.1 8.7 %collective-permute-done.48.three = bf16[64,2560]{1,0:T(8,128)(2,1)S(1)} collective-permute-done((bf16[64,2560]{1,0:T(8,128)(2,1)}, bf16[64,2560]{1,0:T(8,128)(2,1)S(1)}, u32[]{:S(2)}, u32[]{:S(2)}) %collective-permute-start.48) | collective-permute-done | bytes 327712 | tf_op jit(solution)/shard_map/ppermute | solution.py:52
  296.1 12.1 %collective-permute-done.49.one = bf16[64,2560]{1,0:T(8,128)(2,1)S(1)} collective-permute-done((bf16[64,2560]{1,0:T(8,128)(2,1)}, bf16[64,2560]{1,0:T(8,128)(2,1)S(1)}, u32[]{:S(2)}, u32[]{:S(2)}) %collective-permute-start.49) | collective-permute-done | bytes 327712 | tf_op jit(solution)/shard_map/ppermute | solution.py:52
  318.5 9.8 %collective-permute-done.52.refs_2_ = bf16[64,2560]{1,0:T(8,128)(2,1)S(1)} collective-permute-done((bf16[64,2560]{1,0:T(8,128)(2,1)}, bf16[64,2560]{1,0:T(8,128)(2,1)S(1)}, u32[]{:S(2)}, u32[]{:S(2)}) %collective-permute-start.52) | collective-permute-done | bytes 327712 | tf_op jit(solution)/shard_map/ppermute | solution.py:52
  332.3 6.8 %collective-permute-done.53.refs_3_ = bf16[64,2560]{1,0:T(8,128)(2,1)S(1)} collective-permute-done((bf16[64,2560]{1,0:T(8,128)(2,1)S(1)}, bf16[64,2560]{1,0:T(8,128)(2,1)S(1)}, u32[]{:S(2)}, u32[]{:S(2)}) %collective-permute-start.53) | collective-permute-done | bytes 327712 | tf_op jit(solution)/shard_map/ppermute | solution.py:52
  341.6 7.6 %shard_map.248 = (bf16[4,1280,512]{2,1,0:T(8,128)(2,1)}, bf16[512,2560]{1,0:T(8,128)(2,1)}) custom-call(s32[5]{0:T(128)} %stack.36.pos, bf16[64,2560]{1,0:T(8,128)(2,1)} %get-tuple-element.1303.refs_0_.d_own, bf16[64,2560]{1,0:T(8,128)(2,1)} %copy-done.70, bf16[64,2560]{1,0:T(8,128)(2,1)} %copy-done.65, bf16[64,2560]{1,0:T(8,128)(2,1)} %copy-done.72, ...), custom_call_target="tpu_custom_call" | custom-call | flops 7000000000 | tf_op jit(solution)/shard_map/pallas_call | solution.py:638
  349.6 16.2 %shard_map.249 = (bf16[512,896]{1,0:T(8,128)(2,1)}, bf16[512,896]{1,0:T(8,128)(2,1)}, bf16[64,2560]{1,0:T(8,128)(2,1)}, bf16[64,2560]{1,0:T(8,128)(2,1)}, bf16[6...) custom-call(s32[5]{0:T(128)} %stack.36.pos, ...), custom_call_target="tpu_custom_call" | custom-call | flops 16000000000 | tf_op jit(solution)/shard_map/pallas_call | solution.py:587
  370.6 6.3 %shard_map.250 = bf16[4,640,896]{2,1,0:T(8,128)(2,1)} custom-call(s32[5]{0:T(128)} %stack.36.pos, bf16[512,2560]{1,0:T(8,128)(2,1)} %get-tuple-element.1318.left, bf16[512,896]{1,0:T(8,128)(2,1)} %get-tuple-element.1319.right_a, bf16[512,896]{1,0:T(8,128)(2,1)} %get-tuple-element.1320.right_b), custom_call_target="tpu_custom_call" | custom-call | flops 7000000000 | tf_op jit(solution)/shard_map/pallas_call | solution.py:652
  377.0 3.8 collective-permute-done.63.three
  386.1 3.6 collective-permute-start.65
  389.7 6.4 %shard_map.254 = bf16[4,640,896]{2,1,0:T(8,128)(2,1)} custom-call(s32[5]{0:T(128)} %stack.36.pos, bf16[512,2560]{1,0:T(8,128)(2,1)} %get-tuple-element.1318.left, bf16[512,896]{1,0:T(8,128)(2,1)} %get-tuple-element.1319.right_a, bf16[512,896]{1,0:T(8,128)(2,1)} %get-tuple-element.1320.right_b), custom_call_target="tpu_custom_call" | custom-call | flops 7000000000 | tf_op jit(solution)/shard_map/pallas_call | solution.py:652
  396.0 6.1 collective-permute-done.64.one
  408.8 3.4 collective-permute-start.67
  412.2 12.1 %collective-permute-done.68.refs_2_ = bf16[64,2560]{1,0:T(8,128)(2,1)S(1)} collective-permute-done((bf16[64,2560]{1,0:T(8,128)(2,1)S(1)}, bf16[64,2560]{1,0:T(8,128)(2,1)S(1)}, u32[]{:S(2)}, u32[]{:S(2)}) %collective-permute-start.68) | collective-permute-done | bytes 327712 | tf_op jit(solution)/shard_map/ppermute | solution.py:52
  424.9 7.7 %collective-permute-done.69.refs_3_ = bf16[64,2560]{1,0:T(8,128)(2,1)S(1)} collective-permute-done((bf16[64,2560]{1,0:T(8,128)(2,1)S(1)}, bf16[64,2560]{1,0:T(8,128)(2,1)S(1)}, u32[]{:S(2)}, u32[]{:S(2)}) %collective-permute-start.69) | collective-permute-done | bytes 327712 | tf_op jit(solution)/shard_map/ppermute | solution.py:52
  439.8 14.8 %shard_map.255 = (bf16[512,320]{1,0:T(8,128)(2,1)}, f32[512,320]{1,0:T(8,128)}, bf16[512,320]{1,0:T(8,128)(2,1)}, bf16[512,2560]{1,0:T(8,128)(2,1)}) custom-call(s32[5]{0:T(128)} %stack.36.pos, bf16[512,320]{1,0:T(8,128)(2,1)} %get-tuple-element.1379.q_ref, f32[8,512]{1,0:T(8,128)} %get-tuple-element.1380.row_ids, f32[8,512]{1,0:T(8,128)} %get-tuple-element.1381.lse, ...), custom_call_target="tpu_custom_call" | custom-call | flops 17999998976 | tf_op jit(solution)/shard_map/pallas_call | solution.py:737
  456.7 20.5 %reduce-scatter.7.cloned.1.call-done = bf16[640,896]{1,0:T(8,128)(2,1)} async-done(((bf16[2560,896]{1,0:T(8,128)(2,1)}), bf16[640,896]{1,0:T(8,128)(2,1)}) %reduce-scatter.7.cloned.1.call-update) | async-done | bytes 1146896 | tf_op jit(solution)/shard_map/reduce_scatter | solution.py:996
  482.7 3.4 shard_map.256
  486.1 12.7 %shard_map.257 = (bf16[640,512]{1,0:T(8,128)(2,1)}, bf16[640,512]{1,0:T(8,128)(2,1)}, bf16[640,512]{1,0:T(8,128)(2,1)}, bf16[640,512]{1,0:T(8,128)(2,1)}, bf16[4,640,512]{2,1,0:T(8,128)(2,1)}) custom-call(s32[5]{0:T(128)} %stack.36.pos, bf16[512,2560]{1,0:T(8,128)(2,1)} %get-tuple-element.1477.first, bf16[512,2560]{1,0:T(8,128)(2,1)} %get-tuple-element.1478.d_all, ...), custom_call_target="tpu_custom_call" | custom-call | flops 12000000000 | tf_op jit(solution)/shard_map/pallas_call | solution.py:847
  501.4 7.8 %shard_map.258 = (bf16[64,2560]{1,0:T(8,128)(2,1)}, bf16[64,2560]{1,0:T(8,128)(2,1)}, bf16[64,2560]{1,0:T(8,128)(2,1)}, bf16[64,2560]{1,0:T(8,128)(2,1)}, bf16[6...) custom-call(s32[5]{0:T(128)} %stack.36.pos, bf16[512,384]{1,0:T(8,128)(2,1)} %get-tuple-element.1517.refs_0_.d_a, ...), custom_call_target="tpu_custom_call" | custom-call | flops 8000000000 | tf_op jit(solution)/shard_map/pallas_call | solution.py:782
  511.0 8.9 %collective-permute-start.66 = (bf16[320,896]{1,0:T(8,128)(2,1)S(1)}, bf16[320,896]{1,0:T(8,128)(2,1)S(1)}, u32[]{:S(2)}, u32[]{:S(2)}) collective-permute-start(bf16[320,896]{1,0:T(8,128)(2,1)S(1)} %get-tuple-element.1603), channel_id=1, source_target_pairs={{0,16},{8,24},{16,0},{24,8},{1,17},{9,25},{17,1},{25,9},{2,18},{10... | collective-permute-start | bytes 1720328 | tf_op jit(solution)/shard_map/ppermute | solution.py:52
  521.8 5.5 collective-permute-done.85
  529.2 17.2 %collective-permute-done.84 = bf16[640,512]{1,0:T(8,128)(2,1)S(1)} collective-permute-done((bf16[640,512]{1,0:T(8,128)(2,1)S(1)}, bf16[640,512]{1,0:T(8,128)(2,1)S(1)}, u32[]{:S(2)}, u32[]{:S(2)}) %collective-permute-start.84) | collective-permute-done | bytes 655392 | tf_op jit(solution)/shard_map/ppermute | solution.py:52
  559.9 6.2 collective-permute-done.82.one
  579.5 9.6 %collective-permute-done.89.p2 = bf16[64,2560]{1,0:T(8,128)(2,1)S(1)} collective-permute-done((bf16[64,2560]{1,0:T(8,128)(2,1)}, bf16[64,2560]{1,0:T(8,128)(2,1)S(1)}, u32[]{:S(2)}, u32[]{:S(2)}) %collective-permute-start.89) | collective-permute-done | bytes 327712 | tf_op jit(solution)/shard_map/ppermute | solution.py:52
  589.2 6.5 %collective-permute-done.91.refs_2_ = bf16[320,512]{1,0:T(8,128)(2,1)S(1)} collective-permute-done((bf16[320,512]{1,0:T(8,128)(2,1)S(1)}, bf16[320,512]{1,0:T(8,128)(2,1)S(1)}, u32[]{:S(2)}, u32[]{:S(2)}) %collective-permute-start.91) | collective-permute-done | bytes 327712 | tf_op jit(solution)/shard_map/ppermute | solution.py:52
  595.7 6.5 %collective-permute-done.92.refs_3_ = bf16[320,512]{1,0:T(8,128)(2,1)S(1)} collective-permute-done((bf16[320,512]{1,0:T(8,128)(2,1)S(1)}, bf16[320,512]{1,0:T(8,128)(2,1)S(1)}, u32[]{:S(2)}, u32[]{:S(2)}) %collective-permute-start.92) | collective-permute-done | bytes 327712 | tf_op jit(solution)/shard_map/ppermute | solution.py:52
  609.9 4.7 shard_map.266
  618.2 4.1 shard_map.265
  (417 shorter events, 199.9 us)
Async XLA Ops:
  7.2 169.9 %all-gather.5.cloned.1.call-start = ((), (), s32[]{:S(2)}) async-start(), calls=%async_computation.8 | async-start | bytes 9011200 | tf_op jit(solution)/shard_map/all_gather | solution.py:992
  24.1 37.4 %collective-permute-start.1 = (bf16[320,1408]{1,0:T(8,128)(2,1)}, bf16[320,1408]{1,0:T(8,128)(2,1)S(1)}, u32[]{:S(2)}, u32[]{:S(2)}) collective-permute-start(bf16[320,1408]{1,0:T(8,128)(2,1)} %get-tuple-element.814), channel_id=1, source_target_pairs={{0,8},{8,0},{16,24},{24,16},{1,9},{9,1},{17,25},{25,17},{2,10},{10... | collective-permute-start | bytes 2703368 | tf_op jit(solution)/shard_map/ppermute | solution.py:52
  25.8 27.7 %collective-permute-start.5 = (bf16[320,512]{1,0:T(8,128)(2,1)S(1)}, bf16[320,512]{1,0:T(8,128)(2,1)S(1)}, u32[]{:S(2)}, u32[]{:S(2)}) collective-permute-start(bf16[320,512]{1,0:T(8,128)(2,1)S(1)} %copy-done.79), channel_id=1, source_target_pairs={{0,16},{8,24},{16,0},{24,8},{1,17},{9,25},{17,1},{25,9},{2,18},{10... | collective-permute-start | bytes 983048 | tf_op jit(solution)/shard_map/ppermute | solution.py:52
  28.4 33.0 %collective-permute-start.6 = (bf16[320,512]{1,0:T(8,128)(2,1)}, bf16[320,512]{1,0:T(8,128)(2,1)S(1)}, u32[]{:S(2)}, u32[]{:S(2)}) collective-permute-start(bf16[320,512]{1,0:T(8,128)(2,1)} %get-tuple-element.821), channel_id=1, source_target_pairs={{0,24},{8,16},{16,8},{24,0},{1,25},{9,17},{17,9},{25,1},{2,26},{10... | collective-permute-start | bytes 983048 | tf_op jit(solution)/shard_map/ppermute | solution.py:52
  28.4 32.9 %collective-permute-start.3 = (bf16[320,512]{1,0:T(8,128)(2,1)S(1)}, bf16[320,512]{1,0:T(8,128)(2,1)S(1)}, u32[]{:S(2)}, u32[]{:S(2)}) collective-permute-start(bf16[320,512]{1,0:T(8,128)(2,1)S(1)} %copy-done.32), channel_id=1, source_target_pairs={{0,2},{2,0},{1,3},{3,1},{4,6},{6,4},{5,7},{7,5},{8,10},{10,8},{9,1... | collective-permute-start | bytes 983048 | tf_op jit(solution)/shard_map/ppermute | solution.py:52
  30.1 31.3 %collective-permute-start.2 = (bf16[320,512]{1,0:T(8,128)(2,1)S(1)}, bf16[320,512]{1,0:T(8,128)(2,1)S(1)}, u32[]{:S(2)}, u32[]{:S(2)}) collective-permute-start(bf16[320,512]{1,0:T(8,128)(2,1)S(1)} %copy-done.32), channel_id=1, source_target_pairs={{0,4},{4,0},{1,5},{5,1},{2,6},{6,2},{3,7},{7,3},{8,12},{12,8},{9,1... | collective-permute-start | bytes 983048 | tf_op jit(solution)/shard_map/ppermute | solution.py:52
  63.7 185.3 %all-gather.7.cloned.1.call-start = ((), (), s32[]{:S(2)}) async-start(), calls=%async_computation.9 | async-start | bytes 4505600 | tf_op jit(solution)/shard_map/all_gather | solution.py:992
  67.7 21.3 %collective-permute-start.8 = (bf16[320,512]{1,0:T(8,128)(2,1)S(1)}, bf16[320,512]{1,0:T(8,128)(2,1)S(1)}, u32[]{:S(2)}, u32[]{:S(2)}) collective-permute-start(bf16[320,512]{1,0:T(8,128)(2,1)S(1)} %collective-permute-done.refs_10_.refs_4_.refs_12_.refs_6_.refs_2_), channel_id=1, source_target_pairs={{0,4},{4,0},{1,5},{5,1},{2,6},{6,2},{3,7},{7,3},{8,12},{12,8},{9,1... | collective-permute-start | bytes 983048 | tf_op jit(solution)/shard_map/ppermute | solution.py:52
  68.2 33.4 %collective-permute-start.18 = (bf16[64,2688]{1,0:T(8,128)(2,1)S(1)}, bf16[64,2688]{1,0:T(8,128)(2,1)S(1)}, u32[]{:S(2)}, u32[]{:S(2)}) collective-permute-start(bf16[64,2688]{1,0:T(8,128)(2,1)S(1)} %copy-done.24), channel_id=1, source_target_pairs={{0,16},{8,24},{16,0},{24,8},{1,17},{9,25},{17,1},{25,9},{2,18},{10... | collective-permute-start | bytes 1032200 | tf_op jit(solution)/shard_map/ppermute | solution.py:52
  70.5 22.0 %collective-permute-start.15 = (bf16[320,512]{1,0:T(8,128)(2,1)S(1)}, bf16[320,512]{1,0:T(8,128)(2,1)S(1)}, u32[]{:S(2)}, u32[]{:S(2)}) collective-permute-start(bf16[320,512]{1,0:T(8,128)(2,1)S(1)} %collective-permute-done.6.refs_14_.refs_8_.refs_16_.refs_10_.refs_6_), channel_id=1, source_target_pairs={{0,2},{2,0},{1,3},{3,1},{4,6},{6,4},{5,7},{7,5},{8,10},{10,8},{9,1... | collective-permute-start | bytes 983048 | tf_op jit(solution)/shard_map/ppermute | solution.py:52
  75.3 26.2 %collective-permute-start.10 = (bf16[320,512]{1,0:T(8,128)(2,1)S(1)}, bf16[320,512]{1,0:T(8,128)(2,1)S(1)}, u32[]{:S(2)}, u32[]{:S(2)}) collective-permute-start(bf16[320,512]{1,0:T(8,128)(2,1)S(1)} %collective-permute-done.6.refs_14_.refs_8_.refs_16_.refs_10_.refs_6_), channel_id=1, source_target_pairs={{0,4},{4,0},{1,5},{5,1},{2,6},{6,2},{3,7},{7,3},{8,12},{12,8},{9,1... | collective-permute-start | bytes 983048 | tf_op jit(solution)/shard_map/ppermute | solution.py:52
  78.4 25.2 %collective-permute-start.13 = (bf16[320,512]{1,0:T(8,128)(2,1)S(1)}, bf16[320,512]{1,0:T(8,128)(2,1)S(1)}, u32[]{:S(2)}, u32[]{:S(2)}) collective-permute-start(bf16[320,512]{1,0:T(8,128)(2,1)S(1)} %collective-permute-done.5.refs_12_.refs_6_.refs_14_.refs_8_.refs_4_), channel_id=1, source_target_pairs={{0,2},{2,0},{1,3},{3,1},{4,6},{6,4},{5,7},{7,5},{8,10},{10,8},{9,1... | collective-permute-start | bytes 983048 | tf_op jit(solution)/shard_map/ppermute | solution.py:52
  89.0 27.6 %collective-permute-start.7 = (bf16[320,896]{1,0:T(8,128)(2,1)S(1)}, bf16[320,896]{1,0:T(8,128)(2,1)S(1)}, u32[]{:S(2)}, u32[]{:S(2)}) collective-permute-start(bf16[320,896]{1,0:T(8,128)(2,1)S(1)} %copy-done.18), channel_id=1, source_target_pairs={{0,16},{8,24},{16,0},{24,8},{1,17},{9,25},{17,1},{25,9},{2,18},{10... | collective-permute-start | bytes 1720328 | tf_op jit(solution)/shard_map/ppermute | solution.py:52
  92.5 23.1 %collective-permute-start.20 = (bf16[64,2688]{1,0:T(8,128)(2,1)S(1)}, bf16[64,2688]{1,0:T(8,128)(2,1)S(1)}, u32[]{:S(2)}, u32[]{:S(2)}) collective-permute-start(bf16[64,2688]{1,0:T(8,128)(2,1)S(1)} %copy-done.24), channel_id=1, source_target_pairs={{0,1},{1,0},{2,3},{3,2},{4,5},{5,4},{6,7},{7,6},{8,9},{9,8},{10,11... | collective-permute-start | bytes 1032200 | tf_op jit(solution)/shard_map/ppermute | solution.py:52
  129.7 20.0 %collective-permute-start.24 = (bf16[320,512]{1,0:T(8,128)(2,1)}, bf16[320,512]{1,0:T(8,128)(2,1)S(1)}, u32[]{:S(2)}, u32[]{:S(2)}) collective-permute-start(bf16[320,512]{1,0:T(8,128)(2,1)} %get-tuple-element.872), channel_id=1, source_target_pairs={{0,16},{8,24},{16,0},{24,8},{1,17},{9,25},{17,1},{25,9},{2,18},{10... | collective-permute-start | bytes 983048 | tf_op jit(solution)/shard_map/ppermute | solution.py:52
  150.6 283.5 %reduce-scatter.9.cloned.1.call-start = ((), (), s32[]{:S(2)}) async-start(), calls=%async_computation.6 | async-start | bytes 6553600 | tf_op jit(solution)/shard_map/reduce_scatter | solution.py:996
  150.9 16.2 %collective-permute-start.26 = (bf16[512,384]{1,0:T(8,128)(2,1)S(1)}, bf16[512,384]{1,0:T(8,128)(2,1)S(1)}, u32[]{:S(2)}, u32[]{:S(2)}) collective-permute-start(bf16[512,384]{1,0:T(8,128)(2,1)S(1)} %copy-done.21), channel_id=1, source_target_pairs={{0,4},{4,0},{1,5},{5,1},{2,6},{6,2},{3,7},{7,3},{8,12},{12,8},{9,1... | collective-permute-start | bytes 1179656 | tf_op jit(solution)/shard_map/ppermute | solution.py:52
  150.9 26.1 %collective-permute-start.25 = (bf16[320,896]{1,0:T(8,128)(2,1)S(1)}, bf16[320,896]{1,0:T(8,128)(2,1)S(1)}, u32[]{:S(2)}, u32[]{:S(2)}) collective-permute-start(bf16[320,896]{1,0:T(8,128)(2,1)S(1)} %copy-done.15), channel_id=1, source_target_pairs={{0,24},{8,16},{16,8},{24,0},{1,25},{9,17},{17,9},{25,1},{2,26},{10... | collective-permute-start | bytes 1720328 | tf_op jit(solution)/shard_map/ppermute | solution.py:52
  177.7 24.6 %collective-permute-start.29 = (bf16[320,896]{1,0:T(8,128)(2,1)S(1)}, bf16[320,896]{1,0:T(8,128)(2,1)S(1)}, u32[]{:S(2)}, u32[]{:S(2)}) collective-permute-start(bf16[320,896]{1,0:T(8,128)(2,1)S(1)} %collective-permute-done.25.refs_10_.refs_6_), channel_id=1, source_target_pairs={{0,2},{2,0},{1,3},{3,1},{4,6},{6,4},{5,7},{7,5},{8,10},{10,8},{9,1... | collective-permute-start | bytes 1720328 | tf_op jit(solution)/shard_map/ppermute | solution.py:52
  179.1 24.0 %collective-permute-start.28 = (bf16[320,896]{1,0:T(8,128)(2,1)S(1)}, bf16[320,896]{1,0:T(8,128)(2,1)S(1)}, u32[]{:S(2)}, u32[]{:S(2)}) collective-permute-start(bf16[320,896]{1,0:T(8,128)(2,1)S(1)} %collective-permute-done.25.refs_10_.refs_6_), channel_id=1, source_target_pairs={{0,4},{4,0},{1,5},{5,1},{2,6},{6,2},{3,7},{7,3},{8,12},{12,8},{9,1... | collective-permute-start | bytes 1720328 | tf_op jit(solution)/shard_map/ppermute | solution.py:52
  183.0 17.6 %collective-permute-start.27 = (bf16[320,512]{1,0:T(8,128)(2,1)S(1)}, bf16[320,512]{1,0:T(8,128)(2,1)S(1)}, u32[]{:S(2)}, u32[]{:S(2)}) collective-permute-start(bf16[320,512]{1,0:T(8,128)(2,1)S(1)} %copy-done.52), channel_id=1, source_target_pairs={{0,24},{8,16},{16,8},{24,0},{1,25},{9,17},{17,9},{25,1},{2,26},{10... | collective-permute-start | bytes 983048 | tf_op jit(solution)/shard_map/ppermute | solution.py:52
  203.1 17.5 %collective-permute-start.38 = (bf16[64,2560]{1,0:T(8,128)(2,1)}, bf16[64,2560]{1,0:T(8,128)(2,1)S(1)}, u32[]{:S(2)}, u32[]{:S(2)}) collective-permute-start(bf16[64,2560]{1,0:T(8,128)(2,1)} %get-tuple-element.994), channel_id=1, source_target_pairs={{0,16},{8,24},{16,0},{24,8},{1,17},{9,25},{17,1},{25,9},{2,18},{10... | collective-permute-start | bytes 983048 | tf_op jit(solution)/shard_map/ppermute | solution.py:52
  224.6 23.5 %collective-permute-start.33 = (bf16[320,896]{1,0:T(8,128)(2,1)S(1)}, bf16[320,896]{1,0:T(8,128)(2,1)S(1)}, u32[]{:S(2)}, u32[]{:S(2)}) collective-permute-start(bf16[320,896]{1,0:T(8,128)(2,1)S(1)} %collective-permute-done.29.refs_12_.refs_8_), channel_id=1, source_target_pairs={{0,4},{4,0},{1,5},{5,1},{2,6},{6,2},{3,7},{7,3},{8,12},{12,8},{9,1... | collective-permute-start | bytes 1720328 | tf_op jit(solution)/shard_map/ppermute | solution.py:52
  225.9 20.7 %collective-permute-start.34 = (bf16[320,512]{1,0:T(8,128)(2,1)S(1)}, bf16[320,512]{1,0:T(8,128)(2,1)S(1)}, u32[]{:S(2)}, u32[]{:S(2)}) collective-permute-start(bf16[320,512]{1,0:T(8,128)(2,1)S(1)} %collective-permute-done.27.refs_14_.refs_10_), channel_id=1, source_target_pairs={{0,4},{4,0},{1,5},{5,1},{2,6},{6,2},{3,7},{7,3},{8,12},{12,8},{9,1... | collective-permute-start | bytes 983048 | tf_op jit(solution)/shard_map/ppermute | solution.py:52
  227.4 20.8 %collective-permute-start.39 = (bf16[64,2560]{1,0:T(8,128)(2,1)}, bf16[64,2560]{1,0:T(8,128)(2,1)S(1)}, u32[]{:S(2)}, u32[]{:S(2)}) collective-permute-start(bf16[64,2560]{1,0:T(8,128)(2,1)} %get-tuple-element.1021.refs_0_), channel_id=1, source_target_pairs={{0,8},{8,0},{16,24},{24,16},{1,9},{9,1},{17,25},{25,17},{2,10},{10... | collective-permute-start | bytes 983048 | tf_op jit(solution)/shard_map/ppermute | solution.py:52
  293.4 16.8 %collective-permute-start.50 = (bf16[64,2560]{1,0:T(8,128)(2,1)}, bf16[64,2560]{1,0:T(8,128)(2,1)S(1)}, u32[]{:S(2)}, u32[]{:S(2)}) collective-permute-start(bf16[64,2560]{1,0:T(8,128)(2,1)} %get-tuple-element.1046), channel_id=1, source_target_pairs={{0,16},{8,24},{16,0},{24,8},{1,17},{9,25},{17,1},{25,9},{2,18},{10... | collective-permute-start | bytes 983048 | tf_op jit(solution)/shard_map/ppermute | solution.py:52
  316.1 16.2 %collective-permute-start.51 = (bf16[64,2560]{1,0:T(8,128)(2,1)}, bf16[64,2560]{1,0:T(8,128)(2,1)S(1)}, u32[]{:S(2)}, u32[]{:S(2)}) collective-permute-start(bf16[64,2560]{1,0:T(8,128)(2,1)} %get-tuple-element.1303.refs_0_.d_own), channel_id=1, source_target_pairs={{0,8},{8,0},{16,24},{24,16},{1,9},{9,1},{17,25},{25,17},{2,10},{10... | collective-permute-start | bytes 983048 | tf_op jit(solution)/shard_map/ppermute | solution.py:52
  349.2 128.0 %reduce-scatter.7.cloned.1.call-start = ((), (), s32[]{:S(2)}) async-start(), calls=%async_computation.5 | async-start | bytes 5734400 | tf_op jit(solution)/shard_map/reduce_scatter | solution.py:996
  384.9 188.0 %reduce-scatter.5.cloned.1.call-start = ((), (), s32[]{:S(2)}) async-start(), calls=%async_computation.4 | async-start | bytes 5734400 | tf_op jit(solution)/shard_map/reduce_scatter | solution.py:996
  385.9 16.3 %collective-permute-start.64 = (bf16[64,2560]{1,0:T(8,128)(2,1)S(1)}, bf16[64,2560]{1,0:T(8,128)(2,1)S(1)}, u32[]{:S(2)}, u32[]{:S(2)}) collective-permute-start(bf16[64,2560]{1,0:T(8,128)(2,1)S(1)} %copy-done.86), channel_id=1, source_target_pairs={{0,8},{8,0},{16,24},{24,16},{1,9},{9,1},{17,25},{25,17},{2,10},{10... | collective-permute-start | bytes 983048 | tf_op jit(solution)/shard_map/ppermute | solution.py:52
  386.1 16.1 %collective-permute-start.65 = (bf16[64,2560]{1,0:T(8,128)(2,1)S(1)}, bf16[64,2560]{1,0:T(8,128)(2,1)S(1)}, u32[]{:S(2)}, u32[]{:S(2)}) collective-permute-start(bf16[64,2560]{1,0:T(8,128)(2,1)S(1)} %copy-done.84), channel_id=1, source_target_pairs={{0,16},{8,24},{16,0},{24,8},{1,17},{9,25},{17,1},{25,9},{2,18},{10... | collective-permute-start | bytes 983048 | tf_op jit(solution)/shard_map/ppermute | solution.py:52
  406.9 199.9 %reduce-scatter.11.cloned.1.call-start = ((), (), s32[]{:S(2)}) async-start(), calls=%async_computation.7 | async-start | bytes 3276800 | tf_op jit(solution)/shard_map/reduce_scatter | solution.py:996
  407.9 16.4 %collective-permute-start.68 = (bf16[64,2560]{1,0:T(8,128)(2,1)S(1)}, bf16[64,2560]{1,0:T(8,128)(2,1)S(1)}, u32[]{:S(2)}, u32[]{:S(2)}) collective-permute-start(bf16[64,2560]{1,0:T(8,128)(2,1)S(1)} %copy-done.60), channel_id=1, source_target_pairs={{0,16},{8,24},{16,0},{24,8},{1,17},{9,25},{17,1},{25,9},{2,18},{10... | collective-permute-start | bytes 983048 | tf_op jit(solution)/shard_map/ppermute | solution.py:52
  436.5 18.1 %collective-permute-start.75 = (bf16[320,512]{1,0:T(8,128)(2,1)S(1)}, bf16[320,512]{1,0:T(8,128)(2,1)S(1)}, u32[]{:S(2)}, u32[]{:S(2)}) collective-permute-start(bf16[320,512]{1,0:T(8,128)(2,1)S(1)} %get-tuple-element.1598), channel_id=1, source_target_pairs={{0,24},{8,16},{16,8},{24,0},{1,25},{9,17},{17,9},{25,1},{2,26},{10... | collective-permute-start | bytes 983048 | tf_op jit(solution)/shard_map/ppermute | solution.py:52
  455.3 26.6 %collective-permute-start.77 = (bf16[512,320]{1,0:T(8,128)(2,1)}, bf16[512,320]{1,0:T(8,128)(2,1)S(1)}, u32[]{:S(2)}, u32[]{:S(2)}) collective-permute-start(bf16[512,320]{1,0:T(8,128)(2,1)} %get-tuple-element.1434), channel_id=1, source_target_pairs={{0,4},{4,0},{1,5},{5,1},{2,6},{6,2},{3,7},{7,3},{8,12},{12,8},{9,1... | collective-permute-start | bytes 983048 | tf_op jit(solution)/shard_map/ppermute | solution.py:52
  456.0 30.1 %collective-permute-start.76 = (bf16[320,512]{1,0:T(8,128)(2,1)S(1)}, bf16[320,512]{1,0:T(8,128)(2,1)S(1)}, u32[]{:S(2)}, u32[]{:S(2)}) collective-permute-start(bf16[320,512]{1,0:T(8,128)(2,1)S(1)} %get-tuple-element.1429), channel_id=1, source_target_pairs={{0,16},{8,24},{16,0},{24,8},{1,17},{9,25},{17,1},{25,9},{2,18},{10... | collective-permute-start | bytes 983048 | tf_op jit(solution)/shard_map/ppermute | solution.py:52
  478.6 20.3 %collective-permute-start.78 = (bf16[320,896]{1,0:T(8,128)(2,1)S(1)}, bf16[320,896]{1,0:T(8,128)(2,1)S(1)}, u32[]{:S(2)}, u32[]{:S(2)}) collective-permute-start(bf16[320,896]{1,0:T(8,128)(2,1)S(1)} %get-tuple-element.1602), channel_id=1, source_target_pairs={{0,24},{8,16},{16,8},{24,0},{1,25},{9,17},{17,9},{25,1},{2,26},{10... | collective-permute-start | bytes 1720328 | tf_op jit(solution)/shard_map/ppermute | solution.py:52
  499.7 27.6 %collective-permute-start.85 = (bf16[640,512]{1,0:T(8,128)(2,1)}, bf16[640,512]{1,0:T(8,128)(2,1)S(1)}, u32[]{:S(2)}, u32[]{:S(2)}) collective-permute-start(bf16[640,512]{1,0:T(8,128)(2,1)} %get-tuple-element.1563), channel_id=1, source_target_pairs={{0,2},{2,0},{1,3},{3,1},{4,6},{6,4},{5,7},{7,5},{8,10},{10,8},{9,1... | collective-permute-start | bytes 1966088 | tf_op jit(solution)/shard_map/ppermute | solution.py:52
  509.2 37.4 %collective-permute-start.79 = (bf16[192,2560]{1,0:T(8,128)(2,1)}, bf16[192,2560]{1,0:T(8,128)(2,1)S(1)}, u32[]{:S(2)}, u32[]{:S(2)}) collective-permute-start(bf16[192,2560]{1,0:T(8,128)(2,1)} %get-tuple-element.1536), channel_id=1, source_target_pairs={{0,1},{1,0},{2,3},{3,2},{4,5},{5,4},{6,7},{7,6},{8,9},{9,8},{10,11... | collective-permute-start | bytes 2949128 | tf_op jit(solution)/shard_map/ppermute | solution.py:52
  509.7 36.7 %collective-permute-start.84 = (bf16[640,512]{1,0:T(8,128)(2,1)S(1)}, bf16[640,512]{1,0:T(8,128)(2,1)S(1)}, u32[]{:S(2)}, u32[]{:S(2)}) collective-permute-start(bf16[640,512]{1,0:T(8,128)(2,1)S(1)} %copy-done.11), channel_id=1, source_target_pairs={{0,2},{2,0},{1,3},{3,1},{4,6},{6,4},{5,7},{7,5},{8,10},{10,8},{9,1... | collective-permute-start | bytes 1966088 | tf_op jit(solution)/shard_map/ppermute | solution.py:52
  511.0 60.6 %collective-permute-start.66 = (bf16[320,896]{1,0:T(8,128)(2,1)S(1)}, bf16[320,896]{1,0:T(8,128)(2,1)S(1)}, u32[]{:S(2)}, u32[]{:S(2)}) collective-permute-start(bf16[320,896]{1,0:T(8,128)(2,1)S(1)} %get-tuple-element.1603), channel_id=1, source_target_pairs={{0,16},{8,24},{16,0},{24,8},{1,17},{9,25},{17,1},{25,9},{2,18},{10... | collective-permute-start | bytes 1720328 | tf_op jit(solution)/shard_map/ppermute | solution.py:52
  521.8 24.8 %collective-permute-start.81 = (bf16[64,2560]{1,0:T(8,128)(2,1)}, bf16[64,2560]{1,0:T(8,128)(2,1)S(1)}, u32[]{:S(2)}, u32[]{:S(2)}) collective-permute-start(bf16[64,2560]{1,0:T(8,128)(2,1)} %shard_map.259), channel_id=1, source_target_pairs={{0,8},{8,0},{16,24},{24,16},{1,9},{9,1},{17,25},{25,17},{2,10},{10... | collective-permute-start | bytes 983048 | tf_op jit(solution)/shard_map/ppermute | solution.py:52
  527.5 32.2 %collective-permute-start.86 = (bf16[640,512]{1,0:T(8,128)(2,1)S(1)}, bf16[640,512]{1,0:T(8,128)(2,1)S(1)}, u32[]{:S(2)}, u32[]{:S(2)}) collective-permute-start(bf16[640,512]{1,0:T(8,128)(2,1)S(1)} %add_convert_fusion), channel_id=1, source_target_pairs={{0,4},{4,0},{1,5},{5,1},{2,6},{6,2},{3,7},{7,3},{8,12},{12,8},{9,1... | collective-permute-start | bytes 1966088 | tf_op jit(solution)/shard_map/ppermute | solution.py:52
  572.4 16.7 %collective-permute-start.89 = (bf16[64,2560]{1,0:T(8,128)(2,1)}, bf16[64,2560]{1,0:T(8,128)(2,1)S(1)}, u32[]{:S(2)}, u32[]{:S(2)}) collective-permute-start(bf16[64,2560]{1,0:T(8,128)(2,1)} %shard_map.262.p0), channel_id=1, source_target_pairs={{0,2},{2,0},{1,3},{3,1},{4,6},{6,4},{5,7},{7,5},{8,10},{10,8},{9,1... | collective-permute-start | bytes 983048 | tf_op jit(solution)/shard_map/ppermute | solution.py:52
  575.2 27.0 %collective-permute-start.87 = (bf16[320,896]{1,0:T(8,128)(2,1)S(1)}, bf16[320,896]{1,0:T(8,128)(2,1)S(1)}, u32[]{:S(2)}, u32[]{:S(2)}) collective-permute-start(bf16[320,896]{1,0:T(8,128)(2,1)S(1)} %get-tuple-element.1566), channel_id=1, source_target_pairs={{0,8},{8,0},{16,24},{24,16},{1,9},{9,1},{17,25},{25,17},{2,10},{10... | collective-permute-start | bytes 1720328 | tf_op jit(solution)/shard_map/ppermute | solution.py:52
  575.8 19.8 %collective-permute-start.91 = (bf16[320,512]{1,0:T(8,128)(2,1)S(1)}, bf16[320,512]{1,0:T(8,128)(2,1)S(1)}, u32[]{:S(2)}, u32[]{:S(2)}) collective-permute-start(bf16[320,512]{1,0:T(8,128)(2,1)S(1)} %get-tuple-element.1571), channel_id=1, source_target_pairs={{0,16},{8,24},{16,0},{24,8},{1,17},{9,25},{17,1},{25,9},{2,18},{10... | collective-permute-start | bytes 983048 | tf_op jit(solution)/shard_map/ppermute | solution.py:52
  578.3 23.9 %collective-permute-start.92 = (bf16[320,512]{1,0:T(8,128)(2,1)S(1)}, bf16[320,512]{1,0:T(8,128)(2,1)S(1)}, u32[]{:S(2)}, u32[]{:S(2)}) collective-permute-start(bf16[320,512]{1,0:T(8,128)(2,1)S(1)} %get-tuple-element.1572), channel_id=1, source_target_pairs={{0,24},{8,16},{16,8},{24,0},{1,25},{9,17},{17,9},{25,1},{2,26},{10... | collective-permute-start | bytes 983048 | tf_op jit(solution)/shard_map/ppermute | solution.py:52
  579.5 22.6 %collective-permute-start.88 = (bf16[64,2560]{1,0:T(8,128)(2,1)S(1)}, bf16[64,2560]{1,0:T(8,128)(2,1)S(1)}, u32[]{:S(2)}, u32[]{:S(2)}) collective-permute-start(bf16[64,2560]{1,0:T(8,128)(2,1)S(1)} %copy-done.67), channel_id=1, source_target_pairs={{0,1},{1,0},{2,3},{3,2},{4,5},{5,4},{6,7},{7,6},{8,9},{9,8},{10,11... | collective-permute-start | bytes 983048 | tf_op jit(solution)/shard_map/ppermute | solution.py:52
  (155 other events, 1546.1 us)
Sparse Core Ops, SparseCore 0:
  63.9 104.3 all-gather.4
  170.6 57.7 all-gather.6
  349.3 60.6 reduce-scatter.8
  412.9 64.2 reduce-scatter.6
  480.2 77.3 reduce-scatter.4
  560.4 46.4 reduce-scatter.10

commit v7 on v6

--- a/solution.py
+++ b/solution.py
@@ -17,7 +17,7 @@
 F32 = jnp.float32
 FACTOR = HEAD_DIM**-0.5
 LOG2E = 1.4426950408889634
-LIMIT = 56 * 1024 * 1024
+LIMIT = 48 * 1024 * 1024
 
 PLAIN = (((1,), (0,)), ((), ()))
 LAST = (((1,), (1,)), ((), ()))
@@ -39,7 +39,7 @@
         in_specs=in_specs,
         out_specs=out_specs,
         scratch_shapes=list(scratch),
-        compiler_params=pltpu.CompilerParams(vmem_limit_bytes=LIMIT),
+        compiler_params=pltpu.CompilerParams(vmem_limit_bytes=LIMIT if cost > 4 else 16 * 1024 * 1024),
         cost_estimate=pl.CostEstimate(flops=cost * 10**9, bytes_accessed=0, transcendentals=0),
     )
 

time: 638 us -> 617 us (0.967)
  Pallas kernels: 168 us -> 117 us
  starting transfers between devices: 103 us -> 128 us
  local copies, waits for them, and re-layouts: 35.3 us -> 50.2 us
  waiting for transfers between devices: 303 us -> 289 us
    ppermute x95, starting transfers between devices: 102 us -> 127 us  [hop(): return lax.ppermute(value, axis, [(i, i ^ k) for i in range(size)])]
    ppermute x95, waiting for transfers between devices: 282 us -> 258 us  [hop(): return lax.ppermute(value, axis, [(i, i ^ k) for i in range(size)])]
    unnamed x204 -> x260, local copies, waits for them, and re-layouts: 23.4 us -> 39.8 us
    reduce_scatter x4, waiting for transfers between devices: 21.3 us -> 31.1 us  [scatter_blocks(): got = lax.psum_scatter(blocks, ('y', 'x'), scatter_dimension=0, tiled=True)]
    pallas_call x4, Pallas kernels: 9.62 us -> 0.81 us  [second_sum(): call(second_sum_body, [shape(three.shape)] * 2, [VM] * 4, [VM] * 2)]
    pallas_call x4, Pallas kernels: 7.68 us -> 0.32 us  [first_sum(): return call(first_sum_body, shape(mine.shape), [VM] * 2, VM)(mine, got)]
  transfers between devices with their start and end apart: 101 -> 101, of which waited for: 50 -> 44; matrix products, arithmetic and copies ran while one was open for 2% -> 2% of each run, Pallas kernels for 21% -> 15%
where the time goes in v7:
time: 617 us; the launch traced here: 609 us
  waiting for transfers between devices  289 us (47%)
  starting transfers between devices  128 us (21%)
  Pallas kernels  117 us (19%)
  local copies, waits for them, and re-layouts  50.2 us (8%)
  between operations  16.4 us (3%)
  other arithmetic  8.26 us (1%)
    ppermute x95, waiting for transfers between devices, hop(): return lax.ppermute(value, axis, [(i, i ^ k) for i in range(size)])  258 us
    ppermute x95, starting transfers between devices, hop(): return lax.ppermute(value, axis, [(i, i ^ k) for i in range(size)])  127 us
    unnamed x260, local copies, waits for them, and re-layouts  39.8 us
    reduce_scatter x4, waiting for transfers between devices, scatter_blocks(): got = lax.psum_scatter(blocks, ('y', 'x'), scatter_dimension=0, tiled=True)  31.1 us
    pallas_call x1, Pallas kernels, feed(): call(functools.partial(feed_body, fw, inner), [shape((8 * rows, 512))] *...  15.8 us
    pallas_call x1, Pallas kernels, attend_back(): call(functools.partial(attend_back_body, sides), [shape(q.shape), shape((...  13.8 us
    pallas_call x1, Pallas kernels, feed_back(): call(functools.partial(feed_back_body, fw, inner), [shape((rows, 2 * fw))...  13.8 us
  transfers between devices with their start and end apart: 101, of which 44 were waited for; matrix products, arithmetic and copies ran while one was open for 2% of the time, Pallas kernels for 15%

profile of v7, /device:TPU:0, one launch (start us, length us, event | category | flops | bytes accessed | tf_op | source)
XLA Modules:
  0.0 609.0 jit_solution(11999286118413100211)
XLA Ops:
  32.8 21.9 %collective-permute-done.5.refs_12_.refs_6_.refs_14_.refs_8_.refs_4_ = bf16[320,512]{1,0:T(8,128)(2,1)} collective-permute-done((bf16[320,512]{1,0:T(8,128)(2,1)S(1)}, bf16[320,512]{1,0:T(8,128)(2,1)}, u32[]{:S(2)}, u32[]{:S(2)}) %collective-permute-start.5) | collective-permute-done | bytes 327712 | tf_op jit(solution)/shard_map/ppermute | solution.py:52
  59.5 3.1 collective-permute-done.6.refs_14_.refs_8_.refs_16_.refs_10_.refs_6_
  72.8 3.9 collective-permute-done.12.refs_19_.refs_13_.refs_21_.refs_15_.refs_11_
  81.6 8.2 %collective-permute-done.8.refs_11_.refs_5_.refs_13_.refs_7_.refs_3_ = bf16[320,512]{1,0:T(8,128)(2,1)S(1)} collective-permute-done((bf16[320,512]{1,0:T(8,128)(2,1)}, bf16[320,512]{1,0:T(8,128)(2,1)S(1)}, u32[]{:S(2)}, u32[]{:S(2)}) %collective-permute-start.8) | collective-permute-done | bytes 327712 | tf_op jit(solution)/shard_map/ppermute | solution.py:52
  90.2 3.1 collective-permute-done.15.refs_22_.refs_16_.refs_24_.refs_18_.refs_14_
  93.3 9.1 %collective-permute-done.10.refs_15_.refs_9_.refs_17_.refs_11_.refs_7_ = bf16[320,512]{1,0:T(8,128)(2,1)S(1)} collective-permute-done((bf16[320,512]{1,0:T(8,128)(2,1)}, bf16[320,512]{1,0:T(8,128)(2,1)S(1)}, u32[]{:S(2)}, u32[]{:S(2)}) %collective-permute-start.10) | collective-permute-done | bytes 327712 | tf_op jit(solution)/shard_map/ppermute | solution.py:52
  106.8 8.8 %collective-permute-done.9.refs_13_.refs_7_.refs_15_.refs_9_.refs_5_ = bf16[320,512]{1,0:T(8,128)(2,1)S(1)} collective-permute-done((bf16[320,512]{1,0:T(8,128)(2,1)}, bf16[320,512]{1,0:T(8,128)(2,1)S(1)}, u32[]{:S(2)}, u32[]{:S(2)}) %collective-permute-start.9) | collective-permute-done | bytes 327712 | tf_op jit(solution)/shard_map/ppermute | solution.py:52
  120.1 9.4 %collective-permute-done.16.refs_23_.refs_17_.refs_25_.refs_19_.refs_15_ = bf16[320,512]{1,0:T(8,128)(2,1)S(1)} collective-permute-done((bf16[320,512]{1,0:T(8,128)(2,1)S(1)}, bf16[320,512]{1,0:T(8,128)(2,1)S(1)}, u32[]{:S(2)}, u32[]{:S(2)}) %collective-permute-start.16) | collective-permute-done | bytes 327712 | tf_op jit(solution)/shard_map/ppermute | solution.py:52
  132.6 9.3 %shard_map.239 = (bf16[512,2560]{1,0:T(8,128)(2,1)}, bf16[512,320]{1,0:T(8,128)(2,1)}, bf16[512,384]{1,0:T(8,128)(2,1)}, f32[8,2560]{1,0:T(8,128)S(1)}, f32[8,512]{1,0:T(8,128)S(1)}) custom-call(s32[5]{0:T(128)S(1)} %stack.36.pos, f32[512,40]{1,0:T(8,128)S(1)} %get-tuple-element.1609.cosine, f32[512,40]{1,0:T(8,128)S(1)} %get-tuple-element.1608.sine, ...), custom_call_target="tpu_custom_call" | custom-call | flops 12000000000 | tf_op jit(solution)/shard_map/pallas_call | solution.py:359
  142.0 7.9 %collective-permute-done.24 = bf16[320,512]{1,0:T(8,128)(2,1)S(1)} collective-permute-done((bf16[320,512]{1,0:T(8,128)(2,1)S(1)}, bf16[320,512]{1,0:T(8,128)(2,1)S(1)}, u32[]{:S(2)}, u32[]{:S(2)}) %collective-permute-start.24) | collective-permute-done | bytes 327712 | tf_op jit(solution)/shard_map/ppermute | solution.py:52
  153.2 14.4 %collective-permute-done.26.refs_1_.refs_9_ = bf16[512,384]{1,0:T(8,128)(2,1)S(1)} collective-permute-done((bf16[512,384]{1,0:T(8,128)(2,1)}, bf16[512,384]{1,0:T(8,128)(2,1)S(1)}, u32[]{:S(2)}, u32[]{:S(2)}) %collective-permute-start.26) | collective-permute-done | bytes 393248 | tf_op jit(solution)/shard_map/ppermute | solution.py:52
  169.4 8.0 %shard_map.240 = (bf16[512,256]{1,0:T(8,128)(2,1)S(1)}, bf16[512,256]{1,0:T(8,128)(2,1)S(1)}, f32[8,512]{1,0:T(8,128)S(1)}, bf16[64,2560]{1,0:T(8,128)(2,1)S(1)}...) custom-call(s32[5]{0:T(128)S(1)} %stack.36.pos, ...), custom_call_target="tpu_custom_call" | custom-call | flops 12000000000 | tf_op jit(solution)/shard_map/pallas_call | solution.py:471
  188.9 8.1 %collective-permute-done.32.three = bf16[64,2560]{1,0:T(8,128)(2,1)S(1)} collective-permute-done((bf16[64,2560]{1,0:T(8,128)(2,1)S(1)}, bf16[64,2560]{1,0:T(8,128)(2,1)S(1)}, u32[]{:S(2)}, u32[]{:S(2)}) %collective-permute-start.32) | collective-permute-done | bytes 327712 | tf_op jit(solution)/shard_map/ppermute | solution.py:52
  197.2 6.7 %collective-permute-done.27.refs_14_.refs_10_ = bf16[320,512]{1,0:T(8,128)(2,1)S(1)} collective-permute-done((bf16[320,512]{1,0:T(8,128)(2,1)S(1)}, bf16[320,512]{1,0:T(8,128)(2,1)S(1)}, u32[]{:S(2)}, u32[]{:S(2)}) %collective-permute-start.27) | collective-permute-done | bytes 327712 | tf_op jit(solution)/shard_map/ppermute | solution.py:52
  207.9 12.3 %collective-permute-done.37.one = bf16[64,2560]{1,0:T(8,128)(2,1)S(1)} collective-permute-done((bf16[64,2560]{1,0:T(8,128)(2,1)S(1)}, bf16[64,2560]{1,0:T(8,128)(2,1)S(1)}, u32[]{:S(2)}, u32[]{:S(2)}) %collective-permute-start.37) | collective-permute-done | bytes 327712 | tf_op jit(solution)/shard_map/ppermute | solution.py:52
  230.4 7.7 %collective-permute-done.40.refs_2_ = bf16[64,2560]{1,0:T(8,128)(2,1)S(1)} collective-permute-done((bf16[64,2560]{1,0:T(8,128)(2,1)S(1)}, bf16[64,2560]{1,0:T(8,128)(2,1)S(1)}, u32[]{:S(2)}, u32[]{:S(2)}) %collective-permute-start.40) | collective-permute-done | bytes 327712 | tf_op jit(solution)/shard_map/ppermute | solution.py:52
  238.1 8.0 %collective-permute-done.34.refs_15_.refs_11_ = bf16[320,512]{1,0:T(8,128)(2,1)S(1)} collective-permute-done((bf16[320,512]{1,0:T(8,128)(2,1)S(1)}, bf16[320,512]{1,0:T(8,128)(2,1)S(1)}, u32[]{:S(2)}, u32[]{:S(2)}) %collective-permute-start.34) | collective-permute-done | bytes 327712 | tf_op jit(solution)/shard_map/ppermute | solution.py:52
  248.4 6.4 %collective-permute-done.36.refs_17_.refs_13_ = bf16[320,512]{1,0:T(8,128)(2,1)S(1)} collective-permute-done((bf16[320,512]{1,0:T(8,128)(2,1)S(1)}, bf16[320,512]{1,0:T(8,128)(2,1)S(1)}, u32[]{:S(2)}, u32[]{:S(2)}) %collective-permute-start.36) | collective-permute-done | bytes 327712 | tf_op jit(solution)/shard_map/ppermute | solution.py:52
  254.8 15.8 %shard_map.244 = (bf16[512,512]{1,0:T(8,128)(2,1)S(1)}, bf16[512,512]{1,0:T(8,128)(2,1)}, bf16[512,512]{1,0:T(8,128)(2,1)}, bf16[512,512]{1,0:T(8,128)(2,1)}, bf...) custom-call(s32[5]{0:T(128)S(1)} %stack.36.pos, ...), custom_call_target="tpu_custom_call" | custom-call | flops 17999998976 | tf_op jit(solution)/shard_map/pallas_call | solution.py:544
  274.1 9.4 %collective-permute-done.48.three = bf16[64,2560]{1,0:T(8,128)(2,1)S(1)} collective-permute-done((bf16[64,2560]{1,0:T(8,128)(2,1)S(1)}, bf16[64,2560]{1,0:T(8,128)(2,1)S(1)}, u32[]{:S(2)}, u32[]{:S(2)}) %collective-permute-start.48) | collective-permute-done | bytes 327712 | tf_op jit(solution)/shard_map/ppermute | solution.py:52
  284.1 3.8 collective-permute-start.50
  288.0 11.8 %collective-permute-done.49.one = bf16[64,2560]{1,0:T(8,128)(2,1)S(1)} collective-permute-done((bf16[64,2560]{1,0:T(8,128)(2,1)S(1)}, bf16[64,2560]{1,0:T(8,128)(2,1)S(1)}, u32[]{:S(2)}, u32[]{:S(2)}) %collective-permute-start.49) | collective-permute-done | bytes 327712 | tf_op jit(solution)/shard_map/ppermute | solution.py:52
  304.6 9.0 %collective-permute-start.51 = (bf16[64,2560]{1,0:T(8,128)(2,1)S(1)}, bf16[64,2560]{1,0:T(8,128)(2,1)S(1)}, u32[]{:S(2)}, u32[]{:S(2)}) collective-permute-start(bf16[64,2560]{1,0:T(8,128)(2,1)S(1)} %get-tuple-element.1303.refs_0_.d_own), channel_id=1, source_target_pairs={{0,8},{8,0},{16,24},{24,16},{1,9},{9,1},{17,25},{25,17},{2,10},{10... | collective-permute-start | bytes 983048 | tf_op jit(solution)/shard_map/ppermute | solution.py:52
  313.6 7.2 %collective-permute-start.53 = (bf16[64,2560]{1,0:T(8,128)(2,1)S(1)}, bf16[64,2560]{1,0:T(8,128)(2,1)S(1)}, u32[]{:S(2)}, u32[]{:S(2)}) collective-permute-start(bf16[64,2560]{1,0:T(8,128)(2,1)S(1)} %collective-permute-done.52.refs_2_), channel_id=1, source_target_pairs={{0,8},{8,0},{16,24},{24,16},{1,9},{9,1},{17,25},{25,17},{2,10},{10... | collective-permute-start | bytes 983048 | tf_op jit(solution)/shard_map/ppermute | solution.py:52
  322.1 6.8 %collective-permute-done.53.refs_3_ = bf16[64,2560]{1,0:T(8,128)(2,1)S(1)} collective-permute-done((bf16[64,2560]{1,0:T(8,128)(2,1)S(1)}, bf16[64,2560]{1,0:T(8,128)(2,1)S(1)}, u32[]{:S(2)}, u32[]{:S(2)}) %collective-permute-start.53) | collective-permute-done | bytes 327712 | tf_op jit(solution)/shard_map/ppermute | solution.py:52
  330.6 6.1 shard_map.248
  342.9 13.8 %shard_map.249 = (bf16[512,896]{1,0:T(8,128)(2,1)}, bf16[512,896]{1,0:T(8,128)(2,1)}, bf16[64,2560]{1,0:T(8,128)(2,1)S(1)}, bf16[64,2560]{1,0:T(8,128)(2,1)S(1)}...) custom-call(s32[5]{0:T(128)S(1)} %stack.36.pos, ...), custom_call_target="tpu_custom_call" | custom-call | flops 16000000000 | tf_op jit(solution)/shard_map/pallas_call | solution.py:587
  361.0 4.6 shard_map.250
  365.6 3.4 collective-permute-done.63.three
  371.2 4.1 collective-permute-start.65
  379.4 4.7 shard_map.254
  390.1 4.3 collective-permute-start.67
  394.4 9.3 %collective-permute-done.68.refs_2_ = bf16[64,2560]{1,0:T(8,128)(2,1)S(1)} collective-permute-done((bf16[64,2560]{1,0:T(8,128)(2,1)S(1)}, bf16[64,2560]{1,0:T(8,128)(2,1)S(1)}, u32[]{:S(2)}, u32[]{:S(2)}) %collective-permute-start.68) | collective-permute-done | bytes 327712 | tf_op jit(solution)/shard_map/ppermute | solution.py:52
  404.8 7.0 %collective-permute-done.69.refs_3_ = bf16[64,2560]{1,0:T(8,128)(2,1)S(1)} collective-permute-done((bf16[64,2560]{1,0:T(8,128)(2,1)S(1)}, bf16[64,2560]{1,0:T(8,128)(2,1)S(1)}, u32[]{:S(2)}, u32[]{:S(2)}) %collective-permute-start.69) | collective-permute-done | bytes 327712 | tf_op jit(solution)/shard_map/ppermute | solution.py:52
  416.9 4.6 collective-permute-start.75
  421.6 13.8 %shard_map.255 = (bf16[512,320]{1,0:T(8,128)(2,1)}, f32[512,320]{1,0:T(8,128)}, bf16[512,320]{1,0:T(8,128)(2,1)}, bf16[512,2560]{1,0:T(8,128)(2,1)}) custom-call(s32[5]{0:T(128)S(1)} %stack.36.pos, bf16[512,320]{1,0:T(8,128)(2,1)} %get-tuple-element.1379.q_ref, f32[8,512]{1,0:T(8,128)S(1)} %get-tuple-element.1380.row_ids, ...), custom_call_target="tpu_custom_call" | custom-call | flops 17999998976 | tf_op jit(solution)/shard_map/pallas_call | solution.py:737
  439.0 23.8 %reduce-scatter.7.cloned.1.call-done = bf16[640,896]{1,0:T(8,128)(2,1)} async-done(((bf16[2560,896]{1,0:T(8,128)(2,1)}), bf16[640,896]{1,0:T(8,128)(2,1)}) %reduce-scatter.7.cloned.1.call-update) | async-done | bytes 1146896 | tf_op jit(solution)/shard_map/reduce_scatter | solution.py:996
  468.7 11.8 %shard_map.257 = (bf16[640,512]{1,0:T(8,128)(2,1)}, bf16[640,512]{1,0:T(8,128)(2,1)}, bf16[640,512]{1,0:T(8,128)(2,1)}, bf16[640,512]{1,0:T(8,128)(2,1)}, bf16[4,640,512]{2,1,0:T(8,128)(2,1)}) custom-call(s32[5]{0:T(128)S(1)} %stack.36.pos, bf16[512,2560]{1,0:T(8,128)(2,1)} %get-tuple-element.1477.first, bf16[512,2560]{1,0:T(8,128)(2,1)} %get-tuple-element.1478.d_all, ...), custom_call_target="tpu_custom_call" | custom-call | flops 12000000000 | tf_op jit(solution)/shard_map/pallas_call | solution.py:847
  482.7 7.0 %shard_map.258 = (bf16[64,2560]{1,0:T(8,128)(2,1)S(1)}, bf16[64,2560]{1,0:T(8,128)(2,1)S(1)}, bf16[64,2560]{1,0:T(8,128)(2,1)S(1)}, bf16[64,2560]{1,0:T(8,128)(2...) custom-call(s32[5]{0:T(128)S(1)} %stack.36.pos, bf16[512,384]{1,0:T(8,128)(2,1)} %copy-done.85, ...), custom_call_target="tpu_custom_call" | custom-call | flops 8000000000 | tf_op jit(solution)/shard_map/pallas_call | solution.py:782
  494.8 11.4 %collective-permute-start.66 = (bf16[320,896]{1,0:T(8,128)(2,1)}, bf16[320,896]{1,0:T(8,128)(2,1)S(1)}, u32[]{:S(2)}, u32[]{:S(2)}) collective-permute-start(bf16[320,896]{1,0:T(8,128)(2,1)} %get-tuple-element.1603), channel_id=1, source_target_pairs={{0,16},{8,24},{16,0},{24,8},{1,17},{9,25},{17,1},{25,9},{2,18},{10... | collective-permute-start | bytes 1720328 | tf_op jit(solution)/shard_map/ppermute | solution.py:52
  507.7 3.2 collective-permute-done.85
  513.7 15.4 %collective-permute-done.84 = bf16[640,512]{1,0:T(8,128)(2,1)} collective-permute-done((bf16[640,512]{1,0:T(8,128)(2,1)}, bf16[640,512]{1,0:T(8,128)(2,1)}, u32[]{:S(2)}, u32[]{:S(2)}) %collective-permute-start.84) | collective-permute-done | bytes 655392 | tf_op jit(solution)/shard_map/ppermute | solution.py:52
  540.4 5.1 collective-permute-done.82.one
  555.7 7.5 %collective-permute-done.89.p2 = bf16[64,2560]{1,0:T(8,128)(2,1)S(1)} collective-permute-done((bf16[64,2560]{1,0:T(8,128)(2,1)}, bf16[64,2560]{1,0:T(8,128)(2,1)S(1)}, u32[]{:S(2)}, u32[]{:S(2)}) %collective-permute-start.89) | collective-permute-done | bytes 327712 | tf_op jit(solution)/shard_map/ppermute | solution.py:52
  563.2 8.7 %collective-permute-done.91.refs_2_ = bf16[320,512]{1,0:T(8,128)(2,1)S(1)} collective-permute-done((bf16[320,512]{1,0:T(8,128)(2,1)}, bf16[320,512]{1,0:T(8,128)(2,1)S(1)}, u32[]{:S(2)}, u32[]{:S(2)}) %collective-permute-start.91) | collective-permute-done | bytes 327712 | tf_op jit(solution)/shard_map/ppermute | solution.py:52
  571.9 5.3 collective-permute-done.92.refs_3_
  579.3 7.3 %reduce-scatter.11.cloned.1.call-done = bf16[640,512]{1,0:T(8,128)(2,1)} async-done(((bf16[2560,512]{1,0:T(8,128)(2,1)}), bf16[640,512]{1,0:T(8,128)(2,1)}) %reduce-scatter.11.cloned.1.call-update) | async-done | bytes 655376 | tf_op jit(solution)/shard_map/reduce_scatter | solution.py:996
  592.2 5.1 collective-permute-done.93.refs_1_
  (473 shorter events, 185.2 us)
Async XLA Ops:
  7.2 175.2 %all-gather.5.cloned.1.call-start = ((), (), s32[]{:S(2)}) async-start(), calls=%async_computation.8 | async-start | bytes 9011200 | tf_op jit(solution)/shard_map/all_gather | solution.py:992
  25.2 37.4 %collective-permute-start.1 = (bf16[320,1408]{1,0:T(8,128)(2,1)}, bf16[320,1408]{1,0:T(8,128)(2,1)}, u32[]{:S(2)}, u32[]{:S(2)}) collective-permute-start(bf16[320,1408]{1,0:T(8,128)(2,1)} %get-tuple-element.814), channel_id=1, source_target_pairs={{0,8},{8,0},{16,24},{24,16},{1,9},{9,1},{17,25},{25,17},{2,10},{10... | collective-permute-start | bytes 2703368 | tf_op jit(solution)/shard_map/ppermute | solution.py:52
  27.0 27.7 %collective-permute-start.5 = (bf16[320,512]{1,0:T(8,128)(2,1)S(1)}, bf16[320,512]{1,0:T(8,128)(2,1)}, u32[]{:S(2)}, u32[]{:S(2)}) collective-permute-start(bf16[320,512]{1,0:T(8,128)(2,1)S(1)} %get-tuple-element.820), channel_id=1, source_target_pairs={{0,16},{8,24},{16,0},{24,8},{1,17},{9,25},{17,1},{25,9},{2,18},{10... | collective-permute-start | bytes 983048 | tf_op jit(solution)/shard_map/ppermute | solution.py:52
  29.5 33.1 %collective-permute-start.6 = (bf16[320,512]{1,0:T(8,128)(2,1)}, bf16[320,512]{1,0:T(8,128)(2,1)}, u32[]{:S(2)}, u32[]{:S(2)}) collective-permute-start(bf16[320,512]{1,0:T(8,128)(2,1)} %get-tuple-element.821), channel_id=1, source_target_pairs={{0,24},{8,16},{16,8},{24,0},{1,25},{9,17},{17,9},{25,1},{2,26},{10... | collective-permute-start | bytes 983048 | tf_op jit(solution)/shard_map/ppermute | solution.py:52
  29.6 33.0 %collective-permute-start.3 = (bf16[320,512]{1,0:T(8,128)(2,1)}, bf16[320,512]{1,0:T(8,128)(2,1)}, u32[]{:S(2)}, u32[]{:S(2)}) collective-permute-start(bf16[320,512]{1,0:T(8,128)(2,1)} %get-tuple-element.1519.refs_8_.refs_2_.refs_10_.refs_4_.refs_0_), channel_id=1, source_target_pairs={{0,2},{2,0},{1,3},{3,1},{4,6},{6,4},{5,7},{7,5},{8,10},{10,8},{9,1... | collective-permute-start | bytes 983048 | tf_op jit(solution)/shard_map/ppermute | solution.py:52
  31.3 31.4 %collective-permute-start.2 = (bf16[320,512]{1,0:T(8,128)(2,1)}, bf16[320,512]{1,0:T(8,128)(2,1)}, u32[]{:S(2)}, u32[]{:S(2)}) collective-permute-start(bf16[320,512]{1,0:T(8,128)(2,1)} %get-tuple-element.1519.refs_8_.refs_2_.refs_10_.refs_4_.refs_0_), channel_id=1, source_target_pairs={{0,4},{4,0},{1,5},{5,1},{2,6},{6,2},{3,7},{7,3},{8,12},{12,8},{9,1... | collective-permute-start | bytes 983048 | tf_op jit(solution)/shard_map/ppermute | solution.py:52
  65.2 183.2 %all-gather.7.cloned.1.call-start = ((), (), s32[]{:S(2)}) async-start(), calls=%async_computation.9 | async-start | bytes 4505600 | tf_op jit(solution)/shard_map/all_gather | solution.py:992
  68.9 20.9 %collective-permute-start.8 = (bf16[320,512]{1,0:T(8,128)(2,1)}, bf16[320,512]{1,0:T(8,128)(2,1)S(1)}, u32[]{:S(2)}, u32[]{:S(2)}) collective-permute-start(bf16[320,512]{1,0:T(8,128)(2,1)} %collective-permute-done.refs_10_.refs_4_.refs_12_.refs_6_.refs_2_), channel_id=1, source_target_pairs={{0,4},{4,0},{1,5},{5,1},{2,6},{6,2},{3,7},{7,3},{8,12},{12,8},{9,1... | collective-permute-start | bytes 983048 | tf_op jit(solution)/shard_map/ppermute | solution.py:52
  69.4 34.0 %collective-permute-start.18 = (bf16[64,2688]{1,0:T(8,128)(2,1)S(1)}, bf16[64,2688]{1,0:T(8,128)(2,1)S(1)}, u32[]{:S(2)}, u32[]{:S(2)}) collective-permute-start(bf16[64,2688]{1,0:T(8,128)(2,1)S(1)} %copy-done.16), channel_id=1, source_target_pairs={{0,16},{8,24},{16,0},{24,8},{1,17},{9,25},{17,1},{25,9},{2,18},{10... | collective-permute-start | bytes 1032200 | tf_op jit(solution)/shard_map/ppermute | solution.py:52
  72.2 21.1 %collective-permute-start.15 = (bf16[320,512]{1,0:T(8,128)(2,1)}, bf16[320,512]{1,0:T(8,128)(2,1)S(1)}, u32[]{:S(2)}, u32[]{:S(2)}) collective-permute-start(bf16[320,512]{1,0:T(8,128)(2,1)} %collective-permute-done.6.refs_14_.refs_8_.refs_16_.refs_10_.refs_6_), channel_id=1, source_target_pairs={{0,2},{2,0},{1,3},{3,1},{4,6},{6,4},{5,7},{7,5},{8,10},{10,8},{9,1... | collective-permute-start | bytes 983048 | tf_op jit(solution)/shard_map/ppermute | solution.py:52
  76.7 25.6 %collective-permute-start.10 = (bf16[320,512]{1,0:T(8,128)(2,1)}, bf16[320,512]{1,0:T(8,128)(2,1)S(1)}, u32[]{:S(2)}, u32[]{:S(2)}) collective-permute-start(bf16[320,512]{1,0:T(8,128)(2,1)} %collective-permute-done.6.refs_14_.refs_8_.refs_16_.refs_10_.refs_6_), channel_id=1, source_target_pairs={{0,4},{4,0},{1,5},{5,1},{2,6},{6,2},{3,7},{7,3},{8,12},{12,8},{9,1... | collective-permute-start | bytes 983048 | tf_op jit(solution)/shard_map/ppermute | solution.py:52
  79.3 25.1 %collective-permute-start.13 = (bf16[320,512]{1,0:T(8,128)(2,1)}, bf16[320,512]{1,0:T(8,128)(2,1)S(1)}, u32[]{:S(2)}, u32[]{:S(2)}) collective-permute-start(bf16[320,512]{1,0:T(8,128)(2,1)} %collective-permute-done.5.refs_12_.refs_6_.refs_14_.refs_8_.refs_4_), channel_id=1, source_target_pairs={{0,2},{2,0},{1,3},{3,1},{4,6},{6,4},{5,7},{7,5},{8,10},{10,8},{9,1... | collective-permute-start | bytes 983048 | tf_op jit(solution)/shard_map/ppermute | solution.py:52
  89.8 28.7 %collective-permute-start.7 = (bf16[320,896]{1,0:T(8,128)(2,1)S(1)}, bf16[320,896]{1,0:T(8,128)(2,1)S(1)}, u32[]{:S(2)}, u32[]{:S(2)}) collective-permute-start(bf16[320,896]{1,0:T(8,128)(2,1)S(1)} %copy-done.12), channel_id=1, source_target_pairs={{0,16},{8,24},{16,0},{24,8},{1,17},{9,25},{17,1},{25,9},{2,18},{10... | collective-permute-start | bytes 1720328 | tf_op jit(solution)/shard_map/ppermute | solution.py:52
  93.3 24.2 %collective-permute-start.20 = (bf16[64,2688]{1,0:T(8,128)(2,1)S(1)}, bf16[64,2688]{1,0:T(8,128)(2,1)S(1)}, u32[]{:S(2)}, u32[]{:S(2)}) collective-permute-start(bf16[64,2688]{1,0:T(8,128)(2,1)S(1)} %copy-done.16), channel_id=1, source_target_pairs={{0,1},{1,0},{2,3},{3,2},{4,5},{5,4},{6,7},{7,6},{8,9},{9,8},{10,11... | collective-permute-start | bytes 1032200 | tf_op jit(solution)/shard_map/ppermute | solution.py:52
  131.7 18.3 %collective-permute-start.24 = (bf16[320,512]{1,0:T(8,128)(2,1)S(1)}, bf16[320,512]{1,0:T(8,128)(2,1)S(1)}, u32[]{:S(2)}, u32[]{:S(2)}) collective-permute-start(bf16[320,512]{1,0:T(8,128)(2,1)S(1)} %copy-done.54), channel_id=1, source_target_pairs={{0,16},{8,24},{16,0},{24,8},{1,17},{9,25},{17,1},{25,9},{2,18},{10... | collective-permute-start | bytes 983048 | tf_op jit(solution)/shard_map/ppermute | solution.py:52
  151.0 263.7 %reduce-scatter.9.cloned.1.call-start = ((), (), s32[]{:S(2)}) async-start(), calls=%async_computation.6 | async-start | bytes 6553600 | tf_op jit(solution)/shard_map/reduce_scatter | solution.py:996
  151.2 16.4 %collective-permute-start.26 = (bf16[512,384]{1,0:T(8,128)(2,1)}, bf16[512,384]{1,0:T(8,128)(2,1)S(1)}, u32[]{:S(2)}, u32[]{:S(2)}) collective-permute-start(bf16[512,384]{1,0:T(8,128)(2,1)} %get-tuple-element.1390.refs_0_.refs_8_), channel_id=1, source_target_pairs={{0,4},{4,0},{1,5},{5,1},{2,6},{6,2},{3,7},{7,3},{8,12},{12,8},{9,1... | collective-permute-start | bytes 1179656 | tf_op jit(solution)/shard_map/ppermute | solution.py:52
  151.3 31.1 %collective-permute-start.25 = (bf16[320,896]{1,0:T(8,128)(2,1)S(1)}, bf16[320,896]{1,0:T(8,128)(2,1)S(1)}, u32[]{:S(2)}, u32[]{:S(2)}) collective-permute-start(bf16[320,896]{1,0:T(8,128)(2,1)S(1)} %copy-done.10), channel_id=1, source_target_pairs={{0,24},{8,16},{16,8},{24,0},{1,25},{9,17},{17,9},{25,1},{2,26},{10... | collective-permute-start | bytes 1720328 | tf_op jit(solution)/shard_map/ppermute | solution.py:52
  183.0 20.9 %collective-permute-start.29 = (bf16[320,896]{1,0:T(8,128)(2,1)S(1)}, bf16[320,896]{1,0:T(8,128)(2,1)S(1)}, u32[]{:S(2)}, u32[]{:S(2)}) collective-permute-start(bf16[320,896]{1,0:T(8,128)(2,1)S(1)} %collective-permute-done.25.refs_10_.refs_6_), channel_id=1, source_target_pairs={{0,2},{2,0},{1,3},{3,1},{4,6},{6,4},{5,7},{7,5},{8,10},{10,8},{9,1... | collective-permute-start | bytes 1720328 | tf_op jit(solution)/shard_map/ppermute | solution.py:52
  185.1 18.9 %collective-permute-start.28 = (bf16[320,896]{1,0:T(8,128)(2,1)S(1)}, bf16[320,896]{1,0:T(8,128)(2,1)S(1)}, u32[]{:S(2)}, u32[]{:S(2)}) collective-permute-start(bf16[320,896]{1,0:T(8,128)(2,1)S(1)} %collective-permute-done.25.refs_10_.refs_6_), channel_id=1, source_target_pairs={{0,4},{4,0},{1,5},{5,1},{2,6},{6,2},{3,7},{7,3},{8,12},{12,8},{9,1... | collective-permute-start | bytes 1720328 | tf_op jit(solution)/shard_map/ppermute | solution.py:52
  186.9 17.0 %collective-permute-start.27 = (bf16[320,512]{1,0:T(8,128)(2,1)S(1)}, bf16[320,512]{1,0:T(8,128)(2,1)S(1)}, u32[]{:S(2)}, u32[]{:S(2)}) collective-permute-start(bf16[320,512]{1,0:T(8,128)(2,1)S(1)} %copy-done.52), channel_id=1, source_target_pairs={{0,24},{8,16},{16,8},{24,0},{1,25},{9,17},{17,9},{25,1},{2,26},{10... | collective-permute-start | bytes 983048 | tf_op jit(solution)/shard_map/ppermute | solution.py:52
  204.0 16.2 %collective-permute-start.37 = (bf16[64,2560]{1,0:T(8,128)(2,1)S(1)}, bf16[64,2560]{1,0:T(8,128)(2,1)S(1)}, u32[]{:S(2)}, u32[]{:S(2)}) collective-permute-start(bf16[64,2560]{1,0:T(8,128)(2,1)S(1)} %get-tuple-element.993), channel_id=1, source_target_pairs={{0,8},{8,0},{16,24},{24,16},{1,9},{9,1},{17,25},{25,17},{2,10},{10... | collective-permute-start | bytes 983048 | tf_op jit(solution)/shard_map/ppermute | solution.py:52
  205.5 17.0 %collective-permute-start.38 = (bf16[64,2560]{1,0:T(8,128)(2,1)S(1)}, bf16[64,2560]{1,0:T(8,128)(2,1)S(1)}, u32[]{:S(2)}, u32[]{:S(2)}) collective-permute-start(bf16[64,2560]{1,0:T(8,128)(2,1)S(1)} %get-tuple-element.994), channel_id=1, source_target_pairs={{0,16},{8,24},{16,0},{24,8},{1,17},{9,25},{17,1},{25,9},{2,18},{10... | collective-permute-start | bytes 983048 | tf_op jit(solution)/shard_map/ppermute | solution.py:52
  224.2 23.3 %collective-permute-start.33 = (bf16[320,896]{1,0:T(8,128)(2,1)S(1)}, bf16[320,896]{1,0:T(8,128)(2,1)S(1)}, u32[]{:S(2)}, u32[]{:S(2)}) collective-permute-start(bf16[320,896]{1,0:T(8,128)(2,1)S(1)} %collective-permute-done.29.refs_12_.refs_8_), channel_id=1, source_target_pairs={{0,4},{4,0},{1,5},{5,1},{2,6},{6,2},{3,7},{7,3},{8,12},{12,8},{9,1... | collective-permute-start | bytes 1720328 | tf_op jit(solution)/shard_map/ppermute | solution.py:52
  226.4 19.6 %collective-permute-start.34 = (bf16[320,512]{1,0:T(8,128)(2,1)S(1)}, bf16[320,512]{1,0:T(8,128)(2,1)S(1)}, u32[]{:S(2)}, u32[]{:S(2)}) collective-permute-start(bf16[320,512]{1,0:T(8,128)(2,1)S(1)} %collective-permute-done.27.refs_14_.refs_10_), channel_id=1, source_target_pairs={{0,4},{4,0},{1,5},{5,1},{2,6},{6,2},{3,7},{7,3},{8,12},{12,8},{9,1... | collective-permute-start | bytes 983048 | tf_op jit(solution)/shard_map/ppermute | solution.py:52
  227.8 19.7 %collective-permute-start.39 = (bf16[64,2560]{1,0:T(8,128)(2,1)S(1)}, bf16[64,2560]{1,0:T(8,128)(2,1)S(1)}, u32[]{:S(2)}, u32[]{:S(2)}) collective-permute-start(bf16[64,2560]{1,0:T(8,128)(2,1)S(1)} %get-tuple-element.1021.refs_0_), channel_id=1, source_target_pairs={{0,8},{8,0},{16,24},{24,16},{1,9},{9,1},{17,25},{25,17},{2,10},{10... | collective-permute-start | bytes 983048 | tf_op jit(solution)/shard_map/ppermute | solution.py:52
  301.7 19.0 %collective-permute-start.59 = (bf16[64,2560]{1,0:T(8,128)(2,1)S(1)}, bf16[64,2560]{1,0:T(8,128)(2,1)S(1)}, u32[]{:S(2)}, u32[]{:S(2)}) collective-permute-start(bf16[64,2560]{1,0:T(8,128)(2,1)S(1)} %get-tuple-element.1556.p0), channel_id=1, source_target_pairs={{0,2},{2,0},{1,3},{3,1},{4,6},{6,4},{5,7},{7,5},{8,10},{10,8},{9,1... | collective-permute-start | bytes 983048 | tf_op jit(solution)/shard_map/ppermute | solution.py:52
  303.9 17.4 %collective-permute-start.58 = (bf16[64,2560]{1,0:T(8,128)(2,1)S(1)}, bf16[64,2560]{1,0:T(8,128)(2,1)S(1)}, u32[]{:S(2)}, u32[]{:S(2)}) collective-permute-start(bf16[64,2560]{1,0:T(8,128)(2,1)S(1)} %get-tuple-element.1556.p0), channel_id=1, source_target_pairs={{0,1},{1,0},{2,3},{3,2},{4,5},{5,4},{6,7},{7,6},{8,9},{9,8},{10,11... | collective-permute-start | bytes 983048 | tf_op jit(solution)/shard_map/ppermute | solution.py:52
  304.6 17.5 %collective-permute-start.51 = (bf16[64,2560]{1,0:T(8,128)(2,1)S(1)}, bf16[64,2560]{1,0:T(8,128)(2,1)S(1)}, u32[]{:S(2)}, u32[]{:S(2)}) collective-permute-start(bf16[64,2560]{1,0:T(8,128)(2,1)S(1)} %get-tuple-element.1303.refs_0_.d_own), channel_id=1, source_target_pairs={{0,8},{8,0},{16,24},{24,16},{1,9},{9,1},{17,25},{25,17},{2,10},{10... | collective-permute-start | bytes 983048 | tf_op jit(solution)/shard_map/ppermute | solution.py:52
  337.5 125.3 %reduce-scatter.7.cloned.1.call-start = ((), (), s32[]{:S(2)}) async-start(), calls=%async_computation.5 | async-start | bytes 5734400 | tf_op jit(solution)/shard_map/reduce_scatter | solution.py:996
  369.3 180.5 %reduce-scatter.5.cloned.1.call-start = ((), (), s32[]{:S(2)}) async-start(), calls=%async_computation.4 | async-start | bytes 5734400 | tf_op jit(solution)/shard_map/reduce_scatter | solution.py:996
  369.4 16.3 %collective-permute-start.64 = (bf16[64,2560]{1,0:T(8,128)(2,1)S(1)}, bf16[64,2560]{1,0:T(8,128)(2,1)S(1)}, u32[]{:S(2)}, u32[]{:S(2)}) collective-permute-start(bf16[64,2560]{1,0:T(8,128)(2,1)S(1)} %get-tuple-element.1300), channel_id=1, source_target_pairs={{0,8},{8,0},{16,24},{24,16},{1,9},{9,1},{17,25},{25,17},{2,10},{10... | collective-permute-start | bytes 983048 | tf_op jit(solution)/shard_map/ppermute | solution.py:52
  387.2 199.4 %reduce-scatter.11.cloned.1.call-start = ((), (), s32[]{:S(2)}) async-start(), calls=%async_computation.7 | async-start | bytes 3276800 | tf_op jit(solution)/shard_map/reduce_scatter | solution.py:996
  387.4 16.3 %collective-permute-start.68 = (bf16[64,2560]{1,0:T(8,128)(2,1)S(1)}, bf16[64,2560]{1,0:T(8,128)(2,1)S(1)}, u32[]{:S(2)}, u32[]{:S(2)}) collective-permute-start(bf16[64,2560]{1,0:T(8,128)(2,1)S(1)} %get-tuple-element.1382.refs_0_), channel_id=1, source_target_pairs={{0,16},{8,24},{16,0},{24,8},{1,17},{9,25},{17,1},{25,9},{2,18},{10... | collective-permute-start | bytes 983048 | tf_op jit(solution)/shard_map/ppermute | solution.py:52
  416.9 18.5 %collective-permute-start.75 = (bf16[320,512]{1,0:T(8,128)(2,1)S(1)}, bf16[320,512]{1,0:T(8,128)(2,1)S(1)}, u32[]{:S(2)}, u32[]{:S(2)}) collective-permute-start(bf16[320,512]{1,0:T(8,128)(2,1)S(1)} %get-tuple-element.1598), channel_id=1, source_target_pairs={{0,24},{8,16},{16,8},{24,0},{1,25},{9,17},{17,9},{25,1},{2,26},{10... | collective-permute-start | bytes 983048 | tf_op jit(solution)/shard_map/ppermute | solution.py:52
  437.8 28.9 %collective-permute-start.77 = (bf16[512,320]{1,0:T(8,128)(2,1)}, bf16[512,320]{1,0:T(8,128)(2,1)S(1)}, u32[]{:S(2)}, u32[]{:S(2)}) collective-permute-start(bf16[512,320]{1,0:T(8,128)(2,1)} %get-tuple-element.1434), channel_id=1, source_target_pairs={{0,4},{4,0},{1,5},{5,1},{2,6},{6,2},{3,7},{7,3},{8,12},{12,8},{9,1... | collective-permute-start | bytes 983048 | tf_op jit(solution)/shard_map/ppermute | solution.py:52
  437.8 30.8 %collective-permute-start.76 = (bf16[320,512]{1,0:T(8,128)(2,1)}, bf16[320,512]{1,0:T(8,128)(2,1)}, u32[]{:S(2)}, u32[]{:S(2)}) collective-permute-start(bf16[320,512]{1,0:T(8,128)(2,1)} %get-tuple-element.1429), channel_id=1, source_target_pairs={{0,16},{8,24},{16,0},{24,8},{1,17},{9,25},{17,1},{25,9},{2,18},{10... | collective-permute-start | bytes 983048 | tf_op jit(solution)/shard_map/ppermute | solution.py:52
  465.1 16.9 %collective-permute-start.78 = (bf16[320,896]{1,0:T(8,128)(2,1)S(1)}, bf16[320,896]{1,0:T(8,128)(2,1)S(1)}, u32[]{:S(2)}, u32[]{:S(2)}) collective-permute-start(bf16[320,896]{1,0:T(8,128)(2,1)S(1)} %get-tuple-element.1602), channel_id=1, source_target_pairs={{0,24},{8,16},{16,8},{24,0},{1,25},{9,17},{17,9},{25,1},{2,26},{10... | collective-permute-start | bytes 1720328 | tf_op jit(solution)/shard_map/ppermute | solution.py:52
  482.1 28.8 %collective-permute-start.85 = (bf16[640,512]{1,0:T(8,128)(2,1)}, bf16[640,512]{1,0:T(8,128)(2,1)}, u32[]{:S(2)}, u32[]{:S(2)}) collective-permute-start(bf16[640,512]{1,0:T(8,128)(2,1)} %get-tuple-element.1563), channel_id=1, source_target_pairs={{0,2},{2,0},{1,3},{3,1},{4,6},{6,4},{5,7},{7,5},{8,10},{10,8},{9,1... | collective-permute-start | bytes 1966088 | tf_op jit(solution)/shard_map/ppermute | solution.py:52
  492.7 37.7 %collective-permute-start.79 = (bf16[192,2560]{1,0:T(8,128)(2,1)}, bf16[192,2560]{1,0:T(8,128)(2,1)S(1)}, u32[]{:S(2)}, u32[]{:S(2)}) collective-permute-start(bf16[192,2560]{1,0:T(8,128)(2,1)} %get-tuple-element.1536), channel_id=1, source_target_pairs={{0,1},{1,0},{2,3},{3,2},{4,5},{5,4},{6,7},{7,6},{8,9},{9,8},{10,11... | collective-permute-start | bytes 2949128 | tf_op jit(solution)/shard_map/ppermute | solution.py:52
  493.2 35.9 %collective-permute-start.84 = (bf16[640,512]{1,0:T(8,128)(2,1)}, bf16[640,512]{1,0:T(8,128)(2,1)}, u32[]{:S(2)}, u32[]{:S(2)}) collective-permute-start(bf16[640,512]{1,0:T(8,128)(2,1)} %get-tuple-element.1561), channel_id=1, source_target_pairs={{0,2},{2,0},{1,3},{3,1},{4,6},{6,4},{5,7},{7,5},{8,10},{10,8},{9,1... | collective-permute-start | bytes 1966088 | tf_op jit(solution)/shard_map/ppermute | solution.py:52
  494.8 54.4 %collective-permute-start.66 = (bf16[320,896]{1,0:T(8,128)(2,1)}, bf16[320,896]{1,0:T(8,128)(2,1)S(1)}, u32[]{:S(2)}, u32[]{:S(2)}) collective-permute-start(bf16[320,896]{1,0:T(8,128)(2,1)} %get-tuple-element.1603), channel_id=1, source_target_pairs={{0,16},{8,24},{16,0},{24,8},{1,17},{9,25},{17,1},{25,9},{2,18},{10... | collective-permute-start | bytes 1720328 | tf_op jit(solution)/shard_map/ppermute | solution.py:52
  507.3 23.1 %collective-permute-start.81 = (bf16[64,2560]{1,0:T(8,128)(2,1)S(1)}, bf16[64,2560]{1,0:T(8,128)(2,1)S(1)}, u32[]{:S(2)}, u32[]{:S(2)}) collective-permute-start(bf16[64,2560]{1,0:T(8,128)(2,1)S(1)} %shard_map.259), channel_id=1, source_target_pairs={{0,8},{8,0},{16,24},{24,16},{1,9},{9,1},{17,25},{25,17},{2,10},{10... | collective-permute-start | bytes 983048 | tf_op jit(solution)/shard_map/ppermute | solution.py:52
  512.1 27.3 %collective-permute-start.86 = (bf16[640,512]{1,0:T(8,128)(2,1)S(1)}, bf16[640,512]{1,0:T(8,128)(2,1)S(1)}, u32[]{:S(2)}, u32[]{:S(2)}) collective-permute-start(bf16[640,512]{1,0:T(8,128)(2,1)S(1)} %add_convert_fusion), channel_id=1, source_target_pairs={{0,4},{4,0},{1,5},{5,1},{2,6},{6,2},{3,7},{7,3},{8,12},{12,8},{9,1... | collective-permute-start | bytes 1966088 | tf_op jit(solution)/shard_map/ppermute | solution.py:52
  551.2 26.0 %collective-permute-start.87 = (bf16[320,896]{1,0:T(8,128)(2,1)S(1)}, bf16[320,896]{1,0:T(8,128)(2,1)S(1)}, u32[]{:S(2)}, u32[]{:S(2)}) collective-permute-start(bf16[320,896]{1,0:T(8,128)(2,1)S(1)} %get-tuple-element.1566), channel_id=1, source_target_pairs={{0,8},{8,0},{16,24},{24,16},{1,9},{9,1},{17,25},{25,17},{2,10},{10... | collective-permute-start | bytes 1720328 | tf_op jit(solution)/shard_map/ppermute | solution.py:52
  551.6 20.3 %collective-permute-start.91 = (bf16[320,512]{1,0:T(8,128)(2,1)}, bf16[320,512]{1,0:T(8,128)(2,1)S(1)}, u32[]{:S(2)}, u32[]{:S(2)}) collective-permute-start(bf16[320,512]{1,0:T(8,128)(2,1)} %get-tuple-element.1571), channel_id=1, source_target_pairs={{0,16},{8,24},{16,0},{24,8},{1,17},{9,25},{17,1},{25,9},{2,18},{10... | collective-permute-start | bytes 983048 | tf_op jit(solution)/shard_map/ppermute | solution.py:52
  554.2 23.0 %collective-permute-start.92 = (bf16[320,512]{1,0:T(8,128)(2,1)}, bf16[320,512]{1,0:T(8,128)(2,1)S(1)}, u32[]{:S(2)}, u32[]{:S(2)}) collective-permute-start(bf16[320,512]{1,0:T(8,128)(2,1)} %get-tuple-element.1572), channel_id=1, source_target_pairs={{0,24},{8,16},{16,8},{24,0},{1,25},{9,17},{17,9},{25,1},{2,26},{10... | collective-permute-start | bytes 983048 | tf_op jit(solution)/shard_map/ppermute | solution.py:52
  555.7 21.5 %collective-permute-start.88 = (bf16[64,2560]{1,0:T(8,128)(2,1)}, bf16[64,2560]{1,0:T(8,128)(2,1)S(1)}, u32[]{:S(2)}, u32[]{:S(2)}) collective-permute-start(bf16[64,2560]{1,0:T(8,128)(2,1)} %shard_map.262.p0), channel_id=1, source_target_pairs={{0,1},{1,0},{2,3},{3,2},{4,5},{5,4},{6,7},{7,6},{8,9},{9,8},{10,11... | collective-permute-start | bytes 983048 | tf_op jit(solution)/shard_map/ppermute | solution.py:52
  (183 other events, 2238.9 us)
Sparse Core Ops, SparseCore 0:
  65.3 104.2 all-gather.4
  172.1 55.8 all-gather.6
  337.6 62.0 reduce-scatter.8
  402.7 60.1 reduce-scatter.6
  465.8 75.7 reduce-scatter.4
  544.4 42.1 reduce-scatter.10

commit v8 on v7

--- a/solution.py
+++ b/solution.py
@@ -17,7 +17,7 @@
 F32 = jnp.float32
 FACTOR = HEAD_DIM**-0.5
 LOG2E = 1.4426950408889634
-LIMIT = 48 * 1024 * 1024
+LIMIT = 50 * 1024 * 1024
 
 PLAIN = (((1,), (0,)), ((), ()))
 LAST = (((1,), (1,)), ((), ()))

time: 617 us -> 614 us (level)
  waiting for transfers between devices: 289 us -> 311 us
  starting transfers between devices: 128 us -> 110 us
  local copies, waits for them, and re-layouts: 50.2 us -> 39.2 us
    ppermute x95, waiting for transfers between devices: 258 us -> 280 us  [hop(): return lax.ppermute(value, axis, [(i, i ^ k) for i in range(size)])]
    ppermute x95, starting transfers between devices: 127 us -> 109 us  [hop(): return lax.ppermute(value, axis, [(i, i ^ k) for i in range(size)])]
    unnamed x260 -> x202, local copies, waits for them, and re-layouts: 39.8 us -> 28.9 us
  transfers between devices with their start and end apart: 101 -> 101, of which waited for: 44 -> 46; matrix products, arithmetic and copies ran while one was open for 2% -> 2% of each run, Pallas kernels for 15% -> 16%
where the time goes in v8:
time: 614 us; the launch traced here: 607 us
  waiting for transfers between devices  311 us (51%)
  Pallas kernels  123 us (20%)
  starting transfers between devices  110 us (18%)
  local copies, waits for them, and re-layouts  39.2 us (6%)
  between operations  16.2 us (3%)
  other arithmetic  8.26 us (1%)
    ppermute x95, waiting for transfers between devices, hop(): return lax.ppermute(value, axis, [(i, i ^ k) for i in range(size)])  280 us
    ppermute x95, starting transfers between devices, hop(): return lax.ppermute(value, axis, [(i, i ^ k) for i in range(size)])  109 us
    reduce_scatter x4, waiting for transfers between devices, scatter_blocks(): got = lax.psum_scatter(blocks, ('y', 'x'), scatter_dimension=0, tiled=True)  30.6 us
    unnamed x202, local copies, waits for them, and re-layouts  28.9 us
    pallas_call x1, Pallas kernels, feed(): call(functools.partial(feed_body, fw, inner), [shape((8 * rows, 512))] *...  15.4 us
    pallas_call x1, Pallas kernels, feed_back(): call(functools.partial(feed_back_body, fw, inner), [shape((rows, 2 * fw))...  14.6 us
    pallas_call x1, Pallas kernels, attend_back(): call(functools.partial(attend_back_body, sides), [shape(q.shape), shape((...  13.7 us
    pallas_call x1, Pallas kernels, attn_grad(): call(functools.partial(attn_grad_body, inner), [shape((width // 4, 512))]...  12.6 us
  transfers between devices with their start and end apart: 101, of which 46 were waited for; matrix products, arithmetic and copies ran while one was open for 2% of the time, Pallas kernels for 16%

profile of v8, /device:TPU:0, one launch (start us, length us, event | category | flops | bytes accessed | tf_op | source)
XLA Modules:
  0.0 606.9 jit_solution(15679067358149006448)
XLA Ops:
  21.7 3.5 collective-permute-done.refs_10_.refs_4_.refs_12_.refs_6_.refs_2_
  32.8 21.9 %collective-permute-done.5.refs_12_.refs_6_.refs_14_.refs_8_.refs_4_ = bf16[320,512]{1,0:T(8,128)(2,1)} collective-permute-done((bf16[320,512]{1,0:T(8,128)(2,1)S(1)}, bf16[320,512]{1,0:T(8,128)(2,1)}, u32[]{:S(2)}, u32[]{:S(2)}) %collective-permute-start.5) | collective-permute-done | bytes 327712 | tf_op jit(solution)/shard_map/ppermute | solution.py:52
  72.8 3.9 collective-permute-done.12.refs_19_.refs_13_.refs_21_.refs_15_.refs_11_
  81.6 8.2 %collective-permute-done.8.refs_11_.refs_5_.refs_13_.refs_7_.refs_3_ = bf16[320,512]{1,0:T(8,128)(2,1)S(1)} collective-permute-done((bf16[320,512]{1,0:T(8,128)(2,1)}, bf16[320,512]{1,0:T(8,128)(2,1)S(1)}, u32[]{:S(2)}, u32[]{:S(2)}) %collective-permute-start.8) | collective-permute-done | bytes 327712 | tf_op jit(solution)/shard_map/ppermute | solution.py:52
  93.3 9.1 %collective-permute-done.10.refs_15_.refs_9_.refs_17_.refs_11_.refs_7_ = bf16[320,512]{1,0:T(8,128)(2,1)S(1)} collective-permute-done((bf16[320,512]{1,0:T(8,128)(2,1)}, bf16[320,512]{1,0:T(8,128)(2,1)S(1)}, u32[]{:S(2)}, u32[]{:S(2)}) %collective-permute-start.10) | collective-permute-done | bytes 327712 | tf_op jit(solution)/shard_map/ppermute | solution.py:52
  106.8 8.8 %collective-permute-done.9.refs_13_.refs_7_.refs_15_.refs_9_.refs_5_ = bf16[320,512]{1,0:T(8,128)(2,1)S(1)} collective-permute-done((bf16[320,512]{1,0:T(8,128)(2,1)}, bf16[320,512]{1,0:T(8,128)(2,1)S(1)}, u32[]{:S(2)}, u32[]{:S(2)}) %collective-permute-start.9) | collective-permute-done | bytes 327712 | tf_op jit(solution)/shard_map/ppermute | solution.py:52
  120.1 9.4 %collective-permute-done.16.refs_23_.refs_17_.refs_25_.refs_19_.refs_15_ = bf16[320,512]{1,0:T(8,128)(2,1)S(1)} collective-permute-done((bf16[320,512]{1,0:T(8,128)(2,1)S(1)}, bf16[320,512]{1,0:T(8,128)(2,1)S(1)}, u32[]{:S(2)}, u32[]{:S(2)}) %collective-permute-start.16) | collective-permute-done | bytes 327712 | tf_op jit(solution)/shard_map/ppermute | solution.py:52
  132.7 9.4 %shard_map.239 = (bf16[512,2560]{1,0:T(8,128)(2,1)}, bf16[512,320]{1,0:T(8,128)(2,1)}, bf16[512,384]{1,0:T(8,128)(2,1)}, f32[8,2560]{1,0:T(8,128)S(1)}, f32[8,512]{1,0:T(8,128)S(1)}) custom-call(s32[5]{0:T(128)S(1)} %stack.36.pos, f32[512,40]{1,0:T(8,128)S(1)} %get-tuple-element.1609.cosine, f32[512,40]{1,0:T(8,128)S(1)} %get-tuple-element.1608.sine, ...), custom_call_target="tpu_custom_call" | custom-call | flops 12000000000 | tf_op jit(solution)/shard_map/pallas_call | solution.py:359
  142.2 8.0 %collective-permute-done.24 = bf16[320,512]{1,0:T(8,128)(2,1)S(1)} collective-permute-done((bf16[320,512]{1,0:T(8,128)(2,1)}, bf16[320,512]{1,0:T(8,128)(2,1)S(1)}, u32[]{:S(2)}, u32[]{:S(2)}) %collective-permute-start.24) | collective-permute-done | bytes 327712 | tf_op jit(solution)/shard_map/ppermute | solution.py:52
  153.3 14.2 %collective-permute-done.26.refs_1_.refs_9_ = bf16[512,384]{1,0:T(8,128)(2,1)S(1)} collective-permute-done((bf16[512,384]{1,0:T(8,128)(2,1)S(1)}, bf16[512,384]{1,0:T(8,128)(2,1)S(1)}, u32[]{:S(2)}, u32[]{:S(2)}) %collective-permute-start.26) | collective-permute-done | bytes 393248 | tf_op jit(solution)/shard_map/ppermute | solution.py:52
  168.2 9.4 %shard_map.240 = (bf16[512,256]{1,0:T(8,128)(2,1)S(1)}, bf16[512,256]{1,0:T(8,128)(2,1)S(1)}, f32[8,512]{1,0:T(8,128)S(1)}, bf16[64,2560]{1,0:T(8,128)(2,1)S(1)}...) custom-call(s32[5]{0:T(128)S(1)} %stack.36.pos, ...), custom_call_target="tpu_custom_call" | custom-call | flops 12000000000 | tf_op jit(solution)/shard_map/pallas_call | solution.py:471
  184.4 8.2 %collective-permute-done.32.three = bf16[64,2560]{1,0:T(8,128)(2,1)S(1)} collective-permute-done((bf16[64,2560]{1,0:T(8,128)(2,1)S(1)}, bf16[64,2560]{1,0:T(8,128)(2,1)S(1)}, u32[]{:S(2)}, u32[]{:S(2)}) %collective-permute-start.32) | collective-permute-done | bytes 327712 | tf_op jit(solution)/shard_map/ppermute | solution.py:52
  192.8 6.4 %collective-permute-done.27.refs_14_.refs_10_ = bf16[320,512]{1,0:T(8,128)(2,1)S(1)} collective-permute-done((bf16[320,512]{1,0:T(8,128)(2,1)S(1)}, bf16[320,512]{1,0:T(8,128)(2,1)S(1)}, u32[]{:S(2)}, u32[]{:S(2)}) %collective-permute-start.27) | collective-permute-done | bytes 327712 | tf_op jit(solution)/shard_map/ppermute | solution.py:52
  199.1 4.3 collective-permute-done.29.refs_12_.refs_8_
  207.9 12.0 %collective-permute-done.37.one = bf16[64,2560]{1,0:T(8,128)(2,1)S(1)} collective-permute-done((bf16[64,2560]{1,0:T(8,128)(2,1)S(1)}, bf16[64,2560]{1,0:T(8,128)(2,1)S(1)}, u32[]{:S(2)}, u32[]{:S(2)}) %collective-permute-start.37) | collective-permute-done | bytes 327712 | tf_op jit(solution)/shard_map/ppermute | solution.py:52
  230.3 7.7 %collective-permute-done.40.refs_2_ = bf16[64,2560]{1,0:T(8,128)(2,1)S(1)} collective-permute-done((bf16[64,2560]{1,0:T(8,128)(2,1)S(1)}, bf16[64,2560]{1,0:T(8,128)(2,1)S(1)}, u32[]{:S(2)}, u32[]{:S(2)}) %collective-permute-start.40) | collective-permute-done | bytes 327712 | tf_op jit(solution)/shard_map/ppermute | solution.py:52
  238.1 9.5 %collective-permute-done.34.refs_15_.refs_11_ = bf16[320,512]{1,0:T(8,128)(2,1)S(1)} collective-permute-done((bf16[320,512]{1,0:T(8,128)(2,1)S(1)}, bf16[320,512]{1,0:T(8,128)(2,1)S(1)}, u32[]{:S(2)}, u32[]{:S(2)}) %collective-permute-start.34) | collective-permute-done | bytes 327712 | tf_op jit(solution)/shard_map/ppermute | solution.py:52
  249.9 6.6 %collective-permute-done.36.refs_17_.refs_13_ = bf16[320,512]{1,0:T(8,128)(2,1)S(1)} collective-permute-done((bf16[320,512]{1,0:T(8,128)(2,1)S(1)}, bf16[320,512]{1,0:T(8,128)(2,1)S(1)}, u32[]{:S(2)}, u32[]{:S(2)}) %collective-permute-start.36) | collective-permute-done | bytes 327712 | tf_op jit(solution)/shard_map/ppermute | solution.py:52
  257.2 15.4 %shard_map.244 = (bf16[512,512]{1,0:T(8,128)(2,1)}, bf16[512,512]{1,0:T(8,128)(2,1)}, bf16[512,512]{1,0:T(8,128)(2,1)}, bf16[512,512]{1,0:T(8,128)(2,1)}, bf16[5...) custom-call(s32[5]{0:T(128)S(1)} %stack.36.pos, ...), custom_call_target="tpu_custom_call" | custom-call | flops 17999998976 | tf_op jit(solution)/shard_map/pallas_call | solution.py:544
  277.0 8.5 %collective-permute-done.48.three = bf16[64,2560]{1,0:T(8,128)(2,1)S(1)} collective-permute-done((bf16[64,2560]{1,0:T(8,128)(2,1)S(1)}, bf16[64,2560]{1,0:T(8,128)(2,1)S(1)}, u32[]{:S(2)}, u32[]{:S(2)}) %collective-permute-start.48) | collective-permute-done | bytes 327712 | tf_op jit(solution)/shard_map/ppermute | solution.py:52
  289.7 12.0 %collective-permute-done.49.one = bf16[64,2560]{1,0:T(8,128)(2,1)S(1)} collective-permute-done((bf16[64,2560]{1,0:T(8,128)(2,1)S(1)}, bf16[64,2560]{1,0:T(8,128)(2,1)S(1)}, u32[]{:S(2)}, u32[]{:S(2)}) %collective-permute-start.49) | collective-permute-done | bytes 327712 | tf_op jit(solution)/shard_map/ppermute | solution.py:52
  309.9 8.5 %collective-permute-done.52.refs_2_ = bf16[64,2560]{1,0:T(8,128)(2,1)S(1)} collective-permute-done((bf16[64,2560]{1,0:T(8,128)(2,1)S(1)}, bf16[64,2560]{1,0:T(8,128)(2,1)S(1)}, u32[]{:S(2)}, u32[]{:S(2)}) %collective-permute-start.52) | collective-permute-done | bytes 327712 | tf_op jit(solution)/shard_map/ppermute | solution.py:52
  323.1 6.8 %collective-permute-done.53.refs_3_ = bf16[64,2560]{1,0:T(8,128)(2,1)S(1)} collective-permute-done((bf16[64,2560]{1,0:T(8,128)(2,1)S(1)}, bf16[64,2560]{1,0:T(8,128)(2,1)S(1)}, u32[]{:S(2)}, u32[]{:S(2)}) %collective-permute-start.53) | collective-permute-done | bytes 327712 | tf_op jit(solution)/shard_map/ppermute | solution.py:52
  331.6 6.1 %shard_map.248 = (bf16[4,1280,512]{2,1,0:T(8,128)(2,1)}, bf16[512,2560]{1,0:T(8,128)(2,1)}) custom-call(s32[5]{0:T(128)S(1)} %stack.36.pos, bf16[64,2560]{1,0:T(8,128)(2,1)S(1)} %get-tuple-element.1303.refs_0_.d_own, bf16[64,2560]{1,0:T(8,128)(2,1)S(1)} %collective-permute-done.51.refs_1_, bf16[64,2560]{1,0:T(8,128)(2,1)S(1)} %collective-permute-done.52.refs_2_, ...), custom_call_target="tpu_custom_call" | custom-call | flops 7000000000 | tf_op jit(solution)/shard_map/pallas_call | solution.py:638
  341.1 14.6 %shard_map.249 = (bf16[512,896]{1,0:T(8,128)(2,1)}, bf16[512,896]{1,0:T(8,128)(2,1)}, bf16[64,2560]{1,0:T(8,128)(2,1)S(1)}, bf16[64,2560]{1,0:T(8,128)(2,1)S(1)}...) custom-call(s32[5]{0:T(128)S(1)} %stack.36.pos, ...), custom_call_target="tpu_custom_call" | custom-call | flops 16000000000 | tf_op jit(solution)/shard_map/pallas_call | solution.py:587
  357.5 6.0 shard_map.250
  363.6 3.9 collective-permute-done.63.three
  368.0 3.7 collective-permute-start.65
  374.1 6.0 shard_map.254
  380.1 3.9 collective-permute-done.64.one
  387.4 3.5 collective-permute-start.67
  390.9 11.1 %collective-permute-done.68.refs_2_ = bf16[64,2560]{1,0:T(8,128)(2,1)S(1)} collective-permute-done((bf16[64,2560]{1,0:T(8,128)(2,1)S(1)}, bf16[64,2560]{1,0:T(8,128)(2,1)S(1)}, u32[]{:S(2)}, u32[]{:S(2)}) %collective-permute-start.68) | collective-permute-done | bytes 327712 | tf_op jit(solution)/shard_map/ppermute | solution.py:52
  402.6 7.4 %collective-permute-done.69.refs_3_ = bf16[64,2560]{1,0:T(8,128)(2,1)S(1)} collective-permute-done((bf16[64,2560]{1,0:T(8,128)(2,1)S(1)}, bf16[64,2560]{1,0:T(8,128)(2,1)S(1)}, u32[]{:S(2)}, u32[]{:S(2)}) %collective-permute-start.69) | collective-permute-done | bytes 327712 | tf_op jit(solution)/shard_map/ppermute | solution.py:52
  413.7 4.6 collective-permute-start.75
  418.2 13.7 %shard_map.255 = (bf16[512,320]{1,0:T(8,128)(2,1)}, f32[512,320]{1,0:T(8,128)}, bf16[512,320]{1,0:T(8,128)(2,1)}, bf16[512,2560]{1,0:T(8,128)(2,1)}) custom-call(s32[5]{0:T(128)S(1)} %stack.36.pos, bf16[512,320]{1,0:T(8,128)(2,1)} %get-tuple-element.1379.q_ref, f32[8,512]{1,0:T(8,128)S(1)} %get-tuple-element.1380.row_ids, ...), custom_call_target="tpu_custom_call" | custom-call | flops 17999998976 | tf_op jit(solution)/shard_map/pallas_call | solution.py:737
  435.9 23.4 %reduce-scatter.7.cloned.1.call-done = bf16[640,896]{1,0:T(8,128)(2,1)} async-done(((bf16[2560,896]{1,0:T(8,128)(2,1)}), bf16[640,896]{1,0:T(8,128)(2,1)}) %reduce-scatter.7.cloned.1.call-update) | async-done | bytes 1146896 | tf_op jit(solution)/shard_map/reduce_scatter | solution.py:996
  466.6 12.6 %shard_map.257 = (bf16[640,512]{1,0:T(8,128)(2,1)}, bf16[640,512]{1,0:T(8,128)(2,1)}, bf16[640,512]{1,0:T(8,128)(2,1)}, bf16[640,512]{1,0:T(8,128)(2,1)}, bf16[4,640,512]{2,1,0:T(8,128)(2,1)}) custom-call(s32[5]{0:T(128)S(1)} %stack.36.pos, bf16[512,2560]{1,0:T(8,128)(2,1)} %get-tuple-element.1477.first, bf16[512,2560]{1,0:T(8,128)(2,1)} %get-tuple-element.1478.d_all, ...), custom_call_target="tpu_custom_call" | custom-call | flops 12000000000 | tf_op jit(solution)/shard_map/pallas_call | solution.py:847
  480.7 7.2 %shard_map.258 = (bf16[64,2560]{1,0:T(8,128)(2,1)S(1)}, bf16[64,2560]{1,0:T(8,128)(2,1)S(1)}, bf16[64,2560]{1,0:T(8,128)(2,1)S(1)}, bf16[64,2560]{1,0:T(8,128)(2...) custom-call(s32[5]{0:T(128)S(1)} %stack.36.pos, bf16[512,384]{1,0:T(8,128)(2,1)} %copy-done.57, ...), custom_call_target="tpu_custom_call" | custom-call | flops 8000000000 | tf_op jit(solution)/shard_map/pallas_call | solution.py:782
  492.1 10.6 %collective-permute-start.66 = (bf16[320,896]{1,0:T(8,128)(2,1)}, bf16[320,896]{1,0:T(8,128)(2,1)S(1)}, u32[]{:S(2)}, u32[]{:S(2)}) collective-permute-start(bf16[320,896]{1,0:T(8,128)(2,1)} %get-tuple-element.1603), channel_id=1, source_target_pairs={{0,16},{8,24},{16,0},{24,8},{1,17},{9,25},{17,1},{25,9},{2,18},{10... | collective-permute-start | bytes 1720328 | tf_op jit(solution)/shard_map/ppermute | solution.py:52
  503.9 4.9 collective-permute-done.85
  511.6 15.4 %collective-permute-done.84 = bf16[640,512]{1,0:T(8,128)(2,1)} collective-permute-done((bf16[640,512]{1,0:T(8,128)(2,1)}, bf16[640,512]{1,0:T(8,128)(2,1)}, u32[]{:S(2)}, u32[]{:S(2)}) %collective-permute-start.84) | collective-permute-done | bytes 655392 | tf_op jit(solution)/shard_map/ppermute | solution.py:52
  538.1 5.6 collective-permute-done.82.one
  553.6 7.7 %collective-permute-done.89.p2 = bf16[64,2560]{1,0:T(8,128)(2,1)S(1)} collective-permute-done((bf16[64,2560]{1,0:T(8,128)(2,1)}, bf16[64,2560]{1,0:T(8,128)(2,1)S(1)}, u32[]{:S(2)}, u32[]{:S(2)}) %collective-permute-start.89) | collective-permute-done | bytes 327712 | tf_op jit(solution)/shard_map/ppermute | solution.py:52
  561.3 8.2 %collective-permute-done.91.refs_2_ = bf16[320,512]{1,0:T(8,128)(2,1)S(1)} collective-permute-done((bf16[320,512]{1,0:T(8,128)(2,1)}, bf16[320,512]{1,0:T(8,128)(2,1)S(1)}, u32[]{:S(2)}, u32[]{:S(2)}) %collective-permute-start.91) | collective-permute-done | bytes 327712 | tf_op jit(solution)/shard_map/ppermute | solution.py:52
  569.5 5.7 collective-permute-done.92.refs_3_
  577.3 7.2 %reduce-scatter.11.cloned.1.call-done = bf16[640,512]{1,0:T(8,128)(2,1)} async-done(((bf16[2560,512]{1,0:T(8,128)(2,1)}), bf16[640,512]{1,0:T(8,128)(2,1)}) %reduce-scatter.11.cloned.1.call-update) | async-done | bytes 655376 | tf_op jit(solution)/shard_map/reduce_scatter | solution.py:996
  587.1 3.1 shard_map.266
  590.2 4.9 collective-permute-done.93.refs_1_
  (415 shorter events, 178.4 us)
Async XLA Ops:
  7.2 171.9 %all-gather.5.cloned.1.call-start = ((), (), s32[]{:S(2)}) async-start(), calls=%async_computation.8 | async-start | bytes 9011200 | tf_op jit(solution)/shard_map/all_gather | solution.py:992
  25.2 37.4 %collective-permute-start.1 = (bf16[320,1408]{1,0:T(8,128)(2,1)}, bf16[320,1408]{1,0:T(8,128)(2,1)}, u32[]{:S(2)}, u32[]{:S(2)}) collective-permute-start(bf16[320,1408]{1,0:T(8,128)(2,1)} %get-tuple-element.814), channel_id=1, source_target_pairs={{0,8},{8,0},{16,24},{24,16},{1,9},{9,1},{17,25},{25,17},{2,10},{10... | collective-permute-start | bytes 2703368 | tf_op jit(solution)/shard_map/ppermute | solution.py:52
  27.0 27.7 %collective-permute-start.5 = (bf16[320,512]{1,0:T(8,128)(2,1)S(1)}, bf16[320,512]{1,0:T(8,128)(2,1)}, u32[]{:S(2)}, u32[]{:S(2)}) collective-permute-start(bf16[320,512]{1,0:T(8,128)(2,1)S(1)} %get-tuple-element.820), channel_id=1, source_target_pairs={{0,16},{8,24},{16,0},{24,8},{1,17},{9,25},{17,1},{25,9},{2,18},{10... | collective-permute-start | bytes 983048 | tf_op jit(solution)/shard_map/ppermute | solution.py:52
  29.5 33.1 %collective-permute-start.6 = (bf16[320,512]{1,0:T(8,128)(2,1)}, bf16[320,512]{1,0:T(8,128)(2,1)}, u32[]{:S(2)}, u32[]{:S(2)}) collective-permute-start(bf16[320,512]{1,0:T(8,128)(2,1)} %get-tuple-element.821), channel_id=1, source_target_pairs={{0,24},{8,16},{16,8},{24,0},{1,25},{9,17},{17,9},{25,1},{2,26},{10... | collective-permute-start | bytes 983048 | tf_op jit(solution)/shard_map/ppermute | solution.py:52
  29.6 33.0 %collective-permute-start.3 = (bf16[320,512]{1,0:T(8,128)(2,1)}, bf16[320,512]{1,0:T(8,128)(2,1)}, u32[]{:S(2)}, u32[]{:S(2)}) collective-permute-start(bf16[320,512]{1,0:T(8,128)(2,1)} %get-tuple-element.1519.refs_8_.refs_2_.refs_10_.refs_4_.refs_0_), channel_id=1, source_target_pairs={{0,2},{2,0},{1,3},{3,1},{4,6},{6,4},{5,7},{7,5},{8,10},{10,8},{9,1... | collective-permute-start | bytes 983048 | tf_op jit(solution)/shard_map/ppermute | solution.py:52
  31.3 31.4 %collective-permute-start.2 = (bf16[320,512]{1,0:T(8,128)(2,1)}, bf16[320,512]{1,0:T(8,128)(2,1)}, u32[]{:S(2)}, u32[]{:S(2)}) collective-permute-start(bf16[320,512]{1,0:T(8,128)(2,1)} %get-tuple-element.1519.refs_8_.refs_2_.refs_10_.refs_4_.refs_0_), channel_id=1, source_target_pairs={{0,4},{4,0},{1,5},{5,1},{2,6},{6,2},{3,7},{7,3},{8,12},{12,8},{9,1... | collective-permute-start | bytes 983048 | tf_op jit(solution)/shard_map/ppermute | solution.py:52
  65.2 184.7 %all-gather.7.cloned.1.call-start = ((), (), s32[]{:S(2)}) async-start(), calls=%async_computation.9 | async-start | bytes 4505600 | tf_op jit(solution)/shard_map/all_gather | solution.py:992
  68.9 20.9 %collective-permute-start.8 = (bf16[320,512]{1,0:T(8,128)(2,1)}, bf16[320,512]{1,0:T(8,128)(2,1)S(1)}, u32[]{:S(2)}, u32[]{:S(2)}) collective-permute-start(bf16[320,512]{1,0:T(8,128)(2,1)} %collective-permute-done.refs_10_.refs_4_.refs_12_.refs_6_.refs_2_), channel_id=1, source_target_pairs={{0,4},{4,0},{1,5},{5,1},{2,6},{6,2},{3,7},{7,3},{8,12},{12,8},{9,1... | collective-permute-start | bytes 983048 | tf_op jit(solution)/shard_map/ppermute | solution.py:52
  69.4 34.0 %collective-permute-start.18 = (bf16[64,2688]{1,0:T(8,128)(2,1)S(1)}, bf16[64,2688]{1,0:T(8,128)(2,1)S(1)}, u32[]{:S(2)}, u32[]{:S(2)}) collective-permute-start(bf16[64,2688]{1,0:T(8,128)(2,1)S(1)} %copy-done.12), channel_id=1, source_target_pairs={{0,16},{8,24},{16,0},{24,8},{1,17},{9,25},{17,1},{25,9},{2,18},{10... | collective-permute-start | bytes 1032200 | tf_op jit(solution)/shard_map/ppermute | solution.py:52
  72.2 21.1 %collective-permute-start.15 = (bf16[320,512]{1,0:T(8,128)(2,1)}, bf16[320,512]{1,0:T(8,128)(2,1)S(1)}, u32[]{:S(2)}, u32[]{:S(2)}) collective-permute-start(bf16[320,512]{1,0:T(8,128)(2,1)} %collective-permute-done.6.refs_14_.refs_8_.refs_16_.refs_10_.refs_6_), channel_id=1, source_target_pairs={{0,2},{2,0},{1,3},{3,1},{4,6},{6,4},{5,7},{7,5},{8,10},{10,8},{9,1... | collective-permute-start | bytes 983048 | tf_op jit(solution)/shard_map/ppermute | solution.py:52
  76.7 25.6 %collective-permute-start.10 = (bf16[320,512]{1,0:T(8,128)(2,1)}, bf16[320,512]{1,0:T(8,128)(2,1)S(1)}, u32[]{:S(2)}, u32[]{:S(2)}) collective-permute-start(bf16[320,512]{1,0:T(8,128)(2,1)} %collective-permute-done.6.refs_14_.refs_8_.refs_16_.refs_10_.refs_6_), channel_id=1, source_target_pairs={{0,4},{4,0},{1,5},{5,1},{2,6},{6,2},{3,7},{7,3},{8,12},{12,8},{9,1... | collective-permute-start | bytes 983048 | tf_op jit(solution)/shard_map/ppermute | solution.py:52
  79.2 25.1 %collective-permute-start.13 = (bf16[320,512]{1,0:T(8,128)(2,1)}, bf16[320,512]{1,0:T(8,128)(2,1)S(1)}, u32[]{:S(2)}, u32[]{:S(2)}) collective-permute-start(bf16[320,512]{1,0:T(8,128)(2,1)} %collective-permute-done.5.refs_12_.refs_6_.refs_14_.refs_8_.refs_4_), channel_id=1, source_target_pairs={{0,2},{2,0},{1,3},{3,1},{4,6},{6,4},{5,7},{7,5},{8,10},{10,8},{9,1... | collective-permute-start | bytes 983048 | tf_op jit(solution)/shard_map/ppermute | solution.py:52
  89.8 28.7 %collective-permute-start.7 = (bf16[320,896]{1,0:T(8,128)(2,1)S(1)}, bf16[320,896]{1,0:T(8,128)(2,1)S(1)}, u32[]{:S(2)}, u32[]{:S(2)}) collective-permute-start(bf16[320,896]{1,0:T(8,128)(2,1)S(1)} %copy-done.8), channel_id=1, source_target_pairs={{0,16},{8,24},{16,0},{24,8},{1,17},{9,25},{17,1},{25,9},{2,18},{10... | collective-permute-start | bytes 1720328 | tf_op jit(solution)/shard_map/ppermute | solution.py:52
  93.3 24.2 %collective-permute-start.20 = (bf16[64,2688]{1,0:T(8,128)(2,1)S(1)}, bf16[64,2688]{1,0:T(8,128)(2,1)S(1)}, u32[]{:S(2)}, u32[]{:S(2)}) collective-permute-start(bf16[64,2688]{1,0:T(8,128)(2,1)S(1)} %copy-done.12), channel_id=1, source_target_pairs={{0,1},{1,0},{2,3},{3,2},{4,5},{5,4},{6,7},{7,6},{8,9},{9,8},{10,11... | collective-permute-start | bytes 1032200 | tf_op jit(solution)/shard_map/ppermute | solution.py:52
  102.4 16.2 %collective-permute-start.17 = (bf16[64,2688]{1,0:T(8,128)(2,1)S(1)}, bf16[64,2688]{1,0:T(8,128)(2,1)S(1)}, u32[]{:S(2)}, u32[]{:S(2)}) collective-permute-start(bf16[64,2688]{1,0:T(8,128)(2,1)S(1)} %copy-done.12), channel_id=1, source_target_pairs={{0,8},{8,0},{16,24},{24,16},{1,9},{9,1},{17,25},{25,17},{2,10},{10... | collective-permute-start | bytes 1032200 | tf_op jit(solution)/shard_map/ppermute | solution.py:52
  131.6 18.5 %collective-permute-start.24 = (bf16[320,512]{1,0:T(8,128)(2,1)}, bf16[320,512]{1,0:T(8,128)(2,1)S(1)}, u32[]{:S(2)}, u32[]{:S(2)}) collective-permute-start(bf16[320,512]{1,0:T(8,128)(2,1)} %get-tuple-element.872), channel_id=1, source_target_pairs={{0,16},{8,24},{16,0},{24,8},{1,17},{9,25},{17,1},{25,9},{2,18},{10... | collective-permute-start | bytes 983048 | tf_op jit(solution)/shard_map/ppermute | solution.py:52
  151.2 260.4 %reduce-scatter.9.cloned.1.call-start = ((), (), s32[]{:S(2)}) async-start(), calls=%async_computation.6 | async-start | bytes 6553600 | tf_op jit(solution)/shard_map/reduce_scatter | solution.py:996
  151.2 16.2 %collective-permute-start.26 = (bf16[512,384]{1,0:T(8,128)(2,1)S(1)}, bf16[512,384]{1,0:T(8,128)(2,1)S(1)}, u32[]{:S(2)}, u32[]{:S(2)}) collective-permute-start(bf16[512,384]{1,0:T(8,128)(2,1)S(1)} %copy-done.86), channel_id=1, source_target_pairs={{0,4},{4,0},{1,5},{5,1},{2,6},{6,2},{3,7},{7,3},{8,12},{12,8},{9,1... | collective-permute-start | bytes 1179656 | tf_op jit(solution)/shard_map/ppermute | solution.py:52
  151.3 27.7 %collective-permute-start.25 = (bf16[320,896]{1,0:T(8,128)(2,1)S(1)}, bf16[320,896]{1,0:T(8,128)(2,1)}, u32[]{:S(2)}, u32[]{:S(2)}) collective-permute-start(bf16[320,896]{1,0:T(8,128)(2,1)S(1)} %copy-done.6), channel_id=1, source_target_pairs={{0,24},{8,16},{16,8},{24,0},{1,25},{9,17},{17,9},{25,1},{2,26},{10... | collective-permute-start | bytes 1720328 | tf_op jit(solution)/shard_map/ppermute | solution.py:52
  179.6 23.9 %collective-permute-start.29 = (bf16[320,896]{1,0:T(8,128)(2,1)}, bf16[320,896]{1,0:T(8,128)(2,1)S(1)}, u32[]{:S(2)}, u32[]{:S(2)}) collective-permute-start(bf16[320,896]{1,0:T(8,128)(2,1)} %collective-permute-done.25.refs_10_.refs_6_), channel_id=1, source_target_pairs={{0,2},{2,0},{1,3},{3,1},{4,6},{6,4},{5,7},{7,5},{8,10},{10,8},{9,1... | collective-permute-start | bytes 1720328 | tf_op jit(solution)/shard_map/ppermute | solution.py:52
  181.7 22.3 %collective-permute-start.28 = (bf16[320,896]{1,0:T(8,128)(2,1)}, bf16[320,896]{1,0:T(8,128)(2,1)S(1)}, u32[]{:S(2)}, u32[]{:S(2)}) collective-permute-start(bf16[320,896]{1,0:T(8,128)(2,1)} %collective-permute-done.25.refs_10_.refs_6_), channel_id=1, source_target_pairs={{0,4},{4,0},{1,5},{5,1},{2,6},{6,2},{3,7},{7,3},{8,12},{12,8},{9,1... | collective-permute-start | bytes 1720328 | tf_op jit(solution)/shard_map/ppermute | solution.py:52
  182.1 17.0 %collective-permute-start.27 = (bf16[320,512]{1,0:T(8,128)(2,1)S(1)}, bf16[320,512]{1,0:T(8,128)(2,1)S(1)}, u32[]{:S(2)}, u32[]{:S(2)}) collective-permute-start(bf16[320,512]{1,0:T(8,128)(2,1)S(1)} %copy-done.32), channel_id=1, source_target_pairs={{0,24},{8,16},{16,8},{24,0},{1,25},{9,17},{17,9},{25,1},{2,26},{10... | collective-permute-start | bytes 983048 | tf_op jit(solution)/shard_map/ppermute | solution.py:52
  205.5 17.0 %collective-permute-start.38 = (bf16[64,2560]{1,0:T(8,128)(2,1)S(1)}, bf16[64,2560]{1,0:T(8,128)(2,1)S(1)}, u32[]{:S(2)}, u32[]{:S(2)}) collective-permute-start(bf16[64,2560]{1,0:T(8,128)(2,1)S(1)} %get-tuple-element.994), channel_id=1, source_target_pairs={{0,16},{8,24},{16,0},{24,8},{1,17},{9,25},{17,1},{25,9},{2,18},{10... | collective-permute-start | bytes 983048 | tf_op jit(solution)/shard_map/ppermute | solution.py:52
  224.2 24.9 %collective-permute-start.33 = (bf16[320,896]{1,0:T(8,128)(2,1)S(1)}, bf16[320,896]{1,0:T(8,128)(2,1)S(1)}, u32[]{:S(2)}, u32[]{:S(2)}) collective-permute-start(bf16[320,896]{1,0:T(8,128)(2,1)S(1)} %collective-permute-done.29.refs_12_.refs_8_), channel_id=1, source_target_pairs={{0,4},{4,0},{1,5},{5,1},{2,6},{6,2},{3,7},{7,3},{8,12},{12,8},{9,1... | collective-permute-start | bytes 1720328 | tf_op jit(solution)/shard_map/ppermute | solution.py:52
  225.9 21.7 %collective-permute-start.34 = (bf16[320,512]{1,0:T(8,128)(2,1)S(1)}, bf16[320,512]{1,0:T(8,128)(2,1)S(1)}, u32[]{:S(2)}, u32[]{:S(2)}) collective-permute-start(bf16[320,512]{1,0:T(8,128)(2,1)S(1)} %collective-permute-done.27.refs_14_.refs_10_), channel_id=1, source_target_pairs={{0,4},{4,0},{1,5},{5,1},{2,6},{6,2},{3,7},{7,3},{8,12},{12,8},{9,1... | collective-permute-start | bytes 983048 | tf_op jit(solution)/shard_map/ppermute | solution.py:52
  227.3 21.7 %collective-permute-start.39 = (bf16[64,2560]{1,0:T(8,128)(2,1)S(1)}, bf16[64,2560]{1,0:T(8,128)(2,1)S(1)}, u32[]{:S(2)}, u32[]{:S(2)}) collective-permute-start(bf16[64,2560]{1,0:T(8,128)(2,1)S(1)} %get-tuple-element.1021.refs_0_), channel_id=1, source_target_pairs={{0,8},{8,0},{16,24},{24,16},{1,9},{9,1},{17,25},{25,17},{2,10},{10... | collective-permute-start | bytes 983048 | tf_op jit(solution)/shard_map/ppermute | solution.py:52
  285.7 16.0 %collective-permute-start.49 = (bf16[64,2560]{1,0:T(8,128)(2,1)S(1)}, bf16[64,2560]{1,0:T(8,128)(2,1)S(1)}, u32[]{:S(2)}, u32[]{:S(2)}) collective-permute-start(bf16[64,2560]{1,0:T(8,128)(2,1)S(1)} %get-tuple-element.1045), channel_id=1, source_target_pairs={{0,8},{8,0},{16,24},{24,16},{1,9},{9,1},{17,25},{25,17},{2,10},{10... | collective-permute-start | bytes 983048 | tf_op jit(solution)/shard_map/ppermute | solution.py:52
  302.3 16.1 %collective-permute-start.52 = (bf16[64,2560]{1,0:T(8,128)(2,1)S(1)}, bf16[64,2560]{1,0:T(8,128)(2,1)S(1)}, u32[]{:S(2)}, u32[]{:S(2)}) collective-permute-start(bf16[64,2560]{1,0:T(8,128)(2,1)S(1)} %get-tuple-element.1303.refs_0_.d_own), channel_id=1, source_target_pairs={{0,16},{8,24},{16,0},{24,8},{1,17},{9,25},{17,1},{25,9},{2,18},{10... | collective-permute-start | bytes 983048 | tf_op jit(solution)/shard_map/ppermute | solution.py:52
  337.8 121.5 %reduce-scatter.7.cloned.1.call-start = ((), (), s32[]{:S(2)}) async-start(), calls=%async_computation.5 | async-start | bytes 5734400 | tf_op jit(solution)/shard_map/reduce_scatter | solution.py:996
  367.6 180.0 %reduce-scatter.5.cloned.1.call-start = ((), (), s32[]{:S(2)}) async-start(), calls=%async_computation.4 | async-start | bytes 5734400 | tf_op jit(solution)/shard_map/reduce_scatter | solution.py:996
  367.7 16.3 %collective-permute-start.64 = (bf16[64,2560]{1,0:T(8,128)(2,1)S(1)}, bf16[64,2560]{1,0:T(8,128)(2,1)S(1)}, u32[]{:S(2)}, u32[]{:S(2)}) collective-permute-start(bf16[64,2560]{1,0:T(8,128)(2,1)S(1)} %get-tuple-element.1300), channel_id=1, source_target_pairs={{0,8},{8,0},{16,24},{24,16},{1,9},{9,1},{17,25},{25,17},{2,10},{10... | collective-permute-start | bytes 983048 | tf_op jit(solution)/shard_map/ppermute | solution.py:52
  368.0 15.9 %collective-permute-start.65 = (bf16[64,2560]{1,0:T(8,128)(2,1)S(1)}, bf16[64,2560]{1,0:T(8,128)(2,1)S(1)}, u32[]{:S(2)}, u32[]{:S(2)}) collective-permute-start(bf16[64,2560]{1,0:T(8,128)(2,1)S(1)} %get-tuple-element.1301), channel_id=1, source_target_pairs={{0,16},{8,24},{16,0},{24,8},{1,17},{9,25},{17,1},{25,9},{2,18},{10... | collective-permute-start | bytes 983048 | tf_op jit(solution)/shard_map/ppermute | solution.py:52
  385.5 199.0 %reduce-scatter.11.cloned.1.call-start = ((), (), s32[]{:S(2)}) async-start(), calls=%async_computation.7 | async-start | bytes 3276800 | tf_op jit(solution)/shard_map/reduce_scatter | solution.py:996
  385.7 16.3 %collective-permute-start.68 = (bf16[64,2560]{1,0:T(8,128)(2,1)S(1)}, bf16[64,2560]{1,0:T(8,128)(2,1)S(1)}, u32[]{:S(2)}, u32[]{:S(2)}) collective-permute-start(bf16[64,2560]{1,0:T(8,128)(2,1)S(1)} %get-tuple-element.1382.refs_0_), channel_id=1, source_target_pairs={{0,16},{8,24},{16,0},{24,8},{1,17},{9,25},{17,1},{25,9},{2,18},{10... | collective-permute-start | bytes 983048 | tf_op jit(solution)/shard_map/ppermute | solution.py:52
  413.7 18.2 %collective-permute-start.75 = (bf16[320,512]{1,0:T(8,128)(2,1)S(1)}, bf16[320,512]{1,0:T(8,128)(2,1)S(1)}, u32[]{:S(2)}, u32[]{:S(2)}) collective-permute-start(bf16[320,512]{1,0:T(8,128)(2,1)S(1)} %get-tuple-element.1598), channel_id=1, source_target_pairs={{0,24},{8,16},{16,8},{24,0},{1,25},{9,17},{17,9},{25,1},{2,26},{10... | collective-permute-start | bytes 983048 | tf_op jit(solution)/shard_map/ppermute | solution.py:52
  434.1 29.7 %collective-permute-start.77 = (bf16[512,320]{1,0:T(8,128)(2,1)}, bf16[512,320]{1,0:T(8,128)(2,1)S(1)}, u32[]{:S(2)}, u32[]{:S(2)}) collective-permute-start(bf16[512,320]{1,0:T(8,128)(2,1)} %get-tuple-element.1434), channel_id=1, source_target_pairs={{0,4},{4,0},{1,5},{5,1},{2,6},{6,2},{3,7},{7,3},{8,12},{12,8},{9,1... | collective-permute-start | bytes 983048 | tf_op jit(solution)/shard_map/ppermute | solution.py:52
  434.7 31.9 %collective-permute-start.76 = (bf16[320,512]{1,0:T(8,128)(2,1)}, bf16[320,512]{1,0:T(8,128)(2,1)}, u32[]{:S(2)}, u32[]{:S(2)}) collective-permute-start(bf16[320,512]{1,0:T(8,128)(2,1)} %get-tuple-element.1429), channel_id=1, source_target_pairs={{0,16},{8,24},{16,0},{24,8},{1,17},{9,25},{17,1},{25,9},{2,18},{10... | collective-permute-start | bytes 983048 | tf_op jit(solution)/shard_map/ppermute | solution.py:52
  461.5 17.6 %collective-permute-start.78 = (bf16[320,896]{1,0:T(8,128)(2,1)S(1)}, bf16[320,896]{1,0:T(8,128)(2,1)S(1)}, u32[]{:S(2)}, u32[]{:S(2)}) collective-permute-start(bf16[320,896]{1,0:T(8,128)(2,1)S(1)} %get-tuple-element.1602), channel_id=1, source_target_pairs={{0,24},{8,16},{16,8},{24,0},{1,25},{9,17},{17,9},{25,1},{2,26},{10... | collective-permute-start | bytes 1720328 | tf_op jit(solution)/shard_map/ppermute | solution.py:52
  479.2 29.6 %collective-permute-start.85 = (bf16[640,512]{1,0:T(8,128)(2,1)}, bf16[640,512]{1,0:T(8,128)(2,1)}, u32[]{:S(2)}, u32[]{:S(2)}) collective-permute-start(bf16[640,512]{1,0:T(8,128)(2,1)} %get-tuple-element.1563), channel_id=1, source_target_pairs={{0,2},{2,0},{1,3},{3,1},{4,6},{6,4},{5,7},{7,5},{8,10},{10,8},{9,1... | collective-permute-start | bytes 1966088 | tf_op jit(solution)/shard_map/ppermute | solution.py:52
  490.8 37.5 %collective-permute-start.79 = (bf16[192,2560]{1,0:T(8,128)(2,1)}, bf16[192,2560]{1,0:T(8,128)(2,1)S(1)}, u32[]{:S(2)}, u32[]{:S(2)}) collective-permute-start(bf16[192,2560]{1,0:T(8,128)(2,1)} %get-tuple-element.1536), channel_id=1, source_target_pairs={{0,1},{1,0},{2,3},{3,2},{4,5},{5,4},{6,7},{7,6},{8,9},{9,8},{10,11... | collective-permute-start | bytes 2949128 | tf_op jit(solution)/shard_map/ppermute | solution.py:52
  491.3 35.7 %collective-permute-start.84 = (bf16[640,512]{1,0:T(8,128)(2,1)}, bf16[640,512]{1,0:T(8,128)(2,1)}, u32[]{:S(2)}, u32[]{:S(2)}) collective-permute-start(bf16[640,512]{1,0:T(8,128)(2,1)} %get-tuple-element.1561), channel_id=1, source_target_pairs={{0,2},{2,0},{1,3},{3,1},{4,6},{6,4},{5,7},{7,5},{8,10},{10,8},{9,1... | collective-permute-start | bytes 1966088 | tf_op jit(solution)/shard_map/ppermute | solution.py:52
  492.1 55.2 %collective-permute-start.66 = (bf16[320,896]{1,0:T(8,128)(2,1)}, bf16[320,896]{1,0:T(8,128)(2,1)S(1)}, u32[]{:S(2)}, u32[]{:S(2)}) collective-permute-start(bf16[320,896]{1,0:T(8,128)(2,1)} %get-tuple-element.1603), channel_id=1, source_target_pairs={{0,16},{8,24},{16,0},{24,8},{1,17},{9,25},{17,1},{25,9},{2,18},{10... | collective-permute-start | bytes 1720328 | tf_op jit(solution)/shard_map/ppermute | solution.py:52
  503.8 24.4 %collective-permute-start.81 = (bf16[64,2560]{1,0:T(8,128)(2,1)S(1)}, bf16[64,2560]{1,0:T(8,128)(2,1)S(1)}, u32[]{:S(2)}, u32[]{:S(2)}) collective-permute-start(bf16[64,2560]{1,0:T(8,128)(2,1)S(1)} %shard_map.259), channel_id=1, source_target_pairs={{0,8},{8,0},{16,24},{24,16},{1,9},{9,1},{17,25},{25,17},{2,10},{10... | collective-permute-start | bytes 983048 | tf_op jit(solution)/shard_map/ppermute | solution.py:52
  510.0 27.1 %collective-permute-start.86 = (bf16[640,512]{1,0:T(8,128)(2,1)S(1)}, bf16[640,512]{1,0:T(8,128)(2,1)S(1)}, u32[]{:S(2)}, u32[]{:S(2)}) collective-permute-start(bf16[640,512]{1,0:T(8,128)(2,1)S(1)} %add_convert_fusion), channel_id=1, source_target_pairs={{0,4},{4,0},{1,5},{5,1},{2,6},{6,2},{3,7},{7,3},{8,12},{12,8},{9,1... | collective-permute-start | bytes 1966088 | tf_op jit(solution)/shard_map/ppermute | solution.py:52
  549.1 26.1 %collective-permute-start.87 = (bf16[320,896]{1,0:T(8,128)(2,1)S(1)}, bf16[320,896]{1,0:T(8,128)(2,1)S(1)}, u32[]{:S(2)}, u32[]{:S(2)}) collective-permute-start(bf16[320,896]{1,0:T(8,128)(2,1)S(1)} %get-tuple-element.1566), channel_id=1, source_target_pairs={{0,8},{8,0},{16,24},{24,16},{1,9},{9,1},{17,25},{25,17},{2,10},{10... | collective-permute-start | bytes 1720328 | tf_op jit(solution)/shard_map/ppermute | solution.py:52
  549.4 20.0 %collective-permute-start.91 = (bf16[320,512]{1,0:T(8,128)(2,1)}, bf16[320,512]{1,0:T(8,128)(2,1)S(1)}, u32[]{:S(2)}, u32[]{:S(2)}) collective-permute-start(bf16[320,512]{1,0:T(8,128)(2,1)} %get-tuple-element.1571), channel_id=1, source_target_pairs={{0,16},{8,24},{16,0},{24,8},{1,17},{9,25},{17,1},{25,9},{2,18},{10... | collective-permute-start | bytes 983048 | tf_op jit(solution)/shard_map/ppermute | solution.py:52
  552.0 23.2 %collective-permute-start.92 = (bf16[320,512]{1,0:T(8,128)(2,1)}, bf16[320,512]{1,0:T(8,128)(2,1)S(1)}, u32[]{:S(2)}, u32[]{:S(2)}) collective-permute-start(bf16[320,512]{1,0:T(8,128)(2,1)} %get-tuple-element.1572), channel_id=1, source_target_pairs={{0,24},{8,16},{16,8},{24,0},{1,25},{9,17},{17,9},{25,1},{2,26},{10... | collective-permute-start | bytes 983048 | tf_op jit(solution)/shard_map/ppermute | solution.py:52
  553.6 21.6 %collective-permute-start.88 = (bf16[64,2560]{1,0:T(8,128)(2,1)}, bf16[64,2560]{1,0:T(8,128)(2,1)S(1)}, u32[]{:S(2)}, u32[]{:S(2)}) collective-permute-start(bf16[64,2560]{1,0:T(8,128)(2,1)} %shard_map.262.p0), channel_id=1, source_target_pairs={{0,1},{1,0},{2,3},{3,2},{4,5},{5,4},{6,7},{7,6},{8,9},{9,8},{10,11... | collective-permute-start | bytes 983048 | tf_op jit(solution)/shard_map/ppermute | solution.py:52
  (154 other events, 1747.1 us)
Sparse Core Ops, SparseCore 0:
  65.3 104.2 all-gather.4
  172.1 58.9 all-gather.6
  337.9 60.5 reduce-scatter.8
  401.4 57.7 reduce-scatter.6
  462.2 77.5 reduce-scatter.4
  542.6 41.8 reduce-scatter.10
